TPU v7x, 128 devices: a whole 4x4x4 slice. The times are simulated.
128 devices in a mesh: node: 16 (over x_hi, z, core), feat: 8 (over x_lo, y).
Axes of the slice: x: 4 (x_hi: 2, x_lo: 2; x = x_hi * 2 + x_lo), y: 4, z: 4, core: 2. Of those that a mesh axis runs over, the one named last changes fastest.
Arguments:
- features: bfloat16 [128, 98304], P('feat', 'node'), may hold values from -6 to 6
- weight: bfloat16 [128, 256], P('feat'), may hold values from -0.5 to 0.5
- bias: float32 [256], P('feat'), may hold values from -3 to 3
- block_values: bfloat16 [768, 12, 128, 128], P('node'), may hold values from -0.21875 to 0.21875
- block_cols: int32 [768, 12], P('node'), may hold values from 0 to 767
- block_counts: int32 [768], P('node'), may hold values from 1 to 12, as said below
- train_mask: int32 [98304], P('node'), may hold values 0 or 1
- cotangent: bfloat16 [256, 98304], P('feat', 'node'), may hold values from -6 to 6
Outputs:
- activation: bfloat16 [256, 98304], P('feat', 'node')
- grad_features: bfloat16 [128, 98304], P('feat', 'node')
- grad_weight: float32 [128, 256], P('feat')
Inputs may be any that keep to these rules, and one draw needn't show every extreme that they name: `block_counts`: block row 0 has all 12 slots live.
All inputs are finite; a program needn't handle non-finite values. No bound on the sum of `train_mask` on one device may be relied on, other than what follows from the above.
Results may differ from a plain program's by a relative error of at most 0.022.
Values may be sent and summed in bfloat16 or wider, within the bound.
No kernel may reach another device: no remote copies, remote signals or barrier semaphores. Data moves between devices by JAX's collectives and lax.ppermute only.
A program may use at most 128 MiB of HBM per device.

v0:
```python
import jax
import jax.numpy as jnp
from jax import lax
from jax.sharding import PartitionSpec as P


def silu_slope(preact):
    sigma = jax.nn.sigmoid(preact)
    return sigma * (1.0 + preact * (1.0 - sigma))


def local(features, weight, bias, block_values, block_cols, block_counts, train_mask, cotangent):
    block_dev = block_values.shape[0]
    slot_count = block_values.shape[1]
    block_width = block_values.shape[2]
    in_local = features.shape[0]
    rows_local = features.shape[1]
    all_blocks = block_dev * lax.axis_size("node")
    nothing = jnp.zeros((), jnp.bfloat16)
    gathered = lax.all_gather(features, "node", axis=1, tiled=True).reshape(
        in_local, all_blocks, block_width
    )
    living_slots = jnp.arange(slot_count, dtype=jnp.int32)[None, :] < block_counts[:, None]
    picked = jnp.take(gathered, block_cols, axis=1)
    picked = jnp.where(living_slots[None, :, :, None], picked, nothing)
    aggregate = jnp.einsum(
        "fnsk,nskm->fnm", picked, block_values, preferred_element_type=jnp.float32
    )
    mixed = aggregate.reshape(in_local, rows_local).astype(jnp.bfloat16)
    partial_value = lax.dot_general(
        weight, mixed, (((0,), (0,)), ((), ())), preferred_element_type=jnp.float32
    )
    projected = lax.psum_scatter(
        partial_value.astype(jnp.bfloat16), "feat", scatter_dimension=0, tiled=True
    ).astype(jnp.float32)
    preact = projected + bias[:, None]
    activation = jax.nn.silu(preact).astype(jnp.bfloat16)
    grad_pre = (
        cotangent.astype(jnp.float32) * train_mask.astype(jnp.float32)[None, :] * silu_slope(preact)
    ).astype(jnp.bfloat16)
    shard_rows = lax.all_gather(grad_pre, "feat", axis=0, tiled=True)
    grad_in = jnp.dot(weight, shard_rows, preferred_element_type=jnp.float32)
    product_block = lax.dot_general(
        mixed, shard_rows, (((1,), (1,)), ((), ())), preferred_element_type=jnp.float32
    )
    grad_w = product_block
    grad_in, grad_w = (grad_in, grad_w)
    grad_weight = lax.psum(grad_w, "node")
    grad_blocks = grad_in.astype(jnp.bfloat16).reshape(in_local, block_dev, block_width)
    contrib = jnp.einsum(
        "fnm,nskm->nsfk", grad_blocks, block_values, preferred_element_type=jnp.float32
    )
    contrib = jnp.where(living_slots[:, :, None, None], contrib, 0.0)
    contrib = contrib.reshape(block_dev * slot_count, in_local, block_width)
    partial_grad = jax.ops.segment_sum(contrib, block_cols.reshape(-1), num_segments=all_blocks)
    summed = lax.psum_scatter(
        partial_grad.astype(jnp.bfloat16), "node", scatter_dimension=0, tiled=True
    ).astype(jnp.float32)
    grad_features = summed.transpose(1, 0, 2).reshape(in_local, rows_local).astype(jnp.bfloat16)
    return (activation, grad_features, grad_weight)


def solution(mesh):
    placed = (
        P("feat", "node"),
        P("feat", None),
        P("feat"),
        P("node", None, None, None),
        P("node", None),
        P("node"),
        P("node"),
        P("feat", "node"),
    )
    return jax.shard_map(
        local,
        mesh=mesh,
        in_specs=placed,
        out_specs=(P("feat", "node"), P("feat", "node"), P("feat", None)),
        check_vma=False,
    )
```

profile of v0, /device:TPU:1, one launch (start us, length us, event | category | flops | bytes accessed | tf_op | source)
XLA Modules:
  0.0 348.2 jit_solution(5191686236338545950)
XLA Ops:
  7.2 0.7 all-gather.3.cloned.1.call-update
  8.0 0.7 compare_and_fusion
  8.8 0.7 compare_select_fusion
  9.7 0.7 iota_compare_fusion
  10.4 54.7 %all-gather.3.cloned.1.call-done = bf16[16,98304]{1,0:T(8,128)(2,1)} async-done(((bf16[16,6144]{1,0:T(8,128)(2,1)}), bf16[16,98304]{1,0:T(8,128)(2,1)}) %all-gather.3.cloned.1.call-update) | async-done | bytes 3145744 | tf_op jit(solution)/shard_map/all_gather | solution.py:20
  65.1 2.4 copy_bitcast_fusion
  67.5 3.2 gather_fusion
  70.7 8.5 %fusion.16 = bf16[48,2,8,128]{3,2,1,0:T(8,128)(2,1)S(1)} fusion(bf16[48,12,128,128]{3,2,1,0:T(8,128)(2,1)} %param.11, bf16[48,12,16,128]{3,2,1,0:T(8,128)(2,1)} %bitcast.55, pred[48,12]{1,0:T(8,128)(4,1)S(1)} %iota_compare_fusion, pred[48,12]{1,0:T(8,128)(4,1)S(1)} %copy.42), kind=kOutput, calls=%fused_computation.18 | convolution fusion | flops 304447488 | bytes 21431424 | tf_op jit(solution)/shard_map/fnsk,nskm->fnm/dot_general | solution.py:26
  79.2 1.0 fusion
  80.3 3.1 copy.54
  83.4 0.7 copy-done.4
  84.1 40.4 %reduce-scatter.7.cloned.1.call-done = bf16[32,6144]{1,0:T(8,128)(2,1)} async-done(((bf16[256,6144]{1,0:T(8,128)(2,1)}), bf16[32,6144]{1,0:T(8,128)(2,1)}) %reduce-scatter.7.cloned.1.call-update) | async-done | bytes 393232 | tf_op jit(solution)/shard_map/reduce_scatter | solution.py:33
  124.5 2.3 multiply_convert_fusion
  127.1 44.5 %all-gather.5.cloned.1.call-done = bf16[256,6144]{1,0:T(8,128)(2,1)} async-done(((bf16[32,6144]{1,0:T(8,128)(2,1)}), bf16[256,6144]{1,0:T(8,128)(2,1)}) %all-gather.5.cloned.1.call-update) | async-done | bytes 3145744 | tf_op jit(solution)/shard_map/all_gather | solution.py:41
  171.5 2.4 fusion.15
  174.0 10.4 %broadcast_select_fusion = f32[48,16,12,128]{3,1,2,0:T(8,128)} fusion(pred[48,12]{1,0:T(8,128)(4,1)S(1)} %iota_compare_fusion, bf16[48,12,128,128]{3,2,1,0:T(8,128)(2,1)} %param.11, bf16[16,48,128,1]{2,1,0,3:T(8,128)(2,1)S(1)} %bitcast.56), kind=kOutput, calls=%fused_computation.10 | convolution fusion | flops 303169536 | bytes 23790144 | tf_op jit(solution)/shard_map/fnm,nskm->nsfk/dot_general | solution.py:50
  184.4 3.1 broadcast_in_dim.50
  187.4 70.8 %scatter_fusion = f32[768,16,128]{2,1,0:T(8,128)} fusion(f32[768,16,128]{2,1,0:T(8,128)} %broadcast_in_dim.50, s32[576]{0:T(1024)S(1)} %reshape.79, f32[576,16,128]{2,1,0:T(8,128)} %bitcast.54), kind=kCustom, calls=%fused_computation.1 | custom fusion | flops 1179648 | bytes 14158080 | tf_op jit(solution)/shard_map/scatter-add | solution.py:55
  258.2 4.9 %convert_element_type.59 = bf16[768,16,128]{2,1,0:T(8,128)(2,1)} convert(f32[768,16,128]{2,1,0:T(8,128)} %scatter_fusion) | non-fusion elementwise | flops 1572864 | bytes 9437184 | tf_op jit(solution)/shard_map/convert_element_type | solution.py:57
  263.2 1.9 copy-done.1
  265.0 0.9 fusion.19
  265.9 64.2 %psum.7 = f32[16,256]{1,0:T(8,128)} all-reduce(f32[16,256]{1,0:T(8,128)S(1)} %fusion.19), channel_id=1, replica_groups=mesh['node'=16,'feat'=8] {'node'}, use_global_device_ids=true, to_apply=%region_3.4 | all-reduce | flops 4096 | bytes 32768 | tf_op jit(solution)/shard_map/psum | solution.py:48
  330.1 9.9 %reduce-scatter.5.cloned.1.call-done = bf16[48,16,128]{2,1,0:T(8,128)(2,1)} async-done(((bf16[768,16,128]{2,1,0:T(8,128)(2,1)}), bf16[48,16,128]{2,1,0:T(8,128)(2,1)}) %reduce-scatter.5.cloned.1.call-update) | async-done | bytes 196624 | tf_op jit(solution)/shard_map/reduce_scatter | solution.py:56
  340.1 1.6 copy_bitcast_fusion.1
  (25 shorter events, 0.8 us)
Async XLA Ops:
  7.2 72.1 %copy-start = (bf16[16,256]{1,0:T(8,128)(2,1)S(1)}, bf16[16,256]{1,0:T(8,128)(2,1)}, u32[]{:S(2)}) copy-start(bf16[16,256]{1,0:T(8,128)(2,1)} %param.9) | copy-start | bytes 24580
  7.2 57.9 %all-gather.3.cloned.1.call-start = ((), (), s32[]{:S(2)}) async-start(), calls=%async_computation.2 | async-start | bytes 3342336 | tf_op jit(solution)/shard_map/all_gather | solution.py:20
  7.9 116.5 %reduce-scatter.7.cloned.1.call-start = ((), (), s32[]{:S(2)}) async-start(), calls=%async_computation.5 | async-start | bytes 3538944 | tf_op jit(solution)/shard_map/reduce_scatter | solution.py:33
  83.3 0.7 copy-start.4
  83.3 41.1 %copy-start.2 = (bf16[32,6144]{1,0:T(8,128)(2,1)S(1)}, bf16[32,6144]{1,0:T(8,128)(2,1)}, u32[]{:S(2)}) copy-start(bf16[32,6144]{1,0:T(8,128)(2,1)} %param.15) | copy-start | bytes 1179652
  83.3 41.1 %copy-start.5 = (f32[32]{0:T(128)S(1)}, f32[32]{0:T(128)}, u32[]{:S(2)}) copy-start(f32[32]{0:T(128)} %param.10) | copy-start | bytes 388
  83.3 43.5 %copy-start.3 = (s32[48,12]{0,1:T(8,128)S(1)}, s32[48,12]{0,1:T(8,128)}, u32[]{:S(2)}) copy-start(s32[48,12]{0,1:T(8,128)} %param.12) | copy-start | bytes 6916
  83.4 88.1 %all-gather.5.cloned.1.call-start = ((), (), s32[]{:S(2)}) async-start(), calls=%async_computation.3 | async-start | bytes 3538944 | tf_op jit(solution)/shard_map/all_gather | solution.py:41
  126.8 213.3 %reduce-scatter.5.cloned.1.call-start = ((), (), s32[]{:S(2)}) async-start(), calls=%async_computation.4 | async-start | bytes 3342336 | tf_op jit(solution)/shard_map/reduce_scatter | solution.py:56
  263.1 1.9 copy-start.1
Sparse Core Ops, SparseCore 0:
  10.5 54.5 all-gather.2
  83.5 40.9 reduce-scatter.6
  126.9 44.5 all-gather.4
  263.3 76.7 reduce-scatter.4
where the time goes:
time: 350 us; the launch traced here: 348 us
  waiting for transfers between devices  150 us (43%)
  other arithmetic  80.2 us (23%)
  blocking collectives  64.2 us (18%)
  matrix products  23.2 us (7%)
  local copies, waits for them, and re-layouts  16.5 us (5%)
  between operations  13.8 us (4%)
    scatter-add x1, other arithmetic, local(): jax.ops.segment_sum(contrib, block_cols.reshape(-1), num_segments=all_blo...  70.8 us
    psum x1, blocking collectives, local(): grad_weight = lax.psum(grad_w, 'node')  64.2 us
    all_gather x1, waiting for transfers between devices, local(): lax.all_gather(features, 'node', axis=1, tiled=True)  54.7 us
    all_gather x1, waiting for transfers between devices, local(): shard_rows = lax.all_gather(grad_pre, 'feat', axis=0, tiled=True)  44.5 us
    reduce_scatter x1, waiting for transfers between devices, local(): lax.psum_scatter(partial_value.astype(jnp.bfloat16), 'feat', scatter_dime...  40.4 us
    dot_general x1, matrix products, local(): jnp.einsum('fnm,nskm->nsfk', grad_blocks, block_values, preferred_element...  10.4 us
    reduce_scatter x1, waiting for transfers between devices, local(): lax.psum_scatter(partial_grad.astype(jnp.bfloat16), 'node', scatter_dimen...  9.92 us
    dot_general x1, matrix products, local(): jnp.einsum('fnsk,nskm->fnm', picked, block_values, preferred_element_type...  8.47 us
  transfers between devices with their start and end apart: 4, of which 4 were waited for; matrix products, arithmetic and copies ran while one was open for 1% of the time, Pallas kernels for 0%

commit v1 on v0

v1 whole, which is shorter than its diff:
```python
import jax
import jax.numpy as jnp
from jax import lax
from jax.experimental import pallas as pl
from jax.experimental.pallas import tpu as pltpu
from jax.sharding import PartitionSpec as P

BF = jnp.bfloat16
F32 = jnp.float32
ANY = pl.BlockSpec(memory_space=pl.ANY)
SMEM = pl.BlockSpec(memory_space=pltpu.SMEM)
VMEM = pl.BlockSpec(memory_space=pltpu.VMEM)
STEPS = ((1, 2), (1, 1), (1, 3), (0, 2), (1, 0), (0, 1), (0, 3))
BLOCK = 128


def node_at(x, z, core):
    return (x * 4 + z) * 2 + core


def node_pairs(dx, dz, dcore=0):
    return [
        (node_at(x, z, c), node_at(x ^ dx, (z + dz) % 4, c ^ dcore))
        for x in range(2)
        for z in range(4)
        for c in range(2)
    ]


def node_near(dx, dz, dcore):
    me = lax.axis_index("node")
    x, z, c = me >> 3, (me >> 1) & 3, me & 1
    return ((x ^ dx) * 4 + ((z + dz) & 3)) * 2 + (c ^ dcore)


def place_of(column):
    group = lax.shift_right_logical(column * 21846, 20)
    return group, pl.multiple_of((column - group * 48) * BLOCK, BLOCK)


def params(mib):
    return pltpu.CompilerParams(vmem_limit_bytes=mib * 2**20)


def mix_kernel(cols, counts, values, cotangent, *rest):
    pieces, (out, held, sems) = rest[:16], rest[16:]
    step = pl.program_id(0)
    rows = values.shape[0]
    slots = values.shape[1]

    @pl.when(step == 0)
    def _():
        copies = []
        for k, (dx, dz) in enumerate(((0, 0),) + STEPS):
            for core in range(2):
                at = 2 * k + core
                copies.append(
                    pltpu.make_async_copy(
                        pieces[at], held.at[node_near(dx, -dz, core)], sems.at[at]
                    )
                )
        for copy in copies:
            copy.start()
        for copy in copies:
            copy.wait()

    for i in range(rows):
        r = step * rows + i
        count = counts[r]
        parts = []
        for s in range(slots):
            group, lane = place_of(cols[r * slots + s])
            block = held[group, :, pl.ds(lane, BLOCK)]
            parts.append(jnp.where(s < count, block, jnp.zeros_like(block)))
        picked = jnp.concatenate(parts, axis=1)
        total = jnp.dot(
            picked, values[i].reshape(slots * BLOCK, BLOCK), preferred_element_type=F32
        )
        out[0, :16, i * BLOCK : (i + 1) * BLOCK] = total.astype(BF)
    out[0, 16:, :] = cotangent[...]


def dense_kernel(both, weight, bias, mask, out):
    width = both.shape[2]
    mixed = both[:, :16, :].reshape(128, width)
    cotangent = both[:, 16:, :].reshape(256, width)
    kept = mask[:, pl.ds(pl.multiple_of(lax.axis_index("feat") * width, BLOCK), width)]
    preact = (
        lax.dot_general(weight[...], mixed, (((0,), (0,)), ((), ())), preferred_element_type=F32)
        + bias[...]
    )
    sigma = jax.nn.sigmoid(preact)
    activation = (preact * sigma).astype(BF).reshape(8, 32, width)
    slope = sigma * (1.0 + preact * (1.0 - sigma))
    grad_pre = (cotangent.astype(F32) * kept.astype(F32) * slope).astype(BF)
    grad_mixed = jnp.dot(weight[...], grad_pre, preferred_element_type=F32)
    grad_weight = lax.dot_general(
        mixed, grad_pre, (((1,), (1,)), ((), ())), preferred_element_type=F32
    )
    out[:, :, :width] = grad_mixed.astype(BF).reshape(8, 16, width)
    out[:, :, width : width + 256] = grad_weight.astype(BF).reshape(8, 16, 256)
    out[:, :, width + 256 : 2 * width + 256] = activation[:, :16]
    out[:, :, 2 * width + 256 :] = activation[:, 16:]


def spread_kernel(cols, counts, values, grads, activation, own, other, total, grad_w):
    step = pl.program_id(0)
    rows = values.shape[0]
    slots = values.shape[1]
    width = rows * BLOCK
    nodes = total.shape[2]

    @pl.when(step == 0)
    def _():
        total[...] = jnp.zeros_like(total)
        grad_w[...] = jnp.zeros_like(grad_w)

    activation[:16, :] = grads[0, :, width + 256 : 2 * width + 256]
    activation[16:, :] = grads[0, :, 2 * width + 256 :]
    grad_w[...] += grads[0, :, width : width + 256].astype(F32)

    for i in range(rows):
        r = step * rows + i
        count = counts[r]
        contrib = lax.dot_general(
            grads[0, :, i * BLOCK : (i + 1) * BLOCK],
            values[i].reshape(slots * BLOCK, BLOCK),
            (((1,), (1,)), ((), ())),
            preferred_element_type=F32,
        )
        for s in range(slots):
            group, lane = place_of(cols[r * slots + s])
            group = jnp.where(s < count, group, 16)
            total[group, :, pl.ds(lane, BLOCK)] += contrib[:, s * BLOCK : (s + 1) * BLOCK]

    @pl.when(step == pl.num_programs(0) - 1)
    def _():
        weight_part = grad_w[...].astype(BF)
        for k, (dx, dz) in enumerate(((0, 0),) + STEPS):
            for core, to in enumerate((own, other)):
                to[k, :, :nodes] = total[node_near(dx, dz, core)].astype(BF)
                to[k, :, nodes:] = weight_part


def pair_kernel(own, other, *outs):
    for k, out in enumerate(outs):
        out[...] = (own[k].astype(F32) + other[k].astype(F32)).astype(BF)


def local(features, weight, bias, block_values, block_cols, block_counts, train_mask, cotangent):
    block_dev, slots = block_values.shape[:2]
    fin, nodes = features.shape
    rows = block_dev // 8
    width = nodes // 8

    def shape(dims, kind=BF):
        return jax.ShapeDtypeStruct(dims, kind)

    whole_weight = lax.all_gather(weight, "feat", axis=0, tiled=True)
    whole_bias = lax.all_gather(bias, "feat", axis=0, tiled=True)[:, None]

    pieces = [features, lax.ppermute(features, "node", node_pairs(0, 0, 1))]
    for dx, dz in STEPS:
        piece = lax.ppermute(features, "node", node_pairs(dx, dz))
        pieces += [piece, lax.ppermute(piece, "node", node_pairs(0, 0, 1))]

    cols = block_cols.reshape(-1)
    values_spec = pl.BlockSpec((rows, slots, BLOCK, BLOCK), lambda i, *_: (i, 0, 0, 0))
    mixed = pl.pallas_call(
        mix_kernel,
        grid_spec=pltpu.PrefetchScalarGridSpec(
            num_scalar_prefetch=2,
            grid=(8,),
            in_specs=[values_spec, pl.BlockSpec((32, width), lambda i, *_: (0, i))] + [ANY] * 16,
            out_specs=pl.BlockSpec((1, 48, width), lambda i, *_: (i, 0, 0)),
            scratch_shapes=[
                pltpu.VMEM((16, fin, nodes), BF),
                pltpu.SemaphoreType.DMA((16,)),
            ],
        ),
        out_shape=shape((8, 48, width)),
        compiler_params=params(24),
        name="mix",
    )(cols, block_counts, block_values, cotangent, *pieces)

    both = lax.all_to_all(mixed, "feat", 0, 0, tiled=True)

    dense = pl.pallas_call(
        dense_kernel,
        in_specs=[VMEM] * 4,
        out_specs=VMEM,
        out_shape=shape((8, 16, 3 * width + 256)),
        compiler_params=params(24),
        name="dense",
    )(both, whole_weight, whole_bias, train_mask[None, :])

    grads = lax.all_to_all(dense, "feat", 0, 0, tiled=True)

    activation, own, other = pl.pallas_call(
        spread_kernel,
        grid_spec=pltpu.PrefetchScalarGridSpec(
            num_scalar_prefetch=2,
            grid=(8,),
            in_specs=[
                values_spec,
                pl.BlockSpec((1, 16, 3 * width + 256), lambda i, *_: (i, 0, 0)),
            ],
            out_specs=[
                pl.BlockSpec((32, width), lambda i, *_: (0, i)),
                pl.BlockSpec((8, 16, nodes + 256), lambda i, *_: (0, 0, 0)),
                pl.BlockSpec((8, 16, nodes + 256), lambda i, *_: (0, 0, 0)),
            ],
            scratch_shapes=[
                pltpu.VMEM((17, fin, nodes), F32),
                pltpu.VMEM((16, 256), F32),
            ],
        ),
        out_shape=[
            shape((32, nodes)),
            shape((8, 16, nodes + 256)),
            shape((8, 16, nodes + 256)),
        ],
        compiler_params=params(32),
        name="spread",
    )(cols, block_counts, block_values, grads)

    other = lax.ppermute(other, "node", node_pairs(0, 0, 1))
    sums = pl.pallas_call(
        pair_kernel,
        in_specs=[VMEM] * 2,
        out_specs=[VMEM] * 8,
        out_shape=[shape((16, nodes + 256))] * 8,
        compiler_params=params(24),
        name="pair",
    )(own, other)
    landed = [sums[0]]
    for (dx, dz), piece in zip(STEPS, sums[1:]):
        landed.append(lax.ppermute(piece, "node", node_pairs(dx, dz)))
    total = sum(piece.astype(F32) for piece in landed)
    return activation, total[:, :nodes].astype(BF), total[:, nodes:]


def solution(mesh):
    placed = (
        P("feat", "node"),
        P("feat", None),
        P("feat"),
        P("node", None, None, None),
        P("node", None),
        P("node"),
        P("node"),
        P("feat", "node"),
    )
    return jax.shard_map(
        local,
        mesh=mesh,
        in_specs=placed,
        out_specs=(P("feat", "node"), P("feat", "node"), P("feat", None)),
        check_vma=False,
    )
```

time: 350 us -> 164 us (0.47)
  waiting for transfers between devices: 150 us -> 21.7 us
  other arithmetic: 80.2 us -> 0.2 us
  starting transfers between devices: 0.16 us -> 52.6 us
  matrix products: 23.2 us -> 0 us
  Pallas kernels: 0 us -> 19.5 us
  blocking collectives: 64.2 us -> 49.2 us
  between operations: 13.8 us -> 1.43 us
    all_gather x2 -> x0, waiting for transfers between devices: 99.1 us -> none  [the longest x1 54.7 us: local(): lax.all_gather(features, 'node', axis=1, tiled=True)]
    scatter-add x1 -> x0, other arithmetic: 70.8 us -> none  [local(): jax.ops.segment_sum(contrib, block_cols.reshape(-1), num_segments=all_blo...]
    psum x1 -> x0, blocking collectives: 64.2 us -> none  [local(): grad_weight = lax.psum(grad_w, 'node')]
    reduce_scatter x2 -> x0, waiting for transfers between devices: 50.3 us -> none  [the longest x1 40.4 us: local(): lax.psum_scatter(partial_value.astype(jnp.bfloat16), 'feat', scatter_dime...]
    ppermute x0 -> x23, starting transfers between devices: none -> 48.4 us  [the longest x7 12.9 us: local(): piece = lax.ppermute(features, 'node', node_pairs(dx, dz))]
    dot_general x5 -> x0, matrix products: 23.2 us -> none  [the longest x1 10.4 us: local(): jnp.einsum('fnm,nskm->nsfk', grad_blocks, block_values, preferred_element...]
    all_gather x0 -> x1, blocking collectives: none -> 22.1 us  [local(): whole_weight = lax.all_gather(weight, 'feat', axis=0, tiled=True)]
    ppermute x0 -> x23, waiting for transfers between devices: none -> 21.7 us  [the longest x7 14.1 us: local(): landed.append(lax.ppermute(piece, 'node', node_pairs(dx, dz)))]
  transfers between devices with their start and end apart: 4 -> 24, of which waited for: 4 -> 10; matrix products, arithmetic and copies ran while one was open for 1% -> 1% of each run, Pallas kernels for 0% -> 0%
where the time goes in v1:
time: 164 us; the launch traced here: 163 us
  starting transfers between devices  52.6 us (32%)
  blocking collectives  49.2 us (30%)
  waiting for transfers between devices  21.7 us (13%)
  Pallas kernels  19.5 us (12%)
  local copies, waits for them, and re-layouts  18.5 us (11%)
    all_gather x1, blocking collectives, local(): whole_weight = lax.all_gather(weight, 'feat', axis=0, tiled=True)  22.1 us
    unnamed x24, local copies, waits for them, and re-layouts  17 us
    unnamed x1, blocking collectives  16.4 us
    ppermute x7, waiting for transfers between devices, local(): landed.append(lax.ppermute(piece, 'node', node_pairs(dx, dz)))  14.1 us
    ppermute x7, starting transfers between devices, local(): piece = lax.ppermute(features, 'node', node_pairs(dx, dz))  12.9 us
    ppermute x1, starting transfers between devices, local(): other = lax.ppermute(other, 'node', node_pairs(0, 0, 1))  12.2 us
    all_to_all x1, blocking collectives, local(): grads = lax.all_to_all(dense, 'feat', 0, 0, tiled=True)  10.7 us
    pallas_call x1, Pallas kernels, local(): pl.pallas_call(mix_kernel, grid_spec=pltpu.PrefetchScalarGridSpec(num_sca...  10.3 us
  transfers between devices with their start and end apart: 24, of which 10 were waited for; matrix products, arithmetic and copies ran while one was open for 1% of the time, Pallas kernels for 0%

profile of v1, /device:TPU:1, one launch (start us, length us, event | category | flops | bytes accessed | tf_op | source)
XLA Modules:
  0.0 163.3 jit_solution(14879583618290568333)
XLA Ops:
  0.6 2.5 %collective-permute-start.11 = (bf16[16,6144]{1,0:T(8,128)(2,1)}, bf16[16,6144]{1,0:T(8,128)(2,1)S(1)}, u32[]{:S(2)}, u32[]{:S(2)}) collective-permute-start(bf16[16,6144]{1,0:T(8,128)(2,1)} %rest_0_.1), channel_id=1, source_target_pairs={{0,16},{8,24},{16,32},{24,40},{32,48},{40,56},{48,0},{56,8},{64,80... | collective-permute-start | bytes 589832 | tf_op jit(solution)/shard_map/ppermute | solution.py:164
  3.2 2.7 %collective-permute-start.9 = (bf16[16,6144]{1,0:T(8,128)(2,1)}, bf16[16,6144]{1,0:T(8,128)(2,1)S(1)}, u32[]{:S(2)}, u32[]{:S(2)}) collective-permute-start(bf16[16,6144]{1,0:T(8,128)(2,1)} %rest_0_.1), channel_id=1, source_target_pairs={{0,64},{8,72},{16,80},{24,88},{32,96},{40,104},{48,112},{56,120},{... | collective-permute-start | bytes 589832 | tf_op jit(solution)/shard_map/ppermute | solution.py:164
  5.9 3.3 %collective-permute-start.7 = (bf16[16,6144]{1,0:T(8,128)(2,1)}, bf16[16,6144]{1,0:T(8,128)(2,1)S(1)}, u32[]{:S(2)}, u32[]{:S(2)}) collective-permute-start(bf16[16,6144]{1,0:T(8,128)(2,1)} %rest_0_.1), channel_id=1, source_target_pairs={{0,32},{8,40},{16,48},{24,56},{32,0},{40,8},{48,16},{56,24},{64,96... | collective-permute-start | bytes 589832 | tf_op jit(solution)/shard_map/ppermute | solution.py:164
  9.9 3.2 %collective-permute-start.3 = (bf16[16,6144]{1,0:T(8,128)(2,1)}, bf16[16,6144]{1,0:T(8,128)(2,1)S(1)}, u32[]{:S(2)}, u32[]{:S(2)}) collective-permute-start(bf16[16,6144]{1,0:T(8,128)(2,1)} %rest_0_.1), channel_id=1, source_target_pairs={{0,80},{8,88},{16,96},{24,104},{32,112},{40,120},{48,64},{56,72},{... | collective-permute-start | bytes 589832 | tf_op jit(solution)/shard_map/ppermute | solution.py:164
  13.6 6.0 %collective-permute-start = (bf16[16,6144]{1,0:T(8,128)(2,1)}, bf16[16,6144]{1,0:T(8,128)(2,1)S(1)}, u32[]{:S(2)}, u32[]{:S(2)}) collective-permute-start(bf16[16,6144]{1,0:T(8,128)(2,1)} %rest_0_.1), channel_id=1, source_target_pairs={{0,8},{8,0},{16,24},{24,16},{32,40},{40,32},{48,56},{56,48},{64,72... | collective-permute-start | bytes 589832 | tf_op jit(solution)/shard_map/ppermute | solution.py:162
  21.2 2.8 %collective-permute-start.10 = (bf16[16,6144]{1,0:T(8,128)(2,1)S(1)}, bf16[16,6144]{1,0:T(8,128)(2,1)S(1)}, u32[]{:S(2)}, u32[]{:S(2)}) collective-permute-start(bf16[16,6144]{1,0:T(8,128)(2,1)S(1)} %collective-permute-done.9.rest_10_), channel_id=1, source_target_pairs={{0,8},{8,0},{16,24},{24,16},{32,40},{40,32},{48,56},{56,48},{64,72... | collective-permute-start | bytes 589832 | tf_op jit(solution)/shard_map/ppermute | solution.py:165
  24.0 2.2 %collective-permute-done.1.rest_2_ = bf16[16,6144]{1,0:T(8,128)(2,1)S(1)} collective-permute-done((bf16[16,6144]{1,0:T(8,128)(2,1)}, bf16[16,6144]{1,0:T(8,128)(2,1)S(1)}, u32[]{:S(2)}, u32[]{:S(2)}) %collective-permute-start.1) | collective-permute-done | bytes 196640 | tf_op jit(solution)/shard_map/ppermute | solution.py:164
  32.3 6.4 %copy-done = bf16[48,12,128,128]{3,2,1,0:T(8,128)(2,1)S(1)} copy-done((bf16[48,12,128,128]{3,2,1,0:T(8,128)(2,1)S(1)}, bf16[48,12,128,128]{3,2,1,0:T(8,128)(2,1)}, u32[]{:S(2)}) %copy-start) | copy-done | bytes 18874392
  41.2 10.3 %mix.1 = bf16[8,48,768]{2,1,0:T(8,128)(2,1)} custom-call(s32[576]{0:T(1024)S(1)} %reshape.9.cols, s32[48]{0:T(128)S(1)} %copy-done.5, bf16[48,12,128,128]{3,2,1,0:T(8,128)(2,1)S(1)} %copy-done, bf16[32,6144]{1,0:T(8,128)(2,1)S(1)} %copy-done.2, bf16[16,6144]{1,0:T(8,128)(2,1)S(1)} %copy-done.3, bf16[16,6144]{1,0:T(8,128)(2,1)S(1)} %collective-permute-done.rest_1_, ...), custom_call_target="tpu_custom_call" | custom-call | tf_op jit(solution)/shard_map/mix/pallas_call | solution.py:169
  51.6 4.2 %all-to-all-start = ((bf16[8,48,768]{2,1,0:T(8,128)(2,1)}), bf16[8,48,768]{2,1,0:T(8,128)(2,1)S(1)}, u32[]{:S(2)}, u32[]{:S(2)}) async-start(bf16[8,48,768]{2,1,0:T(8,128)(2,1)} %mix.1), calls=%async_computation | async-start | bytes 1179648 | tf_op jit(solution)/shard_map/all_to_all | solution.py:186
  57.3 16.4 %all-reduce = f32[256]{0:T(256)S(1)} all-reduce(f32[256]{0:T(256)S(1)} %dynamic-update-slice), channel_id=1, replica_groups=mesh['node'=16,'feat'=8] {'feat'}, use_global_device_ids=true, to_apply=%add | all-reduce | flops 256 | bytes 2048
  73.9 22.1 %all_gather.6.weight = bf16[128,256]{1,0:T(8,128)(2,1)S(1)} all-gather(bf16[16,256]{1,0:T(8,128)(2,1)S(1)} %copy-done.7), channel_id=1, replica_groups=mesh['node'=16,'feat'=8] {'feat'}, dimensions={0}, use_global_device_ids=true | all-gather | bytes 73728 | tf_op jit(solution)/shard_map/all_gather | solution.py:159
  96.8 10.7 %all_to_all.10.grads = bf16[8,16,2560]{2,1,0:T(8,128)(2,1)S(1)} all-to-all(bf16[8,16,2560]{2,1,0:T(8,128)(2,1)S(1)} %dense.1), channel_id=1, replica_groups=mesh['node'=16,'feat'=8] {'feat'}, dimensions={0} | all-to-all | bytes 1310720 | tf_op jit(solution)/shard_map/all_to_all | solution.py:197
  107.4 6.4 %copy-done.1 = bf16[48,12,128,128]{3,2,1,0:T(8,128)(2,1)S(1)} copy-done((bf16[48,12,128,128]{3,2,1,0:T(8,128)(2,1)S(1)}, bf16[48,12,128,128]{3,2,1,0:T(8,128)(2,1)}, u32[]{:S(2)}) %copy-start.1) | copy-done | bytes 18874392
  113.8 8.1 %spread.1 = (bf16[32,6144]{1,0:T(8,128)(2,1)}, bf16[8,16,6400]{2,1,0:T(8,128)(2,1)S(1)}, bf16[8,16,6400]{2,1,0:T(8,128)(2,1)S(1)}) custom-call(s32[576]{0:T(1024)S(1)} %reshape.9.cols, s32[48]{0:T(128)S(1)} %copy-done.6, bf16[48,12,128,128]{3,2,1,0:T(8,128)(2,1)S(1)} %copy-done.1, bf16[8,16,2560]{2,1,0:T(8,128)(2,1)S(1)} %all_to_all.10.grads), custom_call_target="tpu_custom_call" | custom-call | tf_op jit(solution)/shard_map/spread/pallas_call | solution.py:199
  121.9 12.2 %collective-permute-start.15 = (bf16[8,16,6400]{2,1,0:T(8,128)(2,1)S(1)}, bf16[8,16,6400]{2,1,0:T(8,128)(2,1)S(1)}, u32[]{:S(2)}, u32[]{:S(2)}) collective-permute-start(bf16[8,16,6400]{2,1,0:T(8,128)(2,1)S(1)} %get-tuple-element.16), channel_id=1, source_target_pairs={{0,8},{8,0},{16,24},{24,16},{32,40},{40,32},{48,56},{56,48},{64,72... | collective-permute-start | bytes 4915208 | tf_op jit(solution)/shard_map/ppermute | solution.py:227
  134.1 3.1 %collective-permute-done.15.other = bf16[8,16,6400]{2,1,0:T(8,128)(2,1)S(1)} collective-permute-done((bf16[8,16,6400]{2,1,0:T(8,128)(2,1)S(1)}, bf16[8,16,6400]{2,1,0:T(8,128)(2,1)S(1)}, u32[]{:S(2)}, u32[]{:S(2)}) %collective-permute-start.15) | collective-permute-done | bytes 1638432 | tf_op jit(solution)/shard_map/ppermute | solution.py:227
  137.6 2.7 %collective-permute-start.16 = (bf16[16,6400]{1,0:T(8,128)(2,1)S(1)}, bf16[16,6400]{1,0:T(8,128)(2,1)S(1)}, u32[]{:S(2)}, u32[]{:S(2)}) collective-permute-start(bf16[16,6400]{1,0:T(8,128)(2,1)S(1)} %get-tuple-element.18), channel_id=1, source_target_pairs={{0,96},{8,104},{16,112},{24,120},{32,64},{40,72},{48,80},{56,88},{... | collective-permute-start | bytes 614408 | tf_op jit(solution)/shard_map/ppermute | solution.py:238
  140.3 2.2 %collective-permute-start.17 = (bf16[16,6400]{1,0:T(8,128)(2,1)S(1)}, bf16[16,6400]{1,0:T(8,128)(2,1)S(1)}, u32[]{:S(2)}, u32[]{:S(2)}) collective-permute-start(bf16[16,6400]{1,0:T(8,128)(2,1)S(1)} %get-tuple-element.19), channel_id=1, source_target_pairs={{0,80},{8,88},{16,96},{24,104},{32,112},{40,120},{48,64},{56,72},{... | collective-permute-start | bytes 614408 | tf_op jit(solution)/shard_map/ppermute | solution.py:238
  142.5 2.9 %collective-permute-start.18 = (bf16[16,6400]{1,0:T(8,128)(2,1)S(1)}, bf16[16,6400]{1,0:T(8,128)(2,1)S(1)}, u32[]{:S(2)}, u32[]{:S(2)}) collective-permute-start(bf16[16,6400]{1,0:T(8,128)(2,1)S(1)} %get-tuple-element.20), channel_id=1, source_target_pairs={{0,112},{8,120},{16,64},{24,72},{32,80},{40,88},{48,96},{56,104},{... | collective-permute-start | bytes 614408 | tf_op jit(solution)/shard_map/ppermute | solution.py:238
  147.9 4.2 %collective-permute-done.17 = bf16[16,6400]{1,0:T(8,128)(2,1)S(1)} collective-permute-done((bf16[16,6400]{1,0:T(8,128)(2,1)S(1)}, bf16[16,6400]{1,0:T(8,128)(2,1)S(1)}, u32[]{:S(2)}, u32[]{:S(2)}) %collective-permute-start.17) | collective-permute-done | bytes 204832 | tf_op jit(solution)/shard_map/ppermute | solution.py:238
  152.6 3.5 %collective-permute-done.18 = bf16[16,6400]{1,0:T(8,128)(2,1)S(1)} collective-permute-done((bf16[16,6400]{1,0:T(8,128)(2,1)S(1)}, bf16[16,6400]{1,0:T(8,128)(2,1)S(1)}, u32[]{:S(2)}, u32[]{:S(2)}) %collective-permute-start.18) | collective-permute-done | bytes 204832 | tf_op jit(solution)/shard_map/ppermute | solution.py:238
  157.4 2.2 %collective-permute-done.20 = bf16[16,6400]{1,0:T(8,128)(2,1)S(1)} collective-permute-done((bf16[16,6400]{1,0:T(8,128)(2,1)S(1)}, bf16[16,6400]{1,0:T(8,128)(2,1)S(1)}, u32[]{:S(2)}, u32[]{:S(2)}) %collective-permute-start.20) | collective-permute-done | bytes 204832 | tf_op jit(solution)/shard_map/ppermute | solution.py:238
  159.7 2.1 %collective-permute-done.21 = bf16[16,6400]{1,0:T(8,128)(2,1)S(1)} collective-permute-done((bf16[16,6400]{1,0:T(8,128)(2,1)S(1)}, bf16[16,6400]{1,0:T(8,128)(2,1)S(1)}, u32[]{:S(2)}, u32[]{:S(2)}) %collective-permute-start.21) | collective-permute-done | bytes 204832 | tf_op jit(solution)/shard_map/ppermute | solution.py:238
  (60 shorter events, 19.2 us)
Async XLA Ops:
  0.6 12.5 %collective-permute-start.11 = (bf16[16,6144]{1,0:T(8,128)(2,1)}, bf16[16,6144]{1,0:T(8,128)(2,1)S(1)}, u32[]{:S(2)}, u32[]{:S(2)}) collective-permute-start(bf16[16,6144]{1,0:T(8,128)(2,1)} %rest_0_.1), channel_id=1, source_target_pairs={{0,16},{8,24},{16,32},{24,40},{32,48},{40,56},{48,0},{56,8},{64,80... | collective-permute-start | bytes 589832 | tf_op jit(solution)/shard_map/ppermute | solution.py:164
  3.2 10.4 %collective-permute-start.9 = (bf16[16,6144]{1,0:T(8,128)(2,1)}, bf16[16,6144]{1,0:T(8,128)(2,1)S(1)}, u32[]{:S(2)}, u32[]{:S(2)}) collective-permute-start(bf16[16,6144]{1,0:T(8,128)(2,1)} %rest_0_.1), channel_id=1, source_target_pairs={{0,64},{8,72},{16,80},{24,88},{32,96},{40,104},{48,112},{56,120},{... | collective-permute-start | bytes 589832 | tf_op jit(solution)/shard_map/ppermute | solution.py:164
  5.9 13.7 %collective-permute-start.7 = (bf16[16,6144]{1,0:T(8,128)(2,1)}, bf16[16,6144]{1,0:T(8,128)(2,1)S(1)}, u32[]{:S(2)}, u32[]{:S(2)}) collective-permute-start(bf16[16,6144]{1,0:T(8,128)(2,1)} %rest_0_.1), channel_id=1, source_target_pairs={{0,32},{8,40},{16,48},{24,56},{32,0},{40,8},{48,16},{56,24},{64,96... | collective-permute-start | bytes 589832 | tf_op jit(solution)/shard_map/ppermute | solution.py:164
  9.2 10.4 %collective-permute-start.5 = (bf16[16,6144]{1,0:T(8,128)(2,1)}, bf16[16,6144]{1,0:T(8,128)(2,1)S(1)}, u32[]{:S(2)}, u32[]{:S(2)}) collective-permute-start(bf16[16,6144]{1,0:T(8,128)(2,1)} %rest_0_.1), channel_id=1, source_target_pairs={{0,112},{8,120},{16,64},{24,72},{32,80},{40,88},{48,96},{56,104},{... | collective-permute-start | bytes 589832 | tf_op jit(solution)/shard_map/ppermute | solution.py:164
  9.9 11.3 %collective-permute-start.3 = (bf16[16,6144]{1,0:T(8,128)(2,1)}, bf16[16,6144]{1,0:T(8,128)(2,1)S(1)}, u32[]{:S(2)}, u32[]{:S(2)}) collective-permute-start(bf16[16,6144]{1,0:T(8,128)(2,1)} %rest_0_.1), channel_id=1, source_target_pairs={{0,80},{8,88},{16,96},{24,104},{32,112},{40,120},{48,64},{56,72},{... | collective-permute-start | bytes 589832 | tf_op jit(solution)/shard_map/ppermute | solution.py:164
  13.1 13.1 %collective-permute-start.1 = (bf16[16,6144]{1,0:T(8,128)(2,1)}, bf16[16,6144]{1,0:T(8,128)(2,1)S(1)}, u32[]{:S(2)}, u32[]{:S(2)}) collective-permute-start(bf16[16,6144]{1,0:T(8,128)(2,1)} %rest_0_.1), channel_id=1, source_target_pairs={{0,96},{8,104},{16,112},{24,120},{32,64},{40,72},{48,80},{56,88},{... | collective-permute-start | bytes 589832 | tf_op jit(solution)/shard_map/ppermute | solution.py:164
  13.6 14.3 %collective-permute-start = (bf16[16,6144]{1,0:T(8,128)(2,1)}, bf16[16,6144]{1,0:T(8,128)(2,1)S(1)}, u32[]{:S(2)}, u32[]{:S(2)}) collective-permute-start(bf16[16,6144]{1,0:T(8,128)(2,1)} %rest_0_.1), channel_id=1, source_target_pairs={{0,8},{8,0},{16,24},{24,16},{32,40},{40,32},{48,56},{56,48},{64,72... | collective-permute-start | bytes 589832 | tf_op jit(solution)/shard_map/ppermute | solution.py:162
  19.6 10.3 %collective-permute-start.13 = (bf16[16,6144]{1,0:T(8,128)(2,1)}, bf16[16,6144]{1,0:T(8,128)(2,1)S(1)}, u32[]{:S(2)}, u32[]{:S(2)}) collective-permute-start(bf16[16,6144]{1,0:T(8,128)(2,1)} %rest_0_.1), channel_id=1, source_target_pairs={{0,48},{8,56},{16,0},{24,8},{32,16},{40,24},{48,32},{56,40},{64,11... | collective-permute-start | bytes 589832 | tf_op jit(solution)/shard_map/ppermute | solution.py:164
  19.6 10.9 %collective-permute-start.12 = (bf16[16,6144]{1,0:T(8,128)(2,1)S(1)}, bf16[16,6144]{1,0:T(8,128)(2,1)S(1)}, u32[]{:S(2)}, u32[]{:S(2)}) collective-permute-start(bf16[16,6144]{1,0:T(8,128)(2,1)S(1)} %collective-permute-done.11.rest_12_), channel_id=1, source_target_pairs={{0,8},{8,0},{16,24},{24,16},{32,40},{40,32},{48,56},{56,48},{64,72... | collective-permute-start | bytes 589832 | tf_op jit(solution)/shard_map/ppermute | solution.py:165
  21.2 9.4 %collective-permute-start.10 = (bf16[16,6144]{1,0:T(8,128)(2,1)S(1)}, bf16[16,6144]{1,0:T(8,128)(2,1)S(1)}, u32[]{:S(2)}, u32[]{:S(2)}) collective-permute-start(bf16[16,6144]{1,0:T(8,128)(2,1)S(1)} %collective-permute-done.9.rest_10_), channel_id=1, source_target_pairs={{0,8},{8,0},{16,24},{24,16},{32,40},{40,32},{48,56},{56,48},{64,72... | collective-permute-start | bytes 589832 | tf_op jit(solution)/shard_map/ppermute | solution.py:165
  26.2 5.8 %collective-permute-start.8 = (bf16[16,6144]{1,0:T(8,128)(2,1)S(1)}, bf16[16,6144]{1,0:T(8,128)(2,1)S(1)}, u32[]{:S(2)}, u32[]{:S(2)}) collective-permute-start(bf16[16,6144]{1,0:T(8,128)(2,1)S(1)} %collective-permute-done.7.rest_8_), channel_id=1, source_target_pairs={{0,8},{8,0},{16,24},{24,16},{32,40},{40,32},{48,56},{56,48},{64,72... | collective-permute-start | bytes 589832 | tf_op jit(solution)/shard_map/ppermute | solution.py:165
  27.9 4.1 %collective-permute-start.6 = (bf16[16,6144]{1,0:T(8,128)(2,1)S(1)}, bf16[16,6144]{1,0:T(8,128)(2,1)S(1)}, u32[]{:S(2)}, u32[]{:S(2)}) collective-permute-start(bf16[16,6144]{1,0:T(8,128)(2,1)S(1)} %collective-permute-done.5.rest_6_), channel_id=1, source_target_pairs={{0,8},{8,0},{16,24},{24,16},{32,40},{40,32},{48,56},{56,48},{64,72... | collective-permute-start | bytes 589832 | tf_op jit(solution)/shard_map/ppermute | solution.py:165
  29.9 2.1 %collective-permute-start.4 = (bf16[16,6144]{1,0:T(8,128)(2,1)S(1)}, bf16[16,6144]{1,0:T(8,128)(2,1)S(1)}, u32[]{:S(2)}, u32[]{:S(2)}) collective-permute-start(bf16[16,6144]{1,0:T(8,128)(2,1)S(1)} %collective-permute-done.3.rest_4_), channel_id=1, source_target_pairs={{0,8},{8,0},{16,24},{24,16},{32,40},{40,32},{48,56},{56,48},{64,72... | collective-permute-start | bytes 589832 | tf_op jit(solution)/shard_map/ppermute | solution.py:165
  30.6 1.5 collective-permute-start.2
  30.6 1.7 %collective-permute-start.14 = (bf16[16,6144]{1,0:T(8,128)(2,1)S(1)}, bf16[16,6144]{1,0:T(8,128)(2,1)S(1)}, u32[]{:S(2)}, u32[]{:S(2)}) collective-permute-start(bf16[16,6144]{1,0:T(8,128)(2,1)S(1)} %collective-permute-done.13.rest_14_), channel_id=1, source_target_pairs={{0,8},{8,0},{16,24},{24,16},{32,40},{40,32},{48,56},{56,48},{64,72... | collective-permute-start | bytes 589832 | tf_op jit(solution)/shard_map/ppermute | solution.py:165
  51.6 44.4 %all-to-all-start = ((bf16[8,48,768]{2,1,0:T(8,128)(2,1)}), bf16[8,48,768]{2,1,0:T(8,128)(2,1)S(1)}, u32[]{:S(2)}, u32[]{:S(2)}) async-start(bf16[8,48,768]{2,1,0:T(8,128)(2,1)} %mix.1), calls=%async_computation | async-start | bytes 1179648 | tf_op jit(solution)/shard_map/all_to_all | solution.py:186
  121.9 15.3 %collective-permute-start.15 = (bf16[8,16,6400]{2,1,0:T(8,128)(2,1)S(1)}, bf16[8,16,6400]{2,1,0:T(8,128)(2,1)S(1)}, u32[]{:S(2)}, u32[]{:S(2)}) collective-permute-start(bf16[8,16,6400]{2,1,0:T(8,128)(2,1)S(1)} %get-tuple-element.16), channel_id=1, source_target_pairs={{0,8},{8,0},{16,24},{24,16},{32,40},{40,32},{48,56},{56,48},{64,72... | collective-permute-start | bytes 4915208 | tf_op jit(solution)/shard_map/ppermute | solution.py:227
  137.6 10.3 %collective-permute-start.16 = (bf16[16,6400]{1,0:T(8,128)(2,1)S(1)}, bf16[16,6400]{1,0:T(8,128)(2,1)S(1)}, u32[]{:S(2)}, u32[]{:S(2)}) collective-permute-start(bf16[16,6400]{1,0:T(8,128)(2,1)S(1)} %get-tuple-element.18), channel_id=1, source_target_pairs={{0,96},{8,104},{16,112},{24,120},{32,64},{40,72},{48,80},{56,88},{... | collective-permute-start | bytes 614408 | tf_op jit(solution)/shard_map/ppermute | solution.py:238
  140.3 11.8 %collective-permute-start.17 = (bf16[16,6400]{1,0:T(8,128)(2,1)S(1)}, bf16[16,6400]{1,0:T(8,128)(2,1)S(1)}, u32[]{:S(2)}, u32[]{:S(2)}) collective-permute-start(bf16[16,6400]{1,0:T(8,128)(2,1)S(1)} %get-tuple-element.19), channel_id=1, source_target_pairs={{0,80},{8,88},{16,96},{24,104},{32,112},{40,120},{48,64},{56,72},{... | collective-permute-start | bytes 614408 | tf_op jit(solution)/shard_map/ppermute | solution.py:238
  142.5 13.6 %collective-permute-start.18 = (bf16[16,6400]{1,0:T(8,128)(2,1)S(1)}, bf16[16,6400]{1,0:T(8,128)(2,1)S(1)}, u32[]{:S(2)}, u32[]{:S(2)}) collective-permute-start(bf16[16,6400]{1,0:T(8,128)(2,1)S(1)} %get-tuple-element.20), channel_id=1, source_target_pairs={{0,112},{8,120},{16,64},{24,72},{32,80},{40,88},{48,96},{56,104},{... | collective-permute-start | bytes 614408 | tf_op jit(solution)/shard_map/ppermute | solution.py:238
  145.4 12.0 %collective-permute-start.19 = (bf16[16,6400]{1,0:T(8,128)(2,1)S(1)}, bf16[16,6400]{1,0:T(8,128)(2,1)S(1)}, u32[]{:S(2)}, u32[]{:S(2)}) collective-permute-start(bf16[16,6400]{1,0:T(8,128)(2,1)S(1)} %get-tuple-element.21), channel_id=1, source_target_pairs={{0,32},{8,40},{16,48},{24,56},{32,0},{40,8},{48,16},{56,24},{64,96... | collective-permute-start | bytes 614408 | tf_op jit(solution)/shard_map/ppermute | solution.py:238
  145.5 14.2 %collective-permute-start.20 = (bf16[16,6400]{1,0:T(8,128)(2,1)S(1)}, bf16[16,6400]{1,0:T(8,128)(2,1)S(1)}, u32[]{:S(2)}, u32[]{:S(2)}) collective-permute-start(bf16[16,6400]{1,0:T(8,128)(2,1)S(1)} %get-tuple-element.22), channel_id=1, source_target_pairs={{0,64},{8,72},{16,80},{24,88},{32,96},{40,104},{48,112},{56,120},{... | collective-permute-start | bytes 614408 | tf_op jit(solution)/shard_map/ppermute | solution.py:238
  147.9 13.9 %collective-permute-start.21 = (bf16[16,6400]{1,0:T(8,128)(2,1)S(1)}, bf16[16,6400]{1,0:T(8,128)(2,1)S(1)}, u32[]{:S(2)}, u32[]{:S(2)}) collective-permute-start(bf16[16,6400]{1,0:T(8,128)(2,1)S(1)} %get-tuple-element.23), channel_id=1, source_target_pairs={{0,16},{8,24},{16,32},{24,40},{32,48},{40,56},{48,0},{56,8},{64,80... | collective-permute-start | bytes 614408 | tf_op jit(solution)/shard_map/ppermute | solution.py:238
  152.1 9.6 %collective-permute-start.22 = (bf16[16,6400]{1,0:T(8,128)(2,1)S(1)}, bf16[16,6400]{1,0:T(8,128)(2,1)S(1)}, u32[]{:S(2)}, u32[]{:S(2)}) collective-permute-start(bf16[16,6400]{1,0:T(8,128)(2,1)S(1)} %get-tuple-element.24), channel_id=1, source_target_pairs={{0,48},{8,56},{16,0},{24,8},{32,16},{40,24},{48,32},{56,40},{64,11... | collective-permute-start | bytes 614408 | tf_op jit(solution)/shard_map/ppermute | solution.py:238
  (10 other events, 223.1 us)

commit v2 on v1

v2 whole, which is shorter than its diff:
```python
import jax
import jax.numpy as jnp
from jax import lax
from jax.experimental import pallas as pl
from jax.experimental.pallas import tpu as pltpu
from jax.sharding import PartitionSpec as P

BF = jnp.bfloat16
F32 = jnp.float32
ANY = pl.BlockSpec(memory_space=pl.ANY)
SMEM = pl.BlockSpec(memory_space=pltpu.SMEM)
VMEM = pl.BlockSpec(memory_space=pltpu.VMEM)
STEPS = ((1, 2), (1, 1), (1, 3), (0, 2), (1, 0), (0, 1), (0, 3))
BLOCK = 128


def node_at(x, z, core):
    return (x * 4 + z) * 2 + core


def node_pairs(dx, dz, dcore=0):
    return [
        (node_at(x, z, c), node_at(x ^ dx, (z + dz) % 4, c ^ dcore))
        for x in range(2)
        for z in range(4)
        for c in range(2)
    ]


def node_near(dx, dz, dcore):
    me = lax.axis_index("node")
    x, z, c = me >> 3, (me >> 1) & 3, me & 1
    return ((x ^ dx) * 4 + ((z + dz) & 3)) * 2 + (c ^ dcore)


def place_of(column):
    group = lax.shift_right_logical(column * 21846, 20)
    return group, pl.multiple_of((column - group * 48) * BLOCK, BLOCK)


def params(mib):
    return pltpu.CompilerParams(vmem_limit_bytes=mib * 2**20)


def load_kernel(values, _, out, sems):
    count = sems.shape[0]
    rows = values.shape[0] // count
    copies = [
        pltpu.make_async_copy(
            values.at[pl.ds(i * rows, rows)], out.at[pl.ds(i * rows, rows)], sems.at[i]
        )
        for i in range(count)
    ]
    for copy in copies:
        copy.start()
    for copy in copies:
        copy.wait()


def mix_kernel(cols, counts, values, cotangent, weight, bias_rows, *rest):
    pieces, (out, held, sems) = rest[:16], rest[16:]
    slots = values.shape[1]
    chunks, _, _ = out.shape
    width = cotangent.shape[1] // chunks
    rows = values.shape[0] // chunks

    copies = []
    for k, (dx, dz) in enumerate(((0, 0),) + STEPS):
        for core in range(2):
            at = 2 * k + core
            copies.append(
                pltpu.make_async_copy(pieces[at], held.at[node_near(dx, -dz, core)], sems.at[at])
            )
    for copy in copies:
        copy.start()
    for j in range(chunks):
        out[j, :, width : 2 * width] = cotangent[:16, j * width : (j + 1) * width]
        out[j, :, 2 * width : 3 * width] = cotangent[16:, j * width : (j + 1) * width]
        out[j, :, 3 * width : 3 * width + 256] = weight[...]
        out[j, :, 3 * width + 256 :] = bias_rows[...]
    for copy in copies:
        copy.wait()

    @pl.loop(0, chunks)
    def _(j):
        for i in range(rows):
            r = j * rows + i
            count = counts[r]
            parts = []
            for s in range(slots):
                group, lane = place_of(cols[r, s])
                block = held[group, :, pl.ds(lane, BLOCK)]
                parts.append(jnp.where(s < count, block, jnp.zeros_like(block)))
            total = jnp.dot(
                jnp.concatenate(parts, axis=1),
                values[r].reshape(slots * BLOCK, BLOCK),
                preferred_element_type=F32,
            )
            out[j, :, i * BLOCK : (i + 1) * BLOCK] = total.astype(BF)


def dense_kernel(both, mask, out):
    width = mask.shape[1] // 8
    mixed = both[:, :, :width].reshape(128, width)
    cotangent = jnp.concatenate(
        [both[:, :, width : 2 * width], both[:, :, 2 * width : 3 * width]], axis=1
    ).reshape(256, width)
    weight = both[:, :, 3 * width : 3 * width + 256].reshape(128, 256)
    bias_rows = both[:, :, 3 * width + 256 :].reshape(128, 256)
    kept = mask[:, pl.ds(pl.multiple_of(lax.axis_index("feat") * width, BLOCK), width)]
    preact = lax.dot_general(
        jnp.concatenate([weight, bias_rows], axis=0),
        jnp.concatenate([mixed, jnp.ones_like(mixed)], axis=0),
        (((0,), (0,)), ((), ())),
        preferred_element_type=F32,
    )
    sigma = jax.nn.sigmoid(preact)
    activation = (preact * sigma).astype(BF).reshape(8, 32, width)
    slope = sigma * (1.0 + preact * (1.0 - sigma))
    grad_pre = (cotangent.astype(F32) * kept.astype(F32) * slope).astype(BF)
    grad_mixed = jnp.dot(weight, grad_pre, preferred_element_type=F32)
    grad_weight = lax.dot_general(
        mixed, grad_pre, (((1,), (1,)), ((), ())), preferred_element_type=F32
    )
    out[:, :, :width] = grad_mixed.astype(BF).reshape(8, 16, width)
    out[:, :, width : width + 256] = grad_weight.astype(BF).reshape(8, 16, 256)
    out[:, :, width + 256 : 2 * width + 256] = activation[:, :16]
    out[:, :, 2 * width + 256 :] = activation[:, 16:]


def spread_kernel(cols, counts, values, grads, activation, own, other, total):
    slots = values.shape[1]
    chunks = grads.shape[0]
    rows = values.shape[0] // chunks
    nodes = total.shape[2]
    width = nodes // chunks

    total[...] = jnp.zeros_like(total)
    weight_part = jnp.zeros((16, 256), F32)
    for j in range(chunks):
        at = slice(j * width, (j + 1) * width)
        activation[:16, at] = grads[j, :, width + 256 : 2 * width + 256]
        activation[16:, at] = grads[j, :, 2 * width + 256 :]
        weight_part += grads[j, :, width : width + 256].astype(F32)

    @pl.loop(0, chunks)
    def _(j):
        for i in range(rows):
            r = j * rows + i
            count = counts[r]
            contrib = lax.dot_general(
                grads[j, :, i * BLOCK : (i + 1) * BLOCK],
                values[r].reshape(slots * BLOCK, BLOCK),
                (((1,), (1,)), ((), ())),
                preferred_element_type=F32,
            )
            for s in range(slots):
                group, lane = place_of(cols[r, s])
                group = jnp.where(s < count, group, 16)
                total[group, :, pl.ds(lane, BLOCK)] += contrib[:, s * BLOCK : (s + 1) * BLOCK]

    weight_part = weight_part.astype(BF)
    for k, (dx, dz) in enumerate(((0, 0),) + STEPS):
        for core, to in enumerate((own, other)):
            to[k, :, :nodes] = total[node_near(dx, dz, core)].astype(BF)
            to[k, :, nodes:] = weight_part


def pair_kernel(own, other, *outs):
    for k, out in enumerate(outs):
        out[...] = (own[k].astype(F32) + other[k].astype(F32)).astype(BF)


def local(features, weight, bias, block_values, block_cols, block_counts, train_mask, cotangent):
    fin, nodes = features.shape
    width = nodes // 8

    def shape(dims, kind=BF):
        return jax.ShapeDtypeStruct(dims, kind)

    bias_at = lax.dynamic_update_slice(
        jnp.zeros((1, 256), F32), bias[None, :], (0, lax.axis_index("feat") * bias.shape[0])
    )
    high = lax.reduce_precision(bias_at, 8, 7)
    middle = lax.reduce_precision(bias_at - high, 8, 7)
    bias_rows = jnp.concatenate(
        [high, middle, bias_at - high - middle, jnp.zeros((13, 256), F32)], axis=0
    ).astype(BF)

    pieces = [features, lax.ppermute(features, "node", node_pairs(0, 0, 1))]
    for dx, dz in STEPS:
        piece = lax.ppermute(features, "node", node_pairs(dx, dz))
        pieces += [piece, lax.ppermute(piece, "node", node_pairs(0, 0, 1))]

    values = pl.pallas_call(
        load_kernel,
        in_specs=[ANY, ANY],
        out_specs=VMEM,
        out_shape=pltpu.VMEM(block_values.shape, BF),
        scratch_shapes=[pltpu.SemaphoreType.DMA((8,))],
        compiler_params=params(4),
        cost_estimate=pl.CostEstimate(
            flops=0, bytes_accessed=2 * block_values.size * 2, transcendentals=0
        ),
        name="load",
    )(block_values, pieces[1])

    mixed = pl.pallas_call(
        mix_kernel,
        in_specs=[SMEM, SMEM] + [VMEM] * 4 + [ANY] * 16,
        out_specs=VMEM,
        out_shape=shape((8, 16, 3 * width + 512)),
        scratch_shapes=[pltpu.VMEM((16, fin, nodes), BF), pltpu.SemaphoreType.DMA((16,))],
        compiler_params=params(16),
        name="mix",
    )(block_cols, block_counts, values, cotangent, weight, bias_rows, *pieces)

    both = lax.all_to_all(mixed, "feat", 0, 0, tiled=True)

    dense = pl.pallas_call(
        dense_kernel,
        in_specs=[VMEM] * 2,
        out_specs=VMEM,
        out_shape=shape((8, 16, 3 * width + 256)),
        compiler_params=params(16),
        name="dense",
    )(both, train_mask[None, :])

    grads = lax.all_to_all(dense, "feat", 0, 0, tiled=True)

    activation, own, other = pl.pallas_call(
        spread_kernel,
        in_specs=[SMEM, SMEM] + [VMEM] * 2,
        out_specs=[VMEM] * 3,
        out_shape=[
            shape((32, nodes)),
            shape((8, 16, nodes + 256)),
            shape((8, 16, nodes + 256)),
        ],
        scratch_shapes=[pltpu.VMEM((17, fin, nodes), F32)],
        compiler_params=params(24),
        name="spread",
    )(block_cols, block_counts, values, grads)

    other = lax.ppermute(other, "node", node_pairs(0, 0, 1))
    sums = pl.pallas_call(
        pair_kernel,
        in_specs=[VMEM] * 2,
        out_specs=[VMEM] * 8,
        out_shape=[shape((16, nodes + 256))] * 8,
        compiler_params=params(16),
        name="pair",
    )(own, other)
    landed = [sums[0]]
    for (dx, dz), piece in zip(STEPS, sums[1:]):
        landed.append(lax.ppermute(piece, "node", node_pairs(dx, dz)))
    total = sum(piece.astype(F32) for piece in landed)
    return activation, total[:, :nodes].astype(BF), total[:, nodes:]


def solution(mesh):
    placed = (
        P("feat", "node"),
        P("feat", None),
        P("feat"),
        P("node", None, None, None),
        P("node", None),
        P("node"),
        P("node"),
        P("feat", "node"),
    )
    return jax.shard_map(
        local,
        mesh=mesh,
        in_specs=placed,
        out_specs=(P("feat", "node"), P("feat", "node"), P("feat", None)),
        check_vma=False,
    )
```

time: 164 us -> 118 us (0.72)
  blocking collectives: 49.2 us -> 29.4 us
  starting transfers between devices: 52.6 us -> 36.8 us
  local copies, waits for them, and re-layouts: 18.5 us -> 10.7 us
    all_gather x1 -> x0, blocking collectives: 22.1 us -> none  [local(): whole_weight = lax.all_gather(weight, 'feat', axis=0, tiled=True)]
    unnamed x1 -> x0, blocking collectives: 16.4 us -> none
    all_to_all x0 -> x1, blocking collectives: none -> 15.2 us  [local(): both = lax.all_to_all(mixed, 'feat', 0, 0, tiled=True)]
    ppermute x1, starting transfers between devices: 12.2 us -> 2.03 us  [local(): other = lax.ppermute(other, 'node', node_pairs(0, 0, 1))]
    unnamed x24 -> x21, local copies, waits for them, and re-layouts: 17 us -> 8.53 us
    all_to_all x1 -> x0, starting transfers between devices: 4.23 us -> none  [local(): both = lax.all_to_all(mixed, 'feat', 0, 0, tiled=True)]
    all_to_all x1, blocking collectives: 10.7 us -> 14.2 us  [local(): grads = lax.all_to_all(dense, 'feat', 0, 0, tiled=True)]
    ppermute x1, starting transfers between devices: 6.04 us -> 4.38 us  [local(): pieces = [features, lax.ppermute(features, 'node', node_pairs(0, 0, 1))]]
  transfers between devices with their start and end apart: 24 -> 23, of which waited for: 10 -> 9; matrix products, arithmetic and copies ran while one was open for 1% -> 1% of each run, Pallas kernels for 0% -> 1%
where the time goes in v2:
time: 118 us
  starting transfers between devices  36.8 us (31%)
  blocking collectives  29.4 us (25%)
  waiting for transfers between devices  20.7 us (18%)
  Pallas kernels  19.5 us (17%)
  local copies, waits for them, and re-layouts  10.7 us (9%)
    all_to_all x1, blocking collectives, local(): both = lax.all_to_all(mixed, 'feat', 0, 0, tiled=True)  15.2 us
    all_to_all x1, blocking collectives, local(): grads = lax.all_to_all(dense, 'feat', 0, 0, tiled=True)  14.2 us
    ppermute x7, waiting for transfers between devices, local(): landed.append(lax.ppermute(piece, 'node', node_pairs(dx, dz)))  14 us
    ppermute x7, starting transfers between devices, local(): piece = lax.ppermute(features, 'node', node_pairs(dx, dz))  13 us
    ppermute x7, starting transfers between devices, local(): landed.append(lax.ppermute(piece, 'node', node_pairs(dx, dz)))  10.7 us
    pallas_call x1, Pallas kernels, local(): pl.pallas_call(mix_kernel, in_specs=[SMEM, SMEM] + [VMEM] * 4 + [ANY] * 1...  8.61 us
    unnamed x21, local copies, waits for them, and re-layouts  8.53 us
    pallas_call x1, Pallas kernels, local(): pl.pallas_call(spread_kernel, in_specs=[SMEM, SMEM] + [VMEM] * 2, out_spe...  8.36 us
  transfers between devices with their start and end apart: 23, of which 9 were waited for; matrix products, arithmetic and copies ran while one was open for 1% of the time, Pallas kernels for 1%

profile of v2, /device:TPU:1, one launch (start us, length us, event | category | flops | bytes accessed | tf_op | source)
XLA Modules:
  0.0 118.1 jit_solution(15239775028055008262)
XLA Ops:
  0.6 2.5 %collective-permute-start.11 = (bf16[16,6144]{1,0:T(8,128)(2,1)}, bf16[16,6144]{1,0:T(8,128)(2,1)S(1)}, u32[]{:S(2)}, u32[]{:S(2)}) collective-permute-start(bf16[16,6144]{1,0:T(8,128)(2,1)} %rest_0_.1), channel_id=1, source_target_pairs={{0,16},{8,24},{16,32},{24,40},{32,48},{40,56},{48,0},{56,8},{64,80... | collective-permute-start | bytes 589832 | tf_op jit(solution)/shard_map/ppermute | solution.py:192
  3.2 2.7 %collective-permute-start.9 = (bf16[16,6144]{1,0:T(8,128)(2,1)}, bf16[16,6144]{1,0:T(8,128)(2,1)S(1)}, u32[]{:S(2)}, u32[]{:S(2)}) collective-permute-start(bf16[16,6144]{1,0:T(8,128)(2,1)} %rest_0_.1), channel_id=1, source_target_pairs={{0,64},{8,72},{16,80},{24,88},{32,96},{40,104},{48,112},{56,120},{... | collective-permute-start | bytes 589832 | tf_op jit(solution)/shard_map/ppermute | solution.py:192
  5.9 3.3 %collective-permute-start.7 = (bf16[16,6144]{1,0:T(8,128)(2,1)}, bf16[16,6144]{1,0:T(8,128)(2,1)}, u32[]{:S(2)}, u32[]{:S(2)}) collective-permute-start(bf16[16,6144]{1,0:T(8,128)(2,1)} %rest_0_.1), channel_id=1, source_target_pairs={{0,32},{8,40},{16,48},{24,56},{32,0},{40,8},{48,16},{56,24},{64,96... | collective-permute-start | bytes 589832 | tf_op jit(solution)/shard_map/ppermute | solution.py:192
  9.9 3.2 %collective-permute-start.3 = (bf16[16,6144]{1,0:T(8,128)(2,1)}, bf16[16,6144]{1,0:T(8,128)(2,1)}, u32[]{:S(2)}, u32[]{:S(2)}) collective-permute-start(bf16[16,6144]{1,0:T(8,128)(2,1)} %rest_0_.1), channel_id=1, source_target_pairs={{0,80},{8,88},{16,96},{24,104},{32,112},{40,120},{48,64},{56,72},{... | collective-permute-start | bytes 589832 | tf_op jit(solution)/shard_map/ppermute | solution.py:192
  15.2 4.4 %collective-permute-start = (bf16[16,6144]{1,0:T(8,128)(2,1)}, bf16[16,6144]{1,0:T(8,128)(2,1)S(1)}, u32[]{:S(2)}, u32[]{:S(2)}) collective-permute-start(bf16[16,6144]{1,0:T(8,128)(2,1)} %rest_0_.1), channel_id=1, source_target_pairs={{0,8},{8,0},{16,24},{24,16},{32,40},{40,32},{48,56},{56,48},{64,72... | collective-permute-start | bytes 589832 | tf_op jit(solution)/shard_map/ppermute | solution.py:190
  19.6 1.7 %collective-permute-start.12 = (bf16[16,6144]{1,0:T(8,128)(2,1)S(1)}, bf16[16,6144]{1,0:T(8,128)(2,1)S(1)}, u32[]{:S(2)}, u32[]{:S(2)}) collective-permute-start(bf16[16,6144]{1,0:T(8,128)(2,1)S(1)} %collective-permute-done.11.rest_12_), channel_id=1, source_target_pairs={{0,8},{8,0},{16,24},{24,16},{32,40},{40,32},{48,56},{56,48},{64,72... | collective-permute-start | bytes 589832 | tf_op jit(solution)/shard_map/ppermute | solution.py:193
  22.0 2.1 %collective-permute-start.10 = (bf16[16,6144]{1,0:T(8,128)(2,1)S(1)}, bf16[16,6144]{1,0:T(8,128)(2,1)S(1)}, u32[]{:S(2)}, u32[]{:S(2)}) collective-permute-start(bf16[16,6144]{1,0:T(8,128)(2,1)S(1)} %collective-permute-done.9.rest_10_), channel_id=1, source_target_pairs={{0,8},{8,0},{16,24},{24,16},{32,40},{40,32},{48,56},{56,48},{64,72... | collective-permute-start | bytes 589832 | tf_op jit(solution)/shard_map/ppermute | solution.py:193
  24.8 1.4 %collective-permute-done.1.rest_2_ = bf16[16,6144]{1,0:T(8,128)(2,1)S(1)} collective-permute-done((bf16[16,6144]{1,0:T(8,128)(2,1)}, bf16[16,6144]{1,0:T(8,128)(2,1)S(1)}, u32[]{:S(2)}, u32[]{:S(2)}) %collective-permute-start.1) | collective-permute-done | bytes 196640 | tf_op jit(solution)/shard_map/ppermute | solution.py:192
  26.2 1.7 %collective-permute-start.8 = (bf16[16,6144]{1,0:T(8,128)(2,1)}, bf16[16,6144]{1,0:T(8,128)(2,1)S(1)}, u32[]{:S(2)}, u32[]{:S(2)}) collective-permute-start(bf16[16,6144]{1,0:T(8,128)(2,1)} %collective-permute-done.7.rest_8_), channel_id=1, source_target_pairs={{0,8},{8,0},{16,24},{24,16},{32,40},{40,32},{48,56},{56,48},{64,72... | collective-permute-start | bytes 589832 | tf_op jit(solution)/shard_map/ppermute | solution.py:193
  27.9 2.2 %collective-permute-done.13.rest_14_ = bf16[16,6144]{1,0:T(8,128)(2,1)S(1)} collective-permute-done((bf16[16,6144]{1,0:T(8,128)(2,1)}, bf16[16,6144]{1,0:T(8,128)(2,1)S(1)}, u32[]{:S(2)}, u32[]{:S(2)}) %collective-permute-start.13) | collective-permute-done | bytes 196640 | tf_op jit(solution)/shard_map/ppermute | solution.py:192
  31.3 6.4 %copy-done = bf16[48,12,128,128]{3,2,1,0:T(8,128)(2,1)S(1)} copy-done((bf16[48,12,128,128]{3,2,1,0:T(8,128)(2,1)S(1)}, bf16[48,12,128,128]{3,2,1,0:T(8,128)(2,1)}, u32[]{:S(2)}) %copy-start) | copy-done | bytes 18874392
  39.2 8.6 %mix.1 = bf16[8,16,2816]{2,1,0:T(8,128)(2,1)S(1)} custom-call(s32[48,12]{1,0:T(8,128)S(1)} %copy.12.cols, s32[48]{0:T(128)S(1)} %copy-done.9, bf16[48,12,128,128]{3,2,1,0:T(8,128)(2,1)S(1)} %load.1.values, bf16[32,6144]{1,0:T(8,128)(2,1)S(1)} %copy-done.1, bf16[16,256]{1,0:T(8,128)(2,1)S(1)} %copy-done.8, bf16[16,256]{1,0:T(8,128)(2,1)S(1)} %maximum_maximum_fusion.bias_rows, ...), custom_call_target="tpu_custom_call" | custom-call | tf_op jit(solution)/shard_map/mix/pallas_call | solution.py:208
  47.8 15.2 %all_to_all.10.both = bf16[8,16,2816]{2,1,0:T(8,128)(2,1)S(1)} all-to-all(bf16[8,16,2816]{2,1,0:T(8,128)(2,1)S(1)} %mix.1), channel_id=1, replica_groups=mesh['node'=16,'feat'=8] {'feat'}, dimensions={0} | all-to-all | bytes 1441792 | tf_op jit(solution)/shard_map/all_to_all | solution.py:218
  63.7 14.2 %all_to_all.11.grads = bf16[8,16,2560]{2,1,0:T(8,128)(2,1)S(1)} all-to-all(bf16[8,16,2560]{2,1,0:T(8,128)(2,1)S(1)} %dense.1), channel_id=1, replica_groups=mesh['node'=16,'feat'=8] {'feat'}, dimensions={0} | all-to-all | bytes 1310720 | tf_op jit(solution)/shard_map/all_to_all | solution.py:229
  77.9 8.4 %spread.1 = (bf16[32,6144]{1,0:T(8,128)(2,1)}, bf16[8,16,6400]{2,1,0:T(8,128)(2,1)S(1)}, bf16[8,16,6400]{2,1,0:T(8,128)(2,1)S(1)}) custom-call(s32[48,12]{1,0:T(8,128)S(1)} %copy.12.cols, s32[48]{0:T(128)S(1)} %copy-done.9, bf16[48,12,128,128]{3,2,1,0:T(8,128)(2,1)S(1)} %load.1.values, bf16[8,16,2560]{2,1,0:T(8,128)(2,1)S(1)} %all_to_all.11.grads), custom_call_target="tpu_custom_call" | custom-call | tf_op jit(solution)/shard_map/spread/pallas_call | solution.py:231
  86.3 2.0 %collective-permute-start.15 = (bf16[8,16,6400]{2,1,0:T(8,128)(2,1)S(1)}, bf16[8,16,6400]{2,1,0:T(8,128)(2,1)S(1)}, u32[]{:S(2)}, u32[]{:S(2)}) collective-permute-start(bf16[8,16,6400]{2,1,0:T(8,128)(2,1)S(1)} %get-tuple-element.16), channel_id=1, source_target_pairs={{0,8},{8,0},{16,24},{24,16},{32,40},{40,32},{48,56},{56,48},{64,72... | collective-permute-start | bytes 4915208 | tf_op jit(solution)/shard_map/ppermute | solution.py:245
  88.3 3.1 %collective-permute-done.15.other = bf16[8,16,6400]{2,1,0:T(8,128)(2,1)S(1)} collective-permute-done((bf16[8,16,6400]{2,1,0:T(8,128)(2,1)S(1)}, bf16[8,16,6400]{2,1,0:T(8,128)(2,1)S(1)}, u32[]{:S(2)}, u32[]{:S(2)}) %collective-permute-start.15) | collective-permute-done | bytes 1638432 | tf_op jit(solution)/shard_map/ppermute | solution.py:245
  91.9 3.9 %collective-permute-start.16 = (bf16[16,6400]{1,0:T(8,128)(2,1)S(1)}, bf16[16,6400]{1,0:T(8,128)(2,1)S(1)}, u32[]{:S(2)}, u32[]{:S(2)}) collective-permute-start(bf16[16,6400]{1,0:T(8,128)(2,1)S(1)} %get-tuple-element.18), channel_id=1, source_target_pairs={{0,96},{8,104},{16,112},{24,120},{32,64},{40,72},{48,80},{56,88},{... | collective-permute-start | bytes 614408 | tf_op jit(solution)/shard_map/ppermute | solution.py:256
  96.8 4.0 %collective-permute-start.18 = (bf16[16,6400]{1,0:T(8,128)(2,1)S(1)}, bf16[16,6400]{1,0:T(8,128)(2,1)S(1)}, u32[]{:S(2)}, u32[]{:S(2)}) collective-permute-start(bf16[16,6400]{1,0:T(8,128)(2,1)S(1)} %get-tuple-element.20), channel_id=1, source_target_pairs={{0,112},{8,120},{16,64},{24,72},{32,80},{40,88},{48,96},{56,104},{... | collective-permute-start | bytes 614408 | tf_op jit(solution)/shard_map/ppermute | solution.py:256
  103.3 3.8 %collective-permute-done.17 = bf16[16,6400]{1,0:T(8,128)(2,1)S(1)} collective-permute-done((bf16[16,6400]{1,0:T(8,128)(2,1)S(1)}, bf16[16,6400]{1,0:T(8,128)(2,1)S(1)}, u32[]{:S(2)}, u32[]{:S(2)}) %collective-permute-start.17) | collective-permute-done | bytes 204832 | tf_op jit(solution)/shard_map/ppermute | solution.py:256
  107.1 3.6 %collective-permute-done.18 = bf16[16,6400]{1,0:T(8,128)(2,1)S(1)} collective-permute-done((bf16[16,6400]{1,0:T(8,128)(2,1)S(1)}, bf16[16,6400]{1,0:T(8,128)(2,1)S(1)}, u32[]{:S(2)}, u32[]{:S(2)}) %collective-permute-start.18) | collective-permute-done | bytes 204832 | tf_op jit(solution)/shard_map/ppermute | solution.py:256
  110.7 1.5 %collective-permute-done.19 = bf16[16,6400]{1,0:T(8,128)(2,1)S(1)} collective-permute-done((bf16[16,6400]{1,0:T(8,128)(2,1)S(1)}, bf16[16,6400]{1,0:T(8,128)(2,1)S(1)}, u32[]{:S(2)}, u32[]{:S(2)}) %collective-permute-start.19) | collective-permute-done | bytes 204832 | tf_op jit(solution)/shard_map/ppermute | solution.py:256
  112.2 2.7 %collective-permute-done.20 = bf16[16,6400]{1,0:T(8,128)(2,1)S(1)} collective-permute-done((bf16[16,6400]{1,0:T(8,128)(2,1)S(1)}, bf16[16,6400]{1,0:T(8,128)(2,1)S(1)}, u32[]{:S(2)}, u32[]{:S(2)}) %collective-permute-start.20) | collective-permute-done | bytes 204832 | tf_op jit(solution)/shard_map/ppermute | solution.py:256
  114.9 1.6 %collective-permute-done.21 = bf16[16,6400]{1,0:T(8,128)(2,1)S(1)} collective-permute-done((bf16[16,6400]{1,0:T(8,128)(2,1)S(1)}, bf16[16,6400]{1,0:T(8,128)(2,1)S(1)}, u32[]{:S(2)}, u32[]{:S(2)}) %collective-permute-start.21) | collective-permute-done | bytes 204832 | tf_op jit(solution)/shard_map/ppermute | solution.py:256
  (59 shorter events, 13.0 us)
Async XLA Ops:
  0.6 14.1 %collective-permute-start.11 = (bf16[16,6144]{1,0:T(8,128)(2,1)}, bf16[16,6144]{1,0:T(8,128)(2,1)S(1)}, u32[]{:S(2)}, u32[]{:S(2)}) collective-permute-start(bf16[16,6144]{1,0:T(8,128)(2,1)} %rest_0_.1), channel_id=1, source_target_pairs={{0,16},{8,24},{16,32},{24,40},{32,48},{40,56},{48,0},{56,8},{64,80... | collective-permute-start | bytes 589832 | tf_op jit(solution)/shard_map/ppermute | solution.py:192
  3.2 12.1 %collective-permute-start.9 = (bf16[16,6144]{1,0:T(8,128)(2,1)}, bf16[16,6144]{1,0:T(8,128)(2,1)S(1)}, u32[]{:S(2)}, u32[]{:S(2)}) collective-permute-start(bf16[16,6144]{1,0:T(8,128)(2,1)} %rest_0_.1), channel_id=1, source_target_pairs={{0,64},{8,72},{16,80},{24,88},{32,96},{40,104},{48,112},{56,120},{... | collective-permute-start | bytes 589832 | tf_op jit(solution)/shard_map/ppermute | solution.py:192
  5.9 13.7 %collective-permute-start.7 = (bf16[16,6144]{1,0:T(8,128)(2,1)}, bf16[16,6144]{1,0:T(8,128)(2,1)}, u32[]{:S(2)}, u32[]{:S(2)}) collective-permute-start(bf16[16,6144]{1,0:T(8,128)(2,1)} %rest_0_.1), channel_id=1, source_target_pairs={{0,32},{8,40},{16,48},{24,56},{32,0},{40,8},{48,16},{56,24},{64,96... | collective-permute-start | bytes 589832 | tf_op jit(solution)/shard_map/ppermute | solution.py:192
  9.2 10.4 %collective-permute-start.5 = (bf16[16,6144]{1,0:T(8,128)(2,1)}, bf16[16,6144]{1,0:T(8,128)(2,1)}, u32[]{:S(2)}, u32[]{:S(2)}) collective-permute-start(bf16[16,6144]{1,0:T(8,128)(2,1)} %rest_0_.1), channel_id=1, source_target_pairs={{0,112},{8,120},{16,64},{24,72},{32,80},{40,88},{48,96},{56,104},{... | collective-permute-start | bytes 589832 | tf_op jit(solution)/shard_map/ppermute | solution.py:192
  9.9 12.1 %collective-permute-start.3 = (bf16[16,6144]{1,0:T(8,128)(2,1)}, bf16[16,6144]{1,0:T(8,128)(2,1)}, u32[]{:S(2)}, u32[]{:S(2)}) collective-permute-start(bf16[16,6144]{1,0:T(8,128)(2,1)} %rest_0_.1), channel_id=1, source_target_pairs={{0,80},{8,88},{16,96},{24,104},{32,112},{40,120},{48,64},{56,72},{... | collective-permute-start | bytes 589832 | tf_op jit(solution)/shard_map/ppermute | solution.py:192
  14.7 11.5 %collective-permute-start.1 = (bf16[16,6144]{1,0:T(8,128)(2,1)}, bf16[16,6144]{1,0:T(8,128)(2,1)S(1)}, u32[]{:S(2)}, u32[]{:S(2)}) collective-permute-start(bf16[16,6144]{1,0:T(8,128)(2,1)} %rest_0_.1), channel_id=1, source_target_pairs={{0,96},{8,104},{16,112},{24,120},{32,64},{40,72},{48,80},{56,88},{... | collective-permute-start | bytes 589832 | tf_op jit(solution)/shard_map/ppermute | solution.py:192
  15.2 12.6 %collective-permute-start = (bf16[16,6144]{1,0:T(8,128)(2,1)}, bf16[16,6144]{1,0:T(8,128)(2,1)S(1)}, u32[]{:S(2)}, u32[]{:S(2)}) collective-permute-start(bf16[16,6144]{1,0:T(8,128)(2,1)} %rest_0_.1), channel_id=1, source_target_pairs={{0,8},{8,0},{16,24},{24,16},{32,40},{40,32},{48,56},{56,48},{64,72... | collective-permute-start | bytes 589832 | tf_op jit(solution)/shard_map/ppermute | solution.py:190
  19.6 10.4 %collective-permute-start.13 = (bf16[16,6144]{1,0:T(8,128)(2,1)}, bf16[16,6144]{1,0:T(8,128)(2,1)S(1)}, u32[]{:S(2)}, u32[]{:S(2)}) collective-permute-start(bf16[16,6144]{1,0:T(8,128)(2,1)} %rest_0_.1), channel_id=1, source_target_pairs={{0,48},{8,56},{16,0},{24,8},{32,16},{40,24},{48,32},{56,40},{64,11... | collective-permute-start | bytes 589832 | tf_op jit(solution)/shard_map/ppermute | solution.py:192
  19.6 11.1 %collective-permute-start.12 = (bf16[16,6144]{1,0:T(8,128)(2,1)S(1)}, bf16[16,6144]{1,0:T(8,128)(2,1)S(1)}, u32[]{:S(2)}, u32[]{:S(2)}) collective-permute-start(bf16[16,6144]{1,0:T(8,128)(2,1)S(1)} %collective-permute-done.11.rest_12_), channel_id=1, source_target_pairs={{0,8},{8,0},{16,24},{24,16},{32,40},{40,32},{48,56},{56,48},{64,72... | collective-permute-start | bytes 589832 | tf_op jit(solution)/shard_map/ppermute | solution.py:193
  22.0 8.7 %collective-permute-start.10 = (bf16[16,6144]{1,0:T(8,128)(2,1)S(1)}, bf16[16,6144]{1,0:T(8,128)(2,1)S(1)}, u32[]{:S(2)}, u32[]{:S(2)}) collective-permute-start(bf16[16,6144]{1,0:T(8,128)(2,1)S(1)} %collective-permute-done.9.rest_10_), channel_id=1, source_target_pairs={{0,8},{8,0},{16,24},{24,16},{32,40},{40,32},{48,56},{56,48},{64,72... | collective-permute-start | bytes 589832 | tf_op jit(solution)/shard_map/ppermute | solution.py:193
  26.2 12.9 %collective-permute-start.8 = (bf16[16,6144]{1,0:T(8,128)(2,1)}, bf16[16,6144]{1,0:T(8,128)(2,1)S(1)}, u32[]{:S(2)}, u32[]{:S(2)}) collective-permute-start(bf16[16,6144]{1,0:T(8,128)(2,1)} %collective-permute-done.7.rest_8_), channel_id=1, source_target_pairs={{0,8},{8,0},{16,24},{24,16},{32,40},{40,32},{48,56},{56,48},{64,72... | collective-permute-start | bytes 589832 | tf_op jit(solution)/shard_map/ppermute | solution.py:193
  27.9 11.2 %collective-permute-start.6 = (bf16[16,6144]{1,0:T(8,128)(2,1)}, bf16[16,6144]{1,0:T(8,128)(2,1)S(1)}, u32[]{:S(2)}, u32[]{:S(2)}) collective-permute-start(bf16[16,6144]{1,0:T(8,128)(2,1)} %collective-permute-done.5.rest_6_), channel_id=1, source_target_pairs={{0,8},{8,0},{16,24},{24,16},{32,40},{40,32},{48,56},{56,48},{64,72... | collective-permute-start | bytes 589832 | tf_op jit(solution)/shard_map/ppermute | solution.py:193
  30.0 9.0 %collective-permute-start.4 = (bf16[16,6144]{1,0:T(8,128)(2,1)}, bf16[16,6144]{1,0:T(8,128)(2,1)S(1)}, u32[]{:S(2)}, u32[]{:S(2)}) collective-permute-start(bf16[16,6144]{1,0:T(8,128)(2,1)} %collective-permute-done.3.rest_4_), channel_id=1, source_target_pairs={{0,8},{8,0},{16,24},{24,16},{32,40},{40,32},{48,56},{56,48},{64,72... | collective-permute-start | bytes 589832 | tf_op jit(solution)/shard_map/ppermute | solution.py:193
  30.7 8.4 %collective-permute-start.2 = (bf16[16,6144]{1,0:T(8,128)(2,1)S(1)}, bf16[16,6144]{1,0:T(8,128)(2,1)S(1)}, u32[]{:S(2)}, u32[]{:S(2)}) collective-permute-start(bf16[16,6144]{1,0:T(8,128)(2,1)S(1)} %collective-permute-done.1.rest_2_), channel_id=1, source_target_pairs={{0,8},{8,0},{16,24},{24,16},{32,40},{40,32},{48,56},{56,48},{64,72... | collective-permute-start | bytes 589832 | tf_op jit(solution)/shard_map/ppermute | solution.py:193
  30.7 8.4 %collective-permute-start.14 = (bf16[16,6144]{1,0:T(8,128)(2,1)S(1)}, bf16[16,6144]{1,0:T(8,128)(2,1)S(1)}, u32[]{:S(2)}, u32[]{:S(2)}) collective-permute-start(bf16[16,6144]{1,0:T(8,128)(2,1)S(1)} %collective-permute-done.13.rest_14_), channel_id=1, source_target_pairs={{0,8},{8,0},{16,24},{24,16},{32,40},{40,32},{48,56},{56,48},{64,72... | collective-permute-start | bytes 589832 | tf_op jit(solution)/shard_map/ppermute | solution.py:193
  39.0 23.9 %copy-start.7 = (s32[6144]{0:T(1024)S(1)}, s32[6144]{0:T(1024)}, u32[]{:S(2)}) copy-start(s32[6144]{0:T(1024)} %param.14) | copy-start | bytes 73732
  86.3 5.2 %collective-permute-start.15 = (bf16[8,16,6400]{2,1,0:T(8,128)(2,1)S(1)}, bf16[8,16,6400]{2,1,0:T(8,128)(2,1)S(1)}, u32[]{:S(2)}, u32[]{:S(2)}) collective-permute-start(bf16[8,16,6400]{2,1,0:T(8,128)(2,1)S(1)} %get-tuple-element.16), channel_id=1, source_target_pairs={{0,8},{8,0},{16,24},{24,16},{32,40},{40,32},{48,56},{56,48},{64,72... | collective-permute-start | bytes 4915208 | tf_op jit(solution)/shard_map/ppermute | solution.py:245
  91.9 10.3 %collective-permute-start.16 = (bf16[16,6400]{1,0:T(8,128)(2,1)S(1)}, bf16[16,6400]{1,0:T(8,128)(2,1)S(1)}, u32[]{:S(2)}, u32[]{:S(2)}) collective-permute-start(bf16[16,6400]{1,0:T(8,128)(2,1)S(1)} %get-tuple-element.18), channel_id=1, source_target_pairs={{0,96},{8,104},{16,112},{24,120},{32,64},{40,72},{48,80},{56,88},{... | collective-permute-start | bytes 614408 | tf_op jit(solution)/shard_map/ppermute | solution.py:256
  95.7 11.3 %collective-permute-start.17 = (bf16[16,6400]{1,0:T(8,128)(2,1)S(1)}, bf16[16,6400]{1,0:T(8,128)(2,1)S(1)}, u32[]{:S(2)}, u32[]{:S(2)}) collective-permute-start(bf16[16,6400]{1,0:T(8,128)(2,1)S(1)} %get-tuple-element.19), channel_id=1, source_target_pairs={{0,80},{8,88},{16,96},{24,104},{32,112},{40,120},{48,64},{56,72},{... | collective-permute-start | bytes 614408 | tf_op jit(solution)/shard_map/ppermute | solution.py:256
  96.8 13.9 %collective-permute-start.18 = (bf16[16,6400]{1,0:T(8,128)(2,1)S(1)}, bf16[16,6400]{1,0:T(8,128)(2,1)S(1)}, u32[]{:S(2)}, u32[]{:S(2)}) collective-permute-start(bf16[16,6400]{1,0:T(8,128)(2,1)S(1)} %get-tuple-element.20), channel_id=1, source_target_pairs={{0,112},{8,120},{16,64},{24,72},{32,80},{40,88},{48,96},{56,104},{... | collective-permute-start | bytes 614408 | tf_op jit(solution)/shard_map/ppermute | solution.py:256
  100.8 11.4 %collective-permute-start.19 = (bf16[16,6400]{1,0:T(8,128)(2,1)S(1)}, bf16[16,6400]{1,0:T(8,128)(2,1)S(1)}, u32[]{:S(2)}, u32[]{:S(2)}) collective-permute-start(bf16[16,6400]{1,0:T(8,128)(2,1)S(1)} %get-tuple-element.21), channel_id=1, source_target_pairs={{0,32},{8,40},{16,48},{24,56},{32,0},{40,8},{48,16},{56,24},{64,96... | collective-permute-start | bytes 614408 | tf_op jit(solution)/shard_map/ppermute | solution.py:256
  100.8 14.1 %collective-permute-start.20 = (bf16[16,6400]{1,0:T(8,128)(2,1)S(1)}, bf16[16,6400]{1,0:T(8,128)(2,1)S(1)}, u32[]{:S(2)}, u32[]{:S(2)}) collective-permute-start(bf16[16,6400]{1,0:T(8,128)(2,1)S(1)} %get-tuple-element.22), channel_id=1, source_target_pairs={{0,64},{8,72},{16,80},{24,88},{32,96},{40,104},{48,112},{56,120},{... | collective-permute-start | bytes 614408 | tf_op jit(solution)/shard_map/ppermute | solution.py:256
  102.2 14.4 %collective-permute-start.21 = (bf16[16,6400]{1,0:T(8,128)(2,1)S(1)}, bf16[16,6400]{1,0:T(8,128)(2,1)S(1)}, u32[]{:S(2)}, u32[]{:S(2)}) collective-permute-start(bf16[16,6400]{1,0:T(8,128)(2,1)S(1)} %get-tuple-element.23), channel_id=1, source_target_pairs={{0,16},{8,24},{16,32},{24,40},{32,48},{40,56},{48,0},{56,8},{64,80... | collective-permute-start | bytes 614408 | tf_op jit(solution)/shard_map/ppermute | solution.py:256
  107.1 9.5 %collective-permute-start.22 = (bf16[16,6400]{1,0:T(8,128)(2,1)S(1)}, bf16[16,6400]{1,0:T(8,128)(2,1)S(1)}, u32[]{:S(2)}, u32[]{:S(2)}) collective-permute-start(bf16[16,6400]{1,0:T(8,128)(2,1)S(1)} %get-tuple-element.24), channel_id=1, source_target_pairs={{0,48},{8,56},{16,0},{24,8},{32,16},{40,24},{48,32},{56,40},{64,11... | collective-permute-start | bytes 614408 | tf_op jit(solution)/shard_map/ppermute | solution.py:256
  (9 other events, 16.6 us)

commit v3 on v2

--- a/solution.py
+++ b/solution.py
@@ -11,6 +11,8 @@
 SMEM = pl.BlockSpec(memory_space=pltpu.SMEM)
 VMEM = pl.BlockSpec(memory_space=pltpu.VMEM)
 STEPS = ((1, 2), (1, 1), (1, 3), (0, 2), (1, 0), (0, 1), (0, 3))
+FAR = (1, 2)
+SHARED = (((1, 1), (1, 3)), ((0, 2), (1, 0)), ((0, 1), (0, 3)))
 BLOCK = 128
 
 
@@ -33,6 +35,22 @@
     return ((x ^ dx) * 4 + ((z + dz) & 3)) * 2 + (c ^ dcore)
 
 
+def shared_pairs(steps):
+    return [
+        (node_at(x, z, c), node_at(x ^ steps[c][0], (z + steps[c][1]) % 4, c))
+        for x in range(2)
+        for z in range(4)
+        for c in range(2)
+    ]
+
+
+def shared_near(steps, server, sign, dcore):
+    core = (lax.axis_index("node") & 1) ^ server
+    dx = jnp.where(core == 0, steps[0][0], steps[1][0])
+    dz = jnp.where(core == 0, steps[0][1], steps[1][1])
+    return node_near(dx, sign * dz, dcore)
+
+
 def place_of(column):
     group = lax.shift_right_logical(column * 21846, 20)
     return group, pl.multiple_of((column - group * 48) * BLOCK, BLOCK)
@@ -42,7 +60,7 @@
     return pltpu.CompilerParams(vmem_limit_bytes=mib * 2**20)
 
 
-def load_kernel(values, _, out, sems):
+def load_kernel(values, _, out, loaded, sems):
     count = sems.shape[0]
     rows = values.shape[0] // count
     copies = [
@@ -55,22 +73,30 @@
         copy.start()
     for copy in copies:
         copy.wait()
+    loaded[...] = jnp.zeros_like(loaded)
 
 
 def mix_kernel(cols, counts, values, cotangent, weight, bias_rows, *rest):
-    pieces, (out, held, sems) = rest[:16], rest[16:]
+    pieces, (out, held, sems) = rest[:10], rest[10:]
     slots = values.shape[1]
     chunks, _, _ = out.shape
     width = cotangent.shape[1] // chunks
     rows = values.shape[0] // chunks
 
-    copies = []
-    for k, (dx, dz) in enumerate(((0, 0),) + STEPS):
-        for core in range(2):
-            at = 2 * k + core
-            copies.append(
-                pltpu.make_async_copy(pieces[at], held.at[node_near(dx, -dz, core)], sems.at[at])
-            )
+    sources = []
+    for at, (dx, dz) in enumerate(((0, 0), FAR)):
+        for server in range(2):
+            sources.append((pieces[2 * at + server], node_near(dx, -dz, server)))
+    for at, steps in enumerate(SHARED):
+        for server in range(2):
+            for q in range(2):
+                sources.append(
+                    (pieces[4 + 2 * at + server].at[q], shared_near(steps, server, -1, server ^ q))
+                )
+    copies = [
+        pltpu.make_async_copy(piece, held.at[group], sems.at[at])
+        for at, (piece, group) in enumerate(sources)
+    ]
     for copy in copies:
         copy.start()
     for j in range(chunks):
@@ -187,27 +213,31 @@
         [high, middle, bias_at - high - middle, jnp.zeros((13, 256), F32)], axis=0
     ).astype(BF)
 
-    pieces = [features, lax.ppermute(features, "node", node_pairs(0, 0, 1))]
-    for dx, dz in STEPS:
-        piece = lax.ppermute(features, "node", node_pairs(dx, dz))
-        pieces += [piece, lax.ppermute(piece, "node", node_pairs(0, 0, 1))]
-
-    values = pl.pallas_call(
+    swap = node_pairs(0, 0, 1)
+    pieces = [features, lax.ppermute(features, "node", swap)]
+    pair = jnp.stack(pieces)
+    arrived = [lax.ppermute(features, "node", node_pairs(*FAR))]
+    arrived += [lax.ppermute(pair, "node", shared_pairs(steps)) for steps in SHARED]
+    values, loaded = pl.pallas_call(
         load_kernel,
-        in_specs=[ANY, ANY],
-        out_specs=VMEM,
-        out_shape=pltpu.VMEM(block_values.shape, BF),
+        in_specs=[pl.BlockSpec(memory_space=pltpu.HBM), ANY],
+        out_specs=[VMEM, VMEM],
+        out_shape=[pltpu.VMEM(block_values.shape, BF), shape((8, 128), F32)],
         scratch_shapes=[pltpu.SemaphoreType.DMA((8,))],
         compiler_params=params(4),
         cost_estimate=pl.CostEstimate(
             flops=0, bytes_accessed=2 * block_values.size * 2, transcendentals=0
         ),
         name="load",
-    )(block_values, pieces[1])
+    )(pltpu.with_memory_space_constraint(block_values, pltpu.HBM), pair)
+
+    for piece in arrived:
+        piece, _ = lax.optimization_barrier((piece, loaded))
+        pieces += [piece, lax.ppermute(piece, "node", swap)]
 
     mixed = pl.pallas_call(
         mix_kernel,
-        in_specs=[SMEM, SMEM] + [VMEM] * 4 + [ANY] * 16,
+        in_specs=[SMEM, SMEM] + [VMEM] * 4 + [ANY] * 10,
         out_specs=VMEM,
         out_shape=shape((8, 16, 3 * width + 512)),
         scratch_shapes=[pltpu.VMEM((16, fin, nodes), BF), pltpu.SemaphoreType.DMA((16,))],

time: 118 us -> 112 us (0.949)
  starting transfers between devices: 36.8 us -> 26.7 us
  local copies, waits for them, and re-layouts: 10.7 us -> 3.63 us
  waiting for transfers between devices: 20.7 us -> 26.1 us
  Pallas kernels: 19.5 us -> 24.5 us
  other arithmetic: 0.29 us -> 1.99 us
    ppermute x15 -> x9, starting transfers between devices: 24 us -> 11.5 us  [the longest x3 6.65 us: local(): lax.ppermute(pair, 'node', shared_pairs(steps))]
    unnamed x21 -> x15, local copies, waits for them, and re-layouts: 8.53 us -> 1.49 us
    pallas_call x1, Pallas kernels: 1.35 us -> 7.18 us  [local(): pl.pallas_call(load_kernel, in_specs=[pl.BlockSpec(memory_space=pltpu.HBM...]
    ppermute x15 -> x9, waiting for transfers between devices: 3.6 us -> 9.17 us  [the longest x3 4.62 us: local(): lax.ppermute(pair, 'node', shared_pairs(steps))]
    all_to_all x1, blocking collectives: 14.2 us -> 12.3 us  [local(): grads = lax.all_to_all(dense, 'feat', 0, 0, tiled=True)]
    another operation x1 -> x2, other arithmetic: 0.01 us -> 1.72 us  [the longest x1 1.71 us: local(): pair = jnp.stack(pieces)]
    ppermute x7, starting transfers between devices: 10.7 us -> 12.2 us  [local(): landed.append(lax.ppermute(piece, 'node', node_pairs(dx, dz)))]
  transfers between devices with their start and end apart: 23 -> 17, of which waited for: 9 -> 9; matrix products, arithmetic and copies ran while one was open for 1% -> 2% of each run, Pallas kernels for 1% -> 6%
where the time goes in v3:
time: 112 us
  blocking collectives  28.4 us (25%)
  starting transfers between devices  26.7 us (24%)
  waiting for transfers between devices  26.1 us (23%)
  Pallas kernels  24.5 us (22%)
  local copies, waits for them, and re-layouts  3.63 us (3%)
  other arithmetic  1.99 us (2%)
    all_to_all x1, blocking collectives, local(): both = lax.all_to_all(mixed, 'feat', 0, 0, tiled=True)  16.1 us
    ppermute x7, waiting for transfers between devices, local(): landed.append(lax.ppermute(piece, 'node', node_pairs(dx, dz)))  13.8 us
    all_to_all x1, blocking collectives, local(): grads = lax.all_to_all(dense, 'feat', 0, 0, tiled=True)  12.3 us
    ppermute x7, starting transfers between devices, local(): landed.append(lax.ppermute(piece, 'node', node_pairs(dx, dz)))  12.2 us
    pallas_call x1, Pallas kernels, local(): pl.pallas_call(spread_kernel, in_specs=[SMEM, SMEM] + [VMEM] * 2, out_spe...  8.36 us
    pallas_call x1, Pallas kernels, local(): pl.pallas_call(mix_kernel, in_specs=[SMEM, SMEM] + [VMEM] * 4 + [ANY] * 1...  7.82 us
    pallas_call x1, Pallas kernels, local(): pl.pallas_call(load_kernel, in_specs=[pl.BlockSpec(memory_space=pltpu.HBM...  7.18 us
    ppermute x3, starting transfers between devices, local(): lax.ppermute(pair, 'node', shared_pairs(steps))  6.65 us
  transfers between devices with their start and end apart: 17, of which 9 were waited for; matrix products, arithmetic and copies ran while one was open for 2% of the time, Pallas kernels for 6%

profile of v3, /device:TPU:1, one launch (start us, length us, event | category | flops | bytes accessed | tf_op | source)
XLA Modules:
  0.0 112.1 jit_solution(4278297818454697149)
XLA Ops:
  0.6 1.5 %collective-permute-start = (bf16[16,6144]{1,0:T(8,128)(2,1)}, bf16[16,6144]{1,0:T(8,128)(2,1)S(1)}, u32[]{:S(2)}, u32[]{:S(2)}) collective-permute-start(bf16[16,6144]{1,0:T(8,128)(2,1)} %rest_0_.1), channel_id=1, source_target_pairs={{0,8},{8,0},{16,24},{24,16},{32,40},{40,32},{48,56},{56,48},{64,72... | collective-permute-start | bytes 589832 | tf_op jit(solution)/shard_map/ppermute | solution.py:217
  2.1 1.3 %collective-permute-done.rest_1_ = bf16[16,6144]{1,0:T(8,128)(2,1)S(1)} collective-permute-done((bf16[16,6144]{1,0:T(8,128)(2,1)}, bf16[16,6144]{1,0:T(8,128)(2,1)S(1)}, u32[]{:S(2)}, u32[]{:S(2)}) %collective-permute-start) | collective-permute-done | bytes 196640 | tf_op jit(solution)/shard_map/ppermute | solution.py:217
  3.4 1.7 %pad_maximum_fusion._ = bf16[2,16,6144]{2,1,0:T(8,128)(2,1)} fusion(bf16[1,16,6144]{2,1,0:T(8,128)(2,1)S(1)} %bitcast.5, bf16[1,16,6144]{2,1,0:T(8,128)(2,1)} %bitcast.4), kind=kLoop, calls=%fused_computation.2 | loop fusion | flops 196608 | bytes 786432 | tf_op jit(solution)/shard_map/stack | solution.py:218
  5.8 3.8 %collective-permute-start.7 = (bf16[2,16,6144]{2,1,0:T(8,128)(2,1)}, bf16[2,16,6144]{2,1,0:T(8,128)(2,1)}, u32[]{:S(2)}, u32[]{:S(2)}) collective-permute-start(bf16[2,16,6144]{2,1,0:T(8,128)(2,1)} %pad_maximum_fusion._), channel_id=1, source_target_pairs={{0,16},{8,56},{16,32},{24,8},{32,48},{40,24},{48,0},{56,40},{64,80... | collective-permute-start | bytes 1179656 | tf_op jit(solution)/shard_map/ppermute | solution.py:220
  9.6 2.7 %collective-permute-start.5 = (bf16[2,16,6144]{2,1,0:T(8,128)(2,1)}, bf16[2,16,6144]{2,1,0:T(8,128)(2,1)}, u32[]{:S(2)}, u32[]{:S(2)}) collective-permute-start(bf16[2,16,6144]{2,1,0:T(8,128)(2,1)} %pad_maximum_fusion._), channel_id=1, source_target_pairs={{0,32},{8,72},{16,48},{24,88},{32,0},{40,104},{48,16},{56,120},{64... | collective-permute-start | bytes 1179656 | tf_op jit(solution)/shard_map/ppermute | solution.py:220
  12.4 2.0 %collective-permute-start.1 = (bf16[16,6144]{1,0:T(8,128)(2,1)}, bf16[16,6144]{1,0:T(8,128)(2,1)}, u32[]{:S(2)}, u32[]{:S(2)}) collective-permute-start(bf16[16,6144]{1,0:T(8,128)(2,1)} %rest_0_.1), channel_id=1, source_target_pairs={{0,96},{8,104},{16,112},{24,120},{32,64},{40,72},{48,80},{56,88},{... | collective-permute-start | bytes 589832 | tf_op jit(solution)/shard_map/ppermute | solution.py:219
  14.5 0.8 copy.12.cols
  16.1 7.2 %load.1 = (bf16[48,12,128,128]{3,2,1,0:T(8,128)(2,1)S(1)}, f32[8,128]{1,0:T(8,128)}) custom-call(bf16[48,12,128,128]{3,2,1,0:T(8,128)(2,1)} %values.1, bf16[2,16,6144]{2,1,0:T(8,128)(2,1)} %pad_maximum_fusion._), custom_call_target="tpu_custom_call" | custom-call | bytes 37748736 | tf_op jit(solution)/shard_map/load/pallas_call | solution.py:221
  23.3 4.6 %collective-permute-done.3.rest_4_ = bf16[2,16,6144]{2,1,0:T(8,128)(2,1)} collective-permute-done((bf16[2,16,6144]{2,1,0:T(8,128)(2,1)}, bf16[2,16,6144]{2,1,0:T(8,128)(2,1)}, u32[]{:S(2)}, u32[]{:S(2)}) %collective-permute-start.3) | collective-permute-done | bytes 393248 | tf_op jit(solution)/shard_map/ppermute | solution.py:220
  28.6 2.1 %collective-permute-done.1.rest_2_ = bf16[16,6144]{1,0:T(8,128)(2,1)} collective-permute-done((bf16[16,6144]{1,0:T(8,128)(2,1)}, bf16[16,6144]{1,0:T(8,128)(2,1)}, u32[]{:S(2)}, u32[]{:S(2)}) %collective-permute-start.1) | collective-permute-done | bytes 196640 | tf_op jit(solution)/shard_map/ppermute | solution.py:219
  31.4 1.2 %collective-permute-done.2.rest_3_ = bf16[16,6144]{1,0:T(8,128)(2,1)S(1)} collective-permute-done((bf16[16,6144]{1,0:T(8,128)(2,1)}, bf16[16,6144]{1,0:T(8,128)(2,1)S(1)}, u32[]{:S(2)}, u32[]{:S(2)}) %collective-permute-start.2) | collective-permute-done | bytes 196640 | tf_op jit(solution)/shard_map/ppermute | solution.py:236
  32.7 7.8 %mix.1 = bf16[8,16,2816]{2,1,0:T(8,128)(2,1)S(1)} custom-call(s32[48,12]{1,0:T(8,128)S(1)} %copy.12.cols, s32[48]{0:T(128)S(1)} %copy-done.6, bf16[48,12,128,128]{3,2,1,0:T(8,128)(2,1)S(1)} %get-tuple-element.20.values, bf16[32,6144]{1,0:T(8,128)(2,1)S(1)} %copy-done.3, bf16[16,256]{1,0:T(8,128)(2,1)S(1)} %copy-done.5, ...), custom_call_target="tpu_custom_call" | custom-call | tf_op jit(solution)/shard_map/mix/pallas_call | solution.py:238
  40.5 16.1 %all_to_all.10.both = bf16[8,16,2816]{2,1,0:T(8,128)(2,1)S(1)} all-to-all(bf16[8,16,2816]{2,1,0:T(8,128)(2,1)S(1)} %mix.1), channel_id=1, replica_groups=mesh['node'=16,'feat'=8] {'feat'}, dimensions={0} | all-to-all | bytes 1441792 | tf_op jit(solution)/shard_map/all_to_all | solution.py:248
  57.3 12.3 %all_to_all.11.grads = bf16[8,16,2560]{2,1,0:T(8,128)(2,1)S(1)} all-to-all(bf16[8,16,2560]{2,1,0:T(8,128)(2,1)S(1)} %dense.1), channel_id=1, replica_groups=mesh['node'=16,'feat'=8] {'feat'}, dimensions={0} | all-to-all | bytes 1310720 | tf_op jit(solution)/shard_map/all_to_all | solution.py:259
  69.7 8.4 %spread.1 = (bf16[32,6144]{1,0:T(8,128)(2,1)}, bf16[8,16,6400]{2,1,0:T(8,128)(2,1)S(1)}, bf16[8,16,6400]{2,1,0:T(8,128)(2,1)S(1)}) custom-call(s32[48,12]{1,0:T(8,128)S(1)} %copy.12.cols, s32[48]{0:T(128)S(1)} %copy-done.6, bf16[48,12,128,128]{3,2,1,0:T(8,128)(2,1)S(1)} %get-tuple-element.20.values, bf16[8,16,2560]{2,1,0:T(8,128)(2,1)S(1)} %all_to_all.11.grads), custom_call_target="tpu_custom_call" | custom-call | tf_op jit(solution)/shard_map/spread/pallas_call | solution.py:261
  78.0 3.0 %collective-permute-start.9 = (bf16[8,16,6400]{2,1,0:T(8,128)(2,1)S(1)}, bf16[8,16,6400]{2,1,0:T(8,128)(2,1)S(1)}, u32[]{:S(2)}, u32[]{:S(2)}) collective-permute-start(bf16[8,16,6400]{2,1,0:T(8,128)(2,1)S(1)} %get-tuple-element.28), channel_id=1, source_target_pairs={{0,8},{8,0},{16,24},{24,16},{32,40},{40,32},{48,56},{56,48},{64,72... | collective-permute-start | bytes 4915208 | tf_op jit(solution)/shard_map/ppermute | solution.py:275
  81.1 3.1 %collective-permute-done.9.other = bf16[8,16,6400]{2,1,0:T(8,128)(2,1)S(1)} collective-permute-done((bf16[8,16,6400]{2,1,0:T(8,128)(2,1)S(1)}, bf16[8,16,6400]{2,1,0:T(8,128)(2,1)S(1)}, u32[]{:S(2)}, u32[]{:S(2)}) %collective-permute-start.9) | collective-permute-done | bytes 1638432 | tf_op jit(solution)/shard_map/ppermute | solution.py:275
  84.6 5.5 %collective-permute-start.10 = (bf16[16,6400]{1,0:T(8,128)(2,1)S(1)}, bf16[16,6400]{1,0:T(8,128)(2,1)S(1)}, u32[]{:S(2)}, u32[]{:S(2)}) collective-permute-start(bf16[16,6400]{1,0:T(8,128)(2,1)S(1)} %get-tuple-element.30), channel_id=1, source_target_pairs={{0,96},{8,104},{16,112},{24,120},{32,64},{40,72},{48,80},{56,88},{... | collective-permute-start | bytes 614408 | tf_op jit(solution)/shard_map/ppermute | solution.py:286
  90.1 1.8 %collective-permute-start.11 = (bf16[16,6400]{1,0:T(8,128)(2,1)S(1)}, bf16[16,6400]{1,0:T(8,128)(2,1)S(1)}, u32[]{:S(2)}, u32[]{:S(2)}) collective-permute-start(bf16[16,6400]{1,0:T(8,128)(2,1)S(1)} %get-tuple-element.31), channel_id=1, source_target_pairs={{0,80},{8,88},{16,96},{24,104},{32,112},{40,120},{48,64},{56,72},{... | collective-permute-start | bytes 614408 | tf_op jit(solution)/shard_map/ppermute | solution.py:286
  91.9 3.3 %collective-permute-start.12 = (bf16[16,6400]{1,0:T(8,128)(2,1)S(1)}, bf16[16,6400]{1,0:T(8,128)(2,1)S(1)}, u32[]{:S(2)}, u32[]{:S(2)}) collective-permute-start(bf16[16,6400]{1,0:T(8,128)(2,1)S(1)} %get-tuple-element.32), channel_id=1, source_target_pairs={{0,112},{8,120},{16,64},{24,72},{32,80},{40,88},{48,96},{56,104},{... | collective-permute-start | bytes 614408 | tf_op jit(solution)/shard_map/ppermute | solution.py:286
  95.2 1.0 collective-permute-start.14
  96.8 3.5 %collective-permute-done.11 = bf16[16,6400]{1,0:T(8,128)(2,1)S(1)} collective-permute-done((bf16[16,6400]{1,0:T(8,128)(2,1)S(1)}, bf16[16,6400]{1,0:T(8,128)(2,1)S(1)}, u32[]{:S(2)}, u32[]{:S(2)}) %collective-permute-start.11) | collective-permute-done | bytes 204832 | tf_op jit(solution)/shard_map/ppermute | solution.py:286
  100.3 5.3 %collective-permute-done.12 = bf16[16,6400]{1,0:T(8,128)(2,1)S(1)} collective-permute-done((bf16[16,6400]{1,0:T(8,128)(2,1)S(1)}, bf16[16,6400]{1,0:T(8,128)(2,1)S(1)}, u32[]{:S(2)}, u32[]{:S(2)}) %collective-permute-start.12) | collective-permute-done | bytes 204832 | tf_op jit(solution)/shard_map/ppermute | solution.py:286
  105.6 4.3 %collective-permute-done.14 = bf16[16,6400]{1,0:T(8,128)(2,1)S(1)} collective-permute-done((bf16[16,6400]{1,0:T(8,128)(2,1)S(1)}, bf16[16,6400]{1,0:T(8,128)(2,1)S(1)}, u32[]{:S(2)}, u32[]{:S(2)}) %collective-permute-start.14) | collective-permute-done | bytes 204832 | tf_op jit(solution)/shard_map/ppermute | solution.py:286
  (42 shorter events, 6.9 us)
Async XLA Ops:
  0.6 2.8 %collective-permute-start = (bf16[16,6144]{1,0:T(8,128)(2,1)}, bf16[16,6144]{1,0:T(8,128)(2,1)S(1)}, u32[]{:S(2)}, u32[]{:S(2)}) collective-permute-start(bf16[16,6144]{1,0:T(8,128)(2,1)} %rest_0_.1), channel_id=1, source_target_pairs={{0,8},{8,0},{16,24},{24,16},{32,40},{40,32},{48,56},{56,48},{64,72... | collective-permute-start | bytes 589832 | tf_op jit(solution)/shard_map/ppermute | solution.py:217
  5.1 0.7 copy-start.1
  5.8 17.5 %collective-permute-start.7 = (bf16[2,16,6144]{2,1,0:T(8,128)(2,1)}, bf16[2,16,6144]{2,1,0:T(8,128)(2,1)}, u32[]{:S(2)}, u32[]{:S(2)}) collective-permute-start(bf16[2,16,6144]{2,1,0:T(8,128)(2,1)} %pad_maximum_fusion._), channel_id=1, source_target_pairs={{0,16},{8,56},{16,32},{24,8},{32,48},{40,24},{48,0},{56,40},{64,80... | collective-permute-start | bytes 1179656 | tf_op jit(solution)/shard_map/ppermute | solution.py:220
  9.6 13.7 %collective-permute-start.5 = (bf16[2,16,6144]{2,1,0:T(8,128)(2,1)}, bf16[2,16,6144]{2,1,0:T(8,128)(2,1)}, u32[]{:S(2)}, u32[]{:S(2)}) collective-permute-start(bf16[2,16,6144]{2,1,0:T(8,128)(2,1)} %pad_maximum_fusion._), channel_id=1, source_target_pairs={{0,32},{8,72},{16,48},{24,88},{32,0},{40,104},{48,16},{56,120},{64... | collective-permute-start | bytes 1179656 | tf_op jit(solution)/shard_map/ppermute | solution.py:220
  12.4 15.6 %collective-permute-start.3 = (bf16[2,16,6144]{2,1,0:T(8,128)(2,1)}, bf16[2,16,6144]{2,1,0:T(8,128)(2,1)}, u32[]{:S(2)}, u32[]{:S(2)}) collective-permute-start(bf16[2,16,6144]{2,1,0:T(8,128)(2,1)} %pad_maximum_fusion._), channel_id=1, source_target_pairs={{0,80},{8,120},{16,96},{24,72},{32,112},{40,88},{48,64},{56,104},{... | collective-permute-start | bytes 1179656 | tf_op jit(solution)/shard_map/ppermute | solution.py:220
  12.4 18.2 %collective-permute-start.1 = (bf16[16,6144]{1,0:T(8,128)(2,1)}, bf16[16,6144]{1,0:T(8,128)(2,1)}, u32[]{:S(2)}, u32[]{:S(2)}) collective-permute-start(bf16[16,6144]{1,0:T(8,128)(2,1)} %rest_0_.1), channel_id=1, source_target_pairs={{0,96},{8,104},{16,112},{24,120},{32,64},{40,72},{48,80},{56,88},{... | collective-permute-start | bytes 589832 | tf_op jit(solution)/shard_map/ppermute | solution.py:219
  16.1 16.6 %copy-start = (bf16[16,6144]{1,0:T(8,128)(2,1)S(1)}, bf16[16,6144]{1,0:T(8,128)(2,1)}, u32[]{:S(2)}) copy-start(bf16[16,6144]{1,0:T(8,128)(2,1)} %rest_0_.1) | copy-start | bytes 589828
  16.1 16.6 %copy-start.2 = (bf16[16,6144]{1,0:T(8,128)(2,1)S(1)}, bf16[16,6144]{1,0:T(8,128)(2,1)}, u32[]{:S(2)}) copy-start(bf16[16,6144]{1,0:T(8,128)(2,1)} %copy-done.1) | copy-start | bytes 589828
  16.1 16.6 %copy-start.3 = (bf16[32,6144]{1,0:T(8,128)(2,1)S(1)}, bf16[32,6144]{1,0:T(8,128)(2,1)}, u32[]{:S(2)}) copy-start(bf16[32,6144]{1,0:T(8,128)(2,1)} %cotangent.1) | copy-start | bytes 1179652
  16.1 16.6 %copy-start.5 = (bf16[16,256]{1,0:T(8,128)(2,1)S(1)}, bf16[16,256]{1,0:T(8,128)(2,1)}, u32[]{:S(2)}) copy-start(bf16[16,256]{1,0:T(8,128)(2,1)} %weight.1) | copy-start | bytes 24580
  16.1 16.6 %copy-start.6 = (s32[48]{0:T(128)S(1)}, s32[48]{0:T(128)}, u32[]{:S(2)}) copy-start(s32[48]{0:T(128)} %counts.3) | copy-start | bytes 580
  28.0 4.7 %collective-permute-start.4 = (bf16[2,16,6144]{2,1,0:T(8,128)(2,1)}, bf16[2,16,6144]{2,1,0:T(8,128)(2,1)S(1)}, u32[]{:S(2)}, u32[]{:S(2)}) collective-permute-start(bf16[2,16,6144]{2,1,0:T(8,128)(2,1)} %collective-permute-done.3.rest_4_), channel_id=1, source_target_pairs={{0,8},{8,0},{16,24},{24,16},{32,40},{40,32},{48,56},{56,48},{64,72... | collective-permute-start | bytes 1179656 | tf_op jit(solution)/shard_map/ppermute | solution.py:236
  28.1 4.5 %collective-permute-start.6 = (bf16[2,16,6144]{2,1,0:T(8,128)(2,1)}, bf16[2,16,6144]{2,1,0:T(8,128)(2,1)S(1)}, u32[]{:S(2)}, u32[]{:S(2)}) collective-permute-start(bf16[2,16,6144]{2,1,0:T(8,128)(2,1)} %collective-permute-done.5.rest_6_), channel_id=1, source_target_pairs={{0,8},{8,0},{16,24},{24,16},{32,40},{40,32},{48,56},{56,48},{64,72... | collective-permute-start | bytes 1179656 | tf_op jit(solution)/shard_map/ppermute | solution.py:236
  28.5 4.2 %collective-permute-start.8 = (bf16[2,16,6144]{2,1,0:T(8,128)(2,1)}, bf16[2,16,6144]{2,1,0:T(8,128)(2,1)S(1)}, u32[]{:S(2)}, u32[]{:S(2)}) collective-permute-start(bf16[2,16,6144]{2,1,0:T(8,128)(2,1)} %collective-permute-done.7.rest_8_), channel_id=1, source_target_pairs={{0,8},{8,0},{16,24},{24,16},{32,40},{40,32},{48,56},{56,48},{64,72... | collective-permute-start | bytes 1179656 | tf_op jit(solution)/shard_map/ppermute | solution.py:236
  30.7 1.9 %collective-permute-start.2 = (bf16[16,6144]{1,0:T(8,128)(2,1)}, bf16[16,6144]{1,0:T(8,128)(2,1)S(1)}, u32[]{:S(2)}, u32[]{:S(2)}) collective-permute-start(bf16[16,6144]{1,0:T(8,128)(2,1)} %collective-permute-done.1.rest_2_), channel_id=1, source_target_pairs={{0,8},{8,0},{16,24},{24,16},{32,40},{40,32},{48,56},{56,48},{64,72... | collective-permute-start | bytes 589832 | tf_op jit(solution)/shard_map/ppermute | solution.py:236
  32.7 23.9 %copy-start.4 = (s32[6144]{0:T(1024)S(1)}, s32[6144]{0:T(1024)}, u32[]{:S(2)}) copy-start(s32[6144]{0:T(1024)} %param.14) | copy-start | bytes 73732
  78.0 6.2 %collective-permute-start.9 = (bf16[8,16,6400]{2,1,0:T(8,128)(2,1)S(1)}, bf16[8,16,6400]{2,1,0:T(8,128)(2,1)S(1)}, u32[]{:S(2)}, u32[]{:S(2)}) collective-permute-start(bf16[8,16,6400]{2,1,0:T(8,128)(2,1)S(1)} %get-tuple-element.28), channel_id=1, source_target_pairs={{0,8},{8,0},{16,24},{24,16},{32,40},{40,32},{48,56},{56,48},{64,72... | collective-permute-start | bytes 4915208 | tf_op jit(solution)/shard_map/ppermute | solution.py:275
  84.6 11.6 %collective-permute-start.10 = (bf16[16,6400]{1,0:T(8,128)(2,1)S(1)}, bf16[16,6400]{1,0:T(8,128)(2,1)S(1)}, u32[]{:S(2)}, u32[]{:S(2)}) collective-permute-start(bf16[16,6400]{1,0:T(8,128)(2,1)S(1)} %get-tuple-element.30), channel_id=1, source_target_pairs={{0,96},{8,104},{16,112},{24,120},{32,64},{40,72},{48,80},{56,88},{... | collective-permute-start | bytes 614408 | tf_op jit(solution)/shard_map/ppermute | solution.py:286
  90.1 10.2 %collective-permute-start.11 = (bf16[16,6400]{1,0:T(8,128)(2,1)S(1)}, bf16[16,6400]{1,0:T(8,128)(2,1)S(1)}, u32[]{:S(2)}, u32[]{:S(2)}) collective-permute-start(bf16[16,6400]{1,0:T(8,128)(2,1)S(1)} %get-tuple-element.31), channel_id=1, source_target_pairs={{0,80},{8,88},{16,96},{24,104},{32,112},{40,120},{48,64},{56,72},{... | collective-permute-start | bytes 614408 | tf_op jit(solution)/shard_map/ppermute | solution.py:286
  91.9 13.7 %collective-permute-start.12 = (bf16[16,6400]{1,0:T(8,128)(2,1)S(1)}, bf16[16,6400]{1,0:T(8,128)(2,1)S(1)}, u32[]{:S(2)}, u32[]{:S(2)}) collective-permute-start(bf16[16,6400]{1,0:T(8,128)(2,1)S(1)} %get-tuple-element.32), channel_id=1, source_target_pairs={{0,112},{8,120},{16,64},{24,72},{32,80},{40,88},{48,96},{56,104},{... | collective-permute-start | bytes 614408 | tf_op jit(solution)/shard_map/ppermute | solution.py:286
  95.2 10.4 %collective-permute-start.13 = (bf16[16,6400]{1,0:T(8,128)(2,1)S(1)}, bf16[16,6400]{1,0:T(8,128)(2,1)S(1)}, u32[]{:S(2)}, u32[]{:S(2)}) collective-permute-start(bf16[16,6400]{1,0:T(8,128)(2,1)S(1)} %get-tuple-element.33), channel_id=1, source_target_pairs={{0,32},{8,40},{16,48},{24,56},{32,0},{40,8},{48,16},{56,24},{64,96... | collective-permute-start | bytes 614408 | tf_op jit(solution)/shard_map/ppermute | solution.py:286
  95.2 14.7 %collective-permute-start.14 = (bf16[16,6400]{1,0:T(8,128)(2,1)S(1)}, bf16[16,6400]{1,0:T(8,128)(2,1)S(1)}, u32[]{:S(2)}, u32[]{:S(2)}) collective-permute-start(bf16[16,6400]{1,0:T(8,128)(2,1)S(1)} %get-tuple-element.34), channel_id=1, source_target_pairs={{0,64},{8,72},{16,80},{24,88},{32,96},{40,104},{48,112},{56,120},{... | collective-permute-start | bytes 614408 | tf_op jit(solution)/shard_map/ppermute | solution.py:286
  96.2 13.7 %collective-permute-start.15 = (bf16[16,6400]{1,0:T(8,128)(2,1)S(1)}, bf16[16,6400]{1,0:T(8,128)(2,1)S(1)}, u32[]{:S(2)}, u32[]{:S(2)}) collective-permute-start(bf16[16,6400]{1,0:T(8,128)(2,1)S(1)} %get-tuple-element.35), channel_id=1, source_target_pairs={{0,16},{8,24},{16,32},{24,40},{32,48},{40,56},{48,0},{56,8},{64,80... | collective-permute-start | bytes 614408 | tf_op jit(solution)/shard_map/ppermute | solution.py:286
  100.3 10.2 %collective-permute-start.16 = (bf16[16,6400]{1,0:T(8,128)(2,1)S(1)}, bf16[16,6400]{1,0:T(8,128)(2,1)S(1)}, u32[]{:S(2)}, u32[]{:S(2)}) collective-permute-start(bf16[16,6400]{1,0:T(8,128)(2,1)S(1)} %get-tuple-element.36), channel_id=1, source_target_pairs={{0,48},{8,56},{16,0},{24,8},{32,16},{40,24},{48,32},{56,40},{64,11... | collective-permute-start | bytes 614408 | tf_op jit(solution)/shard_map/ppermute | solution.py:286

commit v4 on v3

--- a/solution.py
+++ b/solution.py
@@ -10,9 +10,8 @@
 ANY = pl.BlockSpec(memory_space=pl.ANY)
 SMEM = pl.BlockSpec(memory_space=pltpu.SMEM)
 VMEM = pl.BlockSpec(memory_space=pltpu.VMEM)
-STEPS = ((1, 2), (1, 1), (1, 3), (0, 2), (1, 0), (0, 1), (0, 3))
-FAR = (1, 2)
-SHARED = (((1, 1), (1, 3)), ((0, 2), (1, 0)), ((0, 1), (0, 3)))
+ALONE = (0, 1)
+SHARED = (((1, 2), (1, 1)), ((1, 3), (0, 2)), ((1, 0), (0, 3)))
 BLOCK = 128
 
 
@@ -58,6 +57,11 @@
 
 def params(mib):
     return pltpu.CompilerParams(vmem_limit_bytes=mib * 2**20)
+
+
+def stack_kernel(first, second, out):
+    out[0] = first[...]
+    out[1] = second[...]
 
 
 def load_kernel(values, _, out, loaded, sems):
@@ -77,38 +81,27 @@
 
 
 def mix_kernel(cols, counts, values, cotangent, weight, bias_rows, *rest):
-    pieces, (out, held, sems) = rest[:10], rest[10:]
+    pieces, (out, held) = rest[:10], rest[10:]
     slots = values.shape[1]
     chunks, _, _ = out.shape
     width = cotangent.shape[1] // chunks
     rows = values.shape[0] // chunks
 
-    sources = []
-    for at, (dx, dz) in enumerate(((0, 0), FAR)):
+    for at, (dx, dz) in ((0, (0, 0)), (8, ALONE)):
         for server in range(2):
-            sources.append((pieces[2 * at + server], node_near(dx, -dz, server)))
-    for at, steps in enumerate(SHARED):
+            held[node_near(dx, -dz, server)] = pieces[at + server][...]
+    for at, steps in ((2, SHARED[2]), (4, SHARED[1]), (6, SHARED[0])):
         for server in range(2):
             for q in range(2):
-                sources.append(
-                    (pieces[4 + 2 * at + server].at[q], shared_near(steps, server, -1, server ^ q))
-                )
-    copies = [
-        pltpu.make_async_copy(piece, held.at[group], sems.at[at])
-        for at, (piece, group) in enumerate(sources)
-    ]
-    for copy in copies:
-        copy.start()
+                near = shared_near(steps, server, -1, server ^ q)
+                held[near] = pieces[at + server][q]
     for j in range(chunks):
         out[j, :, width : 2 * width] = cotangent[:16, j * width : (j + 1) * width]
         out[j, :, 2 * width : 3 * width] = cotangent[16:, j * width : (j + 1) * width]
         out[j, :, 3 * width : 3 * width + 256] = weight[...]
         out[j, :, 3 * width + 256 :] = bias_rows[...]
-    for copy in copies:
-        copy.wait()
-
-    @pl.loop(0, chunks)
-    def _(j):
+
+    for j in range(chunks):
         for i in range(rows):
             r = j * rows + i
             count = counts[r]
@@ -169,8 +162,7 @@
         activation[16:, at] = grads[j, :, 2 * width + 256 :]
         weight_part += grads[j, :, width : width + 256].astype(F32)
 
-    @pl.loop(0, chunks)
-    def _(j):
+    for j in range(chunks):
         for i in range(rows):
             r = j * rows + i
             count = counts[r]
@@ -186,15 +178,36 @@
                 total[group, :, pl.ds(lane, BLOCK)] += contrib[:, s * BLOCK : (s + 1) * BLOCK]
 
     weight_part = weight_part.astype(BF)
-    for k, (dx, dz) in enumerate(((0, 0),) + STEPS):
-        for core, to in enumerate((own, other)):
-            to[k, :, :nodes] = total[node_near(dx, dz, core)].astype(BF)
+    for server, to in enumerate((own, other)):
+        nears = [node_near(0, 0, server), node_near(*ALONE, server)]
+        nears += [shared_near(steps, server, 1, server ^ q) for steps in SHARED for q in range(2)]
+        for k, near in enumerate(nears):
+            to[k, :, :nodes] = total[near].astype(BF)
             to[k, :, nodes:] = weight_part
 
 
-def pair_kernel(own, other, *outs):
-    for k, out in enumerate(outs):
-        out[...] = (own[k].astype(F32) + other[k].astype(F32)).astype(BF)
+def pair_kernel(own, other, stay, alone, *shared):
+    def both(k):
+        return (own[k].astype(F32) + other[k].astype(F32)).astype(BF)
+
+    stay[...] = both(0)
+    alone[...] = both(1)
+    for i, out in enumerate(shared):
+        for q in range(2):
+            out[q] = both(2 + 2 * i + q)
+
+
+def hand_kernel(first, second, third, out):
+    out[...] = (first[1].astype(F32) + second[1].astype(F32) + third[1].astype(F32)).astype(BF)
+
+
+def last_kernel(stay, alone, handed, first, second, third, grad_features, grad_weight):
+    total = stay[...].astype(F32) + alone[...].astype(F32) + handed[...].astype(F32)
+    for piece in (first, second, third):
+        total += piece[0].astype(F32)
+    nodes = grad_features.shape[1]
+    grad_features[...] = total[:, :nodes].astype(BF)
+    grad_weight[...] = total[:, nodes:]
 
 
 def local(features, weight, bias, block_values, block_cols, block_counts, train_mask, cotangent):
@@ -215,9 +228,16 @@
 
     swap = node_pairs(0, 0, 1)
     pieces = [features, lax.ppermute(features, "node", swap)]
-    pair = jnp.stack(pieces)
-    arrived = [lax.ppermute(features, "node", node_pairs(*FAR))]
-    arrived += [lax.ppermute(pair, "node", shared_pairs(steps)) for steps in SHARED]
+    pair = pl.pallas_call(
+        stack_kernel,
+        in_specs=[VMEM] * 2,
+        out_specs=VMEM,
+        out_shape=shape((2, fin, nodes)),
+        compiler_params=params(4),
+        name="stack",
+    )(*pieces)
+    arrived = [lax.ppermute(pair, "node", shared_pairs(steps)) for steps in SHARED[::-1]]
+    arrived.append(lax.ppermute(features, "node", node_pairs(*ALONE)))
     values, loaded = pl.pallas_call(
         load_kernel,
         in_specs=[pl.BlockSpec(memory_space=pltpu.HBM), ANY],
@@ -237,10 +257,10 @@
 
     mixed = pl.pallas_call(
         mix_kernel,
-        in_specs=[SMEM, SMEM] + [VMEM] * 4 + [ANY] * 10,
+        in_specs=[SMEM, SMEM] + [VMEM] * 14,
         out_specs=VMEM,
         out_shape=shape((8, 16, 3 * width + 512)),
-        scratch_shapes=[pltpu.VMEM((16, fin, nodes), BF), pltpu.SemaphoreType.DMA((16,))],
+        scratch_shapes=[pltpu.VMEM((16, fin, nodes), BF)],
         compiler_params=params(16),
         name="mix",
     )(block_cols, block_counts, values, cotangent, weight, bias_rows, *pieces)
@@ -272,20 +292,37 @@
         name="spread",
     )(block_cols, block_counts, values, grads)
 
-    other = lax.ppermute(other, "node", node_pairs(0, 0, 1))
-    sums = pl.pallas_call(
+    other = lax.ppermute(other, "node", swap)
+    stay, alone, *shared = pl.pallas_call(
         pair_kernel,
         in_specs=[VMEM] * 2,
-        out_specs=[VMEM] * 8,
-        out_shape=[shape((16, nodes + 256))] * 8,
+        out_specs=[VMEM] * 5,
+        out_shape=[shape((16, nodes + 256))] * 2 + [shape((2, 16, nodes + 256))] * 3,
         compiler_params=params(16),
         name="pair",
     )(own, other)
-    landed = [sums[0]]
-    for (dx, dz), piece in zip(STEPS, sums[1:]):
-        landed.append(lax.ppermute(piece, "node", node_pairs(dx, dz)))
-    total = sum(piece.astype(F32) for piece in landed)
-    return activation, total[:, :nodes].astype(BF), total[:, nodes:]
+    alone = lax.ppermute(alone, "node", node_pairs(*ALONE))
+    shared = [
+        lax.ppermute(piece, "node", shared_pairs(steps)) for piece, steps in zip(shared, SHARED)
+    ]
+    handed = pl.pallas_call(
+        hand_kernel,
+        in_specs=[VMEM] * 3,
+        out_specs=VMEM,
+        out_shape=shape((16, nodes + 256)),
+        compiler_params=params(16),
+        name="hand",
+    )(*shared)
+    handed = lax.ppermute(handed, "node", swap)
+    grad_features, grad_weight = pl.pallas_call(
+        last_kernel,
+        in_specs=[VMEM] * 6,
+        out_specs=[VMEM] * 2,
+        out_shape=[shape((16, nodes)), shape((16, 256), F32)],
+        compiler_params=params(16),
+        name="last",
+    )(stay, alone, handed, *shared)
+    return activation, grad_features, grad_weight
 
 
 def solution(mesh):

time: 112 us -> 109 us (0.973)
  waiting for transfers between devices: 26.1 us -> 32.7 us
  starting transfers between devices: 26.7 us -> 22 us
  other arithmetic: 1.99 us -> 0.08 us
  Pallas kernels: 24.5 us -> 22.8 us
  local copies, waits for them, and re-layouts: 3.63 us -> 2.32 us
    ppermute x9 -> x7, starting transfers between devices: 17.2 us -> 11.2 us  [the longest x3 7.34 us: local(): lax.ppermute(piece, 'node', shared_pairs(steps))]
    ppermute x9 -> x7, waiting for transfers between devices: 19 us -> 22.3 us  [the longest x3 17.8 us: local(): lax.ppermute(piece, 'node', shared_pairs(steps))]
    ppermute x3, waiting for transfers between devices: 4.62 us -> 6.9 us  [local(): lax.ppermute(pair, 'node', shared_pairs(steps))]
    another operation x2 -> x1, other arithmetic: 1.72 us -> 0.01 us  [the longest x1 1.71 us: local(): pair = jnp.stack(pieces)]
    ppermute x3, starting transfers between devices: 6.65 us -> 8.21 us  [local(): lax.ppermute(pair, 'node', shared_pairs(steps))]
    slice x2 -> x0, local copies, waits for them, and re-layouts: 1.3 us -> none  [local(): return (activation, total[:, :nodes].astype(BF), total[:, nodes:])]
    pallas_call x2 -> x5, Pallas kernels: 8.24 us -> 7.49 us  [the longest x1 4.46 us: local(): pl.pallas_call(mix_kernel, in_specs=[SMEM, SMEM] + [VMEM] * 14, out_specs...]
  transfers between devices with their start and end apart: 17 -> 15, of which waited for: 9 -> 9; matrix products, arithmetic and copies ran while one was open for 2% -> 2% of each run, Pallas kernels for 6% -> 7%
where the time goes in v4:
time: 109 us
  waiting for transfers between devices  32.7 us (30%)
  blocking collectives  27.9 us (26%)
  Pallas kernels  22.8 us (21%)
  starting transfers between devices  22 us (20%)
  local copies, waits for them, and re-layouts  2.32 us (2%)
    ppermute x3, waiting for transfers between devices, local(): lax.ppermute(piece, 'node', shared_pairs(steps))  17.8 us
    all_to_all x1, blocking collectives, local(): both = lax.all_to_all(mixed, 'feat', 0, 0, tiled=True)  15.6 us
    all_to_all x1, blocking collectives, local(): grads = lax.all_to_all(dense, 'feat', 0, 0, tiled=True)  12.3 us
    ppermute x3, starting transfers between devices, local(): lax.ppermute(pair, 'node', shared_pairs(steps))  8.21 us
    pallas_call x1, Pallas kernels, local(): pl.pallas_call(spread_kernel, in_specs=[SMEM, SMEM] + [VMEM] * 2, out_spe...  7.37 us
    ppermute x3, starting transfers between devices, local(): lax.ppermute(piece, 'node', shared_pairs(steps))  7.34 us
    pallas_call x1, Pallas kernels, local(): pl.pallas_call(load_kernel, in_specs=[pl.BlockSpec(memory_space=pltpu.HBM...  7.16 us
    ppermute x3, waiting for transfers between devices, local(): lax.ppermute(pair, 'node', shared_pairs(steps))  6.9 us
  transfers between devices with their start and end apart: 15, of which 9 were waited for; matrix products, arithmetic and copies ran while one was open for 2% of the time, Pallas kernels for 7%

profile of v4, /device:TPU:1, one launch (start us, length us, event | category | flops | bytes accessed | tf_op | source)
XLA Modules:
  0.0 108.5 jit_solution(1828586270971702567)
XLA Ops:
  0.6 1.5 %collective-permute-start = (bf16[16,6144]{1,0:T(8,128)(2,1)}, bf16[16,6144]{1,0:T(8,128)(2,1)S(1)}, u32[]{:S(2)}, u32[]{:S(2)}) collective-permute-start(bf16[16,6144]{1,0:T(8,128)(2,1)} %rest_0_.1), channel_id=1, source_target_pairs={{0,8},{8,0},{16,24},{24,16},{32,40},{40,32},{48,56},{56,48},{64,72... | collective-permute-start | bytes 589832 | tf_op jit(solution)/shard_map/ppermute | solution.py:230
  2.1 1.3 %collective-permute-done.second.rest_1_ = bf16[16,6144]{1,0:T(8,128)(2,1)S(1)} collective-permute-done((bf16[16,6144]{1,0:T(8,128)(2,1)}, bf16[16,6144]{1,0:T(8,128)(2,1)S(1)}, u32[]{:S(2)}, u32[]{:S(2)}) %collective-permute-start) | collective-permute-done | bytes 196640 | tf_op jit(solution)/shard_map/ppermute | solution.py:230
  3.4 1.7 %stack.1._ = bf16[2,16,6144]{2,1,0:T(8,128)(2,1)} custom-call(bf16[16,6144]{1,0:T(8,128)(2,1)} %rest_0_.1, bf16[16,6144]{1,0:T(8,128)(2,1)S(1)} %collective-permute-done.second.rest_1_), custom_call_target="tpu_custom_call" | custom-call | tf_op jit(solution)/shard_map/stack/pallas_call | solution.py:231
  5.8 4.2 %collective-permute-start.5 = (bf16[2,16,6144]{2,1,0:T(8,128)(2,1)}, bf16[2,16,6144]{2,1,0:T(8,128)(2,1)}, u32[]{:S(2)}, u32[]{:S(2)}) collective-permute-start(bf16[2,16,6144]{2,1,0:T(8,128)(2,1)} %stack.1._), channel_id=1, source_target_pairs={{0,96},{8,88},{16,112},{24,104},{32,64},{40,120},{48,80},{56,72},{... | collective-permute-start | bytes 1179656 | tf_op jit(solution)/shard_map/ppermute | solution.py:239
  10.0 3.3 %collective-permute-start.3 = (bf16[2,16,6144]{2,1,0:T(8,128)(2,1)}, bf16[2,16,6144]{2,1,0:T(8,128)(2,1)}, u32[]{:S(2)}, u32[]{:S(2)}) collective-permute-start(bf16[2,16,6144]{2,1,0:T(8,128)(2,1)} %stack.1._), channel_id=1, source_target_pairs={{0,112},{8,40},{16,64},{24,56},{32,80},{40,8},{48,96},{56,24},{64,... | collective-permute-start | bytes 1179656 | tf_op jit(solution)/shard_map/ppermute | solution.py:239
  14.7 0.8 copy.12.cols
  16.4 7.2 %load.1 = (bf16[48,12,128,128]{3,2,1,0:T(8,128)(2,1)S(1)}, f32[8,128]{1,0:T(8,128)}) custom-call(bf16[48,12,128,128]{3,2,1,0:T(8,128)(2,1)} %values.1, bf16[2,16,6144]{2,1,0:T(8,128)(2,1)} %stack.1._), custom_call_target="tpu_custom_call" | custom-call | bytes 37748736 | tf_op jit(solution)/shard_map/load/pallas_call | solution.py:241
  23.6 5.2 %collective-permute-done.3.rest_4_ = bf16[2,16,6144]{2,1,0:T(8,128)(2,1)} collective-permute-done((bf16[2,16,6144]{2,1,0:T(8,128)(2,1)}, bf16[2,16,6144]{2,1,0:T(8,128)(2,1)}, u32[]{:S(2)}, u32[]{:S(2)}) %collective-permute-start.3) | collective-permute-done | bytes 393248 | tf_op jit(solution)/shard_map/ppermute | solution.py:239
  28.8 1.7 %collective-permute-done.1.rest_2_ = bf16[2,16,6144]{2,1,0:T(8,128)(2,1)} collective-permute-done((bf16[2,16,6144]{2,1,0:T(8,128)(2,1)}, bf16[2,16,6144]{2,1,0:T(8,128)(2,1)}, u32[]{:S(2)}, u32[]{:S(2)}) %collective-permute-start.1) | collective-permute-done | bytes 393248 | tf_op jit(solution)/shard_map/ppermute | solution.py:239
  31.7 2.2 %collective-permute-done.8.rest_9_ = bf16[16,6144]{1,0:T(8,128)(2,1)S(1)} collective-permute-done((bf16[16,6144]{1,0:T(8,128)(2,1)}, bf16[16,6144]{1,0:T(8,128)(2,1)S(1)}, u32[]{:S(2)}, u32[]{:S(2)}) %collective-permute-start.8) | collective-permute-done | bytes 196640 | tf_op jit(solution)/shard_map/ppermute | solution.py:256
  33.9 4.5 %mix.1 = bf16[8,16,2816]{2,1,0:T(8,128)(2,1)S(1)} custom-call(s32[48,12]{1,0:T(8,128)S(1)} %copy.12.cols, s32[48]{0:T(128)S(1)} %copy-done.5, bf16[48,12,128,128]{3,2,1,0:T(8,128)(2,1)S(1)} %get-tuple-element.19.values, bf16[32,6144]{1,0:T(8,128)(2,1)S(1)} %copy-done.2, bf16[16,256]{1,0:T(8,128)(2,1)S(1)} %copy-done.4, ...), custom_call_target="tpu_custom_call" | custom-call | tf_op jit(solution)/shard_map/mix/pallas_call | solution.py:258
  38.3 15.6 %all_to_all.10.both = bf16[8,16,2816]{2,1,0:T(8,128)(2,1)S(1)} all-to-all(bf16[8,16,2816]{2,1,0:T(8,128)(2,1)S(1)} %mix.1), channel_id=1, replica_groups=mesh['node'=16,'feat'=8] {'feat'}, dimensions={0} | all-to-all | bytes 1441792 | tf_op jit(solution)/shard_map/all_to_all | solution.py:268
  54.7 12.3 %all_to_all.11.grads = bf16[8,16,2560]{2,1,0:T(8,128)(2,1)S(1)} all-to-all(bf16[8,16,2560]{2,1,0:T(8,128)(2,1)S(1)} %dense.1), channel_id=1, replica_groups=mesh['node'=16,'feat'=8] {'feat'}, dimensions={0} | all-to-all | bytes 1310720 | tf_op jit(solution)/shard_map/all_to_all | solution.py:279
  67.0 7.4 %spread.1 = (bf16[32,6144]{1,0:T(8,128)(2,1)}, bf16[8,16,6400]{2,1,0:T(8,128)(2,1)S(1)}, bf16[8,16,6400]{2,1,0:T(8,128)(2,1)S(1)}) custom-call(s32[48,12]{1,0:T(8,128)S(1)} %copy.12.cols, s32[48]{0:T(128)S(1)} %copy-done.5, bf16[48,12,128,128]{3,2,1,0:T(8,128)(2,1)S(1)} %get-tuple-element.19.values, bf16[8,16,2560]{2,1,0:T(8,128)(2,1)S(1)} %all_to_all.11.grads), custom_call_target="tpu_custom_call" | custom-call | tf_op jit(solution)/shard_map/spread/pallas_call | solution.py:281
  74.4 3.0 %collective-permute-start.9 = (bf16[8,16,6400]{2,1,0:T(8,128)(2,1)S(1)}, bf16[8,16,6400]{2,1,0:T(8,128)(2,1)S(1)}, u32[]{:S(2)}, u32[]{:S(2)}) collective-permute-start(bf16[8,16,6400]{2,1,0:T(8,128)(2,1)S(1)} %get-tuple-element.27), channel_id=1, source_target_pairs={{0,8},{8,0},{16,24},{24,16},{32,40},{40,32},{48,56},{56,48},{64,72... | collective-permute-start | bytes 4915208 | tf_op jit(solution)/shard_map/ppermute | solution.py:295
  77.4 3.1 %collective-permute-done.9.other = bf16[8,16,6400]{2,1,0:T(8,128)(2,1)S(1)} collective-permute-done((bf16[8,16,6400]{2,1,0:T(8,128)(2,1)S(1)}, bf16[8,16,6400]{2,1,0:T(8,128)(2,1)S(1)}, u32[]{:S(2)}, u32[]{:S(2)}) %collective-permute-start.9) | collective-permute-done | bytes 1638432 | tf_op jit(solution)/shard_map/ppermute | solution.py:295
  81.0 2.8 %collective-permute-start.11 = (bf16[2,16,6400]{2,1,0:T(8,128)(2,1)S(1)}, bf16[2,16,6400]{2,1,0:T(8,128)(2,1)S(1)}, u32[]{:S(2)}, u32[]{:S(2)}) collective-permute-start(bf16[2,16,6400]{2,1,0:T(8,128)(2,1)S(1)} %get-tuple-element.30), channel_id=1, source_target_pairs={{0,96},{8,88},{16,112},{24,104},{32,64},{40,120},{48,80},{56,72},{... | collective-permute-start | bytes 1228808 | tf_op jit(solution)/shard_map/ppermute | solution.py:306
  83.8 1.7 %collective-permute-start.12 = (bf16[2,16,6400]{2,1,0:T(8,128)(2,1)S(1)}, bf16[2,16,6400]{2,1,0:T(8,128)(2,1)S(1)}, u32[]{:S(2)}, u32[]{:S(2)}) collective-permute-start(bf16[2,16,6400]{2,1,0:T(8,128)(2,1)S(1)} %get-tuple-element.31), channel_id=1, source_target_pairs={{0,112},{8,40},{16,64},{24,56},{32,80},{40,8},{48,96},{56,24},{64,... | collective-permute-start | bytes 1228808 | tf_op jit(solution)/shard_map/ppermute | solution.py:306
  85.6 2.8 %collective-permute-start.13 = (bf16[2,16,6400]{2,1,0:T(8,128)(2,1)S(1)}, bf16[2,16,6400]{2,1,0:T(8,128)(2,1)S(1)}, u32[]{:S(2)}, u32[]{:S(2)}) collective-permute-start(bf16[2,16,6400]{2,1,0:T(8,128)(2,1)S(1)} %get-tuple-element.32), channel_id=1, source_target_pairs={{0,64},{8,56},{16,80},{24,8},{32,96},{40,24},{48,112},{56,40},{64,... | collective-permute-start | bytes 1228808 | tf_op jit(solution)/shard_map/ppermute | solution.py:306
  88.3 6.5 %collective-permute-done.11.first = bf16[2,16,6400]{2,1,0:T(8,128)(2,1)S(1)} collective-permute-done((bf16[2,16,6400]{2,1,0:T(8,128)(2,1)S(1)}, bf16[2,16,6400]{2,1,0:T(8,128)(2,1)S(1)}, u32[]{:S(2)}, u32[]{:S(2)}) %collective-permute-start.11) | collective-permute-done | bytes 409632 | tf_op jit(solution)/shard_map/ppermute | solution.py:306
  94.8 8.4 %collective-permute-done.12.second = bf16[2,16,6400]{2,1,0:T(8,128)(2,1)S(1)} collective-permute-done((bf16[2,16,6400]{2,1,0:T(8,128)(2,1)S(1)}, bf16[2,16,6400]{2,1,0:T(8,128)(2,1)S(1)}, u32[]{:S(2)}, u32[]{:S(2)}) %collective-permute-start.12) | collective-permute-done | bytes 409632 | tf_op jit(solution)/shard_map/ppermute | solution.py:306
  103.3 2.8 %collective-permute-done.13.third = bf16[2,16,6400]{2,1,0:T(8,128)(2,1)S(1)} collective-permute-done((bf16[2,16,6400]{2,1,0:T(8,128)(2,1)S(1)}, bf16[2,16,6400]{2,1,0:T(8,128)(2,1)S(1)}, u32[]{:S(2)}, u32[]{:S(2)}) %collective-permute-start.13) | collective-permute-done | bytes 409632 | tf_op jit(solution)/shard_map/ppermute | solution.py:306
  106.3 1.4 %collective-permute-done.14.handed = bf16[16,6400]{1,0:T(8,128)(2,1)S(1)} collective-permute-done((bf16[16,6400]{1,0:T(8,128)(2,1)S(1)}, bf16[16,6400]{1,0:T(8,128)(2,1)S(1)}, u32[]{:S(2)}, u32[]{:S(2)}) %collective-permute-start.14) | collective-permute-done | bytes 204832 | tf_op jit(solution)/shard_map/ppermute | solution.py:316
  107.7 0.8 last.1
  (35 shorter events, 5.5 us)
Async XLA Ops:
  0.6 2.8 %collective-permute-start = (bf16[16,6144]{1,0:T(8,128)(2,1)}, bf16[16,6144]{1,0:T(8,128)(2,1)S(1)}, u32[]{:S(2)}, u32[]{:S(2)}) collective-permute-start(bf16[16,6144]{1,0:T(8,128)(2,1)} %rest_0_.1), channel_id=1, source_target_pairs={{0,8},{8,0},{16,24},{24,16},{32,40},{40,32},{48,56},{56,48},{64,72... | collective-permute-start | bytes 589832 | tf_op jit(solution)/shard_map/ppermute | solution.py:230
  5.1 0.7 copy-start
  5.8 17.8 %collective-permute-start.5 = (bf16[2,16,6144]{2,1,0:T(8,128)(2,1)}, bf16[2,16,6144]{2,1,0:T(8,128)(2,1)}, u32[]{:S(2)}, u32[]{:S(2)}) collective-permute-start(bf16[2,16,6144]{2,1,0:T(8,128)(2,1)} %stack.1._), channel_id=1, source_target_pairs={{0,96},{8,88},{16,112},{24,104},{32,64},{40,120},{48,80},{56,72},{... | collective-permute-start | bytes 1179656 | tf_op jit(solution)/shard_map/ppermute | solution.py:239
  10.0 18.8 %collective-permute-start.3 = (bf16[2,16,6144]{2,1,0:T(8,128)(2,1)}, bf16[2,16,6144]{2,1,0:T(8,128)(2,1)}, u32[]{:S(2)}, u32[]{:S(2)}) collective-permute-start(bf16[2,16,6144]{2,1,0:T(8,128)(2,1)} %stack.1._), channel_id=1, source_target_pairs={{0,112},{8,40},{16,64},{24,56},{32,80},{40,8},{48,96},{56,24},{64,... | collective-permute-start | bytes 1179656 | tf_op jit(solution)/shard_map/ppermute | solution.py:239
  13.3 17.2 %collective-permute-start.1 = (bf16[2,16,6144]{2,1,0:T(8,128)(2,1)}, bf16[2,16,6144]{2,1,0:T(8,128)(2,1)}, u32[]{:S(2)}, u32[]{:S(2)}) collective-permute-start(bf16[2,16,6144]{2,1,0:T(8,128)(2,1)} %stack.1._), channel_id=1, source_target_pairs={{0,64},{8,56},{16,80},{24,8},{32,96},{40,24},{48,112},{56,40},{64,... | collective-permute-start | bytes 1179656 | tf_op jit(solution)/shard_map/ppermute | solution.py:239
  14.0 17.0 %collective-permute-start.7 = (bf16[16,6144]{1,0:T(8,128)(2,1)}, bf16[16,6144]{1,0:T(8,128)(2,1)}, u32[]{:S(2)}, u32[]{:S(2)}) collective-permute-start(bf16[16,6144]{1,0:T(8,128)(2,1)} %rest_0_.1), channel_id=1, source_target_pairs={{0,16},{8,24},{16,32},{24,40},{32,48},{40,56},{48,0},{56,8},{64,80... | collective-permute-start | bytes 589832 | tf_op jit(solution)/shard_map/ppermute | solution.py:240
  16.4 17.5 %copy-start.1 = (bf16[16,6144]{1,0:T(8,128)(2,1)S(1)}, bf16[16,6144]{1,0:T(8,128)(2,1)}, u32[]{:S(2)}) copy-start(bf16[16,6144]{1,0:T(8,128)(2,1)} %copy-done) | copy-start | bytes 589828
  16.4 17.5 %copy-start.2 = (bf16[32,6144]{1,0:T(8,128)(2,1)S(1)}, bf16[32,6144]{1,0:T(8,128)(2,1)}, u32[]{:S(2)}) copy-start(bf16[32,6144]{1,0:T(8,128)(2,1)} %cotangent.1) | copy-start | bytes 1179652
  16.4 17.5 %copy-start.4 = (bf16[16,256]{1,0:T(8,128)(2,1)S(1)}, bf16[16,256]{1,0:T(8,128)(2,1)}, u32[]{:S(2)}) copy-start(bf16[16,256]{1,0:T(8,128)(2,1)} %weight.1) | copy-start | bytes 24580
  16.4 17.5 %copy-start.5 = (s32[48]{0:T(128)S(1)}, s32[48]{0:T(128)}, u32[]{:S(2)}) copy-start(s32[48]{0:T(128)} %counts.3) | copy-start | bytes 580
  30.5 3.3 %collective-permute-start.2 = (bf16[2,16,6144]{2,1,0:T(8,128)(2,1)}, bf16[2,16,6144]{2,1,0:T(8,128)(2,1)S(1)}, u32[]{:S(2)}, u32[]{:S(2)}) collective-permute-start(bf16[2,16,6144]{2,1,0:T(8,128)(2,1)} %collective-permute-done.1.rest_2_), channel_id=1, source_target_pairs={{0,8},{8,0},{16,24},{24,16},{32,40},{40,32},{48,56},{56,48},{64,72... | collective-permute-start | bytes 1179656 | tf_op jit(solution)/shard_map/ppermute | solution.py:256
  30.5 3.3 %collective-permute-start.4 = (bf16[2,16,6144]{2,1,0:T(8,128)(2,1)}, bf16[2,16,6144]{2,1,0:T(8,128)(2,1)S(1)}, u32[]{:S(2)}, u32[]{:S(2)}) collective-permute-start(bf16[2,16,6144]{2,1,0:T(8,128)(2,1)} %collective-permute-done.3.rest_4_), channel_id=1, source_target_pairs={{0,8},{8,0},{16,24},{24,16},{32,40},{40,32},{48,56},{56,48},{64,72... | collective-permute-start | bytes 1179656 | tf_op jit(solution)/shard_map/ppermute | solution.py:256
  31.0 2.8 %collective-permute-start.6 = (bf16[2,16,6144]{2,1,0:T(8,128)(2,1)}, bf16[2,16,6144]{2,1,0:T(8,128)(2,1)S(1)}, u32[]{:S(2)}, u32[]{:S(2)}) collective-permute-start(bf16[2,16,6144]{2,1,0:T(8,128)(2,1)} %collective-permute-done.5.rest_6_), channel_id=1, source_target_pairs={{0,8},{8,0},{16,24},{24,16},{32,40},{40,32},{48,56},{56,48},{64,72... | collective-permute-start | bytes 1179656 | tf_op jit(solution)/shard_map/ppermute | solution.py:256
  31.0 2.8 %collective-permute-start.8 = (bf16[16,6144]{1,0:T(8,128)(2,1)}, bf16[16,6144]{1,0:T(8,128)(2,1)S(1)}, u32[]{:S(2)}, u32[]{:S(2)}) collective-permute-start(bf16[16,6144]{1,0:T(8,128)(2,1)} %collective-permute-done.7.rest_8_), channel_id=1, source_target_pairs={{0,8},{8,0},{16,24},{24,16},{32,40},{40,32},{48,56},{56,48},{64,72... | collective-permute-start | bytes 589832 | tf_op jit(solution)/shard_map/ppermute | solution.py:256
  33.9 20.1 %copy-start.3 = (s32[6144]{0:T(1024)S(1)}, s32[6144]{0:T(1024)}, u32[]{:S(2)}) copy-start(s32[6144]{0:T(1024)} %param.14) | copy-start | bytes 73732
  74.4 6.1 %collective-permute-start.9 = (bf16[8,16,6400]{2,1,0:T(8,128)(2,1)S(1)}, bf16[8,16,6400]{2,1,0:T(8,128)(2,1)S(1)}, u32[]{:S(2)}, u32[]{:S(2)}) collective-permute-start(bf16[8,16,6400]{2,1,0:T(8,128)(2,1)S(1)} %get-tuple-element.27), channel_id=1, source_target_pairs={{0,8},{8,0},{16,24},{24,16},{32,40},{40,32},{48,56},{56,48},{64,72... | collective-permute-start | bytes 4915208 | tf_op jit(solution)/shard_map/ppermute | solution.py:295
  81.0 13.8 %collective-permute-start.11 = (bf16[2,16,6400]{2,1,0:T(8,128)(2,1)S(1)}, bf16[2,16,6400]{2,1,0:T(8,128)(2,1)S(1)}, u32[]{:S(2)}, u32[]{:S(2)}) collective-permute-start(bf16[2,16,6400]{2,1,0:T(8,128)(2,1)S(1)} %get-tuple-element.30), channel_id=1, source_target_pairs={{0,96},{8,88},{16,112},{24,104},{32,64},{40,120},{48,80},{56,72},{... | collective-permute-start | bytes 1228808 | tf_op jit(solution)/shard_map/ppermute | solution.py:306
  83.8 19.4 %collective-permute-start.12 = (bf16[2,16,6400]{2,1,0:T(8,128)(2,1)S(1)}, bf16[2,16,6400]{2,1,0:T(8,128)(2,1)S(1)}, u32[]{:S(2)}, u32[]{:S(2)}) collective-permute-start(bf16[2,16,6400]{2,1,0:T(8,128)(2,1)S(1)} %get-tuple-element.31), channel_id=1, source_target_pairs={{0,112},{8,40},{16,64},{24,56},{32,80},{40,8},{48,96},{56,24},{64,... | collective-permute-start | bytes 1228808 | tf_op jit(solution)/shard_map/ppermute | solution.py:306
  85.6 20.5 %collective-permute-start.13 = (bf16[2,16,6400]{2,1,0:T(8,128)(2,1)S(1)}, bf16[2,16,6400]{2,1,0:T(8,128)(2,1)S(1)}, u32[]{:S(2)}, u32[]{:S(2)}) collective-permute-start(bf16[2,16,6400]{2,1,0:T(8,128)(2,1)S(1)} %get-tuple-element.32), channel_id=1, source_target_pairs={{0,64},{8,56},{16,80},{24,8},{32,96},{40,24},{48,112},{56,40},{64,... | collective-permute-start | bytes 1228808 | tf_op jit(solution)/shard_map/ppermute | solution.py:306
  88.3 17.9 %collective-permute-start.10 = (bf16[16,6400]{1,0:T(8,128)(2,1)S(1)}, bf16[16,6400]{1,0:T(8,128)(2,1)S(1)}, u32[]{:S(2)}, u32[]{:S(2)}) collective-permute-start(bf16[16,6400]{1,0:T(8,128)(2,1)S(1)} %get-tuple-element.29), channel_id=1, source_target_pairs={{0,16},{8,24},{16,32},{24,40},{32,48},{40,56},{48,0},{56,8},{64,80... | collective-permute-start | bytes 614408 | tf_op jit(solution)/shard_map/ppermute | solution.py:304
  106.2 1.5 %collective-permute-start.14 = (bf16[16,6400]{1,0:T(8,128)(2,1)S(1)}, bf16[16,6400]{1,0:T(8,128)(2,1)S(1)}, u32[]{:S(2)}, u32[]{:S(2)}) collective-permute-start(bf16[16,6400]{1,0:T(8,128)(2,1)S(1)} %hand.1), channel_id=1, source_target_pairs={{0,8},{8,0},{16,24},{24,16},{32,40},{40,32},{48,56},{56,48},{64,72... | collective-permute-start | bytes 614408 | tf_op jit(solution)/shard_map/ppermute | solution.py:316

commit v5 on v4

--- a/solution.py
+++ b/solution.py
@@ -1,3 +1,5 @@
+import functools
+
 import jax
 import jax.numpy as jnp
 from jax import lax
@@ -10,8 +12,14 @@
 ANY = pl.BlockSpec(memory_space=pl.ANY)
 SMEM = pl.BlockSpec(memory_space=pltpu.SMEM)
 VMEM = pl.BlockSpec(memory_space=pltpu.VMEM)
-ALONE = (0, 1)
-SHARED = (((1, 2), (1, 1)), ((1, 3), (0, 2)), ((1, 0), (0, 3)))
+STEP_A = ((1, 0), (0, 2))
+STEP_B = ((0, 1), (0, 3))
+STEP_C = ((0, 1), (1, 0))
+STEP_D = ((0, 3), (1, 0))
+FROM_A = ((1, 0), (0, 2))
+FROM_B = ((0, 3), (0, 1))
+FROM_C = ((1, 3), (1, 2))
+FROM_D = (1, 1)
 BLOCK = 128
 
 
@@ -43,11 +51,19 @@
     ]
 
 
-def shared_near(steps, server, sign, dcore):
+def back(steps):
+    return tuple((dx, -dz % 4) for dx, dz in steps)
+
+
+def shared_near(steps, server, dcore):
     core = (lax.axis_index("node") & 1) ^ server
     dx = jnp.where(core == 0, steps[0][0], steps[1][0])
     dz = jnp.where(core == 0, steps[0][1], steps[1][1])
-    return node_near(dx, sign * dz, dcore)
+    return node_near(dx, dz, dcore)
+
+
+def pair_near(steps, server):
+    return [shared_near(steps, server, server ^ q) for q in range(2)]
 
 
 def place_of(column):
@@ -64,12 +80,29 @@
     out[1] = second[...]
 
 
-def load_kernel(values, _, out, loaded, sems):
+def pick_kernel(first, second, _, out):
+    core = lax.axis_index("node") & 1
+
+    @pl.when(core == 0)
+    def _():
+        out[...] = first[0]
+
+    @pl.when(core == 1)
+    def _():
+        out[...] = second[0]
+
+
+def bundle_kernel(pair, single, _, out):
+    out[:2] = pair[...]
+    out[2] = single[...]
+
+
+def load_kernel(start, values, _, out, loaded, sems):
     count = sems.shape[0]
-    rows = values.shape[0] // count
+    rows = out.shape[0] // count
     copies = [
         pltpu.make_async_copy(
-            values.at[pl.ds(i * rows, rows)], out.at[pl.ds(i * rows, rows)], sems.at[i]
+            values.at[pl.ds(start + i * rows, rows)], out.at[pl.ds(i * rows, rows)], sems.at[i]
         )
         for i in range(count)
     ]
@@ -80,21 +113,23 @@
     loaded[...] = jnp.zeros_like(loaded)
 
 
-def mix_kernel(cols, counts, values, cotangent, weight, bias_rows, *rest):
-    pieces, (out, held) = rest[:10], rest[10:]
-    slots = values.shape[1]
+def mix_kernel(cols, counts, upper, lower, cotangent, weight, bias_rows, *rest):
+    pieces, (out, held) = rest[:9], rest[9:]
+    half, slots = upper.shape[:2]
     chunks, _, _ = out.shape
     width = cotangent.shape[1] // chunks
-    rows = values.shape[0] // chunks
-
-    for at, (dx, dz) in ((0, (0, 0)), (8, ALONE)):
-        for server in range(2):
-            held[node_near(dx, -dz, server)] = pieces[at + server][...]
-    for at, steps in ((2, SHARED[2]), (4, SHARED[1]), (6, SHARED[0])):
-        for server in range(2):
-            for q in range(2):
-                near = shared_near(steps, server, -1, server ^ q)
-                held[near] = pieces[at + server][q]
+    rows = 2 * half // chunks
+
+    bundle = pieces[8]
+    shards = {(FROM_A, 0): pieces[2], (FROM_A, 1): pieces[3], (FROM_B, 0): pieces[4]}
+    shards |= {(FROM_B, 1): pieces[5], (FROM_C, 0): pieces[6], (FROM_C, 1): bundle}
+    for server in range(2):
+        held[node_near(0, 0, server)] = pieces[server][...]
+        for steps in (FROM_A, FROM_B, FROM_C):
+            for q, near in enumerate(pair_near(steps, server)):
+                held[near] = shards[steps, server][q]
+    held[node_near(*FROM_D, 0)] = pieces[7][...]
+    held[node_near(*FROM_D, 1)] = bundle[2]
     for j in range(chunks):
         out[j, :, width : 2 * width] = cotangent[:16, j * width : (j + 1) * width]
         out[j, :, 2 * width : 3 * width] = cotangent[16:, j * width : (j + 1) * width]
@@ -112,7 +147,7 @@
                 parts.append(jnp.where(s < count, block, jnp.zeros_like(block)))
             total = jnp.dot(
                 jnp.concatenate(parts, axis=1),
-                values[r].reshape(slots * BLOCK, BLOCK),
+                (upper if r < half else lower)[r % half].reshape(slots * BLOCK, BLOCK),
                 preferred_element_type=F32,
             )
             out[j, :, i * BLOCK : (i + 1) * BLOCK] = total.astype(BF)
@@ -147,10 +182,12 @@
     out[:, :, 2 * width + 256 :] = activation[:, 16:]
 
 
-def spread_kernel(cols, counts, values, grads, activation, own, other, total):
-    slots = values.shape[1]
+def spread_kernel(
+    cols, counts, upper, lower, grads, activation, own1, other1, own2, other2, total
+):
+    half, slots = upper.shape[:2]
     chunks = grads.shape[0]
-    rows = values.shape[0] // chunks
+    rows = 2 * half // chunks
     nodes = total.shape[2]
     width = nodes // chunks
 
@@ -168,7 +205,7 @@
             count = counts[r]
             contrib = lax.dot_general(
                 grads[j, :, i * BLOCK : (i + 1) * BLOCK],
-                values[r].reshape(slots * BLOCK, BLOCK),
+                (upper if r < half else lower)[r % half].reshape(slots * BLOCK, BLOCK),
                 (((1,), (1,)), ((), ())),
                 preferred_element_type=F32,
             )
@@ -178,33 +215,49 @@
                 total[group, :, pl.ds(lane, BLOCK)] += contrib[:, s * BLOCK : (s + 1) * BLOCK]
 
     weight_part = weight_part.astype(BF)
-    for server, to in enumerate((own, other)):
-        nears = [node_near(0, 0, server), node_near(*ALONE, server)]
-        nears += [shared_near(steps, server, 1, server ^ q) for steps in SHARED for q in range(2)]
-        for k, near in enumerate(nears):
-            to[k, :, :nodes] = total[near].astype(BF)
-            to[k, :, nodes:] = weight_part
-
-
-def pair_kernel(own, other, stay, alone, *shared):
+    for server, to1, to2 in ((0, own1, own2), (1, other1, other2)):
+        nears1 = pair_near(FROM_C, server) + [node_near(*FROM_D, server)]
+        nears2 = pair_near(FROM_A, server) + pair_near(FROM_B, server) + [node_near(0, 0, server)]
+        for to, nears in ((to1, nears1), (to2, nears2)):
+            for k, near in enumerate(nears):
+                to[k, :, :nodes] = total[near].astype(BF)
+                to[k, :, nodes:] = weight_part
+
+
+def pair_kernel(own, other, to_c, to_d):
     def both(k):
         return (own[k].astype(F32) + other[k].astype(F32)).astype(BF)
 
-    stay[...] = both(0)
-    alone[...] = both(1)
-    for i, out in enumerate(shared):
-        for q in range(2):
-            out[q] = both(2 + 2 * i + q)
-
-
-def hand_kernel(first, second, third, out):
-    out[...] = (first[1].astype(F32) + second[1].astype(F32) + third[1].astype(F32)).astype(BF)
-
-
-def last_kernel(stay, alone, handed, first, second, third, grad_features, grad_weight):
-    total = stay[...].astype(F32) + alone[...].astype(F32) + handed[...].astype(F32)
-    for piece in (first, second, third):
-        total += piece[0].astype(F32)
+    to_c[0] = both(0)
+    to_c[1] = both(1)
+    to_d[...] = both(2)
+
+
+def merge_kernel(own, other, from_c, from_d, to_a, to_b, stay):
+    core = lax.axis_index("node") & 1
+    last = from_d[...].astype(F32)
+
+    def both(k):
+        return own[k].astype(F32) + other[k].astype(F32)
+
+    for q in range(2):
+        total_a = both(q) + from_c[q].astype(F32)
+        total_b = both(2 + q)
+        if q == 0:
+            total_a += jnp.where(core == 0, last, 0.0)
+            total_b += jnp.where(core == 1, last, 0.0)
+        to_a[q] = total_a.astype(BF)
+        to_b[q] = total_b.astype(BF)
+    stay[...] = both(4).astype(BF)
+
+
+def hand_kernel(first, second, out):
+    out[...] = (first[1].astype(F32) + second[1].astype(F32)).astype(BF)
+
+
+def last_kernel(stay, handed, first, second, grad_features, grad_weight):
+    total = stay[...].astype(F32) + handed[...].astype(F32)
+    total += first[0].astype(F32) + second[0].astype(F32)
     nodes = grad_features.shape[1]
     grad_features[...] = total[:, :nodes].astype(BF)
     grad_weight[...] = total[:, nodes:]
@@ -236,24 +289,50 @@
         compiler_params=params(4),
         name="stack",
     )(*pieces)
-    arrived = [lax.ppermute(pair, "node", shared_pairs(steps)) for steps in SHARED[::-1]]
-    arrived.append(lax.ppermute(features, "node", node_pairs(*ALONE)))
-    values, loaded = pl.pallas_call(
-        load_kernel,
-        in_specs=[pl.BlockSpec(memory_space=pltpu.HBM), ANY],
-        out_specs=[VMEM, VMEM],
-        out_shape=[pltpu.VMEM(block_values.shape, BF), shape((8, 128), F32)],
-        scratch_shapes=[pltpu.SemaphoreType.DMA((8,))],
+    half = block_values.shape[0] // 2
+
+    def load(at, after):
+        part = (half,) + block_values.shape[1:]
+        return pl.pallas_call(
+            functools.partial(load_kernel, at * half),
+            in_specs=[pl.BlockSpec(memory_space=pltpu.HBM), ANY],
+            out_specs=[VMEM, VMEM],
+            out_shape=[pltpu.VMEM(part, BF), shape((8, 128), F32)],
+            scratch_shapes=[pltpu.SemaphoreType.DMA((4,))],
+            compiler_params=params(4),
+            cost_estimate=pl.CostEstimate(
+                flops=0, bytes_accessed=2 * block_values.size, transcendentals=0
+            ),
+            name="load",
+        )(pltpu.with_memory_space_constraint(block_values, pltpu.HBM), after)
+
+    def send(piece, steps):
+        return lax.ppermute(piece, "node", shared_pairs(steps))
+
+    by_a = send(pair, STEP_A)
+    by_b = send(pair, STEP_B)
+    upper, loaded = load(0, pair)
+    by_c = send(by_a, STEP_C)
+    picked = pl.pallas_call(
+        pick_kernel,
+        in_specs=[VMEM] * 2 + [ANY],
+        out_specs=VMEM,
+        out_shape=shape((fin, nodes)),
         compiler_params=params(4),
-        cost_estimate=pl.CostEstimate(
-            flops=0, bytes_accessed=2 * block_values.size * 2, transcendentals=0
-        ),
-        name="load",
-    )(pltpu.with_memory_space_constraint(block_values, pltpu.HBM), pair)
-
-    for piece in arrived:
-        piece, _ = lax.optimization_barrier((piece, loaded))
-        pieces += [piece, lax.ppermute(piece, "node", swap)]
+        name="pick",
+    )(by_a, by_b, loaded)
+    by_d = send(picked, STEP_D)
+    lower, loaded = load(1, picked)
+    bundle = pl.pallas_call(
+        bundle_kernel,
+        in_specs=[VMEM] * 2 + [ANY],
+        out_specs=VMEM,
+        out_shape=shape((3, fin, nodes)),
+        compiler_params=params(4),
+        name="bundle",
+    )(by_c, by_d, loaded)
+    pieces += [by_a, lax.ppermute(by_a, "node", swap), by_b, lax.ppermute(by_b, "node", swap)]
+    pieces += [by_c, by_d, lax.ppermute(bundle, "node", swap)]
 
     mixed = pl.pallas_call(
         mix_kernel,
@@ -263,7 +342,7 @@
         scratch_shapes=[pltpu.VMEM((16, fin, nodes), BF)],
         compiler_params=params(16),
         name="mix",
-    )(block_cols, block_counts, values, cotangent, weight, bias_rows, *pieces)
+    )(block_cols, block_counts, upper, lower, cotangent, weight, bias_rows, *pieces)
 
     both = lax.all_to_all(mixed, "feat", 0, 0, tiled=True)
 
@@ -278,50 +357,58 @@
 
     grads = lax.all_to_all(dense, "feat", 0, 0, tiled=True)
 
-    activation, own, other = pl.pallas_call(
+    wide = nodes + 256
+    activation, own1, other1, own2, other2 = pl.pallas_call(
         spread_kernel,
-        in_specs=[SMEM, SMEM] + [VMEM] * 2,
-        out_specs=[VMEM] * 3,
-        out_shape=[
-            shape((32, nodes)),
-            shape((8, 16, nodes + 256)),
-            shape((8, 16, nodes + 256)),
-        ],
+        in_specs=[SMEM, SMEM] + [VMEM] * 3,
+        out_specs=[VMEM] * 5,
+        out_shape=[shape((32, nodes))]
+        + [shape((3, 16, wide))] * 2
+        + [shape((5, 16, wide))] * 2,
         scratch_shapes=[pltpu.VMEM((17, fin, nodes), F32)],
         compiler_params=params(24),
         name="spread",
-    )(block_cols, block_counts, values, grads)
-
-    other = lax.ppermute(other, "node", swap)
-    stay, alone, *shared = pl.pallas_call(
+    )(block_cols, block_counts, upper, lower, grads)
+
+    other1 = lax.ppermute(other1, "node", swap)
+    other2 = lax.ppermute(other2, "node", swap)
+    to_c, to_d = pl.pallas_call(
         pair_kernel,
         in_specs=[VMEM] * 2,
-        out_specs=[VMEM] * 5,
-        out_shape=[shape((16, nodes + 256))] * 2 + [shape((2, 16, nodes + 256))] * 3,
+        out_specs=[VMEM] * 2,
+        out_shape=[shape((2, 16, wide)), shape((16, wide))],
         compiler_params=params(16),
         name="pair",
-    )(own, other)
-    alone = lax.ppermute(alone, "node", node_pairs(*ALONE))
-    shared = [
-        lax.ppermute(piece, "node", shared_pairs(steps)) for piece, steps in zip(shared, SHARED)
-    ]
+    )(own1, other1)
+    from_c = send(to_c, back(STEP_C))
+    from_d = send(to_d, back(STEP_D))
+    to_a, to_b, stay = pl.pallas_call(
+        merge_kernel,
+        in_specs=[VMEM] * 4,
+        out_specs=[VMEM] * 3,
+        out_shape=[shape((2, 16, wide))] * 2 + [shape((16, wide))],
+        compiler_params=params(16),
+        name="merge",
+    )(own2, other2, from_c, from_d)
+    from_a = send(to_a, back(STEP_A))
+    from_b = send(to_b, back(STEP_B))
     handed = pl.pallas_call(
         hand_kernel,
-        in_specs=[VMEM] * 3,
-        out_specs=VMEM,
-        out_shape=shape((16, nodes + 256)),
+        in_specs=[VMEM] * 2,
+        out_specs=VMEM,
+        out_shape=shape((16, wide)),
         compiler_params=params(16),
         name="hand",
-    )(*shared)
+    )(from_a, from_b)
     handed = lax.ppermute(handed, "node", swap)
     grad_features, grad_weight = pl.pallas_call(
         last_kernel,
-        in_specs=[VMEM] * 6,
+        in_specs=[VMEM] * 4,
         out_specs=[VMEM] * 2,
         out_shape=[shape((16, nodes)), shape((16, 256), F32)],
         compiler_params=params(16),
         name="last",
-    )(stay, alone, handed, *shared)
+    )(stay, handed, from_a, from_b)
     return activation, grad_features, grad_weight
 
 

time: 109 us -> 122 us (1.12)
  local copies, waits for them, and re-layouts: 2.32 us -> 19.6 us
  waiting for transfers between devices: 32.7 us -> 30.2 us
  starting transfers between devices: 22 us -> 19.6 us
  blocking collectives: 27.9 us -> 29.8 us
  Pallas kernels: 22.8 us -> 21.3 us
    unnamed x13 -> x29, local copies, waits for them, and re-layouts: 1.48 us -> 19.4 us
    ppermute x13, waiting for transfers between devices: 29.9 us -> 27.5 us  [the longest x8 23.7 us: send(): return lax.ppermute(piece, 'node', shared_pairs(steps))]
    ppermute x13, starting transfers between devices: 20.4 us -> 18 us  [the longest x8 15.2 us: send(): return lax.ppermute(piece, 'node', shared_pairs(steps))]
    all_to_all x1, blocking collectives: 12.3 us -> 14.1 us  [local(): grads = lax.all_to_all(dense, 'feat', 0, 0, tiled=True)]
    pallas_call x1, Pallas kernels: 1.7 us -> 0.03 us  [local(): pl.pallas_call(stack_kernel, in_specs=[VMEM] * 2, out_specs=VMEM, out_sha...]
    pallas_call x5 -> x9, Pallas kernels: 15.9 us -> 16.5 us  [the longest x2 7.71 us: load(): pl.pallas_call(functools.partial(load_kernel, at * half), in_specs=[pl.Bl...]
  transfers between devices with their start and end apart: 15 -> 15, of which waited for: 9 -> 9; matrix products, arithmetic and copies ran while one was open for 2% -> 0% of each run, Pallas kernels for 7% -> 6%
where the time goes in v5:
time: 122 us; the launch traced here: 121 us
  waiting for transfers between devices  30.2 us (25%)
  blocking collectives  29.8 us (24%)
  Pallas kernels  21.3 us (17%)
  starting transfers between devices  19.6 us (16%)
  local copies, waits for them, and re-layouts  19.6 us (16%)
    ppermute x8, waiting for transfers between devices, send(): return lax.ppermute(piece, 'node', shared_pairs(steps))  23.7 us
    unnamed x29, local copies, waits for them, and re-layouts  19.4 us
    all_to_all x1, blocking collectives, local(): both = lax.all_to_all(mixed, 'feat', 0, 0, tiled=True)  15.7 us
    ppermute x8, starting transfers between devices, send(): return lax.ppermute(piece, 'node', shared_pairs(steps))  15.2 us
    all_to_all x1, blocking collectives, local(): grads = lax.all_to_all(dense, 'feat', 0, 0, tiled=True)  14.1 us
    pallas_call x2, Pallas kernels, load(): pl.pallas_call(functools.partial(load_kernel, at * half), in_specs=[pl.Bl...  7.71 us
    pallas_call x1, Pallas kernels, local(): pl.pallas_call(spread_kernel, in_specs=[SMEM, SMEM] + [VMEM] * 3, out_spe...  7.38 us
    pallas_call x1, Pallas kernels, local(): pl.pallas_call(mix_kernel, in_specs=[SMEM, SMEM] + [VMEM] * 14, out_specs...  4.04 us
  transfers between devices with their start and end apart: 15, of which 9 were waited for; matrix products, arithmetic and copies ran while one was open for 0% of the time, Pallas kernels for 6%

profile of v5, /device:TPU:1, one launch (start us, length us, event | category | flops | bytes accessed | tf_op | source)
XLA Modules:
  0.0 121.4 jit_solution(9122598215464080978)
XLA Ops:
  0.6 1.5 %collective-permute-start = (bf16[16,6144]{1,0:T(8,128)(2,1)}, bf16[16,6144]{1,0:T(8,128)(2,1)S(1)}, u32[]{:S(2)}, u32[]{:S(2)}) collective-permute-start(bf16[16,6144]{1,0:T(8,128)(2,1)} %rest_0_.1), channel_id=1, source_target_pairs={{0,8},{8,0},{16,24},{24,16},{32,40},{40,32},{48,56},{56,48},{64,72... | collective-permute-start | bytes 589832 | tf_op jit(solution)/shard_map/ppermute | solution.py:283
  4.4 3.8 %collective-permute-start.1 = (bf16[2,16,6144]{2,1,0:T(8,128)(2,1)S(1)}, bf16[2,16,6144]{2,1,0:T(8,128)(2,1)S(1)}, u32[]{:S(2)}, u32[]{:S(2)}) collective-permute-start(bf16[2,16,6144]{2,1,0:T(8,128)(2,1)S(1)} %stack.1._), channel_id=1, source_target_pairs={{0,64},{8,40},{16,80},{24,56},{32,96},{40,8},{48,112},{56,24},{64,... | collective-permute-start | bytes 1179656 | tf_op jit(solution)/shard_map/ppermute | solution.py:310
  8.6 6.5 %collective-permute-done.1.first.rest_2_ = bf16[2,16,6144]{2,1,0:T(8,128)(2,1)S(1)} collective-permute-done((bf16[2,16,6144]{2,1,0:T(8,128)(2,1)S(1)}, bf16[2,16,6144]{2,1,0:T(8,128)(2,1)S(1)}, u32[]{:S(2)}, u32[]{:S(2)}) %collective-permute-start.1) | collective-permute-done | bytes 393248 | tf_op jit(solution)/shard_map/ppermute | solution.py:310
  15.1 4.1 %collective-permute-start.5 = (bf16[2,16,6144]{2,1,0:T(8,128)(2,1)S(1)}, bf16[2,16,6144]{2,1,0:T(8,128)(2,1)S(1)}, u32[]{:S(2)}, u32[]{:S(2)}) collective-permute-start(bf16[2,16,6144]{2,1,0:T(8,128)(2,1)S(1)} %collective-permute-done.1.first.rest_2_), channel_id=1, source_target_pairs={{0,16},{8,72},{16,32},{24,88},{32,48},{40,104},{48,0},{56,120},{64... | collective-permute-start | bytes 1179656 | tf_op jit(solution)/shard_map/ppermute | solution.py:310
  19.2 3.8 %load.2 = (bf16[24,12,128,128]{3,2,1,0:T(8,128)(2,1)S(1)}, f32[8,128]{1,0:T(8,128)S(1)}) custom-call(bf16[48,12,128,128]{3,2,1,0:T(8,128)(2,1)} %values.3, bf16[2,16,6144]{2,1,0:T(8,128)(2,1)S(1)} %stack.1._), custom_call_target="tpu_custom_call" | custom-call | bytes 18874368 | tf_op jit(solution)/shard_map/load/pallas_call | solution.py:296
  23.0 3.7 %copy-done = bf16[24,12,128,128]{3,2,1,0:T(8,128)(2,1)} copy-done((bf16[24,12,128,128]{3,2,1,0:T(8,128)(2,1)}, bf16[24,12,128,128]{3,2,1,0:T(8,128)(2,1)S(1)}, u32[]{:S(2)}) %copy-start) | copy-done | bytes 9437208
  26.8 3.9 %load.3 = (bf16[24,12,128,128]{3,2,1,0:T(8,128)(2,1)S(1)}, f32[8,128]{1,0:T(8,128)S(1)}) custom-call(bf16[48,12,128,128]{3,2,1,0:T(8,128)(2,1)} %values.3, bf16[16,6144]{1,0:T(8,128)(2,1)S(1)} %pick.1._), custom_call_target="tpu_custom_call" | custom-call | bytes 18874368 | tf_op jit(solution)/shard_map/load/pallas_call | solution.py:296
  30.8 3.6 %copy-done.3 = bf16[24,12,128,128]{3,2,1,0:T(8,128)(2,1)} copy-done((bf16[24,12,128,128]{3,2,1,0:T(8,128)(2,1)}, bf16[24,12,128,128]{3,2,1,0:T(8,128)(2,1)S(1)}, u32[]{:S(2)}) %copy-start.3) | copy-done | bytes 9437208
  35.6 1.5 %collective-permute-done.4.rest_5_ = bf16[2,16,6144]{2,1,0:T(8,128)(2,1)S(1)} collective-permute-done((bf16[2,16,6144]{2,1,0:T(8,128)(2,1)S(1)}, bf16[2,16,6144]{2,1,0:T(8,128)(2,1)S(1)}, u32[]{:S(2)}, u32[]{:S(2)}) %collective-permute-start.4) | collective-permute-done | bytes 393248 | tf_op jit(solution)/shard_map/ppermute | solution.py:334
  37.7 3.7 %copy-done.1 = bf16[24,12,128,128]{3,2,1,0:T(8,128)(2,1)S(1)} copy-done((bf16[24,12,128,128]{3,2,1,0:T(8,128)(2,1)S(1)}, bf16[24,12,128,128]{3,2,1,0:T(8,128)(2,1)}, u32[]{:S(2)}) %copy-start.1) | copy-done | bytes 9437208
  41.4 3.7 %copy-done.4 = bf16[24,12,128,128]{3,2,1,0:T(8,128)(2,1)S(1)} copy-done((bf16[24,12,128,128]{3,2,1,0:T(8,128)(2,1)S(1)}, bf16[24,12,128,128]{3,2,1,0:T(8,128)(2,1)}, u32[]{:S(2)}) %copy-start.4) | copy-done | bytes 9437208
  45.0 4.0 %mix.1 = bf16[8,16,2816]{2,1,0:T(8,128)(2,1)S(1)} custom-call(s32[48,12]{1,0:T(8,128)S(1)} %copy.12.cols, s32[48]{0:T(128)S(1)} %copy-done.11, bf16[24,12,128,128]{3,2,1,0:T(8,128)(2,1)S(1)} %copy-done.1, bf16[24,12,128,128]{3,2,1,0:T(8,128)(2,1)S(1)} %copy-done.4, bf16[32,6144]{1,0:T(8,128)(2,1)S(1)} %copy-done.8, bf16[16,256]{1,0:T(8,128)(2,1)S(1)} %copy-done.10, ...), custom_call_target="tpu_custom_call" | custom-call | tf_op jit(solution)/shard_map/mix/pallas_call | solution.py:337
  49.1 15.7 %all_to_all.10.both = bf16[8,16,2816]{2,1,0:T(8,128)(2,1)S(1)} all-to-all(bf16[8,16,2816]{2,1,0:T(8,128)(2,1)S(1)} %mix.1), channel_id=1, replica_groups=mesh['node'=16,'feat'=8] {'feat'}, dimensions={0} | all-to-all | bytes 1441792 | tf_op jit(solution)/shard_map/all_to_all | solution.py:347
  65.5 14.1 %all_to_all.11.grads = bf16[8,16,2560]{2,1,0:T(8,128)(2,1)S(1)} all-to-all(bf16[8,16,2560]{2,1,0:T(8,128)(2,1)S(1)} %dense.1), channel_id=1, replica_groups=mesh['node'=16,'feat'=8] {'feat'}, dimensions={0} | all-to-all | bytes 1310720 | tf_op jit(solution)/shard_map/all_to_all | solution.py:358
  79.6 3.7 %copy-done.2 = bf16[24,12,128,128]{3,2,1,0:T(8,128)(2,1)S(1)} copy-done((bf16[24,12,128,128]{3,2,1,0:T(8,128)(2,1)S(1)}, bf16[24,12,128,128]{3,2,1,0:T(8,128)(2,1)}, u32[]{:S(2)}) %copy-start.2) | copy-done | bytes 9437208
  83.3 7.4 %spread.1 = (bf16[32,6144]{1,0:T(8,128)(2,1)}, bf16[3,16,6400]{2,1,0:T(8,128)(2,1)S(1)}, bf16[3,16,6400]{2,1,0:T(8,128)(2,1)S(1)}, bf16[5,16,6400]{2,1,0:T(8,128)(2,1)S(1)}, bf16[5,16,6400]{2,1,0:T(8,128)(2,1)S(1)}) custom-call(s32[48,12]{1,0:T(8,128)S(1)} %copy.12.cols, s32[48]{0:T(128)S(1)} %copy-done.11, bf16[24,12,128,128]{3,2,1,0:T(8,128)(2,1)S(1)} %copy-done.2, ...), custom_call_target="tpu_custom_call" | custom-call | tf_op jit(solution)/shard_map/spread/pallas_call | solution.py:361
  90.7 2.1 %collective-permute-start.9 = (bf16[3,16,6400]{2,1,0:T(8,128)(2,1)S(1)}, bf16[3,16,6400]{2,1,0:T(8,128)(2,1)S(1)}, u32[]{:S(2)}, u32[]{:S(2)}) collective-permute-start(bf16[3,16,6400]{2,1,0:T(8,128)(2,1)S(1)} %get-tuple-element.27), channel_id=1, source_target_pairs={{0,8},{8,0},{16,24},{24,16},{32,40},{40,32},{48,56},{56,48},{64,72... | collective-permute-start | bytes 1843208 | tf_op jit(solution)/shard_map/ppermute | solution.py:373
  92.8 1.7 %collective-permute-done.9.other = bf16[3,16,6400]{2,1,0:T(8,128)(2,1)S(1)} collective-permute-done((bf16[3,16,6400]{2,1,0:T(8,128)(2,1)S(1)}, bf16[3,16,6400]{2,1,0:T(8,128)(2,1)S(1)}, u32[]{:S(2)}, u32[]{:S(2)}) %collective-permute-start.9) | collective-permute-done | bytes 614432 | tf_op jit(solution)/shard_map/ppermute | solution.py:373
  94.7 3.2 %collective-permute-start.10 = (bf16[2,16,6400]{2,1,0:T(8,128)(2,1)S(1)}, bf16[2,16,6400]{2,1,0:T(8,128)(2,1)S(1)}, u32[]{:S(2)}, u32[]{:S(2)}) collective-permute-start(bf16[2,16,6400]{2,1,0:T(8,128)(2,1)S(1)} %get-tuple-element.28), channel_id=1, source_target_pairs={{0,48},{8,72},{16,0},{24,88},{32,16},{40,104},{48,32},{56,120},{64... | collective-permute-start | bytes 1228808 | tf_op jit(solution)/shard_map/ppermute | solution.py:310
  98.0 7.5 %collective-permute-done.11.from_d = bf16[16,6400]{1,0:T(8,128)(2,1)S(1)} collective-permute-done((bf16[16,6400]{1,0:T(8,128)(2,1)S(1)}, bf16[16,6400]{1,0:T(8,128)(2,1)S(1)}, u32[]{:S(2)}, u32[]{:S(2)}) %collective-permute-start.11) | collective-permute-done | bytes 204832 | tf_op jit(solution)/shard_map/ppermute | solution.py:310
  105.8 3.5 %collective-permute-start.12 = (bf16[2,16,6400]{2,1,0:T(8,128)(2,1)S(1)}, bf16[2,16,6400]{2,1,0:T(8,128)(2,1)S(1)}, u32[]{:S(2)}, u32[]{:S(2)}) collective-permute-start(bf16[2,16,6400]{2,1,0:T(8,128)(2,1)S(1)} %get-tuple-element.31), channel_id=1, source_target_pairs={{0,64},{8,40},{16,80},{24,56},{32,96},{40,8},{48,112},{56,24},{64,... | collective-permute-start | bytes 1228808 | tf_op jit(solution)/shard_map/ppermute | solution.py:310
  109.3 5.4 %collective-permute-done.12.first = bf16[2,16,6400]{2,1,0:T(8,128)(2,1)S(1)} collective-permute-done((bf16[2,16,6400]{2,1,0:T(8,128)(2,1)S(1)}, bf16[2,16,6400]{2,1,0:T(8,128)(2,1)S(1)}, u32[]{:S(2)}, u32[]{:S(2)}) %collective-permute-start.12) | collective-permute-done | bytes 409632 | tf_op jit(solution)/shard_map/ppermute | solution.py:310
  114.8 4.3 %collective-permute-done.13.second = bf16[2,16,6400]{2,1,0:T(8,128)(2,1)S(1)} collective-permute-done((bf16[2,16,6400]{2,1,0:T(8,128)(2,1)S(1)}, bf16[2,16,6400]{2,1,0:T(8,128)(2,1)S(1)}, u32[]{:S(2)}, u32[]{:S(2)}) %collective-permute-start.13) | collective-permute-done | bytes 409632 | tf_op jit(solution)/shard_map/ppermute | solution.py:310
  119.2 1.4 %collective-permute-done.14.handed = bf16[16,6400]{1,0:T(8,128)(2,1)S(1)} collective-permute-done((bf16[16,6400]{1,0:T(8,128)(2,1)S(1)}, bf16[16,6400]{1,0:T(8,128)(2,1)S(1)}, u32[]{:S(2)}, u32[]{:S(2)}) %collective-permute-start.14) | collective-permute-done | bytes 204832 | tf_op jit(solution)/shard_map/ppermute | solution.py:403
  (55 shorter events, 6.8 us)
Async XLA Ops:
  0.6 2.8 %collective-permute-start = (bf16[16,6144]{1,0:T(8,128)(2,1)}, bf16[16,6144]{1,0:T(8,128)(2,1)S(1)}, u32[]{:S(2)}, u32[]{:S(2)}) collective-permute-start(bf16[16,6144]{1,0:T(8,128)(2,1)} %rest_0_.1), channel_id=1, source_target_pairs={{0,8},{8,0},{16,24},{24,16},{32,40},{40,32},{48,56},{56,48},{64,72... | collective-permute-start | bytes 589832 | tf_op jit(solution)/shard_map/ppermute | solution.py:283
  4.4 10.7 %collective-permute-start.1 = (bf16[2,16,6144]{2,1,0:T(8,128)(2,1)S(1)}, bf16[2,16,6144]{2,1,0:T(8,128)(2,1)S(1)}, u32[]{:S(2)}, u32[]{:S(2)}) collective-permute-start(bf16[2,16,6144]{2,1,0:T(8,128)(2,1)S(1)} %stack.1._), channel_id=1, source_target_pairs={{0,64},{8,40},{16,80},{24,56},{32,96},{40,8},{48,112},{56,24},{64,... | collective-permute-start | bytes 1179656 | tf_op jit(solution)/shard_map/ppermute | solution.py:310
  8.1 18.5 %collective-permute-start.2 = (bf16[2,16,6144]{2,1,0:T(8,128)(2,1)S(1)}, bf16[2,16,6144]{2,1,0:T(8,128)(2,1)S(1)}, u32[]{:S(2)}, u32[]{:S(2)}) collective-permute-start(bf16[2,16,6144]{2,1,0:T(8,128)(2,1)S(1)} %stack.1._), channel_id=1, source_target_pairs={{0,16},{8,56},{16,32},{24,8},{32,48},{40,24},{48,0},{56,40},{64,80... | collective-permute-start | bytes 1179656 | tf_op jit(solution)/shard_map/ppermute | solution.py:310
  15.1 19.3 %collective-permute-start.5 = (bf16[2,16,6144]{2,1,0:T(8,128)(2,1)S(1)}, bf16[2,16,6144]{2,1,0:T(8,128)(2,1)S(1)}, u32[]{:S(2)}, u32[]{:S(2)}) collective-permute-start(bf16[2,16,6144]{2,1,0:T(8,128)(2,1)S(1)} %collective-permute-done.1.first.rest_2_), channel_id=1, source_target_pairs={{0,16},{8,72},{16,32},{24,88},{32,48},{40,104},{48,0},{56,120},{64... | collective-permute-start | bytes 1179656 | tf_op jit(solution)/shard_map/ppermute | solution.py:310
  26.7 7.8 %copy-start.12 = (s32[48,12]{0,1:T(8,128)S(1)}, s32[48,12]{0,1:T(8,128)}, u32[]{:S(2)}) copy-start(s32[48,12]{0,1:T(8,128)} %param.12) | copy-start | bytes 6916
  26.7 8.0 %copy-start.13 = (f32[32]{0:T(128)S(1)}, f32[32]{0:T(128)}, u32[]{:S(2)}) copy-start(f32[32]{0:T(128)} %param.10) | copy-start | bytes 388
  26.7 10.9 %copy-start.7 = (bf16[16,6144]{1,0:T(8,128)(2,1)S(1)}, bf16[16,6144]{1,0:T(8,128)(2,1)}, u32[]{:S(2)}) copy-start(bf16[16,6144]{1,0:T(8,128)(2,1)} %rest_0_.1) | copy-start | bytes 589828
  26.7 10.9 %copy-start.8 = (bf16[32,6144]{1,0:T(8,128)(2,1)S(1)}, bf16[32,6144]{1,0:T(8,128)(2,1)}, u32[]{:S(2)}) copy-start(bf16[32,6144]{1,0:T(8,128)(2,1)} %cotangent.1) | copy-start | bytes 1179652
  26.7 10.9 %copy-start.10 = (bf16[16,256]{1,0:T(8,128)(2,1)S(1)}, bf16[16,256]{1,0:T(8,128)(2,1)}, u32[]{:S(2)}) copy-start(bf16[16,256]{1,0:T(8,128)(2,1)} %weight.1) | copy-start | bytes 24580
  26.7 10.9 %copy-start.11 = (s32[48]{0:T(128)S(1)}, s32[48]{0:T(128)}, u32[]{:S(2)}) copy-start(s32[48]{0:T(128)} %counts.3) | copy-start | bytes 580
  26.8 7.6 %collective-permute-start.6 = (bf16[16,6144]{1,0:T(8,128)(2,1)S(1)}, bf16[16,6144]{1,0:T(8,128)(2,1)S(1)}, u32[]{:S(2)}, u32[]{:S(2)}) collective-permute-start(bf16[16,6144]{1,0:T(8,128)(2,1)S(1)} %pick.1._), channel_id=1, source_target_pairs={{0,48},{8,72},{16,0},{24,88},{32,16},{40,104},{48,32},{56,120},{64... | collective-permute-start | bytes 589832 | tf_op jit(solution)/shard_map/ppermute | solution.py:310
  34.4 3.2 %collective-permute-start.7 = (bf16[3,16,6144]{2,1,0:T(8,128)(2,1)S(1)}, bf16[3,16,6144]{2,1,0:T(8,128)(2,1)S(1)}, u32[]{:S(2)}, u32[]{:S(2)}) collective-permute-start(bf16[3,16,6144]{2,1,0:T(8,128)(2,1)S(1)} %bundle.1), channel_id=1, source_target_pairs={{0,8},{8,0},{16,24},{24,16},{32,40},{40,32},{48,56},{56,48},{64,72... | collective-permute-start | bytes 1769480 | tf_op jit(solution)/shard_map/ppermute | solution.py:335
  34.8 2.2 %collective-permute-start.4 = (bf16[2,16,6144]{2,1,0:T(8,128)(2,1)S(1)}, bf16[2,16,6144]{2,1,0:T(8,128)(2,1)S(1)}, u32[]{:S(2)}, u32[]{:S(2)}) collective-permute-start(bf16[2,16,6144]{2,1,0:T(8,128)(2,1)S(1)} %collective-permute-done.2.second.rest_4_), channel_id=1, source_target_pairs={{0,8},{8,0},{16,24},{24,16},{32,40},{40,32},{48,56},{56,48},{64,72... | collective-permute-start | bytes 1179656 | tf_op jit(solution)/shard_map/ppermute | solution.py:334
  35.4 2.2 %collective-permute-start.3 = (bf16[2,16,6144]{2,1,0:T(8,128)(2,1)S(1)}, bf16[2,16,6144]{2,1,0:T(8,128)(2,1)S(1)}, u32[]{:S(2)}, u32[]{:S(2)}) collective-permute-start(bf16[2,16,6144]{2,1,0:T(8,128)(2,1)S(1)} %collective-permute-done.1.first.rest_2_), channel_id=1, source_target_pairs={{0,8},{8,0},{16,24},{24,16},{32,40},{40,32},{48,56},{56,48},{64,72... | collective-permute-start | bytes 1179656 | tf_op jit(solution)/shard_map/ppermute | solution.py:334
  45.0 19.7 %copy-start.9 = (s32[6144]{0:T(1024)S(1)}, s32[6144]{0:T(1024)}, u32[]{:S(2)}) copy-start(s32[6144]{0:T(1024)} %param.14) | copy-start | bytes 73732
  45.0 34.6 %copy-start.5 = (bf16[24,12,128,128]{3,2,1,0:T(8,128)(2,1)S(1)}, bf16[24,12,128,128]{3,2,1,0:T(8,128)(2,1)}, u32[]{:S(2)}) copy-start(bf16[24,12,128,128]{3,2,1,0:T(8,128)(2,1)} %copy-done.3) | copy-start | bytes 28311556
  79.6 3.7 %copy-start.2 = (bf16[24,12,128,128]{3,2,1,0:T(8,128)(2,1)S(1)}, bf16[24,12,128,128]{3,2,1,0:T(8,128)(2,1)}, u32[]{:S(2)}) copy-start(bf16[24,12,128,128]{3,2,1,0:T(8,128)(2,1)} %copy-done) | copy-start | bytes 28311556
  90.7 3.8 %collective-permute-start.9 = (bf16[3,16,6400]{2,1,0:T(8,128)(2,1)S(1)}, bf16[3,16,6400]{2,1,0:T(8,128)(2,1)S(1)}, u32[]{:S(2)}, u32[]{:S(2)}) collective-permute-start(bf16[3,16,6400]{2,1,0:T(8,128)(2,1)S(1)} %get-tuple-element.27), channel_id=1, source_target_pairs={{0,8},{8,0},{16,24},{24,16},{32,40},{40,32},{48,56},{56,48},{64,72... | collective-permute-start | bytes 1843208 | tf_op jit(solution)/shard_map/ppermute | solution.py:373
  92.8 12.6 %collective-permute-start.8 = (bf16[5,16,6400]{2,1,0:T(8,128)(2,1)S(1)}, bf16[5,16,6400]{2,1,0:T(8,128)(2,1)S(1)}, u32[]{:S(2)}, u32[]{:S(2)}) collective-permute-start(bf16[5,16,6400]{2,1,0:T(8,128)(2,1)S(1)} %get-tuple-element.25), channel_id=1, source_target_pairs={{0,8},{8,0},{16,24},{24,16},{32,40},{40,32},{48,56},{56,48},{64,72... | collective-permute-start | bytes 3072008 | tf_op jit(solution)/shard_map/ppermute | solution.py:374
  94.7 10.8 %collective-permute-start.10 = (bf16[2,16,6400]{2,1,0:T(8,128)(2,1)S(1)}, bf16[2,16,6400]{2,1,0:T(8,128)(2,1)S(1)}, u32[]{:S(2)}, u32[]{:S(2)}) collective-permute-start(bf16[2,16,6400]{2,1,0:T(8,128)(2,1)S(1)} %get-tuple-element.28), channel_id=1, source_target_pairs={{0,48},{8,72},{16,0},{24,88},{32,16},{40,104},{48,32},{56,120},{64... | collective-permute-start | bytes 1228808 | tf_op jit(solution)/shard_map/ppermute | solution.py:310
  97.9 7.5 %collective-permute-start.11 = (bf16[16,6400]{1,0:T(8,128)(2,1)S(1)}, bf16[16,6400]{1,0:T(8,128)(2,1)S(1)}, u32[]{:S(2)}, u32[]{:S(2)}) collective-permute-start(bf16[16,6400]{1,0:T(8,128)(2,1)S(1)} %get-tuple-element.29), channel_id=1, source_target_pairs={{0,16},{8,72},{16,32},{24,88},{32,48},{40,104},{48,0},{56,120},{64... | collective-permute-start | bytes 614408 | tf_op jit(solution)/shard_map/ppermute | solution.py:310
  105.8 8.9 %collective-permute-start.12 = (bf16[2,16,6400]{2,1,0:T(8,128)(2,1)S(1)}, bf16[2,16,6400]{2,1,0:T(8,128)(2,1)S(1)}, u32[]{:S(2)}, u32[]{:S(2)}) collective-permute-start(bf16[2,16,6400]{2,1,0:T(8,128)(2,1)S(1)} %get-tuple-element.31), channel_id=1, source_target_pairs={{0,64},{8,40},{16,80},{24,56},{32,96},{40,8},{48,112},{56,24},{64,... | collective-permute-start | bytes 1228808 | tf_op jit(solution)/shard_map/ppermute | solution.py:310
  109.3 9.7 %collective-permute-start.13 = (bf16[2,16,6400]{2,1,0:T(8,128)(2,1)S(1)}, bf16[2,16,6400]{2,1,0:T(8,128)(2,1)S(1)}, u32[]{:S(2)}, u32[]{:S(2)}) collective-permute-start(bf16[2,16,6400]{2,1,0:T(8,128)(2,1)S(1)} %get-tuple-element.32), channel_id=1, source_target_pairs={{0,48},{8,24},{16,0},{24,40},{32,16},{40,56},{48,32},{56,8},{64,11... | collective-permute-start | bytes 1228808 | tf_op jit(solution)/shard_map/ppermute | solution.py:310
  119.1 1.5 %collective-permute-start.14 = (bf16[16,6400]{1,0:T(8,128)(2,1)S(1)}, bf16[16,6400]{1,0:T(8,128)(2,1)S(1)}, u32[]{:S(2)}, u32[]{:S(2)}) collective-permute-start(bf16[16,6400]{1,0:T(8,128)(2,1)S(1)} %hand.1), channel_id=1, source_target_pairs={{0,8},{8,0},{16,24},{24,16},{32,40},{40,32},{48,56},{56,48},{64,72... | collective-permute-start | bytes 614408 | tf_op jit(solution)/shard_map/ppermute | solution.py:403
  (5 other events, 15.6 us)

commit v6 on v4

--- a/solution.py
+++ b/solution.py
@@ -1,3 +1,5 @@
+import functools
+
 import jax
 import jax.numpy as jnp
 from jax import lax
@@ -10,8 +12,11 @@
 ANY = pl.BlockSpec(memory_space=pl.ANY)
 SMEM = pl.BlockSpec(memory_space=pltpu.SMEM)
 VMEM = pl.BlockSpec(memory_space=pltpu.VMEM)
-ALONE = (0, 1)
-SHARED = (((1, 2), (1, 1)), ((1, 3), (0, 2)), ((1, 0), (0, 3)))
+FIRST = ((0, 2), (1, 0))
+SECOND = ((1, 1), (1, 3))
+THIRD = ((0, 1), (0, 3))
+FORWARD = ((1, 0), (0, 2))
+FARTHEST = (1, 2)
 BLOCK = 128
 
 
@@ -43,11 +48,19 @@
     ]
 
 
-def shared_near(steps, server, sign, dcore):
+def back(steps):
+    return tuple((dx, -dz % 4) for dx, dz in steps)
+
+
+def shared_near(steps, server, dcore):
     core = (lax.axis_index("node") & 1) ^ server
     dx = jnp.where(core == 0, steps[0][0], steps[1][0])
     dz = jnp.where(core == 0, steps[0][1], steps[1][1])
-    return node_near(dx, sign * dz, dcore)
+    return node_near(dx, dz, dcore)
+
+
+def pair_near(steps, server):
+    return [shared_near(steps, server, server ^ q) for q in range(2)]
 
 
 def place_of(column):
@@ -64,9 +77,26 @@
     out[1] = second[...]
 
 
-def load_kernel(values, _, out, loaded, sems):
+def bundle_kernel(_, *refs):
+    pieces, out = refs[:-1], refs[-1]
+    at = 0
+    for piece in pieces:
+        if len(piece.shape) == 3:
+            out[at : at + 2] = piece[...]
+            at += 2
+        else:
+            out[at] = piece[...]
+            at += 1
+
+
+def pick_kernel(pair, out):
+    out[...] = pair[0]
+
+
+def load_kernel(values, *rest):
+    out, loaded, sems = rest[-3:]
     count = sems.shape[0]
-    rows = values.shape[0] // count
+    rows = out.shape[0] // count
     copies = [
         pltpu.make_async_copy(
             values.at[pl.ds(i * rows, rows)], out.at[pl.ds(i * rows, rows)], sems.at[i]
@@ -81,20 +111,20 @@
 
 
 def mix_kernel(cols, counts, values, cotangent, weight, bias_rows, *rest):
-    pieces, (out, held) = rest[:10], rest[10:]
+    pieces, (out, held) = rest[:9], rest[9:]
     slots = values.shape[1]
     chunks, _, _ = out.shape
     width = cotangent.shape[1] // chunks
     rows = values.shape[0] // chunks
 
-    for at, (dx, dz) in ((0, (0, 0)), (8, ALONE)):
-        for server in range(2):
-            held[node_near(dx, -dz, server)] = pieces[at + server][...]
-    for at, steps in ((2, SHARED[2]), (4, SHARED[1]), (6, SHARED[0])):
-        for server in range(2):
-            for q in range(2):
-                near = shared_near(steps, server, -1, server ^ q)
-                held[near] = pieces[at + server][q]
+    first, second, third = pieces[2:4], pieces[4:6], (pieces[6], pieces[8])
+    farthest = (pieces[7], pieces[8].at[2])
+    for server in range(2):
+        held[node_near(0, 0, server)] = pieces[server][...]
+        held[node_near(*FARTHEST, server)] = farthest[server][...]
+        for shards, steps in ((first, FIRST), (second, SECOND), (third, THIRD)):
+            for q, near in enumerate(pair_near(back(steps), server)):
+                held[near] = shards[server][q]
     for j in range(chunks):
         out[j, :, width : 2 * width] = cotangent[:16, j * width : (j + 1) * width]
         out[j, :, 2 * width : 3 * width] = cotangent[16:, j * width : (j + 1) * width]
@@ -147,7 +177,9 @@
     out[:, :, 2 * width + 256 :] = activation[:, 16:]
 
 
-def spread_kernel(cols, counts, values, grads, activation, own, other, total):
+def spread_kernel(
+    cols, counts, values, grads, activation, own1, other1, own2, other2, total
+):
     slots = values.shape[1]
     chunks = grads.shape[0]
     rows = values.shape[0] // chunks
@@ -178,31 +210,41 @@
                 total[group, :, pl.ds(lane, BLOCK)] += contrib[:, s * BLOCK : (s + 1) * BLOCK]
 
     weight_part = weight_part.astype(BF)
-    for server, to in enumerate((own, other)):
-        nears = [node_near(0, 0, server), node_near(*ALONE, server)]
-        nears += [shared_near(steps, server, 1, server ^ q) for steps in SHARED for q in range(2)]
-        for k, near in enumerate(nears):
-            to[k, :, :nodes] = total[near].astype(BF)
-            to[k, :, nodes:] = weight_part
-
-
-def pair_kernel(own, other, stay, alone, *shared):
+    for server, to1, to2 in ((0, own1, own2), (1, other1, other2)):
+        nears1 = [node_near(*FARTHEST, server)]
+        nears1 += pair_near(back(SECOND), server) + pair_near(back(THIRD), server)
+        nears2 = pair_near(back(FIRST), server) + [node_near(0, 0, server)]
+        for to, nears in ((to1, nears1), (to2, nears2)):
+            for k, near in enumerate(nears):
+                to[k, :, :nodes] = total[near].astype(BF)
+                to[k, :, nodes:] = weight_part
+
+
+def pair_kernel(own, other, farthest, second, third):
     def both(k):
         return (own[k].astype(F32) + other[k].astype(F32)).astype(BF)
 
-    stay[...] = both(0)
-    alone[...] = both(1)
-    for i, out in enumerate(shared):
-        for q in range(2):
-            out[q] = both(2 + 2 * i + q)
+    farthest[...] = both(0)
+    for q in range(2):
+        second[q] = both(1 + q)
+        third[q] = both(3 + q)
+
+
+def merge_kernel(own, other, forwarded, first, stay):
+    def both(k):
+        return own[k].astype(F32) + other[k].astype(F32)
+
+    first[0] = (both(0) + forwarded[...].astype(F32)).astype(BF)
+    first[1] = both(1).astype(BF)
+    stay[...] = both(2).astype(BF)
 
 
 def hand_kernel(first, second, third, out):
     out[...] = (first[1].astype(F32) + second[1].astype(F32) + third[1].astype(F32)).astype(BF)
 
 
-def last_kernel(stay, alone, handed, first, second, third, grad_features, grad_weight):
-    total = stay[...].astype(F32) + alone[...].astype(F32) + handed[...].astype(F32)
+def last_kernel(stay, handed, first, second, third, grad_features, grad_weight):
+    total = stay[...].astype(F32) + handed[...].astype(F32)
     for piece in (first, second, third):
         total += piece[0].astype(F32)
     nodes = grad_features.shape[1]
@@ -236,11 +278,22 @@
         compiler_params=params(4),
         name="stack",
     )(*pieces)
-    arrived = [lax.ppermute(pair, "node", shared_pairs(steps)) for steps in SHARED[::-1]]
-    arrived.append(lax.ppermute(features, "node", node_pairs(*ALONE)))
+    def send(piece, steps):
+        return lax.ppermute(piece, "node", shared_pairs(steps))
+
+    first, second, third = (send(pair, steps) for steps in (FIRST, SECOND, THIRD))
+    picked = pl.pallas_call(
+        pick_kernel,
+        in_specs=[VMEM],
+        out_specs=VMEM,
+        out_shape=shape((fin, nodes)),
+        compiler_params=params(4),
+        name="pick",
+    )(first)
+    forwarded = send(picked, FORWARD)
     values, loaded = pl.pallas_call(
         load_kernel,
-        in_specs=[pl.BlockSpec(memory_space=pltpu.HBM), ANY],
+        in_specs=[pl.BlockSpec(memory_space=pltpu.HBM)] + [ANY] * 3,
         out_specs=[VMEM, VMEM],
         out_shape=[pltpu.VMEM(block_values.shape, BF), shape((8, 128), F32)],
         scratch_shapes=[pltpu.SemaphoreType.DMA((8,))],
@@ -249,15 +302,30 @@
             flops=0, bytes_accessed=2 * block_values.size * 2, transcendentals=0
         ),
         name="load",
-    )(pltpu.with_memory_space_constraint(block_values, pltpu.HBM), pair)
-
-    for piece in arrived:
-        piece, _ = lax.optimization_barrier((piece, loaded))
-        pieces += [piece, lax.ppermute(piece, "node", swap)]
+    )(
+        pltpu.with_memory_space_constraint(block_values, pltpu.HBM),
+        picked,
+        bias_rows,
+        block_cols,
+    )
+
+    def bundle(*parts):
+        return pl.pallas_call(
+            bundle_kernel,
+            in_specs=[ANY] + [VMEM] * len(parts),
+            out_specs=VMEM,
+            out_shape=shape((sum(part.ndim - 1 for part in parts), fin, nodes)),
+            compiler_params=params(8),
+            name="bundle",
+        )(loaded, *parts)
+
+    pieces += [first, lax.ppermute(first, "node", swap)]
+    pieces += [second, lax.ppermute(bundle(second), "node", swap)]
+    pieces += [third, forwarded, lax.ppermute(bundle(third, forwarded), "node", swap)]
 
     mixed = pl.pallas_call(
         mix_kernel,
-        in_specs=[SMEM, SMEM] + [VMEM] * 14,
+        in_specs=[SMEM, SMEM] + [VMEM] * 13,
         out_specs=VMEM,
         out_shape=shape((8, 16, 3 * width + 512)),
         scratch_shapes=[pltpu.VMEM((16, fin, nodes), BF)],
@@ -278,50 +346,57 @@
 
     grads = lax.all_to_all(dense, "feat", 0, 0, tiled=True)
 
-    activation, own, other = pl.pallas_call(
+    wide = nodes + 256
+    activation, own1, other1, own2, other2 = pl.pallas_call(
         spread_kernel,
         in_specs=[SMEM, SMEM] + [VMEM] * 2,
-        out_specs=[VMEM] * 3,
-        out_shape=[
-            shape((32, nodes)),
-            shape((8, 16, nodes + 256)),
-            shape((8, 16, nodes + 256)),
-        ],
+        out_specs=[VMEM] * 5,
+        out_shape=[shape((32, nodes))]
+        + [shape((5, 16, wide))] * 2
+        + [shape((3, 16, wide))] * 2,
         scratch_shapes=[pltpu.VMEM((17, fin, nodes), F32)],
         compiler_params=params(24),
         name="spread",
     )(block_cols, block_counts, values, grads)
 
-    other = lax.ppermute(other, "node", swap)
-    stay, alone, *shared = pl.pallas_call(
+    other1 = lax.ppermute(other1, "node", swap)
+    other2 = lax.ppermute(other2, "node", swap)
+    farthest, second, third = pl.pallas_call(
         pair_kernel,
         in_specs=[VMEM] * 2,
-        out_specs=[VMEM] * 5,
-        out_shape=[shape((16, nodes + 256))] * 2 + [shape((2, 16, nodes + 256))] * 3,
+        out_specs=[VMEM] * 3,
+        out_shape=[shape((16, wide))] + [shape((2, 16, wide))] * 2,
         compiler_params=params(16),
         name="pair",
-    )(own, other)
-    alone = lax.ppermute(alone, "node", node_pairs(*ALONE))
-    shared = [
-        lax.ppermute(piece, "node", shared_pairs(steps)) for piece, steps in zip(shared, SHARED)
-    ]
+    )(own1, other1)
+    forwarded = send(farthest, back(FORWARD))
+    second, third = send(second, back(SECOND)), send(third, back(THIRD))
+    first, stay = pl.pallas_call(
+        merge_kernel,
+        in_specs=[VMEM] * 3,
+        out_specs=[VMEM] * 2,
+        out_shape=[shape((2, 16, wide)), shape((16, wide))],
+        compiler_params=params(16),
+        name="merge",
+    )(own2, other2, forwarded)
+    first = send(first, back(FIRST))
     handed = pl.pallas_call(
         hand_kernel,
         in_specs=[VMEM] * 3,
         out_specs=VMEM,
-        out_shape=shape((16, nodes + 256)),
+        out_shape=shape((16, wide)),
         compiler_params=params(16),
         name="hand",
-    )(*shared)
+    )(first, second, third)
     handed = lax.ppermute(handed, "node", swap)
     grad_features, grad_weight = pl.pallas_call(
         last_kernel,
-        in_specs=[VMEM] * 6,
+        in_specs=[VMEM] * 5,
         out_specs=[VMEM] * 2,
         out_shape=[shape((16, nodes)), shape((16, 256), F32)],
         compiler_params=params(16),
         name="last",
-    )(stay, alone, handed, *shared)
+    )(stay, handed, first, second, third)
     return activation, grad_features, grad_weight
 
 

time: 109 us -> 105 us (0.963)
  waiting for transfers between devices: 32.7 us -> 24.2 us
  starting transfers between devices: 22 us -> 27.8 us
  Pallas kernels: 22.8 us -> 20.9 us
    ppermute x13, waiting for transfers between devices: 29.9 us -> 21.5 us  [the longest x8 17.1 us: send(): return lax.ppermute(piece, 'node', shared_pairs(steps))]
    ppermute x13, starting transfers between devices: 20.4 us -> 26.2 us  [the longest x8 21.8 us: send(): return lax.ppermute(piece, 'node', shared_pairs(steps))]
    pallas_call x3 -> x7, Pallas kernels: 5.72 us -> 5.38 us  [the longest x1 4.05 us: local(): pl.pallas_call(mix_kernel, in_specs=[SMEM, SMEM] + [VMEM] * 13, out_specs...]
  transfers between devices with their start and end apart: 15 -> 15, of which waited for: 9 -> 10; matrix products, arithmetic and copies ran while one was open for 2% -> 2% of each run, Pallas kernels for 7% -> 7%
where the time goes in v6:
time: 105 us
  blocking collectives  28.4 us (27%)
  starting transfers between devices  27.8 us (26%)
  waiting for transfers between devices  24.2 us (23%)
  Pallas kernels  20.9 us (20%)
  local copies, waits for them, and re-layouts  2.61 us (2%)
    ppermute x8, starting transfers between devices, send(): return lax.ppermute(piece, 'node', shared_pairs(steps))  21.8 us
    ppermute x8, waiting for transfers between devices, send(): return lax.ppermute(piece, 'node', shared_pairs(steps))  17.1 us
    all_to_all x1, blocking collectives, local(): both = lax.all_to_all(mixed, 'feat', 0, 0, tiled=True)  16.1 us
    all_to_all x1, blocking collectives, local(): grads = lax.all_to_all(dense, 'feat', 0, 0, tiled=True)  12.3 us
    pallas_call x1, Pallas kernels, local(): pl.pallas_call(spread_kernel, in_specs=[SMEM, SMEM] + [VMEM] * 2, out_spe...  7.37 us
    pallas_call x1, Pallas kernels, local(): pl.pallas_call(load_kernel, in_specs=[pl.BlockSpec(memory_space=pltpu.HBM...  6.56 us
    pallas_call x1, Pallas kernels, local(): pl.pallas_call(mix_kernel, in_specs=[SMEM, SMEM] + [VMEM] * 13, out_specs...  4.05 us
    ppermute x1, starting transfers between devices, local(): other1 = lax.ppermute(other1, 'node', swap)  3.02 us
  transfers between devices with their start and end apart: 15, of which 10 were waited for; matrix products, arithmetic and copies ran while one was open for 2% of the time, Pallas kernels for 7%

profile of v6, /device:TPU:1, one launch (start us, length us, event | category | flops | bytes accessed | tf_op | source)
XLA Modules:
  0.0 104.7 jit_solution(13130908725300649896)
XLA Ops:
  0.6 1.5 %collective-permute-start = (bf16[16,6144]{1,0:T(8,128)(2,1)}, bf16[16,6144]{1,0:T(8,128)(2,1)S(1)}, u32[]{:S(2)}, u32[]{:S(2)}) collective-permute-start(bf16[16,6144]{1,0:T(8,128)(2,1)} %rest_0_.1), channel_id=1, source_target_pairs={{0,8},{8,0},{16,24},{24,16},{32,40},{40,32},{48,56},{56,48},{64,72... | collective-permute-start | bytes 589832 | tf_op jit(solution)/shard_map/ppermute | solution.py:272
  2.1 1.3 %collective-permute-done.second.rest_1_ = bf16[16,6144]{1,0:T(8,128)(2,1)S(1)} collective-permute-done((bf16[16,6144]{1,0:T(8,128)(2,1)}, bf16[16,6144]{1,0:T(8,128)(2,1)S(1)}, u32[]{:S(2)}, u32[]{:S(2)}) %collective-permute-start) | collective-permute-done | bytes 196640 | tf_op jit(solution)/shard_map/ppermute | solution.py:272
  3.4 0.9 copy-done.2
  5.1 2.8 %collective-permute-start.1 = (bf16[2,16,6144]{2,1,0:T(8,128)(2,1)}, bf16[2,16,6144]{2,1,0:T(8,128)(2,1)S(1)}, u32[]{:S(2)}, u32[]{:S(2)}) collective-permute-start(bf16[2,16,6144]{2,1,0:T(8,128)(2,1)} %stack.1), channel_id=1, source_target_pairs={{0,32},{8,72},{16,48},{24,88},{32,0},{40,104},{48,16},{56,120},{64... | collective-permute-start | bytes 1179656 | tf_op jit(solution)/shard_map/ppermute | solution.py:282
  8.0 0.8 copy.13.rest_2_.cols
  9.6 3.8 %collective-permute-start.5 = (bf16[2,16,6144]{2,1,0:T(8,128)(2,1)}, bf16[2,16,6144]{2,1,0:T(8,128)(2,1)S(1)}, u32[]{:S(2)}, u32[]{:S(2)}) collective-permute-start(bf16[2,16,6144]{2,1,0:T(8,128)(2,1)} %stack.1), channel_id=1, source_target_pairs={{0,16},{8,56},{16,32},{24,8},{32,48},{40,24},{48,0},{56,40},{64,80... | collective-permute-start | bytes 1179656 | tf_op jit(solution)/shard_map/ppermute | solution.py:282
  13.8 3.5 %collective-permute-start.6 = (bf16[16,6144]{1,0:T(8,128)(2,1)S(1)}, bf16[16,6144]{1,0:T(8,128)(2,1)S(1)}, u32[]{:S(2)}, u32[]{:S(2)}) collective-permute-start(bf16[16,6144]{1,0:T(8,128)(2,1)S(1)} %pick.1.rest_0_), channel_id=1, source_target_pairs={{0,64},{8,40},{16,80},{24,56},{32,96},{40,8},{48,112},{56,24},{64,... | collective-permute-start | bytes 589832 | tf_op jit(solution)/shard_map/ppermute | solution.py:282
  17.4 6.6 %load.1 = (bf16[48,12,128,128]{3,2,1,0:T(8,128)(2,1)S(1)}, f32[8,128]{1,0:T(8,128)S(1)}) custom-call(bf16[48,12,128,128]{3,2,1,0:T(8,128)(2,1)} %values.1, bf16[16,6144]{1,0:T(8,128)(2,1)S(1)} %pick.1.rest_0_, bf16[16,256]{1,0:T(8,128)(2,1)S(1)} %maximum_maximum_fusion.rest_1_.bias_rows, s32[48,12]{1,0:T(8,128)S(1)} %copy.13.rest_2_.cols), custom_call_target="tpu_custom_call" | custom-call | bytes 37748736 | tf_op jit(solution)/shard_map/load/pallas_call | solution.py:294
  23.9 3.0 %collective-permute-done.5.refs_0_.rest_6_ = bf16[2,16,6144]{2,1,0:T(8,128)(2,1)S(1)} collective-permute-done((bf16[2,16,6144]{2,1,0:T(8,128)(2,1)}, bf16[2,16,6144]{2,1,0:T(8,128)(2,1)S(1)}, u32[]{:S(2)}, u32[]{:S(2)}) %collective-permute-start.5) | collective-permute-done | bytes 393248 | tf_op jit(solution)/shard_map/ppermute | solution.py:282
  28.3 1.6 %collective-permute-done.2.rest_3_ = bf16[2,16,6144]{2,1,0:T(8,128)(2,1)S(1)} collective-permute-done((bf16[2,16,6144]{2,1,0:T(8,128)(2,1)S(1)}, bf16[2,16,6144]{2,1,0:T(8,128)(2,1)S(1)}, u32[]{:S(2)}, u32[]{:S(2)}) %collective-permute-start.2) | collective-permute-done | bytes 393248 | tf_op jit(solution)/shard_map/ppermute | solution.py:322
  30.5 4.1 %mix.1 = bf16[8,16,2816]{2,1,0:T(8,128)(2,1)S(1)} custom-call(s32[48,12]{1,0:T(8,128)S(1)} %copy.13.rest_2_.cols, s32[48]{0:T(128)S(1)} %copy-done.9, bf16[48,12,128,128]{3,2,1,0:T(8,128)(2,1)S(1)} %get-tuple-element.17.values, bf16[32,6144]{1,0:T(8,128)(2,1)S(1)} %copy-done.6, bf16[16,256]{1,0:T(8,128)(2,1)S(1)} %copy-done.8, ...), custom_call_target="tpu_custom_call" | custom-call | tf_op jit(solution)/shard_map/mix/pallas_call | solution.py:326
  34.6 16.1 %all_to_all.10.both = bf16[8,16,2816]{2,1,0:T(8,128)(2,1)S(1)} all-to-all(bf16[8,16,2816]{2,1,0:T(8,128)(2,1)S(1)} %mix.1), channel_id=1, replica_groups=mesh['node'=16,'feat'=8] {'feat'}, dimensions={0} | all-to-all | bytes 1441792 | tf_op jit(solution)/shard_map/all_to_all | solution.py:336
  51.4 12.3 %all_to_all.11.grads = bf16[8,16,2560]{2,1,0:T(8,128)(2,1)S(1)} all-to-all(bf16[8,16,2560]{2,1,0:T(8,128)(2,1)S(1)} %dense.1), channel_id=1, replica_groups=mesh['node'=16,'feat'=8] {'feat'}, dimensions={0} | all-to-all | bytes 1310720 | tf_op jit(solution)/shard_map/all_to_all | solution.py:347
  63.7 7.4 %spread.1 = (bf16[32,6144]{1,0:T(8,128)(2,1)}, bf16[5,16,6400]{2,1,0:T(8,128)(2,1)S(1)}, bf16[5,16,6400]{2,1,0:T(8,128)(2,1)S(1)}, bf16[3,16,6400]{2,1,0:T(8,128)(2,1)S(1)}, bf16[3,16,6400]{2,1,0:T(8,128)(2,1)S(1)}) custom-call(s32[48,12]{1,0:T(8,128)S(1)} %copy.13.rest_2_.cols, s32[48]{0:T(128)S(1)} %copy-done.9, ...), custom_call_target="tpu_custom_call" | custom-call | tf_op jit(solution)/shard_map/spread/pallas_call | solution.py:350
  71.1 3.0 %collective-permute-start.9 = (bf16[5,16,6400]{2,1,0:T(8,128)(2,1)S(1)}, bf16[5,16,6400]{2,1,0:T(8,128)(2,1)S(1)}, u32[]{:S(2)}, u32[]{:S(2)}) collective-permute-start(bf16[5,16,6400]{2,1,0:T(8,128)(2,1)S(1)} %get-tuple-element.23), channel_id=1, source_target_pairs={{0,8},{8,0},{16,24},{24,16},{32,40},{40,32},{48,56},{56,48},{64,72... | collective-permute-start | bytes 3072008 | tf_op jit(solution)/shard_map/ppermute | solution.py:362
  74.1 2.2 %collective-permute-done.9.other = bf16[5,16,6400]{2,1,0:T(8,128)(2,1)S(1)} collective-permute-done((bf16[5,16,6400]{2,1,0:T(8,128)(2,1)S(1)}, bf16[5,16,6400]{2,1,0:T(8,128)(2,1)S(1)}, u32[]{:S(2)}, u32[]{:S(2)}) %collective-permute-start.9) | collective-permute-done | bytes 1024032 | tf_op jit(solution)/shard_map/ppermute | solution.py:362
  76.6 1.5 %collective-permute-start.10 = (bf16[16,6400]{1,0:T(8,128)(2,1)S(1)}, bf16[16,6400]{1,0:T(8,128)(2,1)S(1)}, u32[]{:S(2)}, u32[]{:S(2)}) collective-permute-start(bf16[16,6400]{1,0:T(8,128)(2,1)S(1)} %get-tuple-element.24), channel_id=1, source_target_pairs={{0,64},{8,40},{16,80},{24,56},{32,96},{40,8},{48,112},{56,24},{64,... | collective-permute-start | bytes 614408 | tf_op jit(solution)/shard_map/ppermute | solution.py:282
  78.2 7.5 %collective-permute-start.12 = (bf16[2,16,6400]{2,1,0:T(8,128)(2,1)S(1)}, bf16[2,16,6400]{2,1,0:T(8,128)(2,1)S(1)}, u32[]{:S(2)}, u32[]{:S(2)}) collective-permute-start(bf16[2,16,6400]{2,1,0:T(8,128)(2,1)S(1)} %get-tuple-element.27), channel_id=1, source_target_pairs={{0,112},{8,88},{16,64},{24,104},{32,80},{40,120},{48,96},{56,72},{... | collective-permute-start | bytes 1228808 | tf_op jit(solution)/shard_map/ppermute | solution.py:282
  85.8 2.6 %collective-permute-start.11 = (bf16[2,16,6400]{2,1,0:T(8,128)(2,1)S(1)}, bf16[2,16,6400]{2,1,0:T(8,128)(2,1)S(1)}, u32[]{:S(2)}, u32[]{:S(2)}) collective-permute-start(bf16[2,16,6400]{2,1,0:T(8,128)(2,1)S(1)} %get-tuple-element.26), channel_id=1, source_target_pairs={{0,32},{8,72},{16,48},{24,88},{32,0},{40,104},{48,16},{56,120},{64... | collective-permute-start | bytes 1228808 | tf_op jit(solution)/shard_map/ppermute | solution.py:282
  88.5 3.3 %collective-permute-done.12.second = bf16[2,16,6400]{2,1,0:T(8,128)(2,1)S(1)} collective-permute-done((bf16[2,16,6400]{2,1,0:T(8,128)(2,1)S(1)}, bf16[2,16,6400]{2,1,0:T(8,128)(2,1)S(1)}, u32[]{:S(2)}, u32[]{:S(2)}) %collective-permute-start.12) | collective-permute-done | bytes 409632 | tf_op jit(solution)/shard_map/ppermute | solution.py:282
  91.7 5.0 %collective-permute-done.13.third = bf16[2,16,6400]{2,1,0:T(8,128)(2,1)S(1)} collective-permute-done((bf16[2,16,6400]{2,1,0:T(8,128)(2,1)S(1)}, bf16[2,16,6400]{2,1,0:T(8,128)(2,1)S(1)}, u32[]{:S(2)}, u32[]{:S(2)}) %collective-permute-start.13) | collective-permute-done | bytes 409632 | tf_op jit(solution)/shard_map/ppermute | solution.py:282
  96.7 5.6 %collective-permute-done.11.first = bf16[2,16,6400]{2,1,0:T(8,128)(2,1)S(1)} collective-permute-done((bf16[2,16,6400]{2,1,0:T(8,128)(2,1)S(1)}, bf16[2,16,6400]{2,1,0:T(8,128)(2,1)S(1)}, u32[]{:S(2)}, u32[]{:S(2)}) %collective-permute-start.11) | collective-permute-done | bytes 409632 | tf_op jit(solution)/shard_map/ppermute | solution.py:282
  102.5 1.4 %collective-permute-done.14.handed = bf16[16,6400]{1,0:T(8,128)(2,1)S(1)} collective-permute-done((bf16[16,6400]{1,0:T(8,128)(2,1)S(1)}, bf16[16,6400]{1,0:T(8,128)(2,1)S(1)}, u32[]{:S(2)}, u32[]{:S(2)}) %collective-permute-start.14) | collective-permute-done | bytes 204832 | tf_op jit(solution)/shard_map/ppermute | solution.py:391
  103.9 0.8 last.1
  (47 shorter events, 5.4 us)
Async XLA Ops:
  0.6 2.8 %collective-permute-start = (bf16[16,6144]{1,0:T(8,128)(2,1)}, bf16[16,6144]{1,0:T(8,128)(2,1)S(1)}, u32[]{:S(2)}, u32[]{:S(2)}) collective-permute-start(bf16[16,6144]{1,0:T(8,128)(2,1)} %rest_0_.1), channel_id=1, source_target_pairs={{0,8},{8,0},{16,24},{24,16},{32,40},{40,32},{48,56},{56,48},{64,72... | collective-permute-start | bytes 589832 | tf_op jit(solution)/shard_map/ppermute | solution.py:272
  3.4 0.9 copy-start.2
  4.3 26.1 %copy-start.8 = (bf16[16,256]{1,0:T(8,128)(2,1)S(1)}, bf16[16,256]{1,0:T(8,128)(2,1)}, u32[]{:S(2)}) copy-start(bf16[16,256]{1,0:T(8,128)(2,1)} %weight.1) | copy-start | bytes 24580
  4.3 26.1 %copy-start.9 = (s32[48]{0:T(128)S(1)}, s32[48]{0:T(128)}, u32[]{:S(2)}) copy-start(s32[48]{0:T(128)} %counts.3) | copy-start | bytes 580
  5.1 8.6 %collective-permute-start.1 = (bf16[2,16,6144]{2,1,0:T(8,128)(2,1)}, bf16[2,16,6144]{2,1,0:T(8,128)(2,1)S(1)}, u32[]{:S(2)}, u32[]{:S(2)}) collective-permute-start(bf16[2,16,6144]{2,1,0:T(8,128)(2,1)} %stack.1), channel_id=1, source_target_pairs={{0,32},{8,72},{16,48},{24,88},{32,0},{40,104},{48,16},{56,120},{64... | collective-permute-start | bytes 1179656 | tf_op jit(solution)/shard_map/ppermute | solution.py:282
  9.6 20.9 %copy-start.3 = (bf16[16,6144]{1,0:T(8,128)(2,1)S(1)}, bf16[16,6144]{1,0:T(8,128)(2,1)}, u32[]{:S(2)}) copy-start(bf16[16,6144]{1,0:T(8,128)(2,1)} %rest_0_.1) | copy-start | bytes 589828
  9.6 20.9 %copy-start.5 = (bf16[16,6144]{1,0:T(8,128)(2,1)S(1)}, bf16[16,6144]{1,0:T(8,128)(2,1)}, u32[]{:S(2)}) copy-start(bf16[16,6144]{1,0:T(8,128)(2,1)} %copy-done.4) | copy-start | bytes 589828
  9.6 20.9 %copy-start.6 = (bf16[32,6144]{1,0:T(8,128)(2,1)S(1)}, bf16[32,6144]{1,0:T(8,128)(2,1)}, u32[]{:S(2)}) copy-start(bf16[32,6144]{1,0:T(8,128)(2,1)} %cotangent.1) | copy-start | bytes 1179652
  9.6 17.3 %collective-permute-start.5 = (bf16[2,16,6144]{2,1,0:T(8,128)(2,1)}, bf16[2,16,6144]{2,1,0:T(8,128)(2,1)S(1)}, u32[]{:S(2)}, u32[]{:S(2)}) collective-permute-start(bf16[2,16,6144]{2,1,0:T(8,128)(2,1)} %stack.1), channel_id=1, source_target_pairs={{0,16},{8,56},{16,32},{24,8},{32,48},{40,24},{48,0},{56,40},{64,80... | collective-permute-start | bytes 1179656 | tf_op jit(solution)/shard_map/ppermute | solution.py:282
  13.5 14.4 %collective-permute-start.3 = (bf16[2,16,6144]{2,1,0:T(8,128)(2,1)}, bf16[2,16,6144]{2,1,0:T(8,128)(2,1)S(1)}, u32[]{:S(2)}, u32[]{:S(2)}) collective-permute-start(bf16[2,16,6144]{2,1,0:T(8,128)(2,1)} %stack.1), channel_id=1, source_target_pairs={{0,80},{8,120},{16,96},{24,72},{32,112},{40,88},{48,64},{56,104},{... | collective-permute-start | bytes 1179656 | tf_op jit(solution)/shard_map/ppermute | solution.py:282
  13.8 3.5 %copy-start = (bf16[2,16,6144]{2,1,0:T(8,128)(2,1)}, bf16[2,16,6144]{2,1,0:T(8,128)(2,1)S(1)}, u32[]{:S(2)}) copy-start(bf16[2,16,6144]{2,1,0:T(8,128)(2,1)S(1)} %collective-permute-done.1.pair.rest_2_) | copy-start | bytes 1179652
  13.8 13.1 %collective-permute-start.6 = (bf16[16,6144]{1,0:T(8,128)(2,1)S(1)}, bf16[16,6144]{1,0:T(8,128)(2,1)S(1)}, u32[]{:S(2)}, u32[]{:S(2)}) collective-permute-start(bf16[16,6144]{1,0:T(8,128)(2,1)S(1)} %pick.1.rest_0_), channel_id=1, source_target_pairs={{0,64},{8,40},{16,80},{24,56},{32,96},{40,8},{48,112},{56,24},{64,... | collective-permute-start | bytes 589832 | tf_op jit(solution)/shard_map/ppermute | solution.py:282
  17.3 10.4 %copy-start.1 = (bf16[2,16,6144]{2,1,0:T(8,128)(2,1)S(1)}, bf16[2,16,6144]{2,1,0:T(8,128)(2,1)}, u32[]{:S(2)}) copy-start(bf16[2,16,6144]{2,1,0:T(8,128)(2,1)} %copy-done) | copy-start | bytes 1179652
  17.3 33.3 %copy-start.7 = (s32[6144]{0:T(1024)S(1)}, s32[6144]{0:T(1024)}, u32[]{:S(2)}) copy-start(s32[6144]{0:T(1024)} %param.14) | copy-start | bytes 73732
  27.0 3.5 %collective-permute-start.7 = (bf16[3,16,6144]{2,1,0:T(8,128)(2,1)S(1)}, bf16[3,16,6144]{2,1,0:T(8,128)(2,1)S(1)}, u32[]{:S(2)}, u32[]{:S(2)}) collective-permute-start(bf16[3,16,6144]{2,1,0:T(8,128)(2,1)S(1)} %bundle.3), channel_id=1, source_target_pairs={{0,8},{8,0},{16,24},{24,16},{32,40},{40,32},{48,56},{56,48},{64,72... | collective-permute-start | bytes 1769480 | tf_op jit(solution)/shard_map/ppermute | solution.py:324
  27.7 2.2 %collective-permute-start.2 = (bf16[2,16,6144]{2,1,0:T(8,128)(2,1)S(1)}, bf16[2,16,6144]{2,1,0:T(8,128)(2,1)S(1)}, u32[]{:S(2)}, u32[]{:S(2)}) collective-permute-start(bf16[2,16,6144]{2,1,0:T(8,128)(2,1)S(1)} %copy-done.1), channel_id=1, source_target_pairs={{0,8},{8,0},{16,24},{24,16},{32,40},{40,32},{48,56},{56,48},{64,72... | collective-permute-start | bytes 1179656 | tf_op jit(solution)/shard_map/ppermute | solution.py:322
  27.9 2.6 %collective-permute-start.4 = (bf16[2,16,6144]{2,1,0:T(8,128)(2,1)S(1)}, bf16[2,16,6144]{2,1,0:T(8,128)(2,1)S(1)}, u32[]{:S(2)}, u32[]{:S(2)}) collective-permute-start(bf16[2,16,6144]{2,1,0:T(8,128)(2,1)S(1)} %bundle.2), channel_id=1, source_target_pairs={{0,8},{8,0},{16,24},{24,16},{32,40},{40,32},{48,56},{56,48},{64,72... | collective-permute-start | bytes 1179656 | tf_op jit(solution)/shard_map/ppermute | solution.py:323
  71.1 5.3 %collective-permute-start.9 = (bf16[5,16,6400]{2,1,0:T(8,128)(2,1)S(1)}, bf16[5,16,6400]{2,1,0:T(8,128)(2,1)S(1)}, u32[]{:S(2)}, u32[]{:S(2)}) collective-permute-start(bf16[5,16,6400]{2,1,0:T(8,128)(2,1)S(1)} %get-tuple-element.23), channel_id=1, source_target_pairs={{0,8},{8,0},{16,24},{24,16},{32,40},{40,32},{48,56},{56,48},{64,72... | collective-permute-start | bytes 3072008 | tf_op jit(solution)/shard_map/ppermute | solution.py:362
  74.1 11.5 %collective-permute-start.8 = (bf16[3,16,6400]{2,1,0:T(8,128)(2,1)S(1)}, bf16[3,16,6400]{2,1,0:T(8,128)(2,1)S(1)}, u32[]{:S(2)}, u32[]{:S(2)}) collective-permute-start(bf16[3,16,6400]{2,1,0:T(8,128)(2,1)S(1)} %get-tuple-element.21), channel_id=1, source_target_pairs={{0,8},{8,0},{16,24},{24,16},{32,40},{40,32},{48,56},{56,48},{64,72... | collective-permute-start | bytes 1843208 | tf_op jit(solution)/shard_map/ppermute | solution.py:363
  76.6 9.0 %collective-permute-start.10 = (bf16[16,6400]{1,0:T(8,128)(2,1)S(1)}, bf16[16,6400]{1,0:T(8,128)(2,1)S(1)}, u32[]{:S(2)}, u32[]{:S(2)}) collective-permute-start(bf16[16,6400]{1,0:T(8,128)(2,1)S(1)} %get-tuple-element.24), channel_id=1, source_target_pairs={{0,64},{8,40},{16,80},{24,56},{32,96},{40,8},{48,112},{56,24},{64,... | collective-permute-start | bytes 614408 | tf_op jit(solution)/shard_map/ppermute | solution.py:282
  78.2 13.6 %collective-permute-start.12 = (bf16[2,16,6400]{2,1,0:T(8,128)(2,1)S(1)}, bf16[2,16,6400]{2,1,0:T(8,128)(2,1)S(1)}, u32[]{:S(2)}, u32[]{:S(2)}) collective-permute-start(bf16[2,16,6400]{2,1,0:T(8,128)(2,1)S(1)} %get-tuple-element.27), channel_id=1, source_target_pairs={{0,112},{8,88},{16,64},{24,104},{32,80},{40,120},{48,96},{56,72},{... | collective-permute-start | bytes 1228808 | tf_op jit(solution)/shard_map/ppermute | solution.py:282
  85.6 11.1 %collective-permute-start.13 = (bf16[2,16,6400]{2,1,0:T(8,128)(2,1)S(1)}, bf16[2,16,6400]{2,1,0:T(8,128)(2,1)S(1)}, u32[]{:S(2)}, u32[]{:S(2)}) collective-permute-start(bf16[2,16,6400]{2,1,0:T(8,128)(2,1)S(1)} %get-tuple-element.28), channel_id=1, source_target_pairs={{0,48},{8,24},{16,0},{24,40},{32,16},{40,56},{48,32},{56,8},{64,11... | collective-permute-start | bytes 1228808 | tf_op jit(solution)/shard_map/ppermute | solution.py:282
  85.8 16.5 %collective-permute-start.11 = (bf16[2,16,6400]{2,1,0:T(8,128)(2,1)S(1)}, bf16[2,16,6400]{2,1,0:T(8,128)(2,1)S(1)}, u32[]{:S(2)}, u32[]{:S(2)}) collective-permute-start(bf16[2,16,6400]{2,1,0:T(8,128)(2,1)S(1)} %get-tuple-element.26), channel_id=1, source_target_pairs={{0,32},{8,72},{16,48},{24,88},{32,0},{40,104},{48,16},{56,120},{64... | collective-permute-start | bytes 1228808 | tf_op jit(solution)/shard_map/ppermute | solution.py:282
  102.4 1.5 %collective-permute-start.14 = (bf16[16,6400]{1,0:T(8,128)(2,1)S(1)}, bf16[16,6400]{1,0:T(8,128)(2,1)S(1)}, u32[]{:S(2)}, u32[]{:S(2)}) collective-permute-start(bf16[16,6400]{1,0:T(8,128)(2,1)S(1)} %hand.1), channel_id=1, source_target_pairs={{0,8},{8,0},{16,24},{24,16},{32,40},{40,32},{48,56},{56,48},{64,72... | collective-permute-start | bytes 614408 | tf_op jit(solution)/shard_map/ppermute | solution.py:391
  (1 other events, 0.8 us)

commit v7 on v2

--- a/solution.py
+++ b/solution.py
@@ -1,3 +1,5 @@
+import functools
+
 import jax
 import jax.numpy as jnp
 from jax import lax
@@ -11,6 +13,9 @@
 SMEM = pl.BlockSpec(memory_space=pltpu.SMEM)
 VMEM = pl.BlockSpec(memory_space=pltpu.VMEM)
 STEPS = ((1, 2), (1, 1), (1, 3), (0, 2), (1, 0), (0, 1), (0, 3))
+NEAREST = ((0, 1), (0, 3), (0, 2), (1, 0), (1, 1), (1, 3), (1, 2))
+HAND_OVERS = ((0, 3), (3, 5), (5, 8))
+EARLY_SUM = 3
 BLOCK = 128
 
 
@@ -42,9 +47,16 @@
     return pltpu.CompilerParams(vmem_limit_bytes=mib * 2**20)
 
 
-def load_kernel(values, _, out, sems):
+def bundle_kernel(_, *refs):
+    pieces, out = refs[:-1], refs[-1]
+    for at, piece in enumerate(pieces):
+        out[at] = piece[...]
+
+
+def load_kernel(values, *rest):
+    out, loaded, sems = rest[-3:]
     count = sems.shape[0]
-    rows = values.shape[0] // count
+    rows = out.shape[0] // count
     copies = [
         pltpu.make_async_copy(
             values.at[pl.ds(i * rows, rows)], out.at[pl.ds(i * rows, rows)], sems.at[i]
@@ -55,34 +67,29 @@
         copy.start()
     for copy in copies:
         copy.wait()
+    loaded[...] = jnp.zeros_like(loaded)
 
 
 def mix_kernel(cols, counts, values, cotangent, weight, bias_rows, *rest):
-    pieces, (out, held, sems) = rest[:16], rest[16:]
+    pieces, bundles, (out, held) = rest[:8], rest[8:11], rest[11:]
     slots = values.shape[1]
     chunks, _, _ = out.shape
     width = cotangent.shape[1] // chunks
     rows = values.shape[0] // chunks
 
-    copies = []
-    for k, (dx, dz) in enumerate(((0, 0),) + STEPS):
-        for core in range(2):
-            at = 2 * k + core
-            copies.append(
-                pltpu.make_async_copy(pieces[at], held.at[node_near(dx, -dz, core)], sems.at[at])
-            )
-    for copy in copies:
-        copy.start()
+    for at, (dx, dz) in enumerate(((0, 0),) + NEAREST):
+        held[node_near(dx, -dz, 0)] = pieces[at][...]
+    for bundle, (start, end) in zip(bundles, HAND_OVERS):
+        for at in range(start, end):
+            dx, dz = (((0, 0),) + NEAREST)[at]
+            held[node_near(dx, -dz, 1)] = bundle[at - start]
     for j in range(chunks):
         out[j, :, width : 2 * width] = cotangent[:16, j * width : (j + 1) * width]
         out[j, :, 2 * width : 3 * width] = cotangent[16:, j * width : (j + 1) * width]
         out[j, :, 3 * width : 3 * width + 256] = weight[...]
         out[j, :, 3 * width + 256 :] = bias_rows[...]
-    for copy in copies:
-        copy.wait()
-
-    @pl.loop(0, chunks)
-    def _(j):
+
+    for j in range(chunks):
         for i in range(rows):
             r = j * rows + i
             count = counts[r]
@@ -128,7 +135,9 @@
     out[:, :, 2 * width + 256 :] = activation[:, 16:]
 
 
-def spread_kernel(cols, counts, values, grads, activation, own, other, total):
+def spread_kernel(
+    cols, counts, values, grads, activation, own1, other1, own2, other2, total
+):
     slots = values.shape[1]
     chunks = grads.shape[0]
     rows = values.shape[0] // chunks
@@ -143,8 +152,7 @@
         activation[16:, at] = grads[j, :, 2 * width + 256 :]
         weight_part += grads[j, :, width : width + 256].astype(F32)
 
-    @pl.loop(0, chunks)
-    def _(j):
+    for j in range(chunks):
         for i in range(rows):
             r = j * rows + i
             count = counts[r]
@@ -160,15 +168,28 @@
                 total[group, :, pl.ds(lane, BLOCK)] += contrib[:, s * BLOCK : (s + 1) * BLOCK]
 
     weight_part = weight_part.astype(BF)
-    for k, (dx, dz) in enumerate(((0, 0),) + STEPS):
-        for core, to in enumerate((own, other)):
-            to[k, :, :nodes] = total[node_near(dx, dz, core)].astype(BF)
-            to[k, :, nodes:] = weight_part
+    for server, to1, to2 in ((0, own1, own2), (1, other1, other2)):
+        nears = [node_near(dx, dz, server) for dx, dz in STEPS + ((0, 0),)]
+        nears1, nears2 = nears[:EARLY_SUM], nears[EARLY_SUM:]
+        for to, nears in ((to1, nears1), (to2, nears2)):
+            for k, near in enumerate(nears):
+                to[k, :, :nodes] = total[near].astype(BF)
+                to[k, :, nodes:] = weight_part
 
 
 def pair_kernel(own, other, *outs):
     for k, out in enumerate(outs):
         out[...] = (own[k].astype(F32) + other[k].astype(F32)).astype(BF)
+
+
+def last_kernel(*refs):
+    pieces, grad_features, grad_weight = refs[:8], refs[8], refs[9]
+    total = pieces[0][...].astype(F32)
+    for piece in pieces[1:]:
+        total += piece[...].astype(F32)
+    nodes = grad_features.shape[1]
+    grad_features[...] = total[:, :nodes].astype(BF)
+    grad_weight[...] = total[:, nodes:]
 
 
 def local(features, weight, bias, block_values, block_cols, block_counts, train_mask, cotangent):
@@ -187,33 +208,49 @@
         [high, middle, bias_at - high - middle, jnp.zeros((13, 256), F32)], axis=0
     ).astype(BF)
 
-    pieces = [features, lax.ppermute(features, "node", node_pairs(0, 0, 1))]
-    for dx, dz in STEPS:
-        piece = lax.ppermute(features, "node", node_pairs(dx, dz))
-        pieces += [piece, lax.ppermute(piece, "node", node_pairs(0, 0, 1))]
-
-    values = pl.pallas_call(
+    swap = node_pairs(0, 0, 1)
+    pieces = [features]
+    pieces += [lax.ppermute(features, "node", node_pairs(*step)) for step in NEAREST]
+
+    values, loaded = pl.pallas_call(
         load_kernel,
-        in_specs=[ANY, ANY],
-        out_specs=VMEM,
-        out_shape=pltpu.VMEM(block_values.shape, BF),
+        in_specs=[pl.BlockSpec(memory_space=pltpu.HBM)] + [ANY] * 4,
+        out_specs=[VMEM, VMEM],
+        out_shape=[pltpu.VMEM(block_values.shape, BF), shape((8, 128), F32)],
         scratch_shapes=[pltpu.SemaphoreType.DMA((8,))],
         compiler_params=params(4),
         cost_estimate=pl.CostEstimate(
             flops=0, bytes_accessed=2 * block_values.size * 2, transcendentals=0
         ),
         name="load",
-    )(block_values, pieces[1])
+    )(
+        pltpu.with_memory_space_constraint(block_values, pltpu.HBM),
+        *pieces[1:3],
+        bias_rows,
+        block_cols,
+    )
+
+    bundles = []
+    for start, end in HAND_OVERS:
+        bundle = pl.pallas_call(
+            bundle_kernel,
+            in_specs=[ANY] + [VMEM] * (end - start),
+            out_specs=VMEM,
+            out_shape=shape((end - start, fin, nodes)),
+            compiler_params=params(8),
+            name="bundle",
+        )(loaded if start > 0 else pieces[1], *pieces[start:end])
+        bundles.append(lax.ppermute(bundle, "node", swap))
 
     mixed = pl.pallas_call(
         mix_kernel,
-        in_specs=[SMEM, SMEM] + [VMEM] * 4 + [ANY] * 16,
+        in_specs=[SMEM, SMEM] + [VMEM] * 15,
         out_specs=VMEM,
         out_shape=shape((8, 16, 3 * width + 512)),
-        scratch_shapes=[pltpu.VMEM((16, fin, nodes), BF), pltpu.SemaphoreType.DMA((16,))],
+        scratch_shapes=[pltpu.VMEM((16, fin, nodes), BF)],
         compiler_params=params(16),
         name="mix",
-    )(block_cols, block_counts, values, cotangent, weight, bias_rows, *pieces)
+    )(block_cols, block_counts, values, cotangent, weight, bias_rows, *pieces, *bundles)
 
     both = lax.all_to_all(mixed, "feat", 0, 0, tiled=True)
 
@@ -228,34 +265,39 @@
 
     grads = lax.all_to_all(dense, "feat", 0, 0, tiled=True)
 
-    activation, own, other = pl.pallas_call(
+    wide = nodes + 256
+    counts = (EARLY_SUM, 8 - EARLY_SUM)
+    activation, own1, other1, own2, other2 = pl.pallas_call(
         spread_kernel,
         in_specs=[SMEM, SMEM] + [VMEM] * 2,
-        out_specs=[VMEM] * 3,
-        out_shape=[
-            shape((32, nodes)),
-            shape((8, 16, nodes + 256)),
-            shape((8, 16, nodes + 256)),
-        ],
+        out_specs=[VMEM] * 5,
+        out_shape=[shape((32, nodes))]
+        + [shape((count, 16, wide)) for count in counts for _ in range(2)],
         scratch_shapes=[pltpu.VMEM((17, fin, nodes), F32)],
         compiler_params=params(24),
         name="spread",
     )(block_cols, block_counts, values, grads)
 
-    other = lax.ppermute(other, "node", node_pairs(0, 0, 1))
-    sums = pl.pallas_call(
-        pair_kernel,
-        in_specs=[VMEM] * 2,
-        out_specs=[VMEM] * 8,
-        out_shape=[shape((16, nodes + 256))] * 8,
+    sums = []
+    for own, other in ((own1, other1), (own2, other2)):
+        sums += pl.pallas_call(
+            pair_kernel,
+            in_specs=[VMEM] * 2,
+            out_specs=[VMEM] * own.shape[0],
+            out_shape=[shape((16, wide))] * own.shape[0],
+            compiler_params=params(16),
+            name="pair",
+        )(own, lax.ppermute(other, "node", swap))
+    landed = [lax.ppermute(part, "node", node_pairs(*step)) for part, step in zip(sums, STEPS)]
+    grad_features, grad_weight = pl.pallas_call(
+        last_kernel,
+        in_specs=[VMEM] * 8,
+        out_specs=[VMEM] * 2,
+        out_shape=[shape((16, nodes)), shape((16, 256), F32)],
         compiler_params=params(16),
-        name="pair",
-    )(own, other)
-    landed = [sums[0]]
-    for (dx, dz), piece in zip(STEPS, sums[1:]):
-        landed.append(lax.ppermute(piece, "node", node_pairs(dx, dz)))
-    total = sum(piece.astype(F32) for piece in landed)
-    return activation, total[:, :nodes].astype(BF), total[:, nodes:]
+        name="last",
+    )(sums[-1], *landed)
+    return activation, grad_features, grad_weight
 
 
 def solution(mesh):

time: 118 us -> 117 us (level)
  waiting for transfers between devices: 20.7 us -> 25.8 us
  starting transfers between devices: 36.8 us -> 32.2 us
  local copies, waits for them, and re-layouts: 10.7 us -> 7.65 us
  Pallas kernels: 19.5 us -> 21.4 us
    ppermute x23 -> x19, waiting for transfers between devices: 20.7 us -> 25.8 us  [the longest x7 13.3 us: local(): lax.ppermute(part, 'node', node_pairs(*step))]
    ppermute x23 -> x19, starting transfers between devices: 36.8 us -> 32.2 us  [the longest x7 16.2 us: local(): lax.ppermute(features, 'node', node_pairs(*step))]
    pallas_call x3 -> x8, Pallas kernels: 10.4 us -> 13.2 us  [the longest x1 6.52 us: local(): pl.pallas_call(load_kernel, in_specs=[pl.BlockSpec(memory_space=pltpu.HBM...]
    unnamed x21 -> x25, local copies, waits for them, and re-layouts: 8.53 us -> 6.81 us
    slice x2 -> x0, local copies, waits for them, and re-layouts: 1.3 us -> none  [local(): return (activation, total[:, :nodes].astype(BF), total[:, nodes:])]
  transfers between devices with their start and end apart: 23 -> 19, of which waited for: 9 -> 8; matrix products, arithmetic and copies ran while one was open for 1% -> 1% of each run, Pallas kernels for 1% -> 7%
where the time goes in v7:
time: 117 us
  starting transfers between devices  32.2 us (28%)
  blocking collectives  29.2 us (25%)
  waiting for transfers between devices  25.8 us (22%)
  Pallas kernels  21.4 us (18%)
  local copies, waits for them, and re-layouts  7.65 us (7%)
    ppermute x7, starting transfers between devices, local(): lax.ppermute(features, 'node', node_pairs(*step))  16.2 us
    all_to_all x1, blocking collectives, local(): both = lax.all_to_all(mixed, 'feat', 0, 0, tiled=True)  15 us
    all_to_all x1, blocking collectives, local(): grads = lax.all_to_all(dense, 'feat', 0, 0, tiled=True)  14.1 us
    ppermute x7, waiting for transfers between devices, local(): lax.ppermute(part, 'node', node_pairs(*step))  13.3 us
    ppermute x7, starting transfers between devices, local(): lax.ppermute(part, 'node', node_pairs(*step))  12.1 us
    ppermute x7, waiting for transfers between devices, local(): lax.ppermute(features, 'node', node_pairs(*step))  7.46 us
    pallas_call x1, Pallas kernels, local(): pl.pallas_call(spread_kernel, in_specs=[SMEM, SMEM] + [VMEM] * 2, out_spe...  7.37 us
    unnamed x25, local copies, waits for them, and re-layouts  6.81 us
  transfers between devices with their start and end apart: 19, of which 8 were waited for; matrix products, arithmetic and copies ran while one was open for 1% of the time, Pallas kernels for 7%

profile of v7, /device:TPU:1, one launch (start us, length us, event | category | flops | bytes accessed | tf_op | source)
XLA Modules:
  0.0 117.1 jit_solution(16669083461043534347)
XLA Ops:
  0.7 7.0 %collective-permute-start.6 = (bf16[16,6144]{1,0:T(8,128)(2,1)}, bf16[16,6144]{1,0:T(8,128)(2,1)}, u32[]{:S(2)}, u32[]{:S(2)}) collective-permute-start(bf16[16,6144]{1,0:T(8,128)(2,1)} %rest_0_.1), channel_id=1, source_target_pairs={{0,96},{8,104},{16,112},{24,120},{32,64},{40,72},{48,80},{56,88},{... | collective-permute-start | bytes 589832 | tf_op jit(solution)/shard_map/ppermute | solution.py:213
  8.0 3.5 %collective-permute-start.4 = (bf16[16,6144]{1,0:T(8,128)(2,1)}, bf16[16,6144]{1,0:T(8,128)(2,1)}, u32[]{:S(2)}, u32[]{:S(2)}) collective-permute-start(bf16[16,6144]{1,0:T(8,128)(2,1)} %rest_0_.1), channel_id=1, source_target_pairs={{0,80},{8,88},{16,96},{24,104},{32,112},{40,120},{48,64},{56,72},{... | collective-permute-start | bytes 589832 | tf_op jit(solution)/shard_map/ppermute | solution.py:213
  11.5 1.6 %collective-permute-start.1 = (bf16[16,6144]{1,0:T(8,128)(2,1)}, bf16[16,6144]{1,0:T(8,128)(2,1)S(1)}, u32[]{:S(2)}, u32[]{:S(2)}) collective-permute-start(bf16[16,6144]{1,0:T(8,128)(2,1)} %rest_0_.1), channel_id=1, source_target_pairs={{0,48},{8,56},{16,0},{24,8},{32,16},{40,24},{48,32},{56,40},{64,11... | collective-permute-start | bytes 589832 | tf_op jit(solution)/shard_map/ppermute | solution.py:213
  14.8 7.4 %collective-permute-done.1.rest_1_.refs_2_.rest_2_ = bf16[16,6144]{1,0:T(8,128)(2,1)S(1)} collective-permute-done((bf16[16,6144]{1,0:T(8,128)(2,1)}, bf16[16,6144]{1,0:T(8,128)(2,1)S(1)}, u32[]{:S(2)}, u32[]{:S(2)}) %collective-permute-start.1) | collective-permute-done | bytes 196640 | tf_op jit(solution)/shard_map/ppermute | solution.py:213
  22.3 2.8 %collective-permute-start.3 = (bf16[16,6144]{1,0:T(8,128)(2,1)}, bf16[16,6144]{1,0:T(8,128)(2,1)S(1)}, u32[]{:S(2)}, u32[]{:S(2)}) collective-permute-start(bf16[16,6144]{1,0:T(8,128)(2,1)} %rest_0_.1), channel_id=1, source_target_pairs={{0,64},{8,72},{16,80},{24,88},{32,96},{40,104},{48,112},{56,120},{... | collective-permute-start | bytes 589832 | tf_op jit(solution)/shard_map/ppermute | solution.py:213
  30.2 6.5 %load.1 = (bf16[48,12,128,128]{3,2,1,0:T(8,128)(2,1)S(1)}, f32[8,128]{1,0:T(8,128)S(1)}) custom-call(bf16[48,12,128,128]{3,2,1,0:T(8,128)(2,1)} %values.1, bf16[16,6144]{1,0:T(8,128)(2,1)S(1)} %copy-done.1, bf16[16,6144]{1,0:T(8,128)(2,1)S(1)} %copy-done.4, bf16[16,256]{1,0:T(8,128)(2,1)S(1)} %maximum_maximum_fusion.rest_2_.bias_rows, ...), custom_call_target="tpu_custom_call" | custom-call | bytes 37748736 | tf_op jit(solution)/shard_map/load/pallas_call | solution.py:215
  36.7 1.2 %collective-permute-start.7 = (bf16[3,16,6144]{2,1,0:T(8,128)(2,1)S(1)}, bf16[3,16,6144]{2,1,0:T(8,128)(2,1)S(1)}, u32[]{:S(2)}, u32[]{:S(2)}) collective-permute-start(bf16[3,16,6144]{2,1,0:T(8,128)(2,1)S(1)} %bundle.3), channel_id=1, source_target_pairs={{0,8},{8,0},{16,24},{24,16},{32,40},{40,32},{48,56},{56,48},{64,72... | collective-permute-start | bytes 1769480 | tf_op jit(solution)/shard_map/ppermute | solution.py:243
  37.9 1.2 bundle.5
  39.8 1.9 %collective-permute-done.8.rest_9_ = bf16[2,16,6144]{2,1,0:T(8,128)(2,1)S(1)} collective-permute-done((bf16[2,16,6144]{2,1,0:T(8,128)(2,1)S(1)}, bf16[2,16,6144]{2,1,0:T(8,128)(2,1)S(1)}, u32[]{:S(2)}, u32[]{:S(2)}) %collective-permute-start.8) | collective-permute-done | bytes 393248 | tf_op jit(solution)/shard_map/ppermute | solution.py:243
  43.7 4.2 %mix.1 = bf16[8,16,2816]{2,1,0:T(8,128)(2,1)S(1)} custom-call(s32[48,12]{1,0:T(8,128)S(1)} %copy.13.rest_3_.cols, s32[48]{0:T(128)S(1)} %copy-done.11, bf16[48,12,128,128]{3,2,1,0:T(8,128)(2,1)S(1)} %get-tuple-element.20.values, bf16[32,6144]{1,0:T(8,128)(2,1)S(1)} %copy-done.8, bf16[16,256]{1,0:T(8,128)(2,1)S(1)} %copy-done.10, ...), custom_call_target="tpu_custom_call" | custom-call | tf_op jit(solution)/shard_map/mix/pallas_call | solution.py:245
  47.9 15.0 %all_to_all.10.both = bf16[8,16,2816]{2,1,0:T(8,128)(2,1)S(1)} all-to-all(bf16[8,16,2816]{2,1,0:T(8,128)(2,1)S(1)} %mix.1), channel_id=1, replica_groups=mesh['node'=16,'feat'=8] {'feat'}, dimensions={0} | all-to-all | bytes 1441792 | tf_op jit(solution)/shard_map/all_to_all | solution.py:255
  63.7 14.1 %all_to_all.11.grads = bf16[8,16,2560]{2,1,0:T(8,128)(2,1)S(1)} all-to-all(bf16[8,16,2560]{2,1,0:T(8,128)(2,1)S(1)} %dense.1), channel_id=1, replica_groups=mesh['node'=16,'feat'=8] {'feat'}, dimensions={0} | all-to-all | bytes 1310720 | tf_op jit(solution)/shard_map/all_to_all | solution.py:266
  77.8 7.4 %spread.1 = (bf16[32,6144]{1,0:T(8,128)(2,1)}, bf16[3,16,6400]{2,1,0:T(8,128)(2,1)S(1)}, bf16[3,16,6400]{2,1,0:T(8,128)(2,1)S(1)}, bf16[5,16,6400]{2,1,0:T(8,128)(2,1)S(1)}, bf16[5,16,6400]{2,1,0:T(8,128)(2,1)S(1)}) custom-call(s32[48,12]{1,0:T(8,128)S(1)} %copy.13.rest_3_.cols, s32[48]{0:T(128)S(1)} %copy-done.11, ...), custom_call_target="tpu_custom_call" | custom-call | tf_op jit(solution)/shard_map/spread/pallas_call | solution.py:270
  85.1 2.1 %collective-permute-start.10 = (bf16[5,16,6400]{2,1,0:T(8,128)(2,1)S(1)}, bf16[5,16,6400]{2,1,0:T(8,128)(2,1)S(1)}, u32[]{:S(2)}, u32[]{:S(2)}) collective-permute-start(bf16[5,16,6400]{2,1,0:T(8,128)(2,1)S(1)} %get-tuple-element.24), channel_id=1, source_target_pairs={{0,8},{8,0},{16,24},{24,16},{32,40},{40,32},{48,56},{56,48},{64,72... | collective-permute-start | bytes 3072008 | tf_op jit(solution)/shard_map/ppermute | solution.py:290
  87.3 3.1 %collective-permute-done.11.other = bf16[3,16,6400]{2,1,0:T(8,128)(2,1)S(1)} collective-permute-done((bf16[3,16,6400]{2,1,0:T(8,128)(2,1)S(1)}, bf16[3,16,6400]{2,1,0:T(8,128)(2,1)S(1)}, u32[]{:S(2)}, u32[]{:S(2)}) %collective-permute-start.11) | collective-permute-done | bytes 614432 | tf_op jit(solution)/shard_map/ppermute | solution.py:290
  90.6 3.8 %collective-permute-start.12 = (bf16[16,6400]{1,0:T(8,128)(2,1)S(1)}, bf16[16,6400]{1,0:T(8,128)(2,1)S(1)}, u32[]{:S(2)}, u32[]{:S(2)}) collective-permute-start(bf16[16,6400]{1,0:T(8,128)(2,1)S(1)} %get-tuple-element.28), channel_id=1, source_target_pairs={{0,96},{8,104},{16,112},{24,120},{32,64},{40,72},{48,80},{56,88},{... | collective-permute-start | bytes 614408 | tf_op jit(solution)/shard_map/ppermute | solution.py:291
  95.3 4.1 %collective-permute-start.14 = (bf16[16,6400]{1,0:T(8,128)(2,1)S(1)}, bf16[16,6400]{1,0:T(8,128)(2,1)S(1)}, u32[]{:S(2)}, u32[]{:S(2)}) collective-permute-start(bf16[16,6400]{1,0:T(8,128)(2,1)S(1)} %get-tuple-element.30), channel_id=1, source_target_pairs={{0,112},{8,120},{16,64},{24,72},{32,80},{40,88},{48,96},{56,104},{... | collective-permute-start | bytes 614408 | tf_op jit(solution)/shard_map/ppermute | solution.py:291
  99.8 1.3 %collective-permute-start.16 = (bf16[16,6400]{1,0:T(8,128)(2,1)S(1)}, bf16[16,6400]{1,0:T(8,128)(2,1)S(1)}, u32[]{:S(2)}, u32[]{:S(2)}) collective-permute-start(bf16[16,6400]{1,0:T(8,128)(2,1)S(1)} %get-tuple-element.32), channel_id=1, source_target_pairs={{0,64},{8,72},{16,80},{24,88},{32,96},{40,104},{48,112},{56,120},{... | collective-permute-start | bytes 614408 | tf_op jit(solution)/shard_map/ppermute | solution.py:291
  101.1 1.8 %collective-permute-start.17 = (bf16[16,6400]{1,0:T(8,128)(2,1)S(1)}, bf16[16,6400]{1,0:T(8,128)(2,1)S(1)}, u32[]{:S(2)}, u32[]{:S(2)}) collective-permute-start(bf16[16,6400]{1,0:T(8,128)(2,1)S(1)} %get-tuple-element.33), channel_id=1, source_target_pairs={{0,16},{8,24},{16,32},{24,40},{32,48},{40,56},{48,0},{56,8},{64,80... | collective-permute-start | bytes 614408 | tf_op jit(solution)/shard_map/ppermute | solution.py:291
  102.9 4.3 %collective-permute-done.13.refs_2_ = bf16[16,6400]{1,0:T(8,128)(2,1)S(1)} collective-permute-done((bf16[16,6400]{1,0:T(8,128)(2,1)S(1)}, bf16[16,6400]{1,0:T(8,128)(2,1)S(1)}, u32[]{:S(2)}, u32[]{:S(2)}) %collective-permute-start.13) | collective-permute-done | bytes 204832 | tf_op jit(solution)/shard_map/ppermute | solution.py:291
  107.2 2.5 %collective-permute-done.14.refs_3_ = bf16[16,6400]{1,0:T(8,128)(2,1)S(1)} collective-permute-done((bf16[16,6400]{1,0:T(8,128)(2,1)S(1)}, bf16[16,6400]{1,0:T(8,128)(2,1)S(1)}, u32[]{:S(2)}, u32[]{:S(2)}) %collective-permute-start.14) | collective-permute-done | bytes 204832 | tf_op jit(solution)/shard_map/ppermute | solution.py:291
  109.7 2.0 %collective-permute-done.15.refs_4_ = bf16[16,6400]{1,0:T(8,128)(2,1)S(1)} collective-permute-done((bf16[16,6400]{1,0:T(8,128)(2,1)S(1)}, bf16[16,6400]{1,0:T(8,128)(2,1)S(1)}, u32[]{:S(2)}, u32[]{:S(2)}) %collective-permute-start.15) | collective-permute-done | bytes 204832 | tf_op jit(solution)/shard_map/ppermute | solution.py:291
  111.7 2.4 %collective-permute-done.16.refs_5_ = bf16[16,6400]{1,0:T(8,128)(2,1)S(1)} collective-permute-done((bf16[16,6400]{1,0:T(8,128)(2,1)S(1)}, bf16[16,6400]{1,0:T(8,128)(2,1)S(1)}, u32[]{:S(2)}, u32[]{:S(2)}) %collective-permute-start.16) | collective-permute-done | bytes 204832 | tf_op jit(solution)/shard_map/ppermute | solution.py:291
  114.1 2.0 %collective-permute-done.17.refs_6_ = bf16[16,6400]{1,0:T(8,128)(2,1)S(1)} collective-permute-done((bf16[16,6400]{1,0:T(8,128)(2,1)S(1)}, bf16[16,6400]{1,0:T(8,128)(2,1)S(1)}, u32[]{:S(2)}, u32[]{:S(2)}) %collective-permute-start.17) | collective-permute-done | bytes 204832 | tf_op jit(solution)/shard_map/ppermute | solution.py:291
  (57 shorter events, 12.8 us)
Async XLA Ops:
  0.6 41.1 %copy-start.11 = (s32[48]{0:T(128)S(1)}, s32[48]{0:T(128)}, u32[]{:S(2)}) copy-start(s32[48]{0:T(128)} %counts.3) | copy-start | bytes 580
  0.6 41.1 %copy-start.10 = (bf16[16,256]{1,0:T(8,128)(2,1)S(1)}, bf16[16,256]{1,0:T(8,128)(2,1)}, u32[]{:S(2)}) copy-start(bf16[16,256]{1,0:T(8,128)(2,1)} %weight.1) | copy-start | bytes 24580
  0.7 36.1 %collective-permute-start.6 = (bf16[16,6144]{1,0:T(8,128)(2,1)}, bf16[16,6144]{1,0:T(8,128)(2,1)}, u32[]{:S(2)}, u32[]{:S(2)}) collective-permute-start(bf16[16,6144]{1,0:T(8,128)(2,1)} %rest_0_.1), channel_id=1, source_target_pairs={{0,96},{8,104},{16,112},{24,120},{32,64},{40,72},{48,80},{56,88},{... | collective-permute-start | bytes 589832 | tf_op jit(solution)/shard_map/ppermute | solution.py:213
  7.6 30.3 %collective-permute-start.5 = (bf16[16,6144]{1,0:T(8,128)(2,1)}, bf16[16,6144]{1,0:T(8,128)(2,1)}, u32[]{:S(2)}, u32[]{:S(2)}) collective-permute-start(bf16[16,6144]{1,0:T(8,128)(2,1)} %rest_0_.1), channel_id=1, source_target_pairs={{0,112},{8,120},{16,64},{24,72},{32,80},{40,88},{48,96},{56,104},{... | collective-permute-start | bytes 589832 | tf_op jit(solution)/shard_map/ppermute | solution.py:213
  8.0 30.0 %collective-permute-start.4 = (bf16[16,6144]{1,0:T(8,128)(2,1)}, bf16[16,6144]{1,0:T(8,128)(2,1)}, u32[]{:S(2)}, u32[]{:S(2)}) collective-permute-start(bf16[16,6144]{1,0:T(8,128)(2,1)} %rest_0_.1), channel_id=1, source_target_pairs={{0,80},{8,88},{16,96},{24,104},{32,112},{40,120},{48,64},{56,72},{... | collective-permute-start | bytes 589832 | tf_op jit(solution)/shard_map/ppermute | solution.py:213
  11.5 10.8 %collective-permute-start.1 = (bf16[16,6144]{1,0:T(8,128)(2,1)}, bf16[16,6144]{1,0:T(8,128)(2,1)S(1)}, u32[]{:S(2)}, u32[]{:S(2)}) collective-permute-start(bf16[16,6144]{1,0:T(8,128)(2,1)} %rest_0_.1), channel_id=1, source_target_pairs={{0,48},{8,56},{16,0},{24,8},{32,16},{40,24},{48,32},{56,40},{64,11... | collective-permute-start | bytes 589832 | tf_op jit(solution)/shard_map/ppermute | solution.py:213
  13.1 12.0 %collective-permute-start = (bf16[16,6144]{1,0:T(8,128)(2,1)}, bf16[16,6144]{1,0:T(8,128)(2,1)S(1)}, u32[]{:S(2)}, u32[]{:S(2)}) collective-permute-start(bf16[16,6144]{1,0:T(8,128)(2,1)} %rest_0_.1), channel_id=1, source_target_pairs={{0,16},{8,24},{16,32},{24,40},{32,48},{40,56},{48,0},{56,8},{64,80... | collective-permute-start | bytes 589832 | tf_op jit(solution)/shard_map/ppermute | solution.py:213
  22.3 16.9 %collective-permute-start.3 = (bf16[16,6144]{1,0:T(8,128)(2,1)}, bf16[16,6144]{1,0:T(8,128)(2,1)S(1)}, u32[]{:S(2)}, u32[]{:S(2)}) collective-permute-start(bf16[16,6144]{1,0:T(8,128)(2,1)} %rest_0_.1), channel_id=1, source_target_pairs={{0,64},{8,72},{16,80},{24,88},{32,96},{40,104},{48,112},{56,120},{... | collective-permute-start | bytes 589832 | tf_op jit(solution)/shard_map/ppermute | solution.py:213
  25.1 14.1 %collective-permute-start.2 = (bf16[16,6144]{1,0:T(8,128)(2,1)}, bf16[16,6144]{1,0:T(8,128)(2,1)S(1)}, u32[]{:S(2)}, u32[]{:S(2)}) collective-permute-start(bf16[16,6144]{1,0:T(8,128)(2,1)} %rest_0_.1), channel_id=1, source_target_pairs={{0,32},{8,40},{16,48},{24,56},{32,0},{40,8},{48,16},{56,24},{64,96... | collective-permute-start | bytes 589832 | tf_op jit(solution)/shard_map/ppermute | solution.py:213
  26.9 14.8 %copy-start.7 = (bf16[16,6144]{1,0:T(8,128)(2,1)S(1)}, bf16[16,6144]{1,0:T(8,128)(2,1)}, u32[]{:S(2)}) copy-start(bf16[16,6144]{1,0:T(8,128)(2,1)} %rest_0_.1) | copy-start | bytes 589828
  26.9 14.8 %copy-start.8 = (bf16[32,6144]{1,0:T(8,128)(2,1)S(1)}, bf16[32,6144]{1,0:T(8,128)(2,1)}, u32[]{:S(2)}) copy-start(bf16[32,6144]{1,0:T(8,128)(2,1)} %cotangent.1) | copy-start | bytes 1179652
  30.2 32.7 %copy-start.9 = (s32[6144]{0:T(1024)S(1)}, s32[6144]{0:T(1024)}, u32[]{:S(2)}) copy-start(s32[6144]{0:T(1024)} %param.14) | copy-start | bytes 73732
  36.7 5.0 %collective-permute-start.7 = (bf16[3,16,6144]{2,1,0:T(8,128)(2,1)S(1)}, bf16[3,16,6144]{2,1,0:T(8,128)(2,1)S(1)}, u32[]{:S(2)}, u32[]{:S(2)}) collective-permute-start(bf16[3,16,6144]{2,1,0:T(8,128)(2,1)S(1)} %bundle.3), channel_id=1, source_target_pairs={{0,8},{8,0},{16,24},{24,16},{32,40},{40,32},{48,56},{56,48},{64,72... | collective-permute-start | bytes 1769480 | tf_op jit(solution)/shard_map/ppermute | solution.py:243
  39.1 2.7 %collective-permute-start.9 = (bf16[3,16,6144]{2,1,0:T(8,128)(2,1)S(1)}, bf16[3,16,6144]{2,1,0:T(8,128)(2,1)S(1)}, u32[]{:S(2)}, u32[]{:S(2)}) collective-permute-start(bf16[3,16,6144]{2,1,0:T(8,128)(2,1)S(1)} %bundle.5), channel_id=1, source_target_pairs={{0,8},{8,0},{16,24},{24,16},{32,40},{40,32},{48,56},{56,48},{64,72... | collective-permute-start | bytes 1769480 | tf_op jit(solution)/shard_map/ppermute | solution.py:243
  39.3 2.5 %collective-permute-start.8 = (bf16[2,16,6144]{2,1,0:T(8,128)(2,1)S(1)}, bf16[2,16,6144]{2,1,0:T(8,128)(2,1)S(1)}, u32[]{:S(2)}, u32[]{:S(2)}) collective-permute-start(bf16[2,16,6144]{2,1,0:T(8,128)(2,1)S(1)} %bundle.4), channel_id=1, source_target_pairs={{0,8},{8,0},{16,24},{24,16},{32,40},{40,32},{48,56},{56,48},{64,72... | collective-permute-start | bytes 1179656 | tf_op jit(solution)/shard_map/ppermute | solution.py:243
  85.1 14.3 %collective-permute-start.10 = (bf16[5,16,6400]{2,1,0:T(8,128)(2,1)S(1)}, bf16[5,16,6400]{2,1,0:T(8,128)(2,1)S(1)}, u32[]{:S(2)}, u32[]{:S(2)}) collective-permute-start(bf16[5,16,6400]{2,1,0:T(8,128)(2,1)S(1)} %get-tuple-element.24), channel_id=1, source_target_pairs={{0,8},{8,0},{16,24},{24,16},{32,40},{40,32},{48,56},{56,48},{64,72... | collective-permute-start | bytes 3072008 | tf_op jit(solution)/shard_map/ppermute | solution.py:290
  87.3 3.1 %collective-permute-start.11 = (bf16[3,16,6400]{2,1,0:T(8,128)(2,1)S(1)}, bf16[3,16,6400]{2,1,0:T(8,128)(2,1)S(1)}, u32[]{:S(2)}, u32[]{:S(2)}) collective-permute-start(bf16[3,16,6400]{2,1,0:T(8,128)(2,1)S(1)} %get-tuple-element.27), channel_id=1, source_target_pairs={{0,8},{8,0},{16,24},{24,16},{32,40},{40,32},{48,56},{56,48},{64,72... | collective-permute-start | bytes 1843208 | tf_op jit(solution)/shard_map/ppermute | solution.py:290
  90.6 10.5 %collective-permute-start.12 = (bf16[16,6400]{1,0:T(8,128)(2,1)S(1)}, bf16[16,6400]{1,0:T(8,128)(2,1)S(1)}, u32[]{:S(2)}, u32[]{:S(2)}) collective-permute-start(bf16[16,6400]{1,0:T(8,128)(2,1)S(1)} %get-tuple-element.28), channel_id=1, source_target_pairs={{0,96},{8,104},{16,112},{24,120},{32,64},{40,72},{48,80},{56,88},{... | collective-permute-start | bytes 614408 | tf_op jit(solution)/shard_map/ppermute | solution.py:291
  94.4 12.9 %collective-permute-start.13 = (bf16[16,6400]{1,0:T(8,128)(2,1)S(1)}, bf16[16,6400]{1,0:T(8,128)(2,1)S(1)}, u32[]{:S(2)}, u32[]{:S(2)}) collective-permute-start(bf16[16,6400]{1,0:T(8,128)(2,1)S(1)} %get-tuple-element.29), channel_id=1, source_target_pairs={{0,80},{8,88},{16,96},{24,104},{32,112},{40,120},{48,64},{56,72},{... | collective-permute-start | bytes 614408 | tf_op jit(solution)/shard_map/ppermute | solution.py:291
  95.3 14.4 %collective-permute-start.14 = (bf16[16,6400]{1,0:T(8,128)(2,1)S(1)}, bf16[16,6400]{1,0:T(8,128)(2,1)S(1)}, u32[]{:S(2)}, u32[]{:S(2)}) collective-permute-start(bf16[16,6400]{1,0:T(8,128)(2,1)S(1)} %get-tuple-element.30), channel_id=1, source_target_pairs={{0,112},{8,120},{16,64},{24,72},{32,80},{40,88},{48,96},{56,104},{... | collective-permute-start | bytes 614408 | tf_op jit(solution)/shard_map/ppermute | solution.py:291
  99.7 12.0 %collective-permute-start.15 = (bf16[16,6400]{1,0:T(8,128)(2,1)S(1)}, bf16[16,6400]{1,0:T(8,128)(2,1)S(1)}, u32[]{:S(2)}, u32[]{:S(2)}) collective-permute-start(bf16[16,6400]{1,0:T(8,128)(2,1)S(1)} %get-tuple-element.31), channel_id=1, source_target_pairs={{0,32},{8,40},{16,48},{24,56},{32,0},{40,8},{48,16},{56,24},{64,96... | collective-permute-start | bytes 614408 | tf_op jit(solution)/shard_map/ppermute | solution.py:291
  99.8 14.4 %collective-permute-start.16 = (bf16[16,6400]{1,0:T(8,128)(2,1)S(1)}, bf16[16,6400]{1,0:T(8,128)(2,1)S(1)}, u32[]{:S(2)}, u32[]{:S(2)}) collective-permute-start(bf16[16,6400]{1,0:T(8,128)(2,1)S(1)} %get-tuple-element.32), channel_id=1, source_target_pairs={{0,64},{8,72},{16,80},{24,88},{32,96},{40,104},{48,112},{56,120},{... | collective-permute-start | bytes 614408 | tf_op jit(solution)/shard_map/ppermute | solution.py:291
  101.1 15.1 %collective-permute-start.17 = (bf16[16,6400]{1,0:T(8,128)(2,1)S(1)}, bf16[16,6400]{1,0:T(8,128)(2,1)S(1)}, u32[]{:S(2)}, u32[]{:S(2)}) collective-permute-start(bf16[16,6400]{1,0:T(8,128)(2,1)S(1)} %get-tuple-element.33), channel_id=1, source_target_pairs={{0,16},{8,24},{16,32},{24,40},{32,48},{40,56},{48,0},{56,8},{64,80... | collective-permute-start | bytes 614408 | tf_op jit(solution)/shard_map/ppermute | solution.py:291
  107.2 9.0 %collective-permute-start.18 = (bf16[16,6400]{1,0:T(8,128)(2,1)S(1)}, bf16[16,6400]{1,0:T(8,128)(2,1)S(1)}, u32[]{:S(2)}, u32[]{:S(2)}) collective-permute-start(bf16[16,6400]{1,0:T(8,128)(2,1)S(1)} %get-tuple-element.34), channel_id=1, source_target_pairs={{0,48},{8,56},{16,0},{24,8},{32,16},{40,24},{48,32},{56,40},{64,11... | collective-permute-start | bytes 614408 | tf_op jit(solution)/shard_map/ppermute | solution.py:291
  (7 other events, 6.0 us)

commit v8 on v7

--- a/solution.py
+++ b/solution.py
@@ -13,8 +13,7 @@
 SMEM = pl.BlockSpec(memory_space=pltpu.SMEM)
 VMEM = pl.BlockSpec(memory_space=pltpu.VMEM)
 STEPS = ((1, 2), (1, 1), (1, 3), (0, 2), (1, 0), (0, 1), (0, 3))
-NEAREST = ((0, 1), (0, 3), (0, 2), (1, 0), (1, 1), (1, 3), (1, 2))
-HAND_OVERS = ((0, 3), (3, 5), (5, 8))
+GATHERED = ((0, 1), (1, 0), (0, 2), (1, 3), (1, 1), (1, 2), (0, 3))
 EARLY_SUM = 3
 BLOCK = 128
 
@@ -47,42 +46,21 @@
     return pltpu.CompilerParams(vmem_limit_bytes=mib * 2**20)
 
 
-def bundle_kernel(_, *refs):
-    pieces, out = refs[:-1], refs[-1]
-    for at, piece in enumerate(pieces):
-        out[at] = piece[...]
-
-
-def load_kernel(values, *rest):
-    out, loaded, sems = rest[-3:]
-    count = sems.shape[0]
-    rows = out.shape[0] // count
-    copies = [
-        pltpu.make_async_copy(
-            values.at[pl.ds(i * rows, rows)], out.at[pl.ds(i * rows, rows)], sems.at[i]
-        )
-        for i in range(count)
-    ]
-    for copy in copies:
-        copy.start()
-    for copy in copies:
-        copy.wait()
-    loaded[...] = jnp.zeros_like(loaded)
-
-
-def mix_kernel(cols, counts, values, cotangent, weight, bias_rows, *rest):
-    pieces, bundles, (out, held) = rest[:8], rest[8:11], rest[11:]
+def mix_kernel(cols, counts, stored, cotangent, weight, bias_rows, *rest):
+    pieces, (out, values, held, sems) = rest[:16], rest[16:]
     slots = values.shape[1]
     chunks, _, _ = out.shape
     width = cotangent.shape[1] // chunks
     rows = values.shape[0] // chunks
 
-    for at, (dx, dz) in enumerate(((0, 0),) + NEAREST):
-        held[node_near(dx, -dz, 0)] = pieces[at][...]
-    for bundle, (start, end) in zip(bundles, HAND_OVERS):
-        for at in range(start, end):
-            dx, dz = (((0, 0),) + NEAREST)[at]
-            held[node_near(dx, -dz, 1)] = bundle[at - start]
+    copies = []
+    for j in range(chunks):
+        part = pl.ds(j * rows, rows)
+        copies.append(pltpu.make_async_copy(stored.at[part], values.at[part], sems.at[j]))
+        copies[j].start()
+    for at, (dx, dz) in enumerate(((0, 0),) + GATHERED):
+        for core in range(2):
+            held[node_near(dx, -dz, core)] = pieces[2 * at + core][...]
     for j in range(chunks):
         out[j, :, width : 2 * width] = cotangent[:16, j * width : (j + 1) * width]
         out[j, :, 2 * width : 3 * width] = cotangent[16:, j * width : (j + 1) * width]
@@ -90,6 +68,7 @@
         out[j, :, 3 * width + 256 :] = bias_rows[...]
 
     for j in range(chunks):
+        copies[j].wait()
         for i in range(rows):
             r = j * rows + i
             count = counts[r]
@@ -209,48 +188,28 @@
     ).astype(BF)
 
     swap = node_pairs(0, 0, 1)
-    pieces = [features]
-    pieces += [lax.ppermute(features, "node", node_pairs(*step)) for step in NEAREST]
-
-    values, loaded = pl.pallas_call(
-        load_kernel,
-        in_specs=[pl.BlockSpec(memory_space=pltpu.HBM)] + [ANY] * 4,
+    pieces = [features, lax.ppermute(features, "node", swap)]
+    for step in GATHERED:
+        piece = lax.ppermute(features, "node", node_pairs(*step))
+        pieces += [piece, lax.ppermute(piece, "node", swap)]
+
+    mixed, values = pl.pallas_call(
+        mix_kernel,
+        in_specs=[SMEM, SMEM, pl.BlockSpec(memory_space=pltpu.HBM)] + [VMEM] * 19,
         out_specs=[VMEM, VMEM],
-        out_shape=[pltpu.VMEM(block_values.shape, BF), shape((8, 128), F32)],
-        scratch_shapes=[pltpu.SemaphoreType.DMA((8,))],
-        compiler_params=params(4),
-        cost_estimate=pl.CostEstimate(
-            flops=0, bytes_accessed=2 * block_values.size * 2, transcendentals=0
-        ),
-        name="load",
-    )(
-        pltpu.with_memory_space_constraint(block_values, pltpu.HBM),
-        *pieces[1:3],
-        bias_rows,
-        block_cols,
-    )
-
-    bundles = []
-    for start, end in HAND_OVERS:
-        bundle = pl.pallas_call(
-            bundle_kernel,
-            in_specs=[ANY] + [VMEM] * (end - start),
-            out_specs=VMEM,
-            out_shape=shape((end - start, fin, nodes)),
-            compiler_params=params(8),
-            name="bundle",
-        )(loaded if start > 0 else pieces[1], *pieces[start:end])
-        bundles.append(lax.ppermute(bundle, "node", swap))
-
-    mixed = pl.pallas_call(
-        mix_kernel,
-        in_specs=[SMEM, SMEM] + [VMEM] * 15,
-        out_specs=VMEM,
-        out_shape=shape((8, 16, 3 * width + 512)),
-        scratch_shapes=[pltpu.VMEM((16, fin, nodes), BF)],
+        out_shape=[shape((8, 16, 3 * width + 512)), pltpu.VMEM(block_values.shape, BF)],
+        scratch_shapes=[pltpu.VMEM((16, fin, nodes), BF), pltpu.SemaphoreType.DMA((8,))],
         compiler_params=params(16),
         name="mix",
-    )(block_cols, block_counts, values, cotangent, weight, bias_rows, *pieces, *bundles)
+    )(
+        block_cols,
+        block_counts,
+        pltpu.with_memory_space_constraint(block_values, pltpu.HBM),
+        cotangent,
+        weight,
+        bias_rows,
+        *pieces,
+    )
 
     both = lax.all_to_all(mixed, "feat", 0, 0, tiled=True)
 

time: 117 us -> 113 us (0.966)
  starting transfers between devices: 32.2 us -> 39.1 us
  waiting for transfers between devices: 25.8 us -> 20.7 us
  Pallas kernels: 21.4 us -> 17.3 us
  local copies, waits for them, and re-layouts: 7.65 us -> 4.9 us
    ppermute x10 -> x15, starting transfers between devices: 18 us -> 25.9 us  [the longest x7 15.4 us: local(): piece = lax.ppermute(features, 'node', node_pairs(*step))]
    ppermute x10 -> x15, waiting for transfers between devices: 9.41 us -> 3.28 us  [the longest x7 2.15 us: local(): piece = lax.ppermute(features, 'node', node_pairs(*step))]
    pallas_call x5 -> x1, Pallas kernels: 12 us -> 7.95 us  [local(): pl.pallas_call(mix_kernel, in_specs=[SMEM, SMEM, pl.BlockSpec(memory_spac...]
    unnamed x25 -> x13, local copies, waits for them, and re-layouts: 6.81 us -> 4.06 us
    all_to_all x1, blocking collectives: 15 us -> 16.4 us  [local(): both = lax.all_to_all(mixed, 'feat', 0, 0, tiled=True)]
    ppermute x7, starting transfers between devices: 12.1 us -> 10.7 us  [local(): lax.ppermute(part, 'node', node_pairs(*step))]
  transfers between devices with their start and end apart: 19 -> 24, of which waited for: 8 -> 12; matrix products, arithmetic and copies ran while one was open for 1% -> 2% of each run, Pallas kernels for 7% -> 0%
where the time goes in v8:
time: 113 us
  starting transfers between devices  39.1 us (35%)
  blocking collectives  29.9 us (26%)
  waiting for transfers between devices  20.7 us (18%)
  Pallas kernels  17.3 us (15%)
  local copies, waits for them, and re-layouts  4.9 us (4%)
    all_to_all x1, blocking collectives, local(): both = lax.all_to_all(mixed, 'feat', 0, 0, tiled=True)  16.4 us
    ppermute x7, starting transfers between devices, local(): piece = lax.ppermute(features, 'node', node_pairs(*step))  15.4 us
    ppermute x7, waiting for transfers between devices, local(): lax.ppermute(part, 'node', node_pairs(*step))  14.3 us
    all_to_all x1, blocking collectives, local(): grads = lax.all_to_all(dense, 'feat', 0, 0, tiled=True)  13.4 us
    ppermute x7, starting transfers between devices, local(): lax.ppermute(part, 'node', node_pairs(*step))  10.7 us
    pallas_call x1, Pallas kernels, local(): pl.pallas_call(mix_kernel, in_specs=[SMEM, SMEM, pl.BlockSpec(memory_spac...  7.95 us
    pallas_call x1, Pallas kernels, local(): pl.pallas_call(spread_kernel, in_specs=[SMEM, SMEM] + [VMEM] * 2, out_spe...  7.37 us
    ppermute x7, starting transfers between devices, local(): pieces += [piece, lax.ppermute(piece, 'node', swap)]  6.56 us
  transfers between devices with their start and end apart: 24, of which 12 were waited for; matrix products, arithmetic and copies ran while one was open for 2% of the time, Pallas kernels for 0%

profile of v8, /device:TPU:1, one launch (start us, length us, event | category | flops | bytes accessed | tf_op | source)
XLA Modules:
  0.0 112.6 jit_solution(12098880755902414092)
XLA Ops:
  0.7 7.0 %collective-permute-start.11 = (bf16[16,6144]{1,0:T(8,128)(2,1)}, bf16[16,6144]{1,0:T(8,128)(2,1)S(1)}, u32[]{:S(2)}, u32[]{:S(2)}) collective-permute-start(bf16[16,6144]{1,0:T(8,128)(2,1)} %rest_0_.1), channel_id=1, source_target_pairs={{0,96},{8,104},{16,112},{24,120},{32,64},{40,72},{48,80},{56,88},{... | collective-permute-start | bytes 589832 | tf_op jit(solution)/shard_map/ppermute | solution.py:193
  8.3 4.4 %collective-permute-start.7 = (bf16[16,6144]{1,0:T(8,128)(2,1)}, bf16[16,6144]{1,0:T(8,128)(2,1)S(1)}, u32[]{:S(2)}, u32[]{:S(2)}) collective-permute-start(bf16[16,6144]{1,0:T(8,128)(2,1)} %rest_0_.1), channel_id=1, source_target_pairs={{0,112},{8,120},{16,64},{24,72},{32,80},{40,88},{48,96},{56,104},{... | collective-permute-start | bytes 589832 | tf_op jit(solution)/shard_map/ppermute | solution.py:193
  15.3 1.6 %collective-permute-done.9.rest_10_ = bf16[16,6144]{1,0:T(8,128)(2,1)S(1)} collective-permute-done((bf16[16,6144]{1,0:T(8,128)(2,1)}, bf16[16,6144]{1,0:T(8,128)(2,1)S(1)}, u32[]{:S(2)}, u32[]{:S(2)}) %collective-permute-start.9) | collective-permute-done | bytes 196640 | tf_op jit(solution)/shard_map/ppermute | solution.py:193
  16.9 4.0 %collective-permute-start = (bf16[16,6144]{1,0:T(8,128)(2,1)}, bf16[16,6144]{1,0:T(8,128)(2,1)S(1)}, u32[]{:S(2)}, u32[]{:S(2)}) collective-permute-start(bf16[16,6144]{1,0:T(8,128)(2,1)} %rest_0_.1), channel_id=1, source_target_pairs={{0,8},{8,0},{16,24},{24,16},{32,40},{40,32},{48,56},{56,48},{64,72... | collective-permute-start | bytes 589832 | tf_op jit(solution)/shard_map/ppermute | solution.py:191
  21.2 2.4 %collective-permute-start.13 = (bf16[16,6144]{1,0:T(8,128)(2,1)}, bf16[16,6144]{1,0:T(8,128)(2,1)S(1)}, u32[]{:S(2)}, u32[]{:S(2)}) collective-permute-start(bf16[16,6144]{1,0:T(8,128)(2,1)} %rest_0_.1), channel_id=1, source_target_pairs={{0,48},{8,56},{16,0},{24,8},{32,16},{40,24},{48,32},{56,40},{64,11... | collective-permute-start | bytes 589832 | tf_op jit(solution)/shard_map/ppermute | solution.py:193
  23.7 2.4 %collective-permute-start.12 = (bf16[16,6144]{1,0:T(8,128)(2,1)S(1)}, bf16[16,6144]{1,0:T(8,128)(2,1)S(1)}, u32[]{:S(2)}, u32[]{:S(2)}) collective-permute-start(bf16[16,6144]{1,0:T(8,128)(2,1)S(1)} %collective-permute-done.11.rest_12_), channel_id=1, source_target_pairs={{0,8},{8,0},{16,24},{24,16},{32,40},{40,32},{48,56},{56,48},{64,72... | collective-permute-start | bytes 589832 | tf_op jit(solution)/shard_map/ppermute | solution.py:194
  27.3 2.5 %collective-permute-start.4 = (bf16[16,6144]{1,0:T(8,128)(2,1)S(1)}, bf16[16,6144]{1,0:T(8,128)(2,1)S(1)}, u32[]{:S(2)}, u32[]{:S(2)}) collective-permute-start(bf16[16,6144]{1,0:T(8,128)(2,1)S(1)} %collective-permute-done.3.rest_4_), channel_id=1, source_target_pairs={{0,8},{8,0},{16,24},{24,16},{32,40},{40,32},{48,56},{56,48},{64,72... | collective-permute-start | bytes 589832 | tf_op jit(solution)/shard_map/ppermute | solution.py:194
  31.6 1.0 copy-done
  32.6 0.9 copy-done.1
  34.8 7.9 %mix.1 = (bf16[8,16,2816]{2,1,0:T(8,128)(2,1)S(1)}, bf16[48,12,128,128]{3,2,1,0:T(8,128)(2,1)S(1)}) custom-call(s32[48,12]{1,0:T(8,128)S(1)} %copy.12.cols, s32[48]{0:T(128)S(1)} %copy-done.4, bf16[48,12,128,128]{3,2,1,0:T(8,128)(2,1)} %stored.1, bf16[32,6144]{1,0:T(8,128)(2,1)S(1)} %copy-done, bf16[16,256]{1,0:T(8,128)(2,1)S(1)} %copy-done.3, ...), custom_call_target="tpu_custom_call" | custom-call | tf_op jit(solution)/shard_map/mix/pallas_call | solution.py:196
  42.8 16.4 %all_to_all.10.both = bf16[8,16,2816]{2,1,0:T(8,128)(2,1)S(1)} all-to-all(bf16[8,16,2816]{2,1,0:T(8,128)(2,1)S(1)} %get-tuple-element.21), channel_id=1, replica_groups=mesh['node'=16,'feat'=8] {'feat'}, dimensions={0} | all-to-all | bytes 1441792 | tf_op jit(solution)/shard_map/all_to_all | solution.py:214
  60.0 13.4 %all_to_all.11.grads = bf16[8,16,2560]{2,1,0:T(8,128)(2,1)S(1)} all-to-all(bf16[8,16,2560]{2,1,0:T(8,128)(2,1)S(1)} %dense.1), channel_id=1, replica_groups=mesh['node'=16,'feat'=8] {'feat'}, dimensions={0} | all-to-all | bytes 1310720 | tf_op jit(solution)/shard_map/all_to_all | solution.py:225
  73.4 7.4 %spread.1 = (bf16[32,6144]{1,0:T(8,128)(2,1)}, bf16[3,16,6400]{2,1,0:T(8,128)(2,1)S(1)}, bf16[3,16,6400]{2,1,0:T(8,128)(2,1)S(1)}, bf16[5,16,6400]{2,1,0:T(8,128)(2,1)S(1)}, bf16[5,16,6400]{2,1,0:T(8,128)(2,1)S(1)}) custom-call(s32[48,12]{1,0:T(8,128)S(1)} %copy.12.cols, s32[48]{0:T(128)S(1)} %copy-done.5, ...), custom_call_target="tpu_custom_call" | custom-call | tf_op jit(solution)/shard_map/spread/pallas_call | solution.py:229
  80.8 2.5 %collective-permute-start.15 = (bf16[5,16,6400]{2,1,0:T(8,128)(2,1)S(1)}, bf16[5,16,6400]{2,1,0:T(8,128)(2,1)S(1)}, u32[]{:S(2)}, u32[]{:S(2)}) collective-permute-start(bf16[5,16,6400]{2,1,0:T(8,128)(2,1)S(1)} %get-tuple-element.24), channel_id=1, source_target_pairs={{0,8},{8,0},{16,24},{24,16},{32,40},{40,32},{48,56},{56,48},{64,72... | collective-permute-start | bytes 3072008 | tf_op jit(solution)/shard_map/ppermute | solution.py:249
  83.3 3.1 %collective-permute-done.16.other = bf16[3,16,6400]{2,1,0:T(8,128)(2,1)S(1)} collective-permute-done((bf16[3,16,6400]{2,1,0:T(8,128)(2,1)S(1)}, bf16[3,16,6400]{2,1,0:T(8,128)(2,1)S(1)}, u32[]{:S(2)}, u32[]{:S(2)}) %collective-permute-start.16) | collective-permute-done | bytes 614432 | tf_op jit(solution)/shard_map/ppermute | solution.py:249
  86.5 3.2 %collective-permute-start.17 = (bf16[16,6400]{1,0:T(8,128)(2,1)S(1)}, bf16[16,6400]{1,0:T(8,128)(2,1)S(1)}, u32[]{:S(2)}, u32[]{:S(2)}) collective-permute-start(bf16[16,6400]{1,0:T(8,128)(2,1)S(1)} %get-tuple-element.28), channel_id=1, source_target_pairs={{0,96},{8,104},{16,112},{24,120},{32,64},{40,72},{48,80},{56,88},{... | collective-permute-start | bytes 614408 | tf_op jit(solution)/shard_map/ppermute | solution.py:250
  89.7 3.1 %collective-permute-start.18 = (bf16[16,6400]{1,0:T(8,128)(2,1)S(1)}, bf16[16,6400]{1,0:T(8,128)(2,1)S(1)}, u32[]{:S(2)}, u32[]{:S(2)}) collective-permute-start(bf16[16,6400]{1,0:T(8,128)(2,1)S(1)} %get-tuple-element.29), channel_id=1, source_target_pairs={{0,80},{8,88},{16,96},{24,104},{32,112},{40,120},{48,64},{56,72},{... | collective-permute-start | bytes 614408 | tf_op jit(solution)/shard_map/ppermute | solution.py:250
  92.8 2.0 %collective-permute-start.19 = (bf16[16,6400]{1,0:T(8,128)(2,1)S(1)}, bf16[16,6400]{1,0:T(8,128)(2,1)S(1)}, u32[]{:S(2)}, u32[]{:S(2)}) collective-permute-start(bf16[16,6400]{1,0:T(8,128)(2,1)S(1)} %get-tuple-element.30), channel_id=1, source_target_pairs={{0,112},{8,120},{16,64},{24,72},{32,80},{40,88},{48,96},{56,104},{... | collective-permute-start | bytes 614408 | tf_op jit(solution)/shard_map/ppermute | solution.py:250
  95.5 1.4 %collective-permute-start.21 = (bf16[16,6400]{1,0:T(8,128)(2,1)S(1)}, bf16[16,6400]{1,0:T(8,128)(2,1)S(1)}, u32[]{:S(2)}, u32[]{:S(2)}) collective-permute-start(bf16[16,6400]{1,0:T(8,128)(2,1)S(1)} %get-tuple-element.32), channel_id=1, source_target_pairs={{0,64},{8,72},{16,80},{24,88},{32,96},{40,104},{48,112},{56,120},{... | collective-permute-start | bytes 614408 | tf_op jit(solution)/shard_map/ppermute | solution.py:250
  97.4 4.0 %collective-permute-done.18.refs_2_ = bf16[16,6400]{1,0:T(8,128)(2,1)S(1)} collective-permute-done((bf16[16,6400]{1,0:T(8,128)(2,1)S(1)}, bf16[16,6400]{1,0:T(8,128)(2,1)S(1)}, u32[]{:S(2)}, u32[]{:S(2)}) %collective-permute-start.18) | collective-permute-done | bytes 204832 | tf_op jit(solution)/shard_map/ppermute | solution.py:250
  101.5 4.9 %collective-permute-done.19.refs_3_ = bf16[16,6400]{1,0:T(8,128)(2,1)S(1)} collective-permute-done((bf16[16,6400]{1,0:T(8,128)(2,1)S(1)}, bf16[16,6400]{1,0:T(8,128)(2,1)S(1)}, u32[]{:S(2)}, u32[]{:S(2)}) %collective-permute-start.19) | collective-permute-done | bytes 204832 | tf_op jit(solution)/shard_map/ppermute | solution.py:250
  106.4 3.3 %collective-permute-done.21.refs_5_ = bf16[16,6400]{1,0:T(8,128)(2,1)S(1)} collective-permute-done((bf16[16,6400]{1,0:T(8,128)(2,1)S(1)}, bf16[16,6400]{1,0:T(8,128)(2,1)S(1)}, u32[]{:S(2)}, u32[]{:S(2)}) %collective-permute-start.21) | collective-permute-done | bytes 204832 | tf_op jit(solution)/shard_map/ppermute | solution.py:250
  109.7 1.0 collective-permute-done.22.refs_6_
  110.7 1.0 collective-permute-done.23.refs_7_
  (51 shorter events, 11.0 us)
Async XLA Ops:
  0.7 13.9 %collective-permute-start.11 = (bf16[16,6144]{1,0:T(8,128)(2,1)}, bf16[16,6144]{1,0:T(8,128)(2,1)S(1)}, u32[]{:S(2)}, u32[]{:S(2)}) collective-permute-start(bf16[16,6144]{1,0:T(8,128)(2,1)} %rest_0_.1), channel_id=1, source_target_pairs={{0,96},{8,104},{16,112},{24,120},{32,64},{40,72},{48,80},{56,88},{... | collective-permute-start | bytes 589832 | tf_op jit(solution)/shard_map/ppermute | solution.py:193
  7.6 9.3 %collective-permute-start.9 = (bf16[16,6144]{1,0:T(8,128)(2,1)}, bf16[16,6144]{1,0:T(8,128)(2,1)S(1)}, u32[]{:S(2)}, u32[]{:S(2)}) collective-permute-start(bf16[16,6144]{1,0:T(8,128)(2,1)} %rest_0_.1), channel_id=1, source_target_pairs={{0,80},{8,88},{16,96},{24,104},{32,112},{40,120},{48,64},{56,72},{... | collective-permute-start | bytes 589832 | tf_op jit(solution)/shard_map/ppermute | solution.py:193
  8.3 12.9 %collective-permute-start.7 = (bf16[16,6144]{1,0:T(8,128)(2,1)}, bf16[16,6144]{1,0:T(8,128)(2,1)S(1)}, u32[]{:S(2)}, u32[]{:S(2)}) collective-permute-start(bf16[16,6144]{1,0:T(8,128)(2,1)} %rest_0_.1), channel_id=1, source_target_pairs={{0,112},{8,120},{16,64},{24,72},{32,80},{40,88},{48,96},{56,104},{... | collective-permute-start | bytes 589832 | tf_op jit(solution)/shard_map/ppermute | solution.py:193
  12.7 11.0 %collective-permute-start.5 = (bf16[16,6144]{1,0:T(8,128)(2,1)}, bf16[16,6144]{1,0:T(8,128)(2,1)S(1)}, u32[]{:S(2)}, u32[]{:S(2)}) collective-permute-start(bf16[16,6144]{1,0:T(8,128)(2,1)} %rest_0_.1), channel_id=1, source_target_pairs={{0,32},{8,40},{16,48},{24,56},{32,0},{40,8},{48,16},{56,24},{64,96... | collective-permute-start | bytes 589832 | tf_op jit(solution)/shard_map/ppermute | solution.py:193
  12.7 13.4 %collective-permute-start.3 = (bf16[16,6144]{1,0:T(8,128)(2,1)}, bf16[16,6144]{1,0:T(8,128)(2,1)S(1)}, u32[]{:S(2)}, u32[]{:S(2)}) collective-permute-start(bf16[16,6144]{1,0:T(8,128)(2,1)} %rest_0_.1), channel_id=1, source_target_pairs={{0,64},{8,72},{16,80},{24,88},{32,96},{40,104},{48,112},{56,120},{... | collective-permute-start | bytes 589832 | tf_op jit(solution)/shard_map/ppermute | solution.py:193
  14.6 12.3 %collective-permute-start.1 = (bf16[16,6144]{1,0:T(8,128)(2,1)}, bf16[16,6144]{1,0:T(8,128)(2,1)S(1)}, u32[]{:S(2)}, u32[]{:S(2)}) collective-permute-start(bf16[16,6144]{1,0:T(8,128)(2,1)} %rest_0_.1), channel_id=1, source_target_pairs={{0,16},{8,24},{16,32},{24,40},{32,48},{40,56},{48,0},{56,8},{64,80... | collective-permute-start | bytes 589832 | tf_op jit(solution)/shard_map/ppermute | solution.py:193
  16.9 10.4 %collective-permute-start = (bf16[16,6144]{1,0:T(8,128)(2,1)}, bf16[16,6144]{1,0:T(8,128)(2,1)S(1)}, u32[]{:S(2)}, u32[]{:S(2)}) collective-permute-start(bf16[16,6144]{1,0:T(8,128)(2,1)} %rest_0_.1), channel_id=1, source_target_pairs={{0,8},{8,0},{16,24},{24,16},{32,40},{40,32},{48,56},{56,48},{64,72... | collective-permute-start | bytes 589832 | tf_op jit(solution)/shard_map/ppermute | solution.py:191
  21.2 6.1 %collective-permute-start.13 = (bf16[16,6144]{1,0:T(8,128)(2,1)}, bf16[16,6144]{1,0:T(8,128)(2,1)S(1)}, u32[]{:S(2)}, u32[]{:S(2)}) collective-permute-start(bf16[16,6144]{1,0:T(8,128)(2,1)} %rest_0_.1), channel_id=1, source_target_pairs={{0,48},{8,56},{16,0},{24,8},{32,16},{40,24},{48,32},{56,40},{64,11... | collective-permute-start | bytes 589832 | tf_op jit(solution)/shard_map/ppermute | solution.py:193
  23.7 6.2 %collective-permute-start.12 = (bf16[16,6144]{1,0:T(8,128)(2,1)S(1)}, bf16[16,6144]{1,0:T(8,128)(2,1)S(1)}, u32[]{:S(2)}, u32[]{:S(2)}) collective-permute-start(bf16[16,6144]{1,0:T(8,128)(2,1)S(1)} %collective-permute-done.11.rest_12_), channel_id=1, source_target_pairs={{0,8},{8,0},{16,24},{24,16},{32,40},{40,32},{48,56},{56,48},{64,72... | collective-permute-start | bytes 589832 | tf_op jit(solution)/shard_map/ppermute | solution.py:194
  26.1 3.7 %collective-permute-start.10 = (bf16[16,6144]{1,0:T(8,128)(2,1)S(1)}, bf16[16,6144]{1,0:T(8,128)(2,1)S(1)}, u32[]{:S(2)}, u32[]{:S(2)}) collective-permute-start(bf16[16,6144]{1,0:T(8,128)(2,1)S(1)} %collective-permute-done.9.rest_10_), channel_id=1, source_target_pairs={{0,8},{8,0},{16,24},{24,16},{32,40},{40,32},{48,56},{56,48},{64,72... | collective-permute-start | bytes 589832 | tf_op jit(solution)/shard_map/ppermute | solution.py:194
  26.8 3.6 %collective-permute-start.8 = (bf16[16,6144]{1,0:T(8,128)(2,1)S(1)}, bf16[16,6144]{1,0:T(8,128)(2,1)S(1)}, u32[]{:S(2)}, u32[]{:S(2)}) collective-permute-start(bf16[16,6144]{1,0:T(8,128)(2,1)S(1)} %collective-permute-done.7.rest_8_), channel_id=1, source_target_pairs={{0,8},{8,0},{16,24},{24,16},{32,40},{40,32},{48,56},{56,48},{64,72... | collective-permute-start | bytes 589832 | tf_op jit(solution)/shard_map/ppermute | solution.py:194
  27.3 3.1 %collective-permute-start.6 = (bf16[16,6144]{1,0:T(8,128)(2,1)S(1)}, bf16[16,6144]{1,0:T(8,128)(2,1)S(1)}, u32[]{:S(2)}, u32[]{:S(2)}) collective-permute-start(bf16[16,6144]{1,0:T(8,128)(2,1)S(1)} %collective-permute-done.5.rest_6_), channel_id=1, source_target_pairs={{0,8},{8,0},{16,24},{24,16},{32,40},{40,32},{48,56},{56,48},{64,72... | collective-permute-start | bytes 589832 | tf_op jit(solution)/shard_map/ppermute | solution.py:194
  27.3 3.6 %collective-permute-start.4 = (bf16[16,6144]{1,0:T(8,128)(2,1)S(1)}, bf16[16,6144]{1,0:T(8,128)(2,1)S(1)}, u32[]{:S(2)}, u32[]{:S(2)}) collective-permute-start(bf16[16,6144]{1,0:T(8,128)(2,1)S(1)} %collective-permute-done.3.rest_4_), channel_id=1, source_target_pairs={{0,8},{8,0},{16,24},{24,16},{32,40},{40,32},{48,56},{56,48},{64,72... | collective-permute-start | bytes 589832 | tf_op jit(solution)/shard_map/ppermute | solution.py:194
  29.8 1.4 %collective-permute-start.2 = (bf16[16,6144]{1,0:T(8,128)(2,1)S(1)}, bf16[16,6144]{1,0:T(8,128)(2,1)S(1)}, u32[]{:S(2)}, u32[]{:S(2)}) collective-permute-start(bf16[16,6144]{1,0:T(8,128)(2,1)S(1)} %collective-permute-done.1.rest_2_), channel_id=1, source_target_pairs={{0,8},{8,0},{16,24},{24,16},{32,40},{40,32},{48,56},{56,48},{64,72... | collective-permute-start | bytes 589832 | tf_op jit(solution)/shard_map/ppermute | solution.py:194
  29.8 1.7 %collective-permute-start.14 = (bf16[16,6144]{1,0:T(8,128)(2,1)S(1)}, bf16[16,6144]{1,0:T(8,128)(2,1)S(1)}, u32[]{:S(2)}, u32[]{:S(2)}) collective-permute-start(bf16[16,6144]{1,0:T(8,128)(2,1)S(1)} %collective-permute-done.13.rest_14_), channel_id=1, source_target_pairs={{0,8},{8,0},{16,24},{24,16},{32,40},{40,32},{48,56},{56,48},{64,72... | collective-permute-start | bytes 589832 | tf_op jit(solution)/shard_map/ppermute | solution.py:194
  80.8 14.0 %collective-permute-start.15 = (bf16[5,16,6400]{2,1,0:T(8,128)(2,1)S(1)}, bf16[5,16,6400]{2,1,0:T(8,128)(2,1)S(1)}, u32[]{:S(2)}, u32[]{:S(2)}) collective-permute-start(bf16[5,16,6400]{2,1,0:T(8,128)(2,1)S(1)} %get-tuple-element.24), channel_id=1, source_target_pairs={{0,8},{8,0},{16,24},{24,16},{32,40},{40,32},{48,56},{56,48},{64,72... | collective-permute-start | bytes 3072008 | tf_op jit(solution)/shard_map/ppermute | solution.py:249
  83.3 3.1 %collective-permute-start.16 = (bf16[3,16,6400]{2,1,0:T(8,128)(2,1)S(1)}, bf16[3,16,6400]{2,1,0:T(8,128)(2,1)S(1)}, u32[]{:S(2)}, u32[]{:S(2)}) collective-permute-start(bf16[3,16,6400]{2,1,0:T(8,128)(2,1)S(1)} %get-tuple-element.27), channel_id=1, source_target_pairs={{0,8},{8,0},{16,24},{24,16},{32,40},{40,32},{48,56},{56,48},{64,72... | collective-permute-start | bytes 1843208 | tf_op jit(solution)/shard_map/ppermute | solution.py:249
  86.5 10.3 %collective-permute-start.17 = (bf16[16,6400]{1,0:T(8,128)(2,1)S(1)}, bf16[16,6400]{1,0:T(8,128)(2,1)S(1)}, u32[]{:S(2)}, u32[]{:S(2)}) collective-permute-start(bf16[16,6400]{1,0:T(8,128)(2,1)S(1)} %get-tuple-element.28), channel_id=1, source_target_pairs={{0,96},{8,104},{16,112},{24,120},{32,64},{40,72},{48,80},{56,88},{... | collective-permute-start | bytes 614408 | tf_op jit(solution)/shard_map/ppermute | solution.py:250
  89.7 11.6 %collective-permute-start.18 = (bf16[16,6400]{1,0:T(8,128)(2,1)S(1)}, bf16[16,6400]{1,0:T(8,128)(2,1)S(1)}, u32[]{:S(2)}, u32[]{:S(2)}) collective-permute-start(bf16[16,6400]{1,0:T(8,128)(2,1)S(1)} %get-tuple-element.29), channel_id=1, source_target_pairs={{0,80},{8,88},{16,96},{24,104},{32,112},{40,120},{48,64},{56,72},{... | collective-permute-start | bytes 614408 | tf_op jit(solution)/shard_map/ppermute | solution.py:250
  92.8 13.6 %collective-permute-start.19 = (bf16[16,6400]{1,0:T(8,128)(2,1)S(1)}, bf16[16,6400]{1,0:T(8,128)(2,1)S(1)}, u32[]{:S(2)}, u32[]{:S(2)}) collective-permute-start(bf16[16,6400]{1,0:T(8,128)(2,1)S(1)} %get-tuple-element.30), channel_id=1, source_target_pairs={{0,112},{8,120},{16,64},{24,72},{32,80},{40,88},{48,96},{56,104},{... | collective-permute-start | bytes 614408 | tf_op jit(solution)/shard_map/ppermute | solution.py:250
  95.0 11.3 %collective-permute-start.20 = (bf16[16,6400]{1,0:T(8,128)(2,1)S(1)}, bf16[16,6400]{1,0:T(8,128)(2,1)S(1)}, u32[]{:S(2)}, u32[]{:S(2)}) collective-permute-start(bf16[16,6400]{1,0:T(8,128)(2,1)S(1)} %get-tuple-element.31), channel_id=1, source_target_pairs={{0,32},{8,40},{16,48},{24,56},{32,0},{40,8},{48,16},{56,24},{64,96... | collective-permute-start | bytes 614408 | tf_op jit(solution)/shard_map/ppermute | solution.py:250
  95.5 14.2 %collective-permute-start.21 = (bf16[16,6400]{1,0:T(8,128)(2,1)S(1)}, bf16[16,6400]{1,0:T(8,128)(2,1)S(1)}, u32[]{:S(2)}, u32[]{:S(2)}) collective-permute-start(bf16[16,6400]{1,0:T(8,128)(2,1)S(1)} %get-tuple-element.32), channel_id=1, source_target_pairs={{0,64},{8,72},{16,80},{24,88},{32,96},{40,104},{48,112},{56,120},{... | collective-permute-start | bytes 614408 | tf_op jit(solution)/shard_map/ppermute | solution.py:250
  96.9 13.8 %collective-permute-start.22 = (bf16[16,6400]{1,0:T(8,128)(2,1)S(1)}, bf16[16,6400]{1,0:T(8,128)(2,1)S(1)}, u32[]{:S(2)}, u32[]{:S(2)}) collective-permute-start(bf16[16,6400]{1,0:T(8,128)(2,1)S(1)} %get-tuple-element.33), channel_id=1, source_target_pairs={{0,16},{8,24},{16,32},{24,40},{32,48},{40,56},{48,0},{56,8},{64,80... | collective-permute-start | bytes 614408 | tf_op jit(solution)/shard_map/ppermute | solution.py:250
  101.4 10.4 %collective-permute-start.23 = (bf16[16,6400]{1,0:T(8,128)(2,1)S(1)}, bf16[16,6400]{1,0:T(8,128)(2,1)S(1)}, u32[]{:S(2)}, u32[]{:S(2)}) collective-permute-start(bf16[16,6400]{1,0:T(8,128)(2,1)S(1)} %get-tuple-element.34), channel_id=1, source_target_pairs={{0,48},{8,56},{16,0},{24,8},{32,16},{40,24},{48,32},{56,40},{64,11... | collective-permute-start | bytes 614408 | tf_op jit(solution)/shard_map/ppermute | solution.py:250
  (6 other events, 134.6 us)

commit v9 on v6

--- a/solution.py
+++ b/solution.py
@@ -12,10 +12,10 @@
 ANY = pl.BlockSpec(memory_space=pl.ANY)
 SMEM = pl.BlockSpec(memory_space=pltpu.SMEM)
 VMEM = pl.BlockSpec(memory_space=pltpu.VMEM)
-FIRST = ((0, 2), (1, 0))
-SECOND = ((1, 1), (1, 3))
-THIRD = ((0, 1), (0, 3))
-FORWARD = ((1, 0), (0, 2))
+FIRST = ((1, 0), (0, 2))
+SECOND = ((1, 3), (1, 1))
+THIRD = ((0, 3), (0, 1))
+FORWARD = ((0, 2), (1, 0))
 FARTHEST = (1, 2)
 BLOCK = 128
 
@@ -72,9 +72,11 @@
     return pltpu.CompilerParams(vmem_limit_bytes=mib * 2**20)
 
 
-def stack_kernel(first, second, out):
-    out[0] = first[...]
-    out[1] = second[...]
+def place_kernel(at, shard, *rest):
+    out, sem = rest[-2:]
+    copy = pltpu.make_async_copy(shard, out.at[at], sem)
+    copy.start()
+    copy.wait()
 
 
 def bundle_kernel(_, *refs):
@@ -110,12 +112,24 @@
     loaded[...] = jnp.zeros_like(loaded)
 
 
-def mix_kernel(cols, counts, values, cotangent, weight, bias_rows, *rest):
+def mix_kernel(cols, counts, values, cotangent, weight, bias, *rest):
     pieces, (out, held) = rest[:9], rest[9:]
     slots = values.shape[1]
     chunks, _, _ = out.shape
     width = cotangent.shape[1] // chunks
     rows = values.shape[0] // chunks
+
+    hidden = bias.shape[1]
+    high = bias[...].astype(BF).astype(F32)
+    middle = (bias[...] - high).astype(BF).astype(F32)
+    row = lax.broadcasted_iota(jnp.int32, (16, hidden), 0)
+    parts = jnp.where(row == 1, middle, jnp.where(row == 2, bias[...] - high - middle, 0.0))
+    parts = jnp.where(row == 0, high, parts).astype(BF)
+    place = lax.broadcasted_iota(jnp.int32, (hidden, 256), 1) - lax.axis_index("feat") * hidden
+    place = place == lax.broadcasted_iota(jnp.int32, (hidden, 256), 0)
+    bias_rows = jnp.dot(
+        parts, jnp.where(place, 1.0, 0.0).astype(BF), preferred_element_type=F32
+    ).astype(BF)
 
     first, second, third = pieces[2:4], pieces[4:6], (pieces[6], pieces[8])
     farthest = (pieces[7], pieces[8].at[2])
@@ -129,7 +143,7 @@
         out[j, :, width : 2 * width] = cotangent[:16, j * width : (j + 1) * width]
         out[j, :, 2 * width : 3 * width] = cotangent[16:, j * width : (j + 1) * width]
         out[j, :, 3 * width : 3 * width + 256] = weight[...]
-        out[j, :, 3 * width + 256 :] = bias_rows[...]
+        out[j, :, 3 * width + 256 :] = bias_rows
 
     for j in range(chunks):
         for i in range(rows):
@@ -137,7 +151,7 @@
             count = counts[r]
             parts = []
             for s in range(slots):
-                group, lane = place_of(cols[r, s])
+                group, lane = place_of(cols[s, r])
                 block = held[group, :, pl.ds(lane, BLOCK)]
                 parts.append(jnp.where(s < count, block, jnp.zeros_like(block)))
             total = jnp.dot(
@@ -178,8 +192,9 @@
 
 
 def spread_kernel(
-    cols, counts, values, grads, activation, own1, other1, own2, other2, total
+    cols, counts, values, grads, activation, *rest
 ):
+    groups, total = rest[:-1], rest[-1]
     slots = values.shape[1]
     chunks = grads.shape[0]
     rows = values.shape[0] // chunks
@@ -205,38 +220,38 @@
                 preferred_element_type=F32,
             )
             for s in range(slots):
-                group, lane = place_of(cols[r, s])
+                group, lane = place_of(cols[s, r])
                 group = jnp.where(s < count, group, 16)
                 total[group, :, pl.ds(lane, BLOCK)] += contrib[:, s * BLOCK : (s + 1) * BLOCK]
 
     weight_part = weight_part.astype(BF)
-    for server, to1, to2 in ((0, own1, own2), (1, other1, other2)):
-        nears1 = [node_near(*FARTHEST, server)]
-        nears1 += pair_near(back(SECOND), server) + pair_near(back(THIRD), server)
-        nears2 = pair_near(back(FIRST), server) + [node_near(0, 0, server)]
-        for to, nears in ((to1, nears1), (to2, nears2)):
-            for k, near in enumerate(nears):
-                to[k, :, :nodes] = total[near].astype(BF)
-                to[k, :, nodes:] = weight_part
-
-
-def pair_kernel(own, other, farthest, second, third):
-    def both(k):
-        return (own[k].astype(F32) + other[k].astype(F32)).astype(BF)
-
-    farthest[...] = both(0)
+    for server in range(2):
+        nears = [node_near(*FARTHEST, server)]
+        for steps in (SECOND, THIRD, FIRST):
+            nears += pair_near(back(steps), server)
+        nears.append(node_near(0, 0, server))
+        for group in groups[server::2]:
+            for k in range(group.shape[0]):
+                near = nears.pop(0)
+                group[k, :, :nodes] = total[near].astype(BF)
+                group[k, :, nodes:] = weight_part
+
+
+def both(own, other, k):
+    return own[k].astype(F32) + other[k].astype(F32)
+
+
+def pair_kernel(own, other, _, farthest, second, third, later):
+    farthest[...] = both(own, other, 0).astype(BF)
     for q in range(2):
-        second[q] = both(1 + q)
-        third[q] = both(3 + q)
+        second[q] = both(own, other, 1 + q).astype(BF)
+        third[q] = both(own, other, 3 + q).astype(BF)
 
 
 def merge_kernel(own, other, forwarded, first, stay):
-    def both(k):
-        return own[k].astype(F32) + other[k].astype(F32)
-
-    first[0] = (both(0) + forwarded[...].astype(F32)).astype(BF)
-    first[1] = both(1).astype(BF)
-    stay[...] = both(2).astype(BF)
+    first[0] = (both(own, other, 0) + forwarded[...].astype(F32)).astype(BF)
+    first[1] = both(own, other, 1).astype(BF)
+    stay[...] = both(own, other, 2).astype(BF)
 
 
 def hand_kernel(first, second, third, out):
@@ -256,28 +271,26 @@
     fin, nodes = features.shape
     width = nodes // 8
 
+    block_cols = block_cols.T
+
     def shape(dims, kind=BF):
         return jax.ShapeDtypeStruct(dims, kind)
 
-    bias_at = lax.dynamic_update_slice(
-        jnp.zeros((1, 256), F32), bias[None, :], (0, lax.axis_index("feat") * bias.shape[0])
-    )
-    high = lax.reduce_precision(bias_at, 8, 7)
-    middle = lax.reduce_precision(bias_at - high, 8, 7)
-    bias_rows = jnp.concatenate(
-        [high, middle, bias_at - high - middle, jnp.zeros((13, 256), F32)], axis=0
-    ).astype(BF)
-
     swap = node_pairs(0, 0, 1)
     pieces = [features, lax.ppermute(features, "node", swap)]
-    pair = pl.pallas_call(
-        stack_kernel,
-        in_specs=[VMEM] * 2,
-        out_specs=VMEM,
-        out_shape=shape((2, fin, nodes)),
-        compiler_params=params(4),
-        name="stack",
-    )(*pieces)
+    pair = features
+    for at, shard in enumerate(pieces):
+        pair = pl.pallas_call(
+            functools.partial(place_kernel, at),
+            in_specs=[ANY] * (1 + at),
+            out_specs=ANY,
+            out_shape=shape((2, fin, nodes)),
+            scratch_shapes=[pltpu.SemaphoreType.DMA],
+            input_output_aliases={1: 0} if at else {},
+            compiler_params=params(4),
+            name="place",
+        )(*([shard, pair][: 1 + at]))
+
     def send(piece, steps):
         return lax.ppermute(piece, "node", shared_pairs(steps))
 
@@ -293,7 +306,7 @@
     forwarded = send(picked, FORWARD)
     values, loaded = pl.pallas_call(
         load_kernel,
-        in_specs=[pl.BlockSpec(memory_space=pltpu.HBM)] + [ANY] * 3,
+        in_specs=[pl.BlockSpec(memory_space=pltpu.HBM), ANY],
         out_specs=[VMEM, VMEM],
         out_shape=[pltpu.VMEM(block_values.shape, BF), shape((8, 128), F32)],
         scratch_shapes=[pltpu.SemaphoreType.DMA((8,))],
@@ -305,8 +318,6 @@
     )(
         pltpu.with_memory_space_constraint(block_values, pltpu.HBM),
         picked,
-        bias_rows,
-        block_cols,
     )
 
     def bundle(*parts):
@@ -331,7 +342,7 @@
         scratch_shapes=[pltpu.VMEM((16, fin, nodes), BF)],
         compiler_params=params(16),
         name="mix",
-    )(block_cols, block_counts, values, cotangent, weight, bias_rows, *pieces)
+    )(block_cols, block_counts, values, cotangent, weight, bias[None, :], *pieces)
 
     both = lax.all_to_all(mixed, "feat", 0, 0, tiled=True)
 
@@ -352,25 +363,25 @@
         in_specs=[SMEM, SMEM] + [VMEM] * 2,
         out_specs=[VMEM] * 5,
         out_shape=[shape((32, nodes))]
-        + [shape((5, 16, wide))] * 2
-        + [shape((3, 16, wide))] * 2,
+        + [shape((count, 16, wide)) for count in (5, 3) for _ in range(2)],
         scratch_shapes=[pltpu.VMEM((17, fin, nodes), F32)],
         compiler_params=params(24),
         name="spread",
     )(block_cols, block_counts, values, grads)
 
     other1 = lax.ppermute(other1, "node", swap)
-    other2 = lax.ppermute(other2, "node", swap)
-    farthest, second, third = pl.pallas_call(
+    farthest, second, third, other2 = pl.pallas_call(
         pair_kernel,
-        in_specs=[VMEM] * 2,
-        out_specs=[VMEM] * 3,
-        out_shape=[shape((16, wide))] + [shape((2, 16, wide))] * 2,
+        in_specs=[VMEM, VMEM, ANY],
+        out_specs=[VMEM, VMEM, VMEM, ANY],
+        out_shape=[shape((16, wide))] + [shape((2, 16, wide))] * 2 + [shape((3, 16, wide))],
+        input_output_aliases={2: 3},
         compiler_params=params(16),
         name="pair",
-    )(own1, other1)
+    )(own1, other1, other2)
     forwarded = send(farthest, back(FORWARD))
     second, third = send(second, back(SECOND)), send(third, back(THIRD))
+    other2 = lax.ppermute(other2, "node", swap)
     first, stay = pl.pallas_call(
         merge_kernel,
         in_specs=[VMEM] * 3,

time: 105 us -> 101 us (0.962)
  local copies, waits for them, and re-layouts: 2.61 us -> 0.96 us
  waiting for transfers between devices: 24.2 us -> 22.6 us
    ppermute x8, starting transfers between devices: 21.8 us -> 18.3 us  [send(): return lax.ppermute(piece, 'node', shared_pairs(steps))]
    ppermute x1, starting transfers between devices: 0.75 us -> 2.71 us  [local(): lax.ppermute(bundle(third, forwarded), 'node', swap)]
    ppermute x1, waiting for transfers between devices: 1.28 us -> 0.05 us  [local(): pieces = [features, lax.ppermute(features, 'node', swap)]]
    ppermute x1, starting transfers between devices: 0.09 us -> 1.29 us  [local(): handed = lax.ppermute(handed, 'node', swap)]
  transfers between devices with their start and end apart: 15 -> 15, of which waited for: 10 -> 10; matrix products, arithmetic and copies ran while one was open for 2% -> 0% of each run, Pallas kernels for 7% -> 7%
where the time goes in v9:
time: 101 us
  blocking collectives  29.4 us (29%)
  starting transfers between devices  27.3 us (27%)
  waiting for transfers between devices  22.6 us (22%)
  Pallas kernels  20 us (20%)
    ppermute x8, starting transfers between devices, send(): return lax.ppermute(piece, 'node', shared_pairs(steps))  18.3 us
    ppermute x8, waiting for transfers between devices, send(): return lax.ppermute(piece, 'node', shared_pairs(steps))  17.1 us
    all_to_all x1, blocking collectives, local(): both = lax.all_to_all(mixed, 'feat', 0, 0, tiled=True)  16.1 us
    all_to_all x1, blocking collectives, local(): grads = lax.all_to_all(dense, 'feat', 0, 0, tiled=True)  13.4 us
    pallas_call x1, Pallas kernels, local(): pl.pallas_call(spread_kernel, in_specs=[SMEM, SMEM] + [VMEM] * 2, out_spe...  7.1 us
    pallas_call x1, Pallas kernels, local(): pl.pallas_call(load_kernel, in_specs=[pl.BlockSpec(memory_space=pltpu.HBM...  6.52 us
    pallas_call x1, Pallas kernels, local(): pl.pallas_call(mix_kernel, in_specs=[SMEM, SMEM] + [VMEM] * 13, out_specs...  3.74 us
    ppermute x1, starting transfers between devices, local(): lax.ppermute(bundle(third, forwarded), 'node', swap)  2.71 us
  transfers between devices with their start and end apart: 15, of which 10 were waited for; matrix products, arithmetic and copies ran while one was open for 0% of the time, Pallas kernels for 7%

profile of v9, /device:TPU:1, one launch (start us, length us, event | category | flops | bytes accessed | tf_op | source)
XLA Modules:
  0.0 101.0 jit_solution(14983282875735170682)
XLA Ops:
  0.6 1.5 %collective-permute-start = (bf16[16,6144]{1,0:T(8,128)(2,1)}, bf16[16,6144]{1,0:T(8,128)(2,1)S(1)}, u32[]{:S(2)}, u32[]{:S(2)}) collective-permute-start(bf16[16,6144]{1,0:T(8,128)(2,1)} %rest_0_.1), channel_id=1, source_target_pairs={{0,8},{8,0},{16,24},{24,16},{32,40},{40,32},{48,56},{56,48},{64,72... | collective-permute-start | bytes 589832 | tf_op jit(solution)/shard_map/ppermute | solution.py:280
  2.1 0.9 copy-done
  3.7 3.8 %collective-permute-start.1 = (bf16[2,16,6144]{2,1,0:T(8,128)(2,1)S(1)}, bf16[2,16,6144]{2,1,0:T(8,128)(2,1)S(1)}, u32[]{:S(2)}, u32[]{:S(2)}) collective-permute-start(bf16[2,16,6144]{2,1,0:T(8,128)(2,1)S(1)} %place.3), channel_id=1, source_target_pairs={{0,64},{8,40},{16,80},{24,56},{32,96},{40,8},{48,112},{56,24},{64,... | collective-permute-start | bytes 1179656 | tf_op jit(solution)/shard_map/ppermute | solution.py:295
  8.2 2.5 %collective-permute-start.3 = (bf16[2,16,6144]{2,1,0:T(8,128)(2,1)S(1)}, bf16[2,16,6144]{2,1,0:T(8,128)(2,1)S(1)}, u32[]{:S(2)}, u32[]{:S(2)}) collective-permute-start(bf16[2,16,6144]{2,1,0:T(8,128)(2,1)S(1)} %place.3), channel_id=1, source_target_pairs={{0,112},{8,88},{16,64},{24,104},{32,80},{40,120},{48,96},{56,72},{... | collective-permute-start | bytes 1179656 | tf_op jit(solution)/shard_map/ppermute | solution.py:295
  10.6 2.4 %collective-permute-done.1.pair.rest_2_ = bf16[2,16,6144]{2,1,0:T(8,128)(2,1)S(1)} collective-permute-done((bf16[2,16,6144]{2,1,0:T(8,128)(2,1)S(1)}, bf16[2,16,6144]{2,1,0:T(8,128)(2,1)S(1)}, u32[]{:S(2)}, u32[]{:S(2)}) %collective-permute-start.1) | collective-permute-done | bytes 393248 | tf_op jit(solution)/shard_map/ppermute | solution.py:295
  13.0 2.9 %collective-permute-start.6 = (bf16[16,6144]{1,0:T(8,128)(2,1)S(1)}, bf16[16,6144]{1,0:T(8,128)(2,1)S(1)}, u32[]{:S(2)}, u32[]{:S(2)}) collective-permute-start(bf16[16,6144]{1,0:T(8,128)(2,1)S(1)} %pick.1.rest_0_), channel_id=1, source_target_pairs={{0,32},{8,72},{16,48},{24,88},{32,0},{40,104},{48,16},{56,120},{64... | collective-permute-start | bytes 589832 | tf_op jit(solution)/shard_map/ppermute | solution.py:295
  15.9 6.5 %load.1 = (bf16[48,12,128,128]{3,2,1,0:T(8,128)(2,1)S(1)}, f32[8,128]{1,0:T(8,128)S(1)}) custom-call(bf16[48,12,128,128]{3,2,1,0:T(8,128)(2,1)} %values.1, bf16[16,6144]{1,0:T(8,128)(2,1)S(1)} %pick.1.rest_0_), custom_call_target="tpu_custom_call" | custom-call | bytes 37748736 | tf_op jit(solution)/shard_map/load/pallas_call | solution.py:307
  22.8 2.7 %collective-permute-start.7 = (bf16[3,16,6144]{2,1,0:T(8,128)(2,1)S(1)}, bf16[3,16,6144]{2,1,0:T(8,128)(2,1)S(1)}, u32[]{:S(2)}, u32[]{:S(2)}) collective-permute-start(bf16[3,16,6144]{2,1,0:T(8,128)(2,1)S(1)} %bundle.3), channel_id=1, source_target_pairs={{0,8},{8,0},{16,24},{24,16},{32,40},{40,32},{48,56},{56,48},{64,72... | collective-permute-start | bytes 1769480 | tf_op jit(solution)/shard_map/ppermute | solution.py:335
  26.2 1.6 %collective-permute-done.2.rest_3_ = bf16[2,16,6144]{2,1,0:T(8,128)(2,1)S(1)} collective-permute-done((bf16[2,16,6144]{2,1,0:T(8,128)(2,1)S(1)}, bf16[2,16,6144]{2,1,0:T(8,128)(2,1)S(1)}, u32[]{:S(2)}, u32[]{:S(2)}) %collective-permute-start.2) | collective-permute-done | bytes 393248 | tf_op jit(solution)/shard_map/ppermute | solution.py:333
  28.3 3.7 %mix.1 = bf16[8,16,2816]{2,1,0:T(8,128)(2,1)S(1)} custom-call(s32[12,48]{1,0:T(8,128)S(1)} %bitcast.3, s32[48]{0:T(128)S(1)} %copy-done.6, bf16[48,12,128,128]{3,2,1,0:T(8,128)(2,1)S(1)} %get-tuple-element.18.values, bf16[32,6144]{1,0:T(8,128)(2,1)S(1)} %copy-done.2, bf16[16,256]{1,0:T(8,128)(2,1)S(1)} %copy-done.5, f32[1,32]{1,0:T(1,128)S(1)} %bitcast.6, ...), custom_call_target="tpu_custom_call" | custom-call | tf_op jit(solution)/shard_map/mix/pallas_call | solution.py:337
  32.1 16.1 %all_to_all.10.both = bf16[8,16,2816]{2,1,0:T(8,128)(2,1)S(1)} all-to-all(bf16[8,16,2816]{2,1,0:T(8,128)(2,1)S(1)} %mix.1), channel_id=1, replica_groups=mesh['node'=16,'feat'=8] {'feat'}, dimensions={0} | all-to-all | bytes 1441792 | tf_op jit(solution)/shard_map/all_to_all | solution.py:347
  48.9 13.4 %all_to_all.11.grads = bf16[8,16,2560]{2,1,0:T(8,128)(2,1)S(1)} all-to-all(bf16[8,16,2560]{2,1,0:T(8,128)(2,1)S(1)} %dense.1), channel_id=1, replica_groups=mesh['node'=16,'feat'=8] {'feat'}, dimensions={0} | all-to-all | bytes 1310720 | tf_op jit(solution)/shard_map/all_to_all | solution.py:358
  62.2 7.1 %spread.1 = (bf16[32,6144]{1,0:T(8,128)(2,1)}, bf16[5,16,6400]{2,1,0:T(8,128)(2,1)S(1)}, bf16[5,16,6400]{2,1,0:T(8,128)(2,1)S(1)}, bf16[3,16,6400]{2,1,0:T(8,128)(2,1)S(1)}, bf16[3,16,6400]{2,1,0:T(8,128)(2,1)S(1)}) custom-call(s32[12,48]{1,0:T(8,128)S(1)} %bitcast.4, s32[48]{0:T(128)S(1)} %copy-done.6, ...), custom_call_target="tpu_custom_call" | custom-call | tf_op jit(solution)/shard_map/spread/pallas_call | solution.py:361
  69.3 2.5 %collective-permute-start.8 = (bf16[5,16,6400]{2,1,0:T(8,128)(2,1)S(1)}, bf16[5,16,6400]{2,1,0:T(8,128)(2,1)S(1)}, u32[]{:S(2)}, u32[]{:S(2)}) collective-permute-start(bf16[5,16,6400]{2,1,0:T(8,128)(2,1)S(1)} %get-tuple-element.23), channel_id=1, source_target_pairs={{0,8},{8,0},{16,24},{24,16},{32,40},{40,32},{48,56},{56,48},{64,72... | collective-permute-start | bytes 3072008 | tf_op jit(solution)/shard_map/ppermute | solution.py:372
  71.8 2.3 %collective-permute-done.8.other = bf16[5,16,6400]{2,1,0:T(8,128)(2,1)S(1)} collective-permute-done((bf16[5,16,6400]{2,1,0:T(8,128)(2,1)S(1)}, bf16[5,16,6400]{2,1,0:T(8,128)(2,1)S(1)}, u32[]{:S(2)}, u32[]{:S(2)}) %collective-permute-start.8) | collective-permute-done | bytes 1024032 | tf_op jit(solution)/shard_map/ppermute | solution.py:372
  74.8 2.4 %collective-permute-start.10 = (bf16[16,6400]{1,0:T(8,128)(2,1)S(1)}, bf16[16,6400]{1,0:T(8,128)(2,1)S(1)}, u32[]{:S(2)}, u32[]{:S(2)}) collective-permute-start(bf16[16,6400]{1,0:T(8,128)(2,1)S(1)} %get-tuple-element.26), channel_id=1, source_target_pairs={{0,32},{8,72},{16,48},{24,88},{32,0},{40,104},{48,16},{56,120},{64... | collective-permute-start | bytes 614408 | tf_op jit(solution)/shard_map/ppermute | solution.py:295
  77.2 4.4 %collective-permute-start.12 = (bf16[2,16,6400]{2,1,0:T(8,128)(2,1)S(1)}, bf16[2,16,6400]{2,1,0:T(8,128)(2,1)S(1)}, u32[]{:S(2)}, u32[]{:S(2)}) collective-permute-start(bf16[2,16,6400]{2,1,0:T(8,128)(2,1)S(1)} %get-tuple-element.29), channel_id=1, source_target_pairs={{0,80},{8,120},{16,96},{24,72},{32,112},{40,88},{48,64},{56,104},{... | collective-permute-start | bytes 1228808 | tf_op jit(solution)/shard_map/ppermute | solution.py:295
  81.9 1.5 %collective-permute-start.11 = (bf16[2,16,6400]{2,1,0:T(8,128)(2,1)S(1)}, bf16[2,16,6400]{2,1,0:T(8,128)(2,1)S(1)}, u32[]{:S(2)}, u32[]{:S(2)}) collective-permute-start(bf16[2,16,6400]{2,1,0:T(8,128)(2,1)S(1)} %get-tuple-element.28), channel_id=1, source_target_pairs={{0,64},{8,40},{16,80},{24,56},{32,96},{40,8},{48,112},{56,24},{64,... | collective-permute-start | bytes 1228808 | tf_op jit(solution)/shard_map/ppermute | solution.py:295
  83.4 6.3 %collective-permute-done.12.second = bf16[2,16,6400]{2,1,0:T(8,128)(2,1)S(1)} collective-permute-done((bf16[2,16,6400]{2,1,0:T(8,128)(2,1)S(1)}, bf16[2,16,6400]{2,1,0:T(8,128)(2,1)S(1)}, u32[]{:S(2)}, u32[]{:S(2)}) %collective-permute-start.12) | collective-permute-done | bytes 409632 | tf_op jit(solution)/shard_map/ppermute | solution.py:295
  89.7 2.6 %collective-permute-done.13.third = bf16[2,16,6400]{2,1,0:T(8,128)(2,1)S(1)} collective-permute-done((bf16[2,16,6400]{2,1,0:T(8,128)(2,1)S(1)}, bf16[2,16,6400]{2,1,0:T(8,128)(2,1)S(1)}, u32[]{:S(2)}, u32[]{:S(2)}) %collective-permute-start.13) | collective-permute-done | bytes 409632 | tf_op jit(solution)/shard_map/ppermute | solution.py:295
  92.3 5.5 %collective-permute-done.11.first = bf16[2,16,6400]{2,1,0:T(8,128)(2,1)S(1)} collective-permute-done((bf16[2,16,6400]{2,1,0:T(8,128)(2,1)S(1)}, bf16[2,16,6400]{2,1,0:T(8,128)(2,1)S(1)}, u32[]{:S(2)}, u32[]{:S(2)}) %collective-permute-start.11) | collective-permute-done | bytes 409632 | tf_op jit(solution)/shard_map/ppermute | solution.py:295
  97.9 1.3 %collective-permute-start.14 = (bf16[16,6400]{1,0:T(8,128)(2,1)S(1)}, bf16[16,6400]{1,0:T(8,128)(2,1)S(1)}, u32[]{:S(2)}, u32[]{:S(2)}) collective-permute-start(bf16[16,6400]{1,0:T(8,128)(2,1)S(1)} %hand.1), channel_id=1, source_target_pairs={{0,8},{8,0},{16,24},{24,16},{32,40},{40,32},{48,56},{56,48},{64,72... | collective-permute-start | bytes 614408 | tf_op jit(solution)/shard_map/ppermute | solution.py:402
  99.1 1.1 %collective-permute-done.14.handed = bf16[16,6400]{1,0:T(8,128)(2,1)S(1)} collective-permute-done((bf16[16,6400]{1,0:T(8,128)(2,1)S(1)}, bf16[16,6400]{1,0:T(8,128)(2,1)S(1)}, u32[]{:S(2)}, u32[]{:S(2)}) %collective-permute-start.14) | collective-permute-done | bytes 204832 | tf_op jit(solution)/shard_map/ppermute | solution.py:402
  100.2 0.8 last.1
  (37 shorter events, 4.7 us)
Async XLA Ops:
  0.6 2.8 %collective-permute-start = (bf16[16,6144]{1,0:T(8,128)(2,1)}, bf16[16,6144]{1,0:T(8,128)(2,1)S(1)}, u32[]{:S(2)}, u32[]{:S(2)}) collective-permute-start(bf16[16,6144]{1,0:T(8,128)(2,1)} %rest_0_.1), channel_id=1, source_target_pairs={{0,8},{8,0},{16,24},{24,16},{32,40},{40,32},{48,56},{56,48},{64,72... | collective-permute-start | bytes 589832 | tf_op jit(solution)/shard_map/ppermute | solution.py:280
  2.1 0.9 copy-start
  3.1 25.2 %copy-start.1 = (bf16[16,6144]{1,0:T(8,128)(2,1)S(1)}, bf16[16,6144]{1,0:T(8,128)(2,1)}, u32[]{:S(2)}) copy-start(bf16[16,6144]{1,0:T(8,128)(2,1)} %rest_0_.1) | copy-start | bytes 589828
  3.1 25.2 %copy-start.2 = (bf16[32,6144]{1,0:T(8,128)(2,1)S(1)}, bf16[32,6144]{1,0:T(8,128)(2,1)}, u32[]{:S(2)}) copy-start(bf16[32,6144]{1,0:T(8,128)(2,1)} %cotangent.1) | copy-start | bytes 1179652
  3.1 25.2 %copy-start.3 = (s32[48,12]{0,1:T(8,128)S(1)}, s32[48,12]{0,1:T(8,128)}, u32[]{:S(2)}) copy-start(s32[48,12]{0,1:T(8,128)} %param.12) | copy-start | bytes 6916
  3.1 25.2 %copy-start.5 = (bf16[16,256]{1,0:T(8,128)(2,1)S(1)}, bf16[16,256]{1,0:T(8,128)(2,1)}, u32[]{:S(2)}) copy-start(bf16[16,256]{1,0:T(8,128)(2,1)} %weight.1) | copy-start | bytes 24580
  3.1 25.3 %copy-start.6 = (s32[48]{0:T(128)S(1)}, s32[48]{0:T(128)}, u32[]{:S(2)}) copy-start(s32[48]{0:T(128)} %counts.3) | copy-start | bytes 580
  3.1 25.3 %copy-start.7 = (f32[32]{0:T(128)S(1)}, f32[32]{0:T(128)}, u32[]{:S(2)}) copy-start(f32[32]{0:T(128)} %param.10) | copy-start | bytes 388
  3.7 9.3 %collective-permute-start.1 = (bf16[2,16,6144]{2,1,0:T(8,128)(2,1)S(1)}, bf16[2,16,6144]{2,1,0:T(8,128)(2,1)S(1)}, u32[]{:S(2)}, u32[]{:S(2)}) collective-permute-start(bf16[2,16,6144]{2,1,0:T(8,128)(2,1)S(1)} %place.3), channel_id=1, source_target_pairs={{0,64},{8,40},{16,80},{24,56},{32,96},{40,8},{48,112},{56,24},{64,... | collective-permute-start | bytes 1179656 | tf_op jit(solution)/shard_map/ppermute | solution.py:295
  7.4 15.1 %collective-permute-start.5 = (bf16[2,16,6144]{2,1,0:T(8,128)(2,1)S(1)}, bf16[2,16,6144]{2,1,0:T(8,128)(2,1)S(1)}, u32[]{:S(2)}, u32[]{:S(2)}) collective-permute-start(bf16[2,16,6144]{2,1,0:T(8,128)(2,1)S(1)} %place.3), channel_id=1, source_target_pairs={{0,48},{8,24},{16,0},{24,40},{32,16},{40,56},{48,32},{56,8},{64,11... | collective-permute-start | bytes 1179656 | tf_op jit(solution)/shard_map/ppermute | solution.py:295
  8.2 17.5 %collective-permute-start.3 = (bf16[2,16,6144]{2,1,0:T(8,128)(2,1)S(1)}, bf16[2,16,6144]{2,1,0:T(8,128)(2,1)S(1)}, u32[]{:S(2)}, u32[]{:S(2)}) collective-permute-start(bf16[2,16,6144]{2,1,0:T(8,128)(2,1)S(1)} %place.3), channel_id=1, source_target_pairs={{0,112},{8,88},{16,64},{24,104},{32,80},{40,120},{48,96},{56,72},{... | collective-permute-start | bytes 1179656 | tf_op jit(solution)/shard_map/ppermute | solution.py:295
  13.0 35.1 %copy-start.4 = (s32[6144]{0:T(1024)S(1)}, s32[6144]{0:T(1024)}, u32[]{:S(2)}) copy-start(s32[6144]{0:T(1024)} %param.14) | copy-start | bytes 73732
  13.0 9.8 %collective-permute-start.6 = (bf16[16,6144]{1,0:T(8,128)(2,1)S(1)}, bf16[16,6144]{1,0:T(8,128)(2,1)S(1)}, u32[]{:S(2)}, u32[]{:S(2)}) collective-permute-start(bf16[16,6144]{1,0:T(8,128)(2,1)S(1)} %pick.1.rest_0_), channel_id=1, source_target_pairs={{0,32},{8,72},{16,48},{24,88},{32,0},{40,104},{48,16},{56,120},{64... | collective-permute-start | bytes 589832 | tf_op jit(solution)/shard_map/ppermute | solution.py:295
  22.8 5.5 %collective-permute-start.7 = (bf16[3,16,6144]{2,1,0:T(8,128)(2,1)S(1)}, bf16[3,16,6144]{2,1,0:T(8,128)(2,1)S(1)}, u32[]{:S(2)}, u32[]{:S(2)}) collective-permute-start(bf16[3,16,6144]{2,1,0:T(8,128)(2,1)S(1)} %bundle.3), channel_id=1, source_target_pairs={{0,8},{8,0},{16,24},{24,16},{32,40},{40,32},{48,56},{56,48},{64,72... | collective-permute-start | bytes 1769480 | tf_op jit(solution)/shard_map/ppermute | solution.py:335
  25.5 2.2 %collective-permute-start.2 = (bf16[2,16,6144]{2,1,0:T(8,128)(2,1)S(1)}, bf16[2,16,6144]{2,1,0:T(8,128)(2,1)S(1)}, u32[]{:S(2)}, u32[]{:S(2)}) collective-permute-start(bf16[2,16,6144]{2,1,0:T(8,128)(2,1)S(1)} %collective-permute-done.1.pair.rest_2_), channel_id=1, source_target_pairs={{0,8},{8,0},{16,24},{24,16},{32,40},{40,32},{48,56},{56,48},{64,72... | collective-permute-start | bytes 1179656 | tf_op jit(solution)/shard_map/ppermute | solution.py:333
  25.7 2.6 %collective-permute-start.4 = (bf16[2,16,6144]{2,1,0:T(8,128)(2,1)S(1)}, bf16[2,16,6144]{2,1,0:T(8,128)(2,1)S(1)}, u32[]{:S(2)}, u32[]{:S(2)}) collective-permute-start(bf16[2,16,6144]{2,1,0:T(8,128)(2,1)S(1)} %bundle.2), channel_id=1, source_target_pairs={{0,8},{8,0},{16,24},{24,16},{32,40},{40,32},{48,56},{56,48},{64,72... | collective-permute-start | bytes 1179656 | tf_op jit(solution)/shard_map/ppermute | solution.py:334
  69.3 4.7 %collective-permute-start.8 = (bf16[5,16,6400]{2,1,0:T(8,128)(2,1)S(1)}, bf16[5,16,6400]{2,1,0:T(8,128)(2,1)S(1)}, u32[]{:S(2)}, u32[]{:S(2)}) collective-permute-start(bf16[5,16,6400]{2,1,0:T(8,128)(2,1)S(1)} %get-tuple-element.23), channel_id=1, source_target_pairs={{0,8},{8,0},{16,24},{24,16},{32,40},{40,32},{48,56},{56,48},{64,72... | collective-permute-start | bytes 3072008 | tf_op jit(solution)/shard_map/ppermute | solution.py:372
  74.3 7.4 %collective-permute-start.9 = (bf16[3,16,6400]{2,1,0:T(8,128)(2,1)S(1)}, bf16[3,16,6400]{2,1,0:T(8,128)(2,1)S(1)}, u32[]{:S(2)}, u32[]{:S(2)}) collective-permute-start(bf16[3,16,6400]{2,1,0:T(8,128)(2,1)S(1)} %get-tuple-element.25), channel_id=1, source_target_pairs={{0,8},{8,0},{16,24},{24,16},{32,40},{40,32},{48,56},{56,48},{64,72... | collective-permute-start | bytes 1843208 | tf_op jit(solution)/shard_map/ppermute | solution.py:384
  74.8 6.9 %collective-permute-start.10 = (bf16[16,6400]{1,0:T(8,128)(2,1)S(1)}, bf16[16,6400]{1,0:T(8,128)(2,1)S(1)}, u32[]{:S(2)}, u32[]{:S(2)}) collective-permute-start(bf16[16,6400]{1,0:T(8,128)(2,1)S(1)} %get-tuple-element.26), channel_id=1, source_target_pairs={{0,32},{8,72},{16,48},{24,88},{32,0},{40,104},{48,16},{56,120},{64... | collective-permute-start | bytes 614408 | tf_op jit(solution)/shard_map/ppermute | solution.py:295
  77.2 12.5 %collective-permute-start.12 = (bf16[2,16,6400]{2,1,0:T(8,128)(2,1)S(1)}, bf16[2,16,6400]{2,1,0:T(8,128)(2,1)S(1)}, u32[]{:S(2)}, u32[]{:S(2)}) collective-permute-start(bf16[2,16,6400]{2,1,0:T(8,128)(2,1)S(1)} %get-tuple-element.29), channel_id=1, source_target_pairs={{0,80},{8,120},{16,96},{24,72},{32,112},{40,88},{48,64},{56,104},{... | collective-permute-start | bytes 1228808 | tf_op jit(solution)/shard_map/ppermute | solution.py:295
  81.6 10.7 %collective-permute-start.13 = (bf16[2,16,6400]{2,1,0:T(8,128)(2,1)S(1)}, bf16[2,16,6400]{2,1,0:T(8,128)(2,1)S(1)}, u32[]{:S(2)}, u32[]{:S(2)}) collective-permute-start(bf16[2,16,6400]{2,1,0:T(8,128)(2,1)S(1)} %get-tuple-element.30), channel_id=1, source_target_pairs={{0,16},{8,56},{16,32},{24,8},{32,48},{40,24},{48,0},{56,40},{64,80... | collective-permute-start | bytes 1228808 | tf_op jit(solution)/shard_map/ppermute | solution.py:295
  81.9 15.9 %collective-permute-start.11 = (bf16[2,16,6400]{2,1,0:T(8,128)(2,1)S(1)}, bf16[2,16,6400]{2,1,0:T(8,128)(2,1)S(1)}, u32[]{:S(2)}, u32[]{:S(2)}) collective-permute-start(bf16[2,16,6400]{2,1,0:T(8,128)(2,1)S(1)} %get-tuple-element.28), channel_id=1, source_target_pairs={{0,64},{8,40},{16,80},{24,56},{32,96},{40,8},{48,112},{56,24},{64,... | collective-permute-start | bytes 1228808 | tf_op jit(solution)/shard_map/ppermute | solution.py:295
  97.9 2.4 %collective-permute-start.14 = (bf16[16,6400]{1,0:T(8,128)(2,1)S(1)}, bf16[16,6400]{1,0:T(8,128)(2,1)S(1)}, u32[]{:S(2)}, u32[]{:S(2)}) collective-permute-start(bf16[16,6400]{1,0:T(8,128)(2,1)S(1)} %hand.1), channel_id=1, source_target_pairs={{0,8},{8,0},{16,24},{24,16},{32,40},{40,32},{48,56},{56,48},{64,72... | collective-permute-start | bytes 614408 | tf_op jit(solution)/shard_map/ppermute | solution.py:402

commit v10 on v9

--- a/solution.py
+++ b/solution.py
@@ -10,7 +10,7 @@
 BF = jnp.bfloat16
 F32 = jnp.float32
 ANY = pl.BlockSpec(memory_space=pl.ANY)
-SMEM = pl.BlockSpec(memory_space=pltpu.SMEM)
+HBM = pl.BlockSpec(memory_space=pltpu.HBM)
 VMEM = pl.BlockSpec(memory_space=pltpu.VMEM)
 FIRST = ((1, 0), (0, 2))
 SECOND = ((1, 3), (1, 1))
@@ -79,19 +79,7 @@
     copy.wait()
 
 
-def bundle_kernel(_, *refs):
-    pieces, out = refs[:-1], refs[-1]
-    at = 0
-    for piece in pieces:
-        if len(piece.shape) == 3:
-            out[at : at + 2] = piece[...]
-            at += 2
-        else:
-            out[at] = piece[...]
-            at += 1
-
-
-def pick_kernel(pair, out):
+def pick_kernel(pair, _, out):
     out[...] = pair[0]
 
 
@@ -112,8 +100,19 @@
     loaded[...] = jnp.zeros_like(loaded)
 
 
-def mix_kernel(cols, counts, values, cotangent, weight, bias, *rest):
-    pieces, (out, held) = rest[:9], rest[9:]
+def start_small(sources, places, sems):
+    copies = [
+        pltpu.make_async_copy(source, place, sems.at[at])
+        for at, (source, place) in enumerate(zip(sources, places))
+    ]
+    for copy in copies:
+        copy.start()
+    return copies
+
+
+def mix_kernel(cols_in, counts_in, values, cotangent, weight, bias, *rest):
+    pieces, (out, held, cols, counts, sems) = rest[:10], rest[10:]
+    small = start_small((cols_in, counts_in), (cols, counts), sems)
     slots = values.shape[1]
     chunks, _, _ = out.shape
     width = cotangent.shape[1] // chunks
@@ -131,8 +130,7 @@
         parts, jnp.where(place, 1.0, 0.0).astype(BF), preferred_element_type=F32
     ).astype(BF)
 
-    first, second, third = pieces[2:4], pieces[4:6], (pieces[6], pieces[8])
-    farthest = (pieces[7], pieces[8].at[2])
+    first, second, third, farthest = (pieces[at : at + 2] for at in (2, 4, 6, 8))
     for server in range(2):
         held[node_near(0, 0, server)] = pieces[server][...]
         held[node_near(*FARTHEST, server)] = farthest[server][...]
@@ -145,6 +143,8 @@
         out[j, :, 3 * width : 3 * width + 256] = weight[...]
         out[j, :, 3 * width + 256 :] = bias_rows
 
+    for copy in small:
+        copy.wait()
     for j in range(chunks):
         for i in range(rows):
             r = j * rows + i
@@ -192,9 +192,10 @@
 
 
 def spread_kernel(
-    cols, counts, values, grads, activation, *rest
+    cols_in, counts_in, values, grads, activation, *rest
 ):
-    groups, total = rest[:-1], rest[-1]
+    groups, (total, cols, counts, sems) = rest[:-4], rest[-4:]
+    small = start_small((cols_in, counts_in), (cols, counts), sems)
     slots = values.shape[1]
     chunks = grads.shape[0]
     rows = values.shape[0] // chunks
@@ -209,6 +210,8 @@
         activation[16:, at] = grads[j, :, 2 * width + 256 :]
         weight_part += grads[j, :, width : width + 256].astype(F32)
 
+    for copy in small:
+        copy.wait()
     for j in range(chunks):
         for i in range(rows):
             r = j * rows + i
@@ -241,17 +244,21 @@
     return own[k].astype(F32) + other[k].astype(F32)
 
 
-def pair_kernel(own, other, _, farthest, second, third, later):
+def pair_kernel(own, other, _, farthest, second, later):
     farthest[...] = both(own, other, 0).astype(BF)
     for q in range(2):
         second[q] = both(own, other, 1 + q).astype(BF)
-        third[q] = both(own, other, 3 + q).astype(BF)
+
+
+def third_kernel(own, other, third):
+    for q in range(2):
+        third[q] = both(own, other, q).astype(BF)
 
 
 def merge_kernel(own, other, forwarded, first, stay):
-    first[0] = (both(own, other, 0) + forwarded[...].astype(F32)).astype(BF)
-    first[1] = both(own, other, 1).astype(BF)
-    stay[...] = both(own, other, 2).astype(BF)
+    first[0] = (both(own, other, 2) + forwarded[...].astype(F32)).astype(BF)
+    first[1] = both(own, other, 3).astype(BF)
+    stay[...] = both(own, other, 4).astype(BF)
 
 
 def hand_kernel(first, second, third, out):
@@ -271,7 +278,8 @@
     fin, nodes = features.shape
     width = nodes // 8
 
-    block_cols = block_cols.T
+    block_cols = pltpu.with_memory_space_constraint(block_cols.T, pltpu.HBM)
+    block_counts = pltpu.with_memory_space_constraint(block_counts, pltpu.HBM)
 
     def shape(dims, kind=BF):
         return jax.ShapeDtypeStruct(dims, kind)
@@ -295,15 +303,6 @@
         return lax.ppermute(piece, "node", shared_pairs(steps))
 
     first, second, third = (send(pair, steps) for steps in (FIRST, SECOND, THIRD))
-    picked = pl.pallas_call(
-        pick_kernel,
-        in_specs=[VMEM],
-        out_specs=VMEM,
-        out_shape=shape((fin, nodes)),
-        compiler_params=params(4),
-        name="pick",
-    )(first)
-    forwarded = send(picked, FORWARD)
     values, loaded = pl.pallas_call(
         load_kernel,
         in_specs=[pl.BlockSpec(memory_space=pltpu.HBM), ANY],
@@ -315,31 +314,30 @@
             flops=0, bytes_accessed=2 * block_values.size * 2, transcendentals=0
         ),
         name="load",
-    )(
-        pltpu.with_memory_space_constraint(block_values, pltpu.HBM),
-        picked,
-    )
-
-    def bundle(*parts):
-        return pl.pallas_call(
-            bundle_kernel,
-            in_specs=[ANY] + [VMEM] * len(parts),
-            out_specs=VMEM,
-            out_shape=shape((sum(part.ndim - 1 for part in parts), fin, nodes)),
-            compiler_params=params(8),
-            name="bundle",
-        )(loaded, *parts)
-
-    pieces += [first, lax.ppermute(first, "node", swap)]
-    pieces += [second, lax.ppermute(bundle(second), "node", swap)]
-    pieces += [third, forwarded, lax.ppermute(bundle(third, forwarded), "node", swap)]
-
+    )(pltpu.with_memory_space_constraint(block_values, pltpu.HBM), pair)
+    picked = pl.pallas_call(
+        pick_kernel,
+        in_specs=[VMEM, ANY],
+        out_specs=VMEM,
+        out_shape=shape((fin, nodes)),
+        compiler_params=params(4),
+        name="pick",
+    )(first, loaded)
+    forwarded = send(picked, FORWARD)
+    for piece in (first, second, third, forwarded):
+        pieces += [piece, lax.ppermute(piece, "node", swap)]
+
+    index_scratch = [
+        pltpu.SMEM(block_cols.shape, jnp.int32),
+        pltpu.SMEM(block_counts.shape, jnp.int32),
+        pltpu.SemaphoreType.DMA((2,)),
+    ]
     mixed = pl.pallas_call(
         mix_kernel,
-        in_specs=[SMEM, SMEM] + [VMEM] * 13,
+        in_specs=[HBM, HBM] + [VMEM] * 14,
         out_specs=VMEM,
         out_shape=shape((8, 16, 3 * width + 512)),
-        scratch_shapes=[pltpu.VMEM((16, fin, nodes), BF)],
+        scratch_shapes=[pltpu.VMEM((16, fin, nodes), BF)] + index_scratch,
         compiler_params=params(16),
         name="mix",
     )(block_cols, block_counts, values, cotangent, weight, bias[None, :], *pieces)
@@ -360,28 +358,37 @@
     wide = nodes + 256
     activation, own1, other1, own2, other2 = pl.pallas_call(
         spread_kernel,
-        in_specs=[SMEM, SMEM] + [VMEM] * 2,
+        in_specs=[HBM, HBM] + [VMEM] * 2,
         out_specs=[VMEM] * 5,
         out_shape=[shape((32, nodes))]
-        + [shape((count, 16, wide)) for count in (5, 3) for _ in range(2)],
-        scratch_shapes=[pltpu.VMEM((17, fin, nodes), F32)],
+        + [shape((count, 16, wide)) for count in (3, 5) for _ in range(2)],
+        scratch_shapes=[pltpu.VMEM((17, fin, nodes), F32)] + index_scratch,
         compiler_params=params(24),
         name="spread",
     )(block_cols, block_counts, values, grads)
 
     other1 = lax.ppermute(other1, "node", swap)
-    farthest, second, third, other2 = pl.pallas_call(
+    farthest, second, other2 = pl.pallas_call(
         pair_kernel,
         in_specs=[VMEM, VMEM, ANY],
-        out_specs=[VMEM, VMEM, VMEM, ANY],
-        out_shape=[shape((16, wide))] + [shape((2, 16, wide))] * 2 + [shape((3, 16, wide))],
-        input_output_aliases={2: 3},
+        out_specs=[VMEM, VMEM, ANY],
+        out_shape=[shape((16, wide)), shape((2, 16, wide)), shape((5, 16, wide))],
+        input_output_aliases={2: 2},
         compiler_params=params(16),
         name="pair",
     )(own1, other1, other2)
     forwarded = send(farthest, back(FORWARD))
-    second, third = send(second, back(SECOND)), send(third, back(THIRD))
+    second = send(second, back(SECOND))
     other2 = lax.ppermute(other2, "node", swap)
+    third = pl.pallas_call(
+        third_kernel,
+        in_specs=[VMEM] * 2,
+        out_specs=VMEM,
+        out_shape=shape((2, 16, wide)),
+        compiler_params=params(16),
+        name="third",
+    )(own2, other2)
+    third = send(third, back(THIRD))
     first, stay = pl.pallas_call(
         merge_kernel,
         in_specs=[VMEM] * 3,

time: 101 us -> 99 us (0.980)
    ppermute x1, starting transfers between devices: 1.29 us -> 0.09 us  [local(): handed = lax.ppermute(handed, 'node', swap)]
    all_to_all x1, blocking collectives: 13.4 us -> 12.3 us  [local(): grads = lax.all_to_all(dense, 'feat', 0, 0, tiled=True)]
    ppermute x3 -> x4, starting transfers between devices: 3.3 us -> 4.05 us  [local(): pieces += [piece, lax.ppermute(piece, 'node', swap)]]
    pallas_call x5 -> x4, Pallas kernels: 10.9 us -> 10.7 us  [the longest x1 6.88 us: local(): pl.pallas_call(spread_kernel, in_specs=[HBM, HBM] + [VMEM] * 2, out_specs...]
    ppermute x3 -> x4, waiting for transfers between devices: 2.13 us -> 1.93 us  [local(): pieces += [piece, lax.ppermute(piece, 'node', swap)]]
  transfers between devices with their start and end apart: 15 -> 16, of which waited for: 10 -> 12; matrix products, arithmetic and copies ran while one was open for 0% -> 0% of each run, Pallas kernels for 7% -> 7%
where the time goes in v10:
time: 99 us; the launch traced here: 98.8 us
  blocking collectives  28.4 us (29%)
  starting transfers between devices  27.1 us (27%)
  waiting for transfers between devices  21.9 us (22%)
  Pallas kernels  19.6 us (20%)
    ppermute x8, starting transfers between devices, send(): return lax.ppermute(piece, 'node', shared_pairs(steps))  18 us
    ppermute x8, waiting for transfers between devices, send(): return lax.ppermute(piece, 'node', shared_pairs(steps))  16.8 us
    all_to_all x1, blocking collectives, local(): both = lax.all_to_all(mixed, 'feat', 0, 0, tiled=True)  16.1 us
    all_to_all x1, blocking collectives, local(): grads = lax.all_to_all(dense, 'feat', 0, 0, tiled=True)  12.3 us
    pallas_call x1, Pallas kernels, local(): pl.pallas_call(spread_kernel, in_specs=[HBM, HBM] + [VMEM] * 2, out_specs...  6.88 us
    pallas_call x1, Pallas kernels, local(): pl.pallas_call(load_kernel, in_specs=[pl.BlockSpec(memory_space=pltpu.HBM...  6.52 us
    ppermute x4, starting transfers between devices, local(): pieces += [piece, lax.ppermute(piece, 'node', swap)]  4.05 us
    pallas_call x1, Pallas kernels, local(): pl.pallas_call(mix_kernel, in_specs=[HBM, HBM] + [VMEM] * 14, out_specs=V...  3.7 us
  transfers between devices with their start and end apart: 16, of which 12 were waited for; matrix products, arithmetic and copies ran while one was open for 0% of the time, Pallas kernels for 7%

profile of v10, /device:TPU:1, one launch (start us, length us, event | category | flops | bytes accessed | tf_op | source)
XLA Modules:
  0.0 98.8 jit_solution(8791190794571970245)
XLA Ops:
  0.6 1.5 %collective-permute-start = (bf16[16,6144]{1,0:T(8,128)(2,1)}, bf16[16,6144]{1,0:T(8,128)(2,1)S(1)}, u32[]{:S(2)}, u32[]{:S(2)}) collective-permute-start(bf16[16,6144]{1,0:T(8,128)(2,1)} %rest_0_.1), channel_id=1, source_target_pairs={{0,8},{8,0},{16,24},{24,16},{32,40},{40,32},{48,56},{56,48},{64,72... | collective-permute-start | bytes 589832 | tf_op jit(solution)/shard_map/ppermute | solution.py:288
  2.1 0.9 copy-done
  3.7 3.8 %collective-permute-start.1 = (bf16[2,16,6144]{2,1,0:T(8,128)(2,1)S(1)}, bf16[2,16,6144]{2,1,0:T(8,128)(2,1)S(1)}, u32[]{:S(2)}, u32[]{:S(2)}) collective-permute-start(bf16[2,16,6144]{2,1,0:T(8,128)(2,1)S(1)} %place.3.rest_0_), channel_id=1, source_target_pairs={{0,64},{8,40},{16,80},{24,56},{32,96},{40,8},{48,112},{56,24},{64,... | collective-permute-start | bytes 1179656 | tf_op jit(solution)/shard_map/ppermute | solution.py:303
  7.4 0.7 collective-permute-start.5
  8.2 2.5 %collective-permute-start.3 = (bf16[2,16,6144]{2,1,0:T(8,128)(2,1)S(1)}, bf16[2,16,6144]{2,1,0:T(8,128)(2,1)S(1)}, u32[]{:S(2)}, u32[]{:S(2)}) collective-permute-start(bf16[2,16,6144]{2,1,0:T(8,128)(2,1)S(1)} %place.3.rest_0_), channel_id=1, source_target_pairs={{0,112},{8,88},{16,64},{24,104},{32,80},{40,120},{48,96},{56,72},{... | collective-permute-start | bytes 1179656 | tf_op jit(solution)/shard_map/ppermute | solution.py:303
  10.6 6.5 %load.1 = (bf16[48,12,128,128]{3,2,1,0:T(8,128)(2,1)S(1)}, f32[8,128]{1,0:T(8,128)S(1)}) custom-call(bf16[48,12,128,128]{3,2,1,0:T(8,128)(2,1)} %values.1, bf16[2,16,6144]{2,1,0:T(8,128)(2,1)S(1)} %place.3.rest_0_), custom_call_target="tpu_custom_call" | custom-call | bytes 37748736 | tf_op jit(solution)/shard_map/load/pallas_call | solution.py:306
  17.6 4.1 %collective-permute-done.5.rest_6_ = bf16[2,16,6144]{2,1,0:T(8,128)(2,1)S(1)} collective-permute-done((bf16[2,16,6144]{2,1,0:T(8,128)(2,1)S(1)}, bf16[2,16,6144]{2,1,0:T(8,128)(2,1)S(1)}, u32[]{:S(2)}, u32[]{:S(2)}) %collective-permute-start.5) | collective-permute-done | bytes 393248 | tf_op jit(solution)/shard_map/ppermute | solution.py:303
  21.6 3.2 %collective-permute-start.6 = (bf16[2,16,6144]{2,1,0:T(8,128)(2,1)S(1)}, bf16[2,16,6144]{2,1,0:T(8,128)(2,1)S(1)}, u32[]{:S(2)}, u32[]{:S(2)}) collective-permute-start(bf16[2,16,6144]{2,1,0:T(8,128)(2,1)S(1)} %collective-permute-done.5.rest_6_), channel_id=1, source_target_pairs={{0,8},{8,0},{16,24},{24,16},{32,40},{40,32},{48,56},{56,48},{64,72... | collective-permute-start | bytes 1179656 | tf_op jit(solution)/shard_map/ppermute | solution.py:328
  27.6 3.7 %mix.1 = bf16[8,16,2816]{2,1,0:T(8,128)(2,1)S(1)} custom-call(s32[12,48]{1,0:T(8,128)} %bitcast.5, s32[48]{0:T(128)} %counts_in.3, bf16[48,12,128,128]{3,2,1,0:T(8,128)(2,1)S(1)} %get-tuple-element.17.values, bf16[32,6144]{1,0:T(8,128)(2,1)S(1)} %copy-done.2, bf16[16,256]{1,0:T(8,128)(2,1)S(1)} %copy-done.4, f32[1,32]{1,0:T(1,128)S(1)} %bitcast.4, ...), custom_call_target="tpu_custom_call" | custom-call | tf_op jit(solution)/shard_map/mix/pallas_call | solution.py:335
  31.3 16.1 %all_to_all.10.both = bf16[8,16,2816]{2,1,0:T(8,128)(2,1)S(1)} all-to-all(bf16[8,16,2816]{2,1,0:T(8,128)(2,1)S(1)} %mix.1), channel_id=1, replica_groups=mesh['node'=16,'feat'=8] {'feat'}, dimensions={0} | all-to-all | bytes 1441792 | tf_op jit(solution)/shard_map/all_to_all | solution.py:345
  47.4 0.7 dense.1
  48.1 12.3 %all_to_all.11.grads = bf16[8,16,2560]{2,1,0:T(8,128)(2,1)S(1)} all-to-all(bf16[8,16,2560]{2,1,0:T(8,128)(2,1)S(1)} %dense.1), channel_id=1, replica_groups=mesh['node'=16,'feat'=8] {'feat'}, dimensions={0} | all-to-all | bytes 1310720 | tf_op jit(solution)/shard_map/all_to_all | solution.py:356
  60.4 6.9 %spread.1 = (bf16[32,6144]{1,0:T(8,128)(2,1)}, bf16[3,16,6400]{2,1,0:T(8,128)(2,1)S(1)}, bf16[3,16,6400]{2,1,0:T(8,128)(2,1)S(1)}, bf16[5,16,6400]{2,1,0:T(8,128)(2,1)S(1)}, bf16[5,16,6400]{2,1,0:T(8,128)(2,1)S(1)}) custom-call(s32[12,48]{1,0:T(8,128)} %bitcast.6, s32[48]{0:T(128)} %counts_in.3, bf16[48,12,128,128]{3,2,1,0:T(8,128)(2,1)S(1)} %get-tuple-element.17.values, ...), custom_call_target="tpu_custom_call" | custom-call | tf_op jit(solution)/shard_map/spread/pallas_call | solution.py:359
  67.3 3.1 %collective-permute-start.9 = (bf16[3,16,6400]{2,1,0:T(8,128)(2,1)S(1)}, bf16[3,16,6400]{2,1,0:T(8,128)(2,1)S(1)}, u32[]{:S(2)}, u32[]{:S(2)}) collective-permute-start(bf16[3,16,6400]{2,1,0:T(8,128)(2,1)S(1)} %get-tuple-element.22), channel_id=1, source_target_pairs={{0,8},{8,0},{16,24},{24,16},{32,40},{40,32},{48,56},{56,48},{64,72... | collective-permute-start | bytes 1843208 | tf_op jit(solution)/shard_map/ppermute | solution.py:370
  70.4 1.7 %collective-permute-done.9.other = bf16[3,16,6400]{2,1,0:T(8,128)(2,1)S(1)} collective-permute-done((bf16[3,16,6400]{2,1,0:T(8,128)(2,1)S(1)}, bf16[3,16,6400]{2,1,0:T(8,128)(2,1)S(1)}, u32[]{:S(2)}, u32[]{:S(2)}) %collective-permute-start.9) | collective-permute-done | bytes 614432 | tf_op jit(solution)/shard_map/ppermute | solution.py:370
  72.7 2.5 %collective-permute-start.11 = (bf16[16,6400]{1,0:T(8,128)(2,1)S(1)}, bf16[16,6400]{1,0:T(8,128)(2,1)S(1)}, u32[]{:S(2)}, u32[]{:S(2)}) collective-permute-start(bf16[16,6400]{1,0:T(8,128)(2,1)S(1)} %get-tuple-element.25), channel_id=1, source_target_pairs={{0,32},{8,72},{16,48},{24,88},{32,0},{40,104},{48,16},{56,120},{64... | collective-permute-start | bytes 614408 | tf_op jit(solution)/shard_map/ppermute | solution.py:303
  75.2 3.6 %collective-permute-start.13 = (bf16[2,16,6400]{2,1,0:T(8,128)(2,1)S(1)}, bf16[2,16,6400]{2,1,0:T(8,128)(2,1)S(1)}, u32[]{:S(2)}, u32[]{:S(2)}) collective-permute-start(bf16[2,16,6400]{2,1,0:T(8,128)(2,1)S(1)} %get-tuple-element.28), channel_id=1, source_target_pairs={{0,80},{8,120},{16,96},{24,72},{32,112},{40,88},{48,64},{56,104},{... | collective-permute-start | bytes 1228808 | tf_op jit(solution)/shard_map/ppermute | solution.py:303
  79.3 1.2 %collective-permute-start.12 = (bf16[2,16,6400]{2,1,0:T(8,128)(2,1)S(1)}, bf16[2,16,6400]{2,1,0:T(8,128)(2,1)S(1)}, u32[]{:S(2)}, u32[]{:S(2)}) collective-permute-start(bf16[2,16,6400]{2,1,0:T(8,128)(2,1)S(1)} %get-tuple-element.27), channel_id=1, source_target_pairs={{0,64},{8,40},{16,80},{24,56},{32,96},{40,8},{48,112},{56,24},{64,... | collective-permute-start | bytes 1228808 | tf_op jit(solution)/shard_map/ppermute | solution.py:303
  80.6 3.4 %collective-permute-start.14 = (bf16[2,16,6400]{2,1,0:T(8,128)(2,1)S(1)}, bf16[2,16,6400]{2,1,0:T(8,128)(2,1)S(1)}, u32[]{:S(2)}, u32[]{:S(2)}) collective-permute-start(bf16[2,16,6400]{2,1,0:T(8,128)(2,1)S(1)} %third.1), channel_id=1, source_target_pairs={{0,16},{8,56},{16,32},{24,8},{32,48},{40,24},{48,0},{56,40},{64,80... | collective-permute-start | bytes 1228808 | tf_op jit(solution)/shard_map/ppermute | solution.py:303
  83.9 5.9 %collective-permute-done.13.second = bf16[2,16,6400]{2,1,0:T(8,128)(2,1)S(1)} collective-permute-done((bf16[2,16,6400]{2,1,0:T(8,128)(2,1)S(1)}, bf16[2,16,6400]{2,1,0:T(8,128)(2,1)S(1)}, u32[]{:S(2)}, u32[]{:S(2)}) %collective-permute-start.13) | collective-permute-done | bytes 409632 | tf_op jit(solution)/shard_map/ppermute | solution.py:303
  89.8 3.9 %collective-permute-done.12.first = bf16[2,16,6400]{2,1,0:T(8,128)(2,1)S(1)} collective-permute-done((bf16[2,16,6400]{2,1,0:T(8,128)(2,1)S(1)}, bf16[2,16,6400]{2,1,0:T(8,128)(2,1)S(1)}, u32[]{:S(2)}, u32[]{:S(2)}) %collective-permute-start.12) | collective-permute-done | bytes 409632 | tf_op jit(solution)/shard_map/ppermute | solution.py:303
  93.7 2.7 %collective-permute-done.14.third = bf16[2,16,6400]{2,1,0:T(8,128)(2,1)S(1)} collective-permute-done((bf16[2,16,6400]{2,1,0:T(8,128)(2,1)S(1)}, bf16[2,16,6400]{2,1,0:T(8,128)(2,1)S(1)}, u32[]{:S(2)}, u32[]{:S(2)}) %collective-permute-start.14) | collective-permute-done | bytes 409632 | tf_op jit(solution)/shard_map/ppermute | solution.py:303
  96.5 1.4 %collective-permute-done.15.handed = bf16[16,6400]{1,0:T(8,128)(2,1)S(1)} collective-permute-done((bf16[16,6400]{1,0:T(8,128)(2,1)S(1)}, bf16[16,6400]{1,0:T(8,128)(2,1)S(1)}, u32[]{:S(2)}, u32[]{:S(2)}) %collective-permute-start.15) | collective-permute-done | bytes 204832 | tf_op jit(solution)/shard_map/ppermute | solution.py:409
  98.0 0.8 last.1
  (34 shorter events, 5.1 us)
Async XLA Ops:
  0.6 2.8 %collective-permute-start = (bf16[16,6144]{1,0:T(8,128)(2,1)}, bf16[16,6144]{1,0:T(8,128)(2,1)S(1)}, u32[]{:S(2)}, u32[]{:S(2)}) collective-permute-start(bf16[16,6144]{1,0:T(8,128)(2,1)} %rest_0_.1), channel_id=1, source_target_pairs={{0,8},{8,0},{16,24},{24,16},{32,40},{40,32},{48,56},{56,48},{64,72... | collective-permute-start | bytes 589832 | tf_op jit(solution)/shard_map/ppermute | solution.py:288
  2.1 0.9 copy-start
  3.1 24.5 %copy-start.1 = (bf16[16,6144]{1,0:T(8,128)(2,1)S(1)}, bf16[16,6144]{1,0:T(8,128)(2,1)}, u32[]{:S(2)}) copy-start(bf16[16,6144]{1,0:T(8,128)(2,1)} %rest_0_.1) | copy-start | bytes 589828
  3.1 24.5 %copy-start.2 = (bf16[32,6144]{1,0:T(8,128)(2,1)S(1)}, bf16[32,6144]{1,0:T(8,128)(2,1)}, u32[]{:S(2)}) copy-start(bf16[32,6144]{1,0:T(8,128)(2,1)} %cotangent.1) | copy-start | bytes 1179652
  3.1 24.5 %copy-start.4 = (bf16[16,256]{1,0:T(8,128)(2,1)S(1)}, bf16[16,256]{1,0:T(8,128)(2,1)}, u32[]{:S(2)}) copy-start(bf16[16,256]{1,0:T(8,128)(2,1)} %weight.1) | copy-start | bytes 24580
  3.1 24.5 %copy-start.5 = (f32[32]{0:T(128)S(1)}, f32[32]{0:T(128)}, u32[]{:S(2)}) copy-start(f32[32]{0:T(128)} %param.10) | copy-start | bytes 388
  3.7 43.7 %copy-start.3 = (s32[6144]{0:T(1024)S(1)}, s32[6144]{0:T(1024)}, u32[]{:S(2)}) copy-start(s32[6144]{0:T(1024)} %param.14) | copy-start | bytes 73732
  3.7 13.5 %collective-permute-start.1 = (bf16[2,16,6144]{2,1,0:T(8,128)(2,1)S(1)}, bf16[2,16,6144]{2,1,0:T(8,128)(2,1)S(1)}, u32[]{:S(2)}, u32[]{:S(2)}) collective-permute-start(bf16[2,16,6144]{2,1,0:T(8,128)(2,1)S(1)} %place.3.rest_0_), channel_id=1, source_target_pairs={{0,64},{8,40},{16,80},{24,56},{32,96},{40,8},{48,112},{56,24},{64,... | collective-permute-start | bytes 1179656 | tf_op jit(solution)/shard_map/ppermute | solution.py:303
  7.4 14.2 %collective-permute-start.5 = (bf16[2,16,6144]{2,1,0:T(8,128)(2,1)S(1)}, bf16[2,16,6144]{2,1,0:T(8,128)(2,1)S(1)}, u32[]{:S(2)}, u32[]{:S(2)}) collective-permute-start(bf16[2,16,6144]{2,1,0:T(8,128)(2,1)S(1)} %place.3.rest_0_), channel_id=1, source_target_pairs={{0,48},{8,24},{16,0},{24,40},{32,16},{40,56},{48,32},{56,8},{64,11... | collective-permute-start | bytes 1179656 | tf_op jit(solution)/shard_map/ppermute | solution.py:303
  8.2 16.7 %collective-permute-start.3 = (bf16[2,16,6144]{2,1,0:T(8,128)(2,1)S(1)}, bf16[2,16,6144]{2,1,0:T(8,128)(2,1)S(1)}, u32[]{:S(2)}, u32[]{:S(2)}) collective-permute-start(bf16[2,16,6144]{2,1,0:T(8,128)(2,1)S(1)} %place.3.rest_0_), channel_id=1, source_target_pairs={{0,112},{8,88},{16,64},{24,104},{32,80},{40,120},{48,96},{56,72},{... | collective-permute-start | bytes 1179656 | tf_op jit(solution)/shard_map/ppermute | solution.py:303
  17.2 8.2 %collective-permute-start.7 = (bf16[16,6144]{1,0:T(8,128)(2,1)S(1)}, bf16[16,6144]{1,0:T(8,128)(2,1)S(1)}, u32[]{:S(2)}, u32[]{:S(2)}) collective-permute-start(bf16[16,6144]{1,0:T(8,128)(2,1)S(1)} %pick.1), channel_id=1, source_target_pairs={{0,32},{8,72},{16,48},{24,88},{32,0},{40,104},{48,16},{56,120},{64... | collective-permute-start | bytes 589832 | tf_op jit(solution)/shard_map/ppermute | solution.py:303
  21.6 4.6 %collective-permute-start.6 = (bf16[2,16,6144]{2,1,0:T(8,128)(2,1)S(1)}, bf16[2,16,6144]{2,1,0:T(8,128)(2,1)S(1)}, u32[]{:S(2)}, u32[]{:S(2)}) collective-permute-start(bf16[2,16,6144]{2,1,0:T(8,128)(2,1)S(1)} %collective-permute-done.5.rest_6_), channel_id=1, source_target_pairs={{0,8},{8,0},{16,24},{24,16},{32,40},{40,32},{48,56},{56,48},{64,72... | collective-permute-start | bytes 1179656 | tf_op jit(solution)/shard_map/ppermute | solution.py:328
  24.9 1.9 %collective-permute-start.4 = (bf16[2,16,6144]{2,1,0:T(8,128)(2,1)S(1)}, bf16[2,16,6144]{2,1,0:T(8,128)(2,1)S(1)}, u32[]{:S(2)}, u32[]{:S(2)}) collective-permute-start(bf16[2,16,6144]{2,1,0:T(8,128)(2,1)S(1)} %collective-permute-done.3.rest_4_), channel_id=1, source_target_pairs={{0,8},{8,0},{16,24},{24,16},{32,40},{40,32},{48,56},{56,48},{64,72... | collective-permute-start | bytes 1179656 | tf_op jit(solution)/shard_map/ppermute | solution.py:328
  24.9 2.5 %collective-permute-start.2 = (bf16[2,16,6144]{2,1,0:T(8,128)(2,1)S(1)}, bf16[2,16,6144]{2,1,0:T(8,128)(2,1)S(1)}, u32[]{:S(2)}, u32[]{:S(2)}) collective-permute-start(bf16[2,16,6144]{2,1,0:T(8,128)(2,1)S(1)} %collective-permute-done.1.pair.rest_2_), channel_id=1, source_target_pairs={{0,8},{8,0},{16,24},{24,16},{32,40},{40,32},{48,56},{56,48},{64,72... | collective-permute-start | bytes 1179656 | tf_op jit(solution)/shard_map/ppermute | solution.py:328
  25.4 2.2 %collective-permute-start.8 = (bf16[16,6144]{1,0:T(8,128)(2,1)S(1)}, bf16[16,6144]{1,0:T(8,128)(2,1)S(1)}, u32[]{:S(2)}, u32[]{:S(2)}) collective-permute-start(bf16[16,6144]{1,0:T(8,128)(2,1)S(1)} %collective-permute-done.7.rest_8_), channel_id=1, source_target_pairs={{0,8},{8,0},{16,24},{24,16},{32,40},{40,32},{48,56},{56,48},{64,72... | collective-permute-start | bytes 589832 | tf_op jit(solution)/shard_map/ppermute | solution.py:328
  67.3 4.8 %collective-permute-start.9 = (bf16[3,16,6400]{2,1,0:T(8,128)(2,1)S(1)}, bf16[3,16,6400]{2,1,0:T(8,128)(2,1)S(1)}, u32[]{:S(2)}, u32[]{:S(2)}) collective-permute-start(bf16[3,16,6400]{2,1,0:T(8,128)(2,1)S(1)} %get-tuple-element.22), channel_id=1, source_target_pairs={{0,8},{8,0},{16,24},{24,16},{32,40},{40,32},{48,56},{56,48},{64,72... | collective-permute-start | bytes 1843208 | tf_op jit(solution)/shard_map/ppermute | solution.py:370
  72.2 6.9 %collective-permute-start.10 = (bf16[5,16,6400]{2,1,0:T(8,128)(2,1)S(1)}, bf16[5,16,6400]{2,1,0:T(8,128)(2,1)S(1)}, u32[]{:S(2)}, u32[]{:S(2)}) collective-permute-start(bf16[5,16,6400]{2,1,0:T(8,128)(2,1)S(1)} %get-tuple-element.24), channel_id=1, source_target_pairs={{0,8},{8,0},{16,24},{24,16},{32,40},{40,32},{48,56},{56,48},{64,72... | collective-permute-start | bytes 3072008 | tf_op jit(solution)/shard_map/ppermute | solution.py:382
  72.7 6.4 %collective-permute-start.11 = (bf16[16,6400]{1,0:T(8,128)(2,1)S(1)}, bf16[16,6400]{1,0:T(8,128)(2,1)S(1)}, u32[]{:S(2)}, u32[]{:S(2)}) collective-permute-start(bf16[16,6400]{1,0:T(8,128)(2,1)S(1)} %get-tuple-element.25), channel_id=1, source_target_pairs={{0,32},{8,72},{16,48},{24,88},{32,0},{40,104},{48,16},{56,120},{64... | collective-permute-start | bytes 614408 | tf_op jit(solution)/shard_map/ppermute | solution.py:303
  75.2 14.6 %collective-permute-start.13 = (bf16[2,16,6400]{2,1,0:T(8,128)(2,1)S(1)}, bf16[2,16,6400]{2,1,0:T(8,128)(2,1)S(1)}, u32[]{:S(2)}, u32[]{:S(2)}) collective-permute-start(bf16[2,16,6400]{2,1,0:T(8,128)(2,1)S(1)} %get-tuple-element.28), channel_id=1, source_target_pairs={{0,80},{8,120},{16,96},{24,72},{32,112},{40,88},{48,64},{56,104},{... | collective-permute-start | bytes 1228808 | tf_op jit(solution)/shard_map/ppermute | solution.py:303
  79.3 14.4 %collective-permute-start.12 = (bf16[2,16,6400]{2,1,0:T(8,128)(2,1)S(1)}, bf16[2,16,6400]{2,1,0:T(8,128)(2,1)S(1)}, u32[]{:S(2)}, u32[]{:S(2)}) collective-permute-start(bf16[2,16,6400]{2,1,0:T(8,128)(2,1)S(1)} %get-tuple-element.27), channel_id=1, source_target_pairs={{0,64},{8,40},{16,80},{24,56},{32,96},{40,8},{48,112},{56,24},{64,... | collective-permute-start | bytes 1228808 | tf_op jit(solution)/shard_map/ppermute | solution.py:303
  80.6 15.8 %collective-permute-start.14 = (bf16[2,16,6400]{2,1,0:T(8,128)(2,1)S(1)}, bf16[2,16,6400]{2,1,0:T(8,128)(2,1)S(1)}, u32[]{:S(2)}, u32[]{:S(2)}) collective-permute-start(bf16[2,16,6400]{2,1,0:T(8,128)(2,1)S(1)} %third.1), channel_id=1, source_target_pairs={{0,16},{8,56},{16,32},{24,8},{32,48},{40,24},{48,0},{56,40},{64,80... | collective-permute-start | bytes 1228808 | tf_op jit(solution)/shard_map/ppermute | solution.py:303
  96.4 1.5 %collective-permute-start.15 = (bf16[16,6400]{1,0:T(8,128)(2,1)S(1)}, bf16[16,6400]{1,0:T(8,128)(2,1)S(1)}, u32[]{:S(2)}, u32[]{:S(2)}) collective-permute-start(bf16[16,6400]{1,0:T(8,128)(2,1)S(1)} %hand.1), channel_id=1, source_target_pairs={{0,8},{8,0},{16,24},{24,16},{32,40},{40,32},{48,56},{56,48},{64,72... | collective-permute-start | bytes 614408 | tf_op jit(solution)/shard_map/ppermute | solution.py:409

commit v11 on v10

--- a/solution.py
+++ b/solution.py
@@ -79,8 +79,8 @@
     copy.wait()
 
 
-def pick_kernel(pair, _, out):
-    out[...] = pair[0]
+def gate_kernel(*refs):
+    pass
 
 
 def load_kernel(values, *rest):
@@ -111,7 +111,7 @@
 
 
 def mix_kernel(cols_in, counts_in, values, cotangent, weight, bias, *rest):
-    pieces, (out, held, cols, counts, sems) = rest[:10], rest[10:]
+    pieces, (out, held, cols, counts, sems) = rest[:12], rest[12:]
     small = start_small((cols_in, counts_in), (cols, counts), sems)
     slots = values.shape[1]
     chunks, _, _ = out.shape
@@ -130,13 +130,17 @@
         parts, jnp.where(place, 1.0, 0.0).astype(BF), preferred_element_type=F32
     ).astype(BF)
 
-    first, second, third, farthest = (pieces[at : at + 2] for at in (2, 4, 6, 8))
+    def shard(server, steps, q):
+        if steps is FIRST:
+            return pieces[2 + 2 * q + server][...]
+        return pieces[(6 if steps is SECOND else 8) + server][q]
+
     for server in range(2):
         held[node_near(0, 0, server)] = pieces[server][...]
-        held[node_near(*FARTHEST, server)] = farthest[server][...]
-        for shards, steps in ((first, FIRST), (second, SECOND), (third, THIRD)):
+        held[node_near(*FARTHEST, server)] = pieces[10 + server][...]
+        for steps in (FIRST, SECOND, THIRD):
             for q, near in enumerate(pair_near(back(steps), server)):
-                held[near] = shards[server][q]
+                held[near] = shard(server, steps, q)
     for j in range(chunks):
         out[j, :, width : 2 * width] = cotangent[:16, j * width : (j + 1) * width]
         out[j, :, 2 * width : 3 * width] = cotangent[16:, j * width : (j + 1) * width]
@@ -244,21 +248,17 @@
     return own[k].astype(F32) + other[k].astype(F32)
 
 
-def pair_kernel(own, other, _, farthest, second, later):
+def pair_kernel(own, other, _, farthest, second, third, later):
     farthest[...] = both(own, other, 0).astype(BF)
     for q in range(2):
         second[q] = both(own, other, 1 + q).astype(BF)
-
-
-def third_kernel(own, other, third):
-    for q in range(2):
-        third[q] = both(own, other, q).astype(BF)
+        third[q] = both(own, other, 3 + q).astype(BF)
 
 
 def merge_kernel(own, other, forwarded, first, stay):
-    first[0] = (both(own, other, 2) + forwarded[...].astype(F32)).astype(BF)
-    first[1] = both(own, other, 3).astype(BF)
-    stay[...] = both(own, other, 4).astype(BF)
+    first[0] = (both(own, other, 0) + forwarded[...].astype(F32)).astype(BF)
+    first[1] = both(own, other, 1).astype(BF)
+    stay[...] = both(own, other, 2).astype(BF)
 
 
 def hand_kernel(first, second, third, out):
@@ -286,23 +286,26 @@
 
     swap = node_pairs(0, 0, 1)
     pieces = [features, lax.ppermute(features, "node", swap)]
+
+    def send(piece, steps):
+        return lax.ppermute(piece, "node", shared_pairs(steps))
+
+    first = [send(shard, FIRST) for shard in pieces]
     pair = features
     for at, shard in enumerate(pieces):
         pair = pl.pallas_call(
             functools.partial(place_kernel, at),
-            in_specs=[ANY] * (1 + at),
+            in_specs=[ANY] * (1 + 2 * at),
             out_specs=ANY,
             out_shape=shape((2, fin, nodes)),
             scratch_shapes=[pltpu.SemaphoreType.DMA],
             input_output_aliases={1: 0} if at else {},
             compiler_params=params(4),
             name="place",
-        )(*([shard, pair][: 1 + at]))
-
-    def send(piece, steps):
-        return lax.ppermute(piece, "node", shared_pairs(steps))
-
-    first, second, third = (send(pair, steps) for steps in (FIRST, SECOND, THIRD))
+        )(*([shard, pair, first[0]][: 1 + 2 * at]))
+
+    forwarded = send(first[0], FORWARD)
+    second, third = send(pair, SECOND), send(pair, THIRD)
     values, loaded = pl.pallas_call(
         load_kernel,
         in_specs=[pl.BlockSpec(memory_space=pltpu.HBM), ANY],
@@ -315,16 +318,20 @@
         ),
         name="load",
     )(pltpu.with_memory_space_constraint(block_values, pltpu.HBM), pair)
-    picked = pl.pallas_call(
-        pick_kernel,
-        in_specs=[VMEM, ANY],
-        out_specs=VMEM,
-        out_shape=shape((fin, nodes)),
-        compiler_params=params(4),
-        name="pick",
-    )(first, loaded)
-    forwarded = send(picked, FORWARD)
-    for piece in (first, second, third, forwarded):
+    def gate(*parts):
+        return pl.pallas_call(
+            gate_kernel,
+            in_specs=[ANY] * (len(parts) + 1),
+            out_specs=[ANY] * len(parts),
+            out_shape=[shape(part.shape) for part in parts],
+            input_output_aliases={at: at for at in range(len(parts))},
+            compiler_params=params(4),
+            name="gate",
+        )(*parts, loaded)
+
+    first[1], third = gate(first[1], third)
+    second, forwarded = gate(second, forwarded)
+    for piece in (*first, second, third, forwarded):
         pieces += [piece, lax.ppermute(piece, "node", swap)]
 
     index_scratch = [
@@ -334,7 +341,7 @@
     ]
     mixed = pl.pallas_call(
         mix_kernel,
-        in_specs=[HBM, HBM] + [VMEM] * 14,
+        in_specs=[HBM, HBM] + [VMEM] * 16,
         out_specs=VMEM,
         out_shape=shape((8, 16, 3 * width + 512)),
         scratch_shapes=[pltpu.VMEM((16, fin, nodes), BF)] + index_scratch,
@@ -361,34 +368,25 @@
         in_specs=[HBM, HBM] + [VMEM] * 2,
         out_specs=[VMEM] * 5,
         out_shape=[shape((32, nodes))]
-        + [shape((count, 16, wide)) for count in (3, 5) for _ in range(2)],
+        + [shape((count, 16, wide)) for count in (5, 3) for _ in range(2)],
         scratch_shapes=[pltpu.VMEM((17, fin, nodes), F32)] + index_scratch,
         compiler_params=params(24),
         name="spread",
     )(block_cols, block_counts, values, grads)
 
     other1 = lax.ppermute(other1, "node", swap)
-    farthest, second, other2 = pl.pallas_call(
+    farthest, second, third, other2 = pl.pallas_call(
         pair_kernel,
         in_specs=[VMEM, VMEM, ANY],
-        out_specs=[VMEM, VMEM, ANY],
-        out_shape=[shape((16, wide)), shape((2, 16, wide)), shape((5, 16, wide))],
-        input_output_aliases={2: 2},
+        out_specs=[VMEM, VMEM, VMEM, ANY],
+        out_shape=[shape((16, wide))] + [shape((2, 16, wide))] * 2 + [shape((3, 16, wide))],
+        input_output_aliases={2: 3},
         compiler_params=params(16),
         name="pair",
     )(own1, other1, other2)
     forwarded = send(farthest, back(FORWARD))
-    second = send(second, back(SECOND))
+    second, third = send(second, back(SECOND)), send(third, back(THIRD))
     other2 = lax.ppermute(other2, "node", swap)
-    third = pl.pallas_call(
-        third_kernel,
-        in_specs=[VMEM] * 2,
-        out_specs=VMEM,
-        out_shape=shape((2, 16, wide)),
-        compiler_params=params(16),
-        name="third",
-    )(own2, other2)
-    third = send(third, back(THIRD))
     first, stay = pl.pallas_call(
         merge_kernel,
         in_specs=[VMEM] * 3,

time: 99 us -> 104 us (1.051)
  starting transfers between devices: 27.1 us -> 30.2 us
  waiting for transfers between devices: 21.9 us -> 24.1 us
    ppermute x8 -> x9, waiting for transfers between devices: 16.8 us -> 18.8 us  [send(): return lax.ppermute(piece, 'node', shared_pairs(steps))]
    ppermute x4 -> x5, starting transfers between devices: 4.05 us -> 5.85 us  [local(): pieces += [piece, lax.ppermute(piece, 'node', swap)]]
    ppermute x8 -> x9, starting transfers between devices: 18 us -> 19.2 us  [send(): return lax.ppermute(piece, 'node', shared_pairs(steps))]
  transfers between devices with their start and end apart: 16 -> 18, of which waited for: 12 -> 11; matrix products, arithmetic and copies ran while one was open for 0% -> 0% of each run, Pallas kernels for 7% -> 7%
where the time goes in v11:
time: 104 us
  starting transfers between devices  30.2 us (29%)
  blocking collectives  28 us (27%)
  waiting for transfers between devices  24.1 us (23%)
  Pallas kernels  19.6 us (19%)
    ppermute x9, starting transfers between devices, send(): return lax.ppermute(piece, 'node', shared_pairs(steps))  19.2 us
    ppermute x9, waiting for transfers between devices, send(): return lax.ppermute(piece, 'node', shared_pairs(steps))  18.8 us
    all_to_all x1, blocking collectives, local(): both = lax.all_to_all(mixed, 'feat', 0, 0, tiled=True)  15.7 us
    all_to_all x1, blocking collectives, local(): grads = lax.all_to_all(dense, 'feat', 0, 0, tiled=True)  12.3 us
    pallas_call x1, Pallas kernels, local(): pl.pallas_call(spread_kernel, in_specs=[HBM, HBM] + [VMEM] * 2, out_specs...  6.88 us
    pallas_call x1, Pallas kernels, local(): pl.pallas_call(load_kernel, in_specs=[pl.BlockSpec(memory_space=pltpu.HBM...  6.52 us
    ppermute x5, starting transfers between devices, local(): pieces += [piece, lax.ppermute(piece, 'node', swap)]  5.85 us
    pallas_call x1, Pallas kernels, local(): pl.pallas_call(mix_kernel, in_specs=[HBM, HBM] + [VMEM] * 16, out_specs=V...  3.71 us
  transfers between devices with their start and end apart: 18, of which 11 were waited for; matrix products, arithmetic and copies ran while one was open for 0% of the time, Pallas kernels for 7%

profile of v11, /device:TPU:1, one launch (start us, length us, event | category | flops | bytes accessed | tf_op | source)
XLA Modules:
  0.0 103.6 jit_solution(2517911548119809136)
XLA Ops:
  0.6 1.5 %collective-permute-start = (bf16[16,6144]{1,0:T(8,128)(2,1)}, bf16[16,6144]{1,0:T(8,128)(2,1)S(1)}, u32[]{:S(2)}, u32[]{:S(2)}) collective-permute-start(bf16[16,6144]{1,0:T(8,128)(2,1)} %rest_0_.1), channel_id=1, source_target_pairs={{0,8},{8,0},{16,24},{24,16},{32,40},{40,32},{48,56},{56,48},{64,72... | collective-permute-start | bytes 589832 | tf_op jit(solution)/shard_map/ppermute | solution.py:288
  2.1 3.7 %collective-permute-start.1 = (bf16[16,6144]{1,0:T(8,128)(2,1)}, bf16[16,6144]{1,0:T(8,128)(2,1)S(1)}, u32[]{:S(2)}, u32[]{:S(2)}) collective-permute-start(bf16[16,6144]{1,0:T(8,128)(2,1)} %rest_0_.1), channel_id=1, source_target_pairs={{0,64},{8,40},{16,80},{24,56},{32,96},{40,8},{48,112},{56,24},{64,... | collective-permute-start | bytes 589832 | tf_op jit(solution)/shard_map/ppermute | solution.py:291
  5.8 1.0 copy-done
  7.1 2.1 %collective-permute-done.1.rest_1_.rest_2_ = bf16[16,6144]{1,0:T(8,128)(2,1)S(1)} collective-permute-done((bf16[16,6144]{1,0:T(8,128)(2,1)}, bf16[16,6144]{1,0:T(8,128)(2,1)S(1)}, u32[]{:S(2)}, u32[]{:S(2)}) %collective-permute-start.1) | collective-permute-done | bytes 196640 | tf_op jit(solution)/shard_map/ppermute | solution.py:291
  9.5 3.7 %collective-permute-start.6 = (bf16[2,16,6144]{2,1,0:T(8,128)(2,1)S(1)}, bf16[2,16,6144]{2,1,0:T(8,128)(2,1)S(1)}, u32[]{:S(2)}, u32[]{:S(2)}) collective-permute-start(bf16[2,16,6144]{2,1,0:T(8,128)(2,1)S(1)} %place.3.rest_0_), channel_id=1, source_target_pairs={{0,112},{8,88},{16,64},{24,104},{32,80},{40,120},{48,96},{56,72},{... | collective-permute-start | bytes 1179656 | tf_op jit(solution)/shard_map/ppermute | solution.py:291
  13.2 1.6 %collective-permute-start.4 = (bf16[2,16,6144]{2,1,0:T(8,128)(2,1)S(1)}, bf16[2,16,6144]{2,1,0:T(8,128)(2,1)S(1)}, u32[]{:S(2)}, u32[]{:S(2)}) collective-permute-start(bf16[2,16,6144]{2,1,0:T(8,128)(2,1)S(1)} %place.3.rest_0_), channel_id=1, source_target_pairs={{0,48},{8,24},{16,0},{24,40},{32,16},{40,56},{48,32},{56,8},{64,11... | collective-permute-start | bytes 1179656 | tf_op jit(solution)/shard_map/ppermute | solution.py:291
  15.0 1.7 %collective-permute-start.3 = (bf16[16,6144]{1,0:T(8,128)(2,1)S(1)}, bf16[16,6144]{1,0:T(8,128)(2,1)S(1)}, u32[]{:S(2)}, u32[]{:S(2)}) collective-permute-start(bf16[16,6144]{1,0:T(8,128)(2,1)S(1)} %collective-permute-done.shard.rest_1_), channel_id=1, source_target_pairs={{0,64},{8,40},{16,80},{24,56},{32,96},{40,8},{48,112},{56,24},{64,... | collective-permute-start | bytes 589832 | tf_op jit(solution)/shard_map/ppermute | solution.py:291
  16.7 6.5 %load.1 = (bf16[48,12,128,128]{3,2,1,0:T(8,128)(2,1)S(1)}, f32[8,128]{1,0:T(8,128)S(1)}) custom-call(bf16[48,12,128,128]{3,2,1,0:T(8,128)(2,1)} %values.1, bf16[2,16,6144]{2,1,0:T(8,128)(2,1)S(1)} %place.3.rest_0_), custom_call_target="tpu_custom_call" | custom-call | bytes 37748736 | tf_op jit(solution)/shard_map/load/pallas_call | solution.py:309
  23.7 4.8 %collective-permute-start.8 = (bf16[2,16,6144]{2,1,0:T(8,128)(2,1)S(1)}, bf16[2,16,6144]{2,1,0:T(8,128)(2,1)S(1)}, u32[]{:S(2)}, u32[]{:S(2)}) collective-permute-start(bf16[2,16,6144]{2,1,0:T(8,128)(2,1)S(1)} %get-tuple-element.25.rest_6_), channel_id=1, source_target_pairs={{0,8},{8,0},{16,24},{24,16},{32,40},{40,32},{48,56},{56,48},{64,72... | collective-permute-start | bytes 1179656 | tf_op jit(solution)/shard_map/ppermute | solution.py:335
  28.5 1.3 %collective-permute-done.3.refs_0_ = bf16[16,6144]{1,0:T(8,128)(2,1)S(1)} collective-permute-done((bf16[16,6144]{1,0:T(8,128)(2,1)S(1)}, bf16[16,6144]{1,0:T(8,128)(2,1)S(1)}, u32[]{:S(2)}, u32[]{:S(2)}) %collective-permute-start.3) | collective-permute-done | bytes 196640 | tf_op jit(solution)/shard_map/ppermute | solution.py:291
  30.8 1.0 collective-permute-done.2.rest_3_
  32.4 3.7 %mix.1 = bf16[8,16,2816]{2,1,0:T(8,128)(2,1)S(1)} custom-call(s32[12,48]{1,0:T(8,128)} %bitcast.5, s32[48]{0:T(128)} %counts_in.3, bf16[48,12,128,128]{3,2,1,0:T(8,128)(2,1)S(1)} %get-tuple-element.22.values, bf16[32,6144]{1,0:T(8,128)(2,1)S(1)} %copy-done.2, bf16[16,256]{1,0:T(8,128)(2,1)S(1)} %copy-done.4, f32[1,32]{1,0:T(1,128)S(1)} %bitcast.4, ...), custom_call_target="tpu_custom_call" | custom-call | tf_op jit(solution)/shard_map/mix/pallas_call | solution.py:342
  36.1 15.7 %all_to_all.10.both = bf16[8,16,2816]{2,1,0:T(8,128)(2,1)S(1)} all-to-all(bf16[8,16,2816]{2,1,0:T(8,128)(2,1)S(1)} %mix.1), channel_id=1, replica_groups=mesh['node'=16,'feat'=8] {'feat'}, dimensions={0} | all-to-all | bytes 1441792 | tf_op jit(solution)/shard_map/all_to_all | solution.py:352
  52.5 12.3 %all_to_all.11.grads = bf16[8,16,2560]{2,1,0:T(8,128)(2,1)S(1)} all-to-all(bf16[8,16,2560]{2,1,0:T(8,128)(2,1)S(1)} %dense.1), channel_id=1, replica_groups=mesh['node'=16,'feat'=8] {'feat'}, dimensions={0} | all-to-all | bytes 1310720 | tf_op jit(solution)/shard_map/all_to_all | solution.py:363
  64.9 6.9 %spread.1 = (bf16[32,6144]{1,0:T(8,128)(2,1)}, bf16[5,16,6400]{2,1,0:T(8,128)(2,1)S(1)}, bf16[5,16,6400]{2,1,0:T(8,128)(2,1)S(1)}, bf16[3,16,6400]{2,1,0:T(8,128)(2,1)S(1)}, bf16[3,16,6400]{2,1,0:T(8,128)(2,1)S(1)}) custom-call(s32[12,48]{1,0:T(8,128)} %bitcast.6, s32[48]{0:T(128)} %counts_in.3, bf16[48,12,128,128]{3,2,1,0:T(8,128)(2,1)S(1)} %get-tuple-element.22.values, ...), custom_call_target="tpu_custom_call" | custom-call | tf_op jit(solution)/shard_map/spread/pallas_call | solution.py:366
  71.7 3.1 %collective-permute-start.11 = (bf16[5,16,6400]{2,1,0:T(8,128)(2,1)S(1)}, bf16[5,16,6400]{2,1,0:T(8,128)(2,1)S(1)}, u32[]{:S(2)}, u32[]{:S(2)}) collective-permute-start(bf16[5,16,6400]{2,1,0:T(8,128)(2,1)S(1)} %get-tuple-element.31), channel_id=1, source_target_pairs={{0,8},{8,0},{16,24},{24,16},{32,40},{40,32},{48,56},{56,48},{64,72... | collective-permute-start | bytes 3072008 | tf_op jit(solution)/shard_map/ppermute | solution.py:377
  74.8 2.3 %collective-permute-done.11.other = bf16[5,16,6400]{2,1,0:T(8,128)(2,1)S(1)} collective-permute-done((bf16[5,16,6400]{2,1,0:T(8,128)(2,1)S(1)}, bf16[5,16,6400]{2,1,0:T(8,128)(2,1)S(1)}, u32[]{:S(2)}, u32[]{:S(2)}) %collective-permute-start.11) | collective-permute-done | bytes 1024032 | tf_op jit(solution)/shard_map/ppermute | solution.py:377
  77.8 1.7 %collective-permute-start.13 = (bf16[16,6400]{1,0:T(8,128)(2,1)S(1)}, bf16[16,6400]{1,0:T(8,128)(2,1)S(1)}, u32[]{:S(2)}, u32[]{:S(2)}) collective-permute-start(bf16[16,6400]{1,0:T(8,128)(2,1)S(1)} %get-tuple-element.34), channel_id=1, source_target_pairs={{0,32},{8,72},{16,48},{24,88},{32,0},{40,104},{48,16},{56,120},{64... | collective-permute-start | bytes 614408 | tf_op jit(solution)/shard_map/ppermute | solution.py:291
  79.5 4.8 %collective-permute-start.15 = (bf16[2,16,6400]{2,1,0:T(8,128)(2,1)S(1)}, bf16[2,16,6400]{2,1,0:T(8,128)(2,1)S(1)}, u32[]{:S(2)}, u32[]{:S(2)}) collective-permute-start(bf16[2,16,6400]{2,1,0:T(8,128)(2,1)S(1)} %get-tuple-element.37), channel_id=1, source_target_pairs={{0,80},{8,120},{16,96},{24,72},{32,112},{40,88},{48,64},{56,104},{... | collective-permute-start | bytes 1228808 | tf_op jit(solution)/shard_map/ppermute | solution.py:291
  84.5 1.7 %collective-permute-start.14 = (bf16[2,16,6400]{2,1,0:T(8,128)(2,1)S(1)}, bf16[2,16,6400]{2,1,0:T(8,128)(2,1)S(1)}, u32[]{:S(2)}, u32[]{:S(2)}) collective-permute-start(bf16[2,16,6400]{2,1,0:T(8,128)(2,1)S(1)} %get-tuple-element.36), channel_id=1, source_target_pairs={{0,64},{8,40},{16,80},{24,56},{32,96},{40,8},{48,112},{56,24},{64,... | collective-permute-start | bytes 1228808 | tf_op jit(solution)/shard_map/ppermute | solution.py:291
  86.2 8.8 %collective-permute-done.15.second = bf16[2,16,6400]{2,1,0:T(8,128)(2,1)S(1)} collective-permute-done((bf16[2,16,6400]{2,1,0:T(8,128)(2,1)S(1)}, bf16[2,16,6400]{2,1,0:T(8,128)(2,1)S(1)}, u32[]{:S(2)}, u32[]{:S(2)}) %collective-permute-start.15) | collective-permute-done | bytes 409632 | tf_op jit(solution)/shard_map/ppermute | solution.py:291
  95.4 5.7 %collective-permute-done.14.first = bf16[2,16,6400]{2,1,0:T(8,128)(2,1)S(1)} collective-permute-done((bf16[2,16,6400]{2,1,0:T(8,128)(2,1)S(1)}, bf16[2,16,6400]{2,1,0:T(8,128)(2,1)S(1)}, u32[]{:S(2)}, u32[]{:S(2)}) %collective-permute-start.14) | collective-permute-done | bytes 409632 | tf_op jit(solution)/shard_map/ppermute | solution.py:291
  101.4 1.4 %collective-permute-done.17.handed = bf16[16,6400]{1,0:T(8,128)(2,1)S(1)} collective-permute-done((bf16[16,6400]{1,0:T(8,128)(2,1)S(1)}, bf16[16,6400]{1,0:T(8,128)(2,1)S(1)}, u32[]{:S(2)}, u32[]{:S(2)}) %collective-permute-start.17) | collective-permute-done | bytes 204832 | tf_op jit(solution)/shard_map/ppermute | solution.py:407
  102.8 0.8 last.1
  (38 shorter events, 4.9 us)
Async XLA Ops:
  0.6 6.4 %collective-permute-start = (bf16[16,6144]{1,0:T(8,128)(2,1)}, bf16[16,6144]{1,0:T(8,128)(2,1)S(1)}, u32[]{:S(2)}, u32[]{:S(2)}) collective-permute-start(bf16[16,6144]{1,0:T(8,128)(2,1)} %rest_0_.1), channel_id=1, source_target_pairs={{0,8},{8,0},{16,24},{24,16},{32,40},{40,32},{48,56},{56,48},{64,72... | collective-permute-start | bytes 589832 | tf_op jit(solution)/shard_map/ppermute | solution.py:288
  2.1 7.1 %collective-permute-start.1 = (bf16[16,6144]{1,0:T(8,128)(2,1)}, bf16[16,6144]{1,0:T(8,128)(2,1)S(1)}, u32[]{:S(2)}, u32[]{:S(2)}) collective-permute-start(bf16[16,6144]{1,0:T(8,128)(2,1)} %rest_0_.1), channel_id=1, source_target_pairs={{0,64},{8,40},{16,80},{24,56},{32,96},{40,8},{48,112},{56,24},{64,... | collective-permute-start | bytes 589832 | tf_op jit(solution)/shard_map/ppermute | solution.py:291
  5.8 1.0 copy-start
  6.8 25.6 %copy-start.1 = (bf16[16,6144]{1,0:T(8,128)(2,1)S(1)}, bf16[16,6144]{1,0:T(8,128)(2,1)}, u32[]{:S(2)}) copy-start(bf16[16,6144]{1,0:T(8,128)(2,1)} %rest_0_.1) | copy-start | bytes 589828
  6.8 25.6 %copy-start.2 = (bf16[32,6144]{1,0:T(8,128)(2,1)S(1)}, bf16[32,6144]{1,0:T(8,128)(2,1)}, u32[]{:S(2)}) copy-start(bf16[32,6144]{1,0:T(8,128)(2,1)} %cotangent.1) | copy-start | bytes 1179652
  6.8 25.6 %copy-start.4 = (bf16[16,256]{1,0:T(8,128)(2,1)S(1)}, bf16[16,256]{1,0:T(8,128)(2,1)}, u32[]{:S(2)}) copy-start(bf16[16,256]{1,0:T(8,128)(2,1)} %weight.1) | copy-start | bytes 24580
  6.8 25.6 %copy-start.5 = (f32[32]{0:T(128)S(1)}, f32[32]{0:T(128)}, u32[]{:S(2)}) copy-start(f32[32]{0:T(128)} %param.10) | copy-start | bytes 388
  9.5 42.3 %copy-start.3 = (s32[6144]{0:T(1024)S(1)}, s32[6144]{0:T(1024)}, u32[]{:S(2)}) copy-start(s32[6144]{0:T(1024)} %param.14) | copy-start | bytes 73732
  9.5 14.2 %collective-permute-start.6 = (bf16[2,16,6144]{2,1,0:T(8,128)(2,1)S(1)}, bf16[2,16,6144]{2,1,0:T(8,128)(2,1)S(1)}, u32[]{:S(2)}, u32[]{:S(2)}) collective-permute-start(bf16[2,16,6144]{2,1,0:T(8,128)(2,1)S(1)} %place.3.rest_0_), channel_id=1, source_target_pairs={{0,112},{8,88},{16,64},{24,104},{32,80},{40,120},{48,96},{56,72},{... | collective-permute-start | bytes 1179656 | tf_op jit(solution)/shard_map/ppermute | solution.py:291
  13.2 16.6 %collective-permute-start.4 = (bf16[2,16,6144]{2,1,0:T(8,128)(2,1)S(1)}, bf16[2,16,6144]{2,1,0:T(8,128)(2,1)S(1)}, u32[]{:S(2)}, u32[]{:S(2)}) collective-permute-start(bf16[2,16,6144]{2,1,0:T(8,128)(2,1)S(1)} %place.3.rest_0_), channel_id=1, source_target_pairs={{0,48},{8,24},{16,0},{24,40},{32,16},{40,56},{48,32},{56,8},{64,11... | collective-permute-start | bytes 1179656 | tf_op jit(solution)/shard_map/ppermute | solution.py:291
  14.8 8.9 %collective-permute-start.7 = (bf16[16,6144]{1,0:T(8,128)(2,1)S(1)}, bf16[16,6144]{1,0:T(8,128)(2,1)S(1)}, u32[]{:S(2)}, u32[]{:S(2)}) collective-permute-start(bf16[16,6144]{1,0:T(8,128)(2,1)S(1)} %collective-permute-done.1.rest_1_.rest_2_), channel_id=1, source_target_pairs={{0,32},{8,72},{16,48},{24,88},{32,0},{40,104},{48,16},{56,120},{64... | collective-permute-start | bytes 589832 | tf_op jit(solution)/shard_map/ppermute | solution.py:291
  15.0 14.7 %collective-permute-start.3 = (bf16[16,6144]{1,0:T(8,128)(2,1)S(1)}, bf16[16,6144]{1,0:T(8,128)(2,1)S(1)}, u32[]{:S(2)}, u32[]{:S(2)}) collective-permute-start(bf16[16,6144]{1,0:T(8,128)(2,1)S(1)} %collective-permute-done.shard.rest_1_), channel_id=1, source_target_pairs={{0,64},{8,40},{16,80},{24,56},{32,96},{40,8},{48,112},{56,24},{64,... | collective-permute-start | bytes 589832 | tf_op jit(solution)/shard_map/ppermute | solution.py:291
  23.7 8.7 %collective-permute-start.8 = (bf16[2,16,6144]{2,1,0:T(8,128)(2,1)S(1)}, bf16[2,16,6144]{2,1,0:T(8,128)(2,1)S(1)}, u32[]{:S(2)}, u32[]{:S(2)}) collective-permute-start(bf16[2,16,6144]{2,1,0:T(8,128)(2,1)S(1)} %get-tuple-element.25.rest_6_), channel_id=1, source_target_pairs={{0,8},{8,0},{16,24},{24,16},{32,40},{40,32},{48,56},{56,48},{64,72... | collective-permute-start | bytes 1179656 | tf_op jit(solution)/shard_map/ppermute | solution.py:335
  29.8 2.6 %collective-permute-start.9 = (bf16[2,16,6144]{2,1,0:T(8,128)(2,1)S(1)}, bf16[2,16,6144]{2,1,0:T(8,128)(2,1)S(1)}, u32[]{:S(2)}, u32[]{:S(2)}) collective-permute-start(bf16[2,16,6144]{2,1,0:T(8,128)(2,1)S(1)} %get-tuple-element.26.rest_8_), channel_id=1, source_target_pairs={{0,8},{8,0},{16,24},{24,16},{32,40},{40,32},{48,56},{56,48},{64,72... | collective-permute-start | bytes 1179656 | tf_op jit(solution)/shard_map/ppermute | solution.py:335
  30.1 1.7 %collective-permute-start.2 = (bf16[16,6144]{1,0:T(8,128)(2,1)S(1)}, bf16[16,6144]{1,0:T(8,128)(2,1)S(1)}, u32[]{:S(2)}, u32[]{:S(2)}) collective-permute-start(bf16[16,6144]{1,0:T(8,128)(2,1)S(1)} %collective-permute-done.1.rest_1_.rest_2_), channel_id=1, source_target_pairs={{0,8},{8,0},{16,24},{24,16},{32,40},{40,32},{48,56},{56,48},{64,72... | collective-permute-start | bytes 589832 | tf_op jit(solution)/shard_map/ppermute | solution.py:335
  30.3 1.8 %collective-permute-start.10 = (bf16[16,6144]{1,0:T(8,128)(2,1)S(1)}, bf16[16,6144]{1,0:T(8,128)(2,1)S(1)}, u32[]{:S(2)}, u32[]{:S(2)}) collective-permute-start(bf16[16,6144]{1,0:T(8,128)(2,1)S(1)} %get-tuple-element.27.rest_10_), channel_id=1, source_target_pairs={{0,8},{8,0},{16,24},{24,16},{32,40},{40,32},{48,56},{56,48},{64,72... | collective-permute-start | bytes 589832 | tf_op jit(solution)/shard_map/ppermute | solution.py:335
  30.6 1.8 %collective-permute-start.5 = (bf16[16,6144]{1,0:T(8,128)(2,1)S(1)}, bf16[16,6144]{1,0:T(8,128)(2,1)S(1)}, u32[]{:S(2)}, u32[]{:S(2)}) collective-permute-start(bf16[16,6144]{1,0:T(8,128)(2,1)S(1)} %get-tuple-element.24.rest_4_), channel_id=1, source_target_pairs={{0,8},{8,0},{16,24},{24,16},{32,40},{40,32},{48,56},{56,48},{64,72... | collective-permute-start | bytes 589832 | tf_op jit(solution)/shard_map/ppermute | solution.py:335
  71.7 5.3 %collective-permute-start.11 = (bf16[5,16,6400]{2,1,0:T(8,128)(2,1)S(1)}, bf16[5,16,6400]{2,1,0:T(8,128)(2,1)S(1)}, u32[]{:S(2)}, u32[]{:S(2)}) collective-permute-start(bf16[5,16,6400]{2,1,0:T(8,128)(2,1)S(1)} %get-tuple-element.31), channel_id=1, source_target_pairs={{0,8},{8,0},{16,24},{24,16},{32,40},{40,32},{48,56},{56,48},{64,72... | collective-permute-start | bytes 3072008 | tf_op jit(solution)/shard_map/ppermute | solution.py:377
  77.3 7.0 %collective-permute-start.12 = (bf16[3,16,6400]{2,1,0:T(8,128)(2,1)S(1)}, bf16[3,16,6400]{2,1,0:T(8,128)(2,1)S(1)}, u32[]{:S(2)}, u32[]{:S(2)}) collective-permute-start(bf16[3,16,6400]{2,1,0:T(8,128)(2,1)S(1)} %get-tuple-element.33), channel_id=1, source_target_pairs={{0,8},{8,0},{16,24},{24,16},{32,40},{40,32},{48,56},{56,48},{64,72... | collective-permute-start | bytes 1843208 | tf_op jit(solution)/shard_map/ppermute | solution.py:389
  77.8 6.5 %collective-permute-start.13 = (bf16[16,6400]{1,0:T(8,128)(2,1)S(1)}, bf16[16,6400]{1,0:T(8,128)(2,1)S(1)}, u32[]{:S(2)}, u32[]{:S(2)}) collective-permute-start(bf16[16,6400]{1,0:T(8,128)(2,1)S(1)} %get-tuple-element.34), channel_id=1, source_target_pairs={{0,32},{8,72},{16,48},{24,88},{32,0},{40,104},{48,16},{56,120},{64... | collective-permute-start | bytes 614408 | tf_op jit(solution)/shard_map/ppermute | solution.py:291
  79.5 15.6 %collective-permute-start.15 = (bf16[2,16,6400]{2,1,0:T(8,128)(2,1)S(1)}, bf16[2,16,6400]{2,1,0:T(8,128)(2,1)S(1)}, u32[]{:S(2)}, u32[]{:S(2)}) collective-permute-start(bf16[2,16,6400]{2,1,0:T(8,128)(2,1)S(1)} %get-tuple-element.37), channel_id=1, source_target_pairs={{0,80},{8,120},{16,96},{24,72},{32,112},{40,88},{48,64},{56,104},{... | collective-permute-start | bytes 1228808 | tf_op jit(solution)/shard_map/ppermute | solution.py:291
  84.3 11.1 %collective-permute-start.16 = (bf16[2,16,6400]{2,1,0:T(8,128)(2,1)S(1)}, bf16[2,16,6400]{2,1,0:T(8,128)(2,1)S(1)}, u32[]{:S(2)}, u32[]{:S(2)}) collective-permute-start(bf16[2,16,6400]{2,1,0:T(8,128)(2,1)S(1)} %get-tuple-element.38), channel_id=1, source_target_pairs={{0,16},{8,56},{16,32},{24,8},{32,48},{40,24},{48,0},{56,40},{64,80... | collective-permute-start | bytes 1228808 | tf_op jit(solution)/shard_map/ppermute | solution.py:291
  84.5 16.7 %collective-permute-start.14 = (bf16[2,16,6400]{2,1,0:T(8,128)(2,1)S(1)}, bf16[2,16,6400]{2,1,0:T(8,128)(2,1)S(1)}, u32[]{:S(2)}, u32[]{:S(2)}) collective-permute-start(bf16[2,16,6400]{2,1,0:T(8,128)(2,1)S(1)} %get-tuple-element.36), channel_id=1, source_target_pairs={{0,64},{8,40},{16,80},{24,56},{32,96},{40,8},{48,112},{56,24},{64,... | collective-permute-start | bytes 1228808 | tf_op jit(solution)/shard_map/ppermute | solution.py:291
  101.3 1.5 %collective-permute-start.17 = (bf16[16,6400]{1,0:T(8,128)(2,1)S(1)}, bf16[16,6400]{1,0:T(8,128)(2,1)S(1)}, u32[]{:S(2)}, u32[]{:S(2)}) collective-permute-start(bf16[16,6400]{1,0:T(8,128)(2,1)S(1)} %hand.1), channel_id=1, source_target_pairs={{0,8},{8,0},{16,24},{24,16},{32,40},{40,32},{48,56},{56,48},{64,72... | collective-permute-start | bytes 614408 | tf_op jit(solution)/shard_map/ppermute | solution.py:407

commit v12 on v10

--- a/solution.py
+++ b/solution.py
@@ -232,7 +232,7 @@
         nears = [node_near(*FARTHEST, server)]
         for steps in (SECOND, THIRD, FIRST):
             nears += pair_near(back(steps), server)
-        nears.append(node_near(0, 0, server))
+        nears[5:] = [nears[6], nears[5], node_near(0, 0, server)]
         for group in groups[server::2]:
             for k in range(group.shape[0]):
                 near = nears.pop(0)
@@ -244,30 +244,26 @@
     return own[k].astype(F32) + other[k].astype(F32)
 
 
-def pair_kernel(own, other, _, farthest, second, later):
+def pair_kernel(own, other, _, farthest, second, third, first, later):
     farthest[...] = both(own, other, 0).astype(BF)
     for q in range(2):
         second[q] = both(own, other, 1 + q).astype(BF)
-
-
-def third_kernel(own, other, third):
-    for q in range(2):
-        third[q] = both(own, other, q).astype(BF)
+        third[q] = both(own, other, 3 + q).astype(BF)
+    first[...] = both(own, other, 5).astype(BF)
 
 
 def merge_kernel(own, other, forwarded, first, stay):
-    first[0] = (both(own, other, 2) + forwarded[...].astype(F32)).astype(BF)
-    first[1] = both(own, other, 3).astype(BF)
-    stay[...] = both(own, other, 4).astype(BF)
+    first[...] = (both(own, other, 0) + forwarded[...].astype(F32)).astype(BF)
+    stay[...] = both(own, other, 1).astype(BF)
 
 
 def hand_kernel(first, second, third, out):
-    out[...] = (first[1].astype(F32) + second[1].astype(F32) + third[1].astype(F32)).astype(BF)
+    out[...] = (first[...].astype(F32) + second[1].astype(F32) + third[1].astype(F32)).astype(BF)
 
 
 def last_kernel(stay, handed, first, second, third, grad_features, grad_weight):
-    total = stay[...].astype(F32) + handed[...].astype(F32)
-    for piece in (first, second, third):
+    total = stay[...].astype(F32) + handed[...].astype(F32) + first[...].astype(F32)
+    for piece in (second, third):
         total += piece[0].astype(F32)
     nodes = grad_features.shape[1]
     grad_features[...] = total[:, :nodes].astype(BF)
@@ -361,43 +357,37 @@
         in_specs=[HBM, HBM] + [VMEM] * 2,
         out_specs=[VMEM] * 5,
         out_shape=[shape((32, nodes))]
-        + [shape((count, 16, wide)) for count in (3, 5) for _ in range(2)],
+        + [shape((count, 16, wide)) for count in (6, 2) for _ in range(2)],
         scratch_shapes=[pltpu.VMEM((17, fin, nodes), F32)] + index_scratch,
         compiler_params=params(24),
         name="spread",
     )(block_cols, block_counts, values, grads)
 
     other1 = lax.ppermute(other1, "node", swap)
-    farthest, second, other2 = pl.pallas_call(
+    farthest, second, third, first, other2 = pl.pallas_call(
         pair_kernel,
         in_specs=[VMEM, VMEM, ANY],
-        out_specs=[VMEM, VMEM, ANY],
-        out_shape=[shape((16, wide)), shape((2, 16, wide)), shape((5, 16, wide))],
-        input_output_aliases={2: 2},
+        out_specs=[VMEM] * 4 + [ANY],
+        out_shape=[shape((16, wide))]
+        + [shape((2, 16, wide))] * 2
+        + [shape((16, wide)), shape((2, 16, wide))],
+        input_output_aliases={2: 4},
         compiler_params=params(16),
         name="pair",
     )(own1, other1, other2)
     forwarded = send(farthest, back(FORWARD))
-    second = send(second, back(SECOND))
+    second, third = send(second, back(SECOND)), send(third, back(THIRD))
+    first = [send(first, back(FIRST))]
     other2 = lax.ppermute(other2, "node", swap)
-    third = pl.pallas_call(
-        third_kernel,
-        in_specs=[VMEM] * 2,
-        out_specs=VMEM,
-        out_shape=shape((2, 16, wide)),
-        compiler_params=params(16),
-        name="third",
-    )(own2, other2)
-    third = send(third, back(THIRD))
-    first, stay = pl.pallas_call(
+    merged, stay = pl.pallas_call(
         merge_kernel,
         in_specs=[VMEM] * 3,
         out_specs=[VMEM] * 2,
-        out_shape=[shape((2, 16, wide)), shape((16, wide))],
+        out_shape=[shape((16, wide))] * 2,
         compiler_params=params(16),
         name="merge",
     )(own2, other2, forwarded)
-    first = send(first, back(FIRST))
+    first.append(send(merged, back(FIRST)))
     handed = pl.pallas_call(
         hand_kernel,
         in_specs=[VMEM] * 3,
@@ -405,7 +395,7 @@
         out_shape=shape((16, wide)),
         compiler_params=params(16),
         name="hand",
-    )(first, second, third)
+    )(first[0], second, third)
     handed = lax.ppermute(handed, "node", swap)
     grad_features, grad_weight = pl.pallas_call(
         last_kernel,
@@ -414,7 +404,7 @@
         out_shape=[shape((16, nodes)), shape((16, 256), F32)],
         compiler_params=params(16),
         name="last",
-    )(stay, handed, first, second, third)
+    )(stay, handed, first[1], second, third)
     return activation, grad_features, grad_weight
 
 

time: 99 us -> 102 us (1.030)
  waiting for transfers between devices: 21.9 us -> 25 us
    ppermute x8 -> x9, starting transfers between devices: 18 us -> 14 us  [send(): return lax.ppermute(piece, 'node', shared_pairs(steps))]
    ppermute x8 -> x9, waiting for transfers between devices: 16.8 us -> 20.4 us  [send(): return lax.ppermute(piece, 'node', shared_pairs(steps))]
    ppermute x1, starting transfers between devices: 0.09 us -> 3.21 us  [local(): handed = lax.ppermute(handed, 'node', swap)]
    ppermute x1, waiting for transfers between devices: 1.44 us -> 0.01 us  [local(): handed = lax.ppermute(handed, 'node', swap)]
  transfers between devices with their start and end apart: 16 -> 17, of which waited for: 12 -> 9; matrix products, arithmetic and copies ran while one was open for 0% -> 0% of each run, Pallas kernels for 7% -> 7%
where the time goes in v12:
time: 102 us; the launch traced here: 101 us
  blocking collectives  28.4 us (28%)
  starting transfers between devices  26.3 us (26%)
  waiting for transfers between devices  25 us (25%)
  Pallas kernels  19.6 us (19%)
    ppermute x9, waiting for transfers between devices, send(): return lax.ppermute(piece, 'node', shared_pairs(steps))  20.4 us
    all_to_all x1, blocking collectives, local(): both = lax.all_to_all(mixed, 'feat', 0, 0, tiled=True)  16.1 us
    ppermute x9, starting transfers between devices, send(): return lax.ppermute(piece, 'node', shared_pairs(steps))  14 us
    all_to_all x1, blocking collectives, local(): grads = lax.all_to_all(dense, 'feat', 0, 0, tiled=True)  12.3 us
    pallas_call x1, Pallas kernels, local(): pl.pallas_call(spread_kernel, in_specs=[HBM, HBM] + [VMEM] * 2, out_specs...  6.88 us
    pallas_call x1, Pallas kernels, local(): pl.pallas_call(load_kernel, in_specs=[pl.BlockSpec(memory_space=pltpu.HBM...  6.52 us
    ppermute x4, starting transfers between devices, local(): pieces += [piece, lax.ppermute(piece, 'node', swap)]  4.05 us
    pallas_call x1, Pallas kernels, local(): pl.pallas_call(mix_kernel, in_specs=[HBM, HBM] + [VMEM] * 14, out_specs=V...  3.71 us
  transfers between devices with their start and end apart: 17, of which 9 were waited for; matrix products, arithmetic and copies ran while one was open for 0% of the time, Pallas kernels for 7%

profile of v12, /device:TPU:1, one launch (start us, length us, event | category | flops | bytes accessed | tf_op | source)
XLA Modules:
  0.0 101.0 jit_solution(1506297162323390460)
XLA Ops:
  0.6 1.5 %collective-permute-start = (bf16[16,6144]{1,0:T(8,128)(2,1)}, bf16[16,6144]{1,0:T(8,128)(2,1)S(1)}, u32[]{:S(2)}, u32[]{:S(2)}) collective-permute-start(bf16[16,6144]{1,0:T(8,128)(2,1)} %rest_0_.1), channel_id=1, source_target_pairs={{0,8},{8,0},{16,24},{24,16},{32,40},{40,32},{48,56},{56,48},{64,72... | collective-permute-start | bytes 589832 | tf_op jit(solution)/shard_map/ppermute | solution.py:284
  2.1 0.9 copy-done
  3.7 3.8 %collective-permute-start.1 = (bf16[2,16,6144]{2,1,0:T(8,128)(2,1)S(1)}, bf16[2,16,6144]{2,1,0:T(8,128)(2,1)S(1)}, u32[]{:S(2)}, u32[]{:S(2)}) collective-permute-start(bf16[2,16,6144]{2,1,0:T(8,128)(2,1)S(1)} %place.3.rest_0_), channel_id=1, source_target_pairs={{0,64},{8,40},{16,80},{24,56},{32,96},{40,8},{48,112},{56,24},{64,... | collective-permute-start | bytes 1179656 | tf_op jit(solution)/shard_map/ppermute | solution.py:299
  7.5 0.7 collective-permute-start.5
  8.2 2.5 %collective-permute-start.3 = (bf16[2,16,6144]{2,1,0:T(8,128)(2,1)S(1)}, bf16[2,16,6144]{2,1,0:T(8,128)(2,1)S(1)}, u32[]{:S(2)}, u32[]{:S(2)}) collective-permute-start(bf16[2,16,6144]{2,1,0:T(8,128)(2,1)S(1)} %place.3.rest_0_), channel_id=1, source_target_pairs={{0,112},{8,88},{16,64},{24,104},{32,80},{40,120},{48,96},{56,72},{... | collective-permute-start | bytes 1179656 | tf_op jit(solution)/shard_map/ppermute | solution.py:299
  10.7 6.5 %load.1 = (bf16[48,12,128,128]{3,2,1,0:T(8,128)(2,1)S(1)}, f32[8,128]{1,0:T(8,128)S(1)}) custom-call(bf16[48,12,128,128]{3,2,1,0:T(8,128)(2,1)} %values.1, bf16[2,16,6144]{2,1,0:T(8,128)(2,1)S(1)} %place.3.rest_0_), custom_call_target="tpu_custom_call" | custom-call | bytes 37748736 | tf_op jit(solution)/shard_map/load/pallas_call | solution.py:302
  17.6 4.1 %collective-permute-done.5.rest_6_ = bf16[2,16,6144]{2,1,0:T(8,128)(2,1)S(1)} collective-permute-done((bf16[2,16,6144]{2,1,0:T(8,128)(2,1)S(1)}, bf16[2,16,6144]{2,1,0:T(8,128)(2,1)S(1)}, u32[]{:S(2)}, u32[]{:S(2)}) %collective-permute-start.5) | collective-permute-done | bytes 393248 | tf_op jit(solution)/shard_map/ppermute | solution.py:299
  21.6 3.2 %collective-permute-start.6 = (bf16[2,16,6144]{2,1,0:T(8,128)(2,1)S(1)}, bf16[2,16,6144]{2,1,0:T(8,128)(2,1)S(1)}, u32[]{:S(2)}, u32[]{:S(2)}) collective-permute-start(bf16[2,16,6144]{2,1,0:T(8,128)(2,1)S(1)} %collective-permute-done.5.rest_6_), channel_id=1, source_target_pairs={{0,8},{8,0},{16,24},{24,16},{32,40},{40,32},{48,56},{56,48},{64,72... | collective-permute-start | bytes 1179656 | tf_op jit(solution)/shard_map/ppermute | solution.py:324
  26.2 0.6 collective-permute-done.4.rest_5_
  26.8 0.6 collective-permute-done.2.rest_3_
  27.7 3.7 %mix.1 = bf16[8,16,2816]{2,1,0:T(8,128)(2,1)S(1)} custom-call(s32[12,48]{1,0:T(8,128)} %bitcast.5, s32[48]{0:T(128)} %counts_in.3, bf16[48,12,128,128]{3,2,1,0:T(8,128)(2,1)S(1)} %get-tuple-element.19.values, bf16[32,6144]{1,0:T(8,128)(2,1)S(1)} %copy-done.2, bf16[16,256]{1,0:T(8,128)(2,1)S(1)} %copy-done.4, f32[1,32]{1,0:T(1,128)S(1)} %bitcast.4, ...), custom_call_target="tpu_custom_call" | custom-call | tf_op jit(solution)/shard_map/mix/pallas_call | solution.py:331
  31.4 16.1 %all_to_all.10.both = bf16[8,16,2816]{2,1,0:T(8,128)(2,1)S(1)} all-to-all(bf16[8,16,2816]{2,1,0:T(8,128)(2,1)S(1)} %mix.1), channel_id=1, replica_groups=mesh['node'=16,'feat'=8] {'feat'}, dimensions={0} | all-to-all | bytes 1441792 | tf_op jit(solution)/shard_map/all_to_all | solution.py:341
  47.4 0.7 dense.1
  48.2 12.3 %all_to_all.11.grads = bf16[8,16,2560]{2,1,0:T(8,128)(2,1)S(1)} all-to-all(bf16[8,16,2560]{2,1,0:T(8,128)(2,1)S(1)} %dense.1), channel_id=1, replica_groups=mesh['node'=16,'feat'=8] {'feat'}, dimensions={0} | all-to-all | bytes 1310720 | tf_op jit(solution)/shard_map/all_to_all | solution.py:352
  60.5 6.9 %spread.1 = (bf16[32,6144]{1,0:T(8,128)(2,1)}, bf16[6,16,6400]{2,1,0:T(8,128)(2,1)S(1)}, bf16[6,16,6400]{2,1,0:T(8,128)(2,1)S(1)}, bf16[2,16,6400]{2,1,0:T(8,128)(2,1)S(1)}, bf16[2,16,6400]{2,1,0:T(8,128)(2,1)S(1)}) custom-call(s32[12,48]{1,0:T(8,128)} %bitcast.6, s32[48]{0:T(128)} %counts_in.3, bf16[48,12,128,128]{3,2,1,0:T(8,128)(2,1)S(1)} %get-tuple-element.19.values, ...), custom_call_target="tpu_custom_call" | custom-call | tf_op jit(solution)/shard_map/spread/pallas_call | solution.py:355
  67.4 3.1 %collective-permute-start.9 = (bf16[6,16,6400]{2,1,0:T(8,128)(2,1)S(1)}, bf16[6,16,6400]{2,1,0:T(8,128)(2,1)S(1)}, u32[]{:S(2)}, u32[]{:S(2)}) collective-permute-start(bf16[6,16,6400]{2,1,0:T(8,128)(2,1)S(1)} %get-tuple-element.24), channel_id=1, source_target_pairs={{0,8},{8,0},{16,24},{24,16},{32,40},{40,32},{48,56},{56,48},{64,72... | collective-permute-start | bytes 3686408 | tf_op jit(solution)/shard_map/ppermute | solution.py:366
  70.5 2.5 %collective-permute-done.9.other = bf16[6,16,6400]{2,1,0:T(8,128)(2,1)S(1)} collective-permute-done((bf16[6,16,6400]{2,1,0:T(8,128)(2,1)S(1)}, bf16[6,16,6400]{2,1,0:T(8,128)(2,1)S(1)}, u32[]{:S(2)}, u32[]{:S(2)}) %collective-permute-start.9) | collective-permute-done | bytes 1228832 | tf_op jit(solution)/shard_map/ppermute | solution.py:366
  73.8 4.5 %collective-permute-start.13 = (bf16[2,16,6400]{2,1,0:T(8,128)(2,1)S(1)}, bf16[2,16,6400]{2,1,0:T(8,128)(2,1)S(1)}, u32[]{:S(2)}, u32[]{:S(2)}) collective-permute-start(bf16[2,16,6400]{2,1,0:T(8,128)(2,1)S(1)} %get-tuple-element.30), channel_id=1, source_target_pairs={{0,80},{8,120},{16,96},{24,72},{32,112},{40,88},{48,64},{56,104},{... | collective-permute-start | bytes 1228808 | tf_op jit(solution)/shard_map/ppermute | solution.py:299
  78.6 1.2 %collective-permute-start.11 = (bf16[16,6400]{1,0:T(8,128)(2,1)S(1)}, bf16[16,6400]{1,0:T(8,128)(2,1)S(1)}, u32[]{:S(2)}, u32[]{:S(2)}) collective-permute-start(bf16[16,6400]{1,0:T(8,128)(2,1)S(1)} %get-tuple-element.27), channel_id=1, source_target_pairs={{0,32},{8,72},{16,48},{24,88},{32,0},{40,104},{48,16},{56,120},{64... | collective-permute-start | bytes 614408 | tf_op jit(solution)/shard_map/ppermute | solution.py:299
  79.8 0.5 collective-permute-start.12
  80.4 13.2 %collective-permute-done.11.forwarded = bf16[16,6400]{1,0:T(8,128)(2,1)S(1)} collective-permute-done((bf16[16,6400]{1,0:T(8,128)(2,1)S(1)}, bf16[16,6400]{1,0:T(8,128)(2,1)S(1)}, u32[]{:S(2)}, u32[]{:S(2)}) %collective-permute-start.11) | collective-permute-done | bytes 204832 | tf_op jit(solution)/shard_map/ppermute | solution.py:299
  93.9 3.2 %collective-permute-start.15 = (bf16[16,6400]{1,0:T(8,128)(2,1)S(1)}, bf16[16,6400]{1,0:T(8,128)(2,1)S(1)}, u32[]{:S(2)}, u32[]{:S(2)}) collective-permute-start(bf16[16,6400]{1,0:T(8,128)(2,1)S(1)} %hand.1), channel_id=1, source_target_pairs={{0,8},{8,0},{16,24},{24,16},{32,40},{40,32},{48,56},{56,48},{64,72... | collective-permute-start | bytes 614408 | tf_op jit(solution)/shard_map/ppermute | solution.py:399
  97.1 3.1 %collective-permute-done.16.first = bf16[16,6400]{1,0:T(8,128)(2,1)S(1)} collective-permute-done((bf16[16,6400]{1,0:T(8,128)(2,1)S(1)}, bf16[16,6400]{1,0:T(8,128)(2,1)S(1)}, u32[]{:S(2)}, u32[]{:S(2)}) %collective-permute-start.16) | collective-permute-done | bytes 204832 | tf_op jit(solution)/shard_map/ppermute | solution.py:299
  100.2 0.8 last.1
  (35 shorter events, 4.0 us)
Async XLA Ops:
  0.6 2.8 %collective-permute-start = (bf16[16,6144]{1,0:T(8,128)(2,1)}, bf16[16,6144]{1,0:T(8,128)(2,1)S(1)}, u32[]{:S(2)}, u32[]{:S(2)}) collective-permute-start(bf16[16,6144]{1,0:T(8,128)(2,1)} %rest_0_.1), channel_id=1, source_target_pairs={{0,8},{8,0},{16,24},{24,16},{32,40},{40,32},{48,56},{56,48},{64,72... | collective-permute-start | bytes 589832 | tf_op jit(solution)/shard_map/ppermute | solution.py:284
  2.1 0.9 copy-start
  3.6 24.0 %copy-start.1 = (bf16[16,6144]{1,0:T(8,128)(2,1)S(1)}, bf16[16,6144]{1,0:T(8,128)(2,1)}, u32[]{:S(2)}) copy-start(bf16[16,6144]{1,0:T(8,128)(2,1)} %rest_0_.1) | copy-start | bytes 589828
  3.7 24.0 %copy-start.2 = (bf16[32,6144]{1,0:T(8,128)(2,1)S(1)}, bf16[32,6144]{1,0:T(8,128)(2,1)}, u32[]{:S(2)}) copy-start(bf16[32,6144]{1,0:T(8,128)(2,1)} %cotangent.1) | copy-start | bytes 1179652
  3.7 24.0 %copy-start.4 = (bf16[16,256]{1,0:T(8,128)(2,1)S(1)}, bf16[16,256]{1,0:T(8,128)(2,1)}, u32[]{:S(2)}) copy-start(bf16[16,256]{1,0:T(8,128)(2,1)} %weight.1) | copy-start | bytes 24580
  3.7 24.0 %copy-start.5 = (f32[32]{0:T(128)S(1)}, f32[32]{0:T(128)}, u32[]{:S(2)}) copy-start(f32[32]{0:T(128)} %param.10) | copy-start | bytes 388
  3.7 13.5 %collective-permute-start.1 = (bf16[2,16,6144]{2,1,0:T(8,128)(2,1)S(1)}, bf16[2,16,6144]{2,1,0:T(8,128)(2,1)S(1)}, u32[]{:S(2)}, u32[]{:S(2)}) collective-permute-start(bf16[2,16,6144]{2,1,0:T(8,128)(2,1)S(1)} %place.3.rest_0_), channel_id=1, source_target_pairs={{0,64},{8,40},{16,80},{24,56},{32,96},{40,8},{48,112},{56,24},{64,... | collective-permute-start | bytes 1179656 | tf_op jit(solution)/shard_map/ppermute | solution.py:299
  7.5 14.2 %collective-permute-start.5 = (bf16[2,16,6144]{2,1,0:T(8,128)(2,1)S(1)}, bf16[2,16,6144]{2,1,0:T(8,128)(2,1)S(1)}, u32[]{:S(2)}, u32[]{:S(2)}) collective-permute-start(bf16[2,16,6144]{2,1,0:T(8,128)(2,1)S(1)} %place.3.rest_0_), channel_id=1, source_target_pairs={{0,48},{8,24},{16,0},{24,40},{32,16},{40,56},{48,32},{56,8},{64,11... | collective-permute-start | bytes 1179656 | tf_op jit(solution)/shard_map/ppermute | solution.py:299
  8.2 16.7 %collective-permute-start.3 = (bf16[2,16,6144]{2,1,0:T(8,128)(2,1)S(1)}, bf16[2,16,6144]{2,1,0:T(8,128)(2,1)S(1)}, u32[]{:S(2)}, u32[]{:S(2)}) collective-permute-start(bf16[2,16,6144]{2,1,0:T(8,128)(2,1)S(1)} %place.3.rest_0_), channel_id=1, source_target_pairs={{0,112},{8,88},{16,64},{24,104},{32,80},{40,120},{48,96},{56,72},{... | collective-permute-start | bytes 1179656 | tf_op jit(solution)/shard_map/ppermute | solution.py:299
  17.2 8.2 %collective-permute-start.7 = (bf16[16,6144]{1,0:T(8,128)(2,1)S(1)}, bf16[16,6144]{1,0:T(8,128)(2,1)S(1)}, u32[]{:S(2)}, u32[]{:S(2)}) collective-permute-start(bf16[16,6144]{1,0:T(8,128)(2,1)S(1)} %pick.1), channel_id=1, source_target_pairs={{0,32},{8,72},{16,48},{24,88},{32,0},{40,104},{48,16},{56,120},{64... | collective-permute-start | bytes 589832 | tf_op jit(solution)/shard_map/ppermute | solution.py:299
  21.6 4.6 %collective-permute-start.6 = (bf16[2,16,6144]{2,1,0:T(8,128)(2,1)S(1)}, bf16[2,16,6144]{2,1,0:T(8,128)(2,1)S(1)}, u32[]{:S(2)}, u32[]{:S(2)}) collective-permute-start(bf16[2,16,6144]{2,1,0:T(8,128)(2,1)S(1)} %collective-permute-done.5.rest_6_), channel_id=1, source_target_pairs={{0,8},{8,0},{16,24},{24,16},{32,40},{40,32},{48,56},{56,48},{64,72... | collective-permute-start | bytes 1179656 | tf_op jit(solution)/shard_map/ppermute | solution.py:324
  24.9 1.9 %collective-permute-start.4 = (bf16[2,16,6144]{2,1,0:T(8,128)(2,1)S(1)}, bf16[2,16,6144]{2,1,0:T(8,128)(2,1)S(1)}, u32[]{:S(2)}, u32[]{:S(2)}) collective-permute-start(bf16[2,16,6144]{2,1,0:T(8,128)(2,1)S(1)} %collective-permute-done.3.rest_4_), channel_id=1, source_target_pairs={{0,8},{8,0},{16,24},{24,16},{32,40},{40,32},{48,56},{56,48},{64,72... | collective-permute-start | bytes 1179656 | tf_op jit(solution)/shard_map/ppermute | solution.py:324
  24.9 2.5 %collective-permute-start.2 = (bf16[2,16,6144]{2,1,0:T(8,128)(2,1)S(1)}, bf16[2,16,6144]{2,1,0:T(8,128)(2,1)S(1)}, u32[]{:S(2)}, u32[]{:S(2)}) collective-permute-start(bf16[2,16,6144]{2,1,0:T(8,128)(2,1)S(1)} %collective-permute-done.1.pair.rest_2_), channel_id=1, source_target_pairs={{0,8},{8,0},{16,24},{24,16},{32,40},{40,32},{48,56},{56,48},{64,72... | collective-permute-start | bytes 1179656 | tf_op jit(solution)/shard_map/ppermute | solution.py:324
  25.4 2.2 %collective-permute-start.8 = (bf16[16,6144]{1,0:T(8,128)(2,1)S(1)}, bf16[16,6144]{1,0:T(8,128)(2,1)S(1)}, u32[]{:S(2)}, u32[]{:S(2)}) collective-permute-start(bf16[16,6144]{1,0:T(8,128)(2,1)S(1)} %collective-permute-done.7.rest_8_), channel_id=1, source_target_pairs={{0,8},{8,0},{16,24},{24,16},{32,40},{40,32},{48,56},{56,48},{64,72... | collective-permute-start | bytes 589832 | tf_op jit(solution)/shard_map/ppermute | solution.py:324
  31.4 16.1 %copy-start.3 = (s32[6144]{0:T(1024)S(1)}, s32[6144]{0:T(1024)}, u32[]{:S(2)}) copy-start(s32[6144]{0:T(1024)} %param.14) | copy-start | bytes 73732
  67.4 5.7 %collective-permute-start.9 = (bf16[6,16,6400]{2,1,0:T(8,128)(2,1)S(1)}, bf16[6,16,6400]{2,1,0:T(8,128)(2,1)S(1)}, u32[]{:S(2)}, u32[]{:S(2)}) collective-permute-start(bf16[6,16,6400]{2,1,0:T(8,128)(2,1)S(1)} %get-tuple-element.24), channel_id=1, source_target_pairs={{0,8},{8,0},{16,24},{24,16},{32,40},{40,32},{48,56},{56,48},{64,72... | collective-permute-start | bytes 3686408 | tf_op jit(solution)/shard_map/ppermute | solution.py:366
  73.3 20.3 %collective-permute-start.10 = (bf16[2,16,6400]{2,1,0:T(8,128)(2,1)S(1)}, bf16[2,16,6400]{2,1,0:T(8,128)(2,1)S(1)}, u32[]{:S(2)}, u32[]{:S(2)}) collective-permute-start(bf16[2,16,6400]{2,1,0:T(8,128)(2,1)S(1)} %get-tuple-element.26), channel_id=1, source_target_pairs={{0,8},{8,0},{16,24},{24,16},{32,40},{40,32},{48,56},{56,48},{64,72... | collective-permute-start | bytes 1228808 | tf_op jit(solution)/shard_map/ppermute | solution.py:381
  73.8 20.0 %collective-permute-start.13 = (bf16[2,16,6400]{2,1,0:T(8,128)(2,1)S(1)}, bf16[2,16,6400]{2,1,0:T(8,128)(2,1)S(1)}, u32[]{:S(2)}, u32[]{:S(2)}) collective-permute-start(bf16[2,16,6400]{2,1,0:T(8,128)(2,1)S(1)} %get-tuple-element.30), channel_id=1, source_target_pairs={{0,80},{8,120},{16,96},{24,72},{32,112},{40,88},{48,64},{56,104},{... | collective-permute-start | bytes 1228808 | tf_op jit(solution)/shard_map/ppermute | solution.py:299
  78.2 15.6 %collective-permute-start.14 = (bf16[2,16,6400]{2,1,0:T(8,128)(2,1)S(1)}, bf16[2,16,6400]{2,1,0:T(8,128)(2,1)S(1)}, u32[]{:S(2)}, u32[]{:S(2)}) collective-permute-start(bf16[2,16,6400]{2,1,0:T(8,128)(2,1)S(1)} %get-tuple-element.31), channel_id=1, source_target_pairs={{0,16},{8,56},{16,32},{24,8},{32,48},{40,24},{48,0},{56,40},{64,80... | collective-permute-start | bytes 1228808 | tf_op jit(solution)/shard_map/ppermute | solution.py:299
  78.6 15.0 %collective-permute-start.11 = (bf16[16,6400]{1,0:T(8,128)(2,1)S(1)}, bf16[16,6400]{1,0:T(8,128)(2,1)S(1)}, u32[]{:S(2)}, u32[]{:S(2)}) collective-permute-start(bf16[16,6400]{1,0:T(8,128)(2,1)S(1)} %get-tuple-element.27), channel_id=1, source_target_pairs={{0,32},{8,72},{16,48},{24,88},{32,0},{40,104},{48,16},{56,120},{64... | collective-permute-start | bytes 614408 | tf_op jit(solution)/shard_map/ppermute | solution.py:299
  79.8 14.0 %collective-permute-start.12 = (bf16[16,6400]{1,0:T(8,128)(2,1)S(1)}, bf16[16,6400]{1,0:T(8,128)(2,1)S(1)}, u32[]{:S(2)}, u32[]{:S(2)}) collective-permute-start(bf16[16,6400]{1,0:T(8,128)(2,1)S(1)} %get-tuple-element.29), channel_id=1, source_target_pairs={{0,64},{8,40},{16,80},{24,56},{32,96},{40,8},{48,112},{56,24},{64,... | collective-permute-start | bytes 614408 | tf_op jit(solution)/shard_map/ppermute | solution.py:299
  93.7 6.5 %collective-permute-start.16 = (bf16[16,6400]{1,0:T(8,128)(2,1)S(1)}, bf16[16,6400]{1,0:T(8,128)(2,1)S(1)}, u32[]{:S(2)}, u32[]{:S(2)}) collective-permute-start(bf16[16,6400]{1,0:T(8,128)(2,1)S(1)} %get-tuple-element.32), channel_id=1, source_target_pairs={{0,64},{8,40},{16,80},{24,56},{32,96},{40,8},{48,112},{56,24},{64,... | collective-permute-start | bytes 614408 | tf_op jit(solution)/shard_map/ppermute | solution.py:299
  93.9 6.3 %collective-permute-start.15 = (bf16[16,6400]{1,0:T(8,128)(2,1)S(1)}, bf16[16,6400]{1,0:T(8,128)(2,1)S(1)}, u32[]{:S(2)}, u32[]{:S(2)}) collective-permute-start(bf16[16,6400]{1,0:T(8,128)(2,1)S(1)} %hand.1), channel_id=1, source_target_pairs={{0,8},{8,0},{16,24},{24,16},{32,40},{40,32},{48,56},{56,48},{64,72... | collective-permute-start | bytes 614408 | tf_op jit(solution)/shard_map/ppermute | solution.py:399

commit v13 on v10

--- a/solution.py
+++ b/solution.py
@@ -244,21 +244,17 @@
     return own[k].astype(F32) + other[k].astype(F32)
 
 
-def pair_kernel(own, other, _, farthest, second, later):
+def pair_kernel(own, other, _, farthest, second, third, later):
     farthest[...] = both(own, other, 0).astype(BF)
     for q in range(2):
         second[q] = both(own, other, 1 + q).astype(BF)
-
-
-def third_kernel(own, other, third):
-    for q in range(2):
-        third[q] = both(own, other, q).astype(BF)
+        third[q] = both(own, other, 3 + q).astype(BF)
 
 
 def merge_kernel(own, other, forwarded, first, stay):
-    first[0] = (both(own, other, 2) + forwarded[...].astype(F32)).astype(BF)
-    first[1] = both(own, other, 3).astype(BF)
-    stay[...] = both(own, other, 4).astype(BF)
+    first[0] = (both(own, other, 0) + forwarded[...].astype(F32)).astype(BF)
+    first[1] = both(own, other, 1).astype(BF)
+    stay[...] = both(own, other, 2).astype(BF)
 
 
 def hand_kernel(first, second, third, out):
@@ -361,34 +357,25 @@
         in_specs=[HBM, HBM] + [VMEM] * 2,
         out_specs=[VMEM] * 5,
         out_shape=[shape((32, nodes))]
-        + [shape((count, 16, wide)) for count in (3, 5) for _ in range(2)],
+        + [shape((count, 16, wide)) for count in (5, 3) for _ in range(2)],
         scratch_shapes=[pltpu.VMEM((17, fin, nodes), F32)] + index_scratch,
         compiler_params=params(24),
         name="spread",
     )(block_cols, block_counts, values, grads)
 
     other1 = lax.ppermute(other1, "node", swap)
-    farthest, second, other2 = pl.pallas_call(
+    farthest, second, third, other2 = pl.pallas_call(
         pair_kernel,
         in_specs=[VMEM, VMEM, ANY],
-        out_specs=[VMEM, VMEM, ANY],
-        out_shape=[shape((16, wide)), shape((2, 16, wide)), shape((5, 16, wide))],
-        input_output_aliases={2: 2},
+        out_specs=[VMEM, VMEM, VMEM, ANY],
+        out_shape=[shape((16, wide))] + [shape((2, 16, wide))] * 2 + [shape((3, 16, wide))],
+        input_output_aliases={2: 3},
         compiler_params=params(16),
         name="pair",
     )(own1, other1, other2)
     forwarded = send(farthest, back(FORWARD))
-    second = send(second, back(SECOND))
+    second, third = send(second, back(SECOND)), send(third, back(THIRD))
     other2 = lax.ppermute(other2, "node", swap)
-    third = pl.pallas_call(
-        third_kernel,
-        in_specs=[VMEM] * 2,
-        out_specs=VMEM,
-        out_shape=shape((2, 16, wide)),
-        compiler_params=params(16),
-        name="third",
-    )(own2, other2)
-    third = send(third, back(THIRD))
     first, stay = pl.pallas_call(
         merge_kernel,
         in_specs=[VMEM] * 3,

time: 99 us -> 99 us (level)
  waiting for transfers between devices: 21.9 us -> 25.3 us
  starting transfers between devices: 27.1 us -> 23.8 us
    ppermute x8, starting transfers between devices: 18 us -> 14.6 us  [send(): return lax.ppermute(piece, 'node', shared_pairs(steps))]
    ppermute x8, waiting for transfers between devices: 16.8 us -> 19.6 us  [send(): return lax.ppermute(piece, 'node', shared_pairs(steps))]
where the time goes in v13:
time: 99 us; the launch traced here: 98.7 us
  blocking collectives  28.4 us (29%)
  waiting for transfers between devices  25.3 us (26%)
  starting transfers between devices  23.8 us (24%)
  Pallas kernels  19.6 us (20%)
    ppermute x8, waiting for transfers between devices, send(): return lax.ppermute(piece, 'node', shared_pairs(steps))  19.6 us
    all_to_all x1, blocking collectives, local(): both = lax.all_to_all(mixed, 'feat', 0, 0, tiled=True)  16.1 us
    ppermute x8, starting transfers between devices, send(): return lax.ppermute(piece, 'node', shared_pairs(steps))  14.6 us
    all_to_all x1, blocking collectives, local(): grads = lax.all_to_all(dense, 'feat', 0, 0, tiled=True)  12.3 us
    pallas_call x1, Pallas kernels, local(): pl.pallas_call(spread_kernel, in_specs=[HBM, HBM] + [VMEM] * 2, out_specs...  6.88 us
    pallas_call x1, Pallas kernels, local(): pl.pallas_call(load_kernel, in_specs=[pl.BlockSpec(memory_space=pltpu.HBM...  6.52 us
    ppermute x4, starting transfers between devices, local(): pieces += [piece, lax.ppermute(piece, 'node', swap)]  4.05 us
    pallas_call x1, Pallas kernels, local(): pl.pallas_call(mix_kernel, in_specs=[HBM, HBM] + [VMEM] * 14, out_specs=V...  3.7 us
  transfers between devices with their start and end apart: 16, of which 12 were waited for; matrix products, arithmetic and copies ran while one was open for 0% of the time, Pallas kernels for 7%

profile of v13, /device:TPU:1, one launch (start us, length us, event | category | flops | bytes accessed | tf_op | source)
XLA Modules:
  0.0 98.7 jit_solution(9774336447669665467)
XLA Ops:
  0.6 1.5 %collective-permute-start = (bf16[16,6144]{1,0:T(8,128)(2,1)}, bf16[16,6144]{1,0:T(8,128)(2,1)S(1)}, u32[]{:S(2)}, u32[]{:S(2)}) collective-permute-start(bf16[16,6144]{1,0:T(8,128)(2,1)} %rest_0_.1), channel_id=1, source_target_pairs={{0,8},{8,0},{16,24},{24,16},{32,40},{40,32},{48,56},{56,48},{64,72... | collective-permute-start | bytes 589832 | tf_op jit(solution)/shard_map/ppermute | solution.py:284
  2.1 0.9 copy-done
  3.7 3.8 %collective-permute-start.1 = (bf16[2,16,6144]{2,1,0:T(8,128)(2,1)S(1)}, bf16[2,16,6144]{2,1,0:T(8,128)(2,1)S(1)}, u32[]{:S(2)}, u32[]{:S(2)}) collective-permute-start(bf16[2,16,6144]{2,1,0:T(8,128)(2,1)S(1)} %place.3.rest_0_), channel_id=1, source_target_pairs={{0,64},{8,40},{16,80},{24,56},{32,96},{40,8},{48,112},{56,24},{64,... | collective-permute-start | bytes 1179656 | tf_op jit(solution)/shard_map/ppermute | solution.py:299
  7.4 0.7 collective-permute-start.5
  8.2 2.5 %collective-permute-start.3 = (bf16[2,16,6144]{2,1,0:T(8,128)(2,1)S(1)}, bf16[2,16,6144]{2,1,0:T(8,128)(2,1)S(1)}, u32[]{:S(2)}, u32[]{:S(2)}) collective-permute-start(bf16[2,16,6144]{2,1,0:T(8,128)(2,1)S(1)} %place.3.rest_0_), channel_id=1, source_target_pairs={{0,112},{8,88},{16,64},{24,104},{32,80},{40,120},{48,96},{56,72},{... | collective-permute-start | bytes 1179656 | tf_op jit(solution)/shard_map/ppermute | solution.py:299
  10.6 6.5 %load.1 = (bf16[48,12,128,128]{3,2,1,0:T(8,128)(2,1)S(1)}, f32[8,128]{1,0:T(8,128)S(1)}) custom-call(bf16[48,12,128,128]{3,2,1,0:T(8,128)(2,1)} %values.1, bf16[2,16,6144]{2,1,0:T(8,128)(2,1)S(1)} %place.3.rest_0_), custom_call_target="tpu_custom_call" | custom-call | bytes 37748736 | tf_op jit(solution)/shard_map/load/pallas_call | solution.py:302
  17.6 4.1 %collective-permute-done.5.rest_6_ = bf16[2,16,6144]{2,1,0:T(8,128)(2,1)S(1)} collective-permute-done((bf16[2,16,6144]{2,1,0:T(8,128)(2,1)S(1)}, bf16[2,16,6144]{2,1,0:T(8,128)(2,1)S(1)}, u32[]{:S(2)}, u32[]{:S(2)}) %collective-permute-start.5) | collective-permute-done | bytes 393248 | tf_op jit(solution)/shard_map/ppermute | solution.py:299
  21.6 3.2 %collective-permute-start.6 = (bf16[2,16,6144]{2,1,0:T(8,128)(2,1)S(1)}, bf16[2,16,6144]{2,1,0:T(8,128)(2,1)S(1)}, u32[]{:S(2)}, u32[]{:S(2)}) collective-permute-start(bf16[2,16,6144]{2,1,0:T(8,128)(2,1)S(1)} %collective-permute-done.5.rest_6_), channel_id=1, source_target_pairs={{0,8},{8,0},{16,24},{24,16},{32,40},{40,32},{48,56},{56,48},{64,72... | collective-permute-start | bytes 1179656 | tf_op jit(solution)/shard_map/ppermute | solution.py:324
  26.2 0.6 collective-permute-done.4.rest_5_
  26.8 0.6 collective-permute-done.2.rest_3_
  27.6 3.7 %mix.1 = bf16[8,16,2816]{2,1,0:T(8,128)(2,1)S(1)} custom-call(s32[12,48]{1,0:T(8,128)} %bitcast.5, s32[48]{0:T(128)} %counts_in.3, bf16[48,12,128,128]{3,2,1,0:T(8,128)(2,1)S(1)} %get-tuple-element.18.values, bf16[32,6144]{1,0:T(8,128)(2,1)S(1)} %copy-done.2, bf16[16,256]{1,0:T(8,128)(2,1)S(1)} %copy-done.4, f32[1,32]{1,0:T(1,128)S(1)} %bitcast.4, ...), custom_call_target="tpu_custom_call" | custom-call | tf_op jit(solution)/shard_map/mix/pallas_call | solution.py:331
  31.3 16.1 %all_to_all.10.both = bf16[8,16,2816]{2,1,0:T(8,128)(2,1)S(1)} all-to-all(bf16[8,16,2816]{2,1,0:T(8,128)(2,1)S(1)} %mix.1), channel_id=1, replica_groups=mesh['node'=16,'feat'=8] {'feat'}, dimensions={0} | all-to-all | bytes 1441792 | tf_op jit(solution)/shard_map/all_to_all | solution.py:341
  47.4 0.7 dense.1
  48.1 12.3 %all_to_all.11.grads = bf16[8,16,2560]{2,1,0:T(8,128)(2,1)S(1)} all-to-all(bf16[8,16,2560]{2,1,0:T(8,128)(2,1)S(1)} %dense.1), channel_id=1, replica_groups=mesh['node'=16,'feat'=8] {'feat'}, dimensions={0} | all-to-all | bytes 1310720 | tf_op jit(solution)/shard_map/all_to_all | solution.py:352
  60.5 6.9 %spread.1 = (bf16[32,6144]{1,0:T(8,128)(2,1)}, bf16[5,16,6400]{2,1,0:T(8,128)(2,1)S(1)}, bf16[5,16,6400]{2,1,0:T(8,128)(2,1)S(1)}, bf16[3,16,6400]{2,1,0:T(8,128)(2,1)S(1)}, bf16[3,16,6400]{2,1,0:T(8,128)(2,1)S(1)}) custom-call(s32[12,48]{1,0:T(8,128)} %bitcast.6, s32[48]{0:T(128)} %counts_in.3, bf16[48,12,128,128]{3,2,1,0:T(8,128)(2,1)S(1)} %get-tuple-element.18.values, ...), custom_call_target="tpu_custom_call" | custom-call | tf_op jit(solution)/shard_map/spread/pallas_call | solution.py:355
  67.3 3.1 %collective-permute-start.9 = (bf16[5,16,6400]{2,1,0:T(8,128)(2,1)S(1)}, bf16[5,16,6400]{2,1,0:T(8,128)(2,1)S(1)}, u32[]{:S(2)}, u32[]{:S(2)}) collective-permute-start(bf16[5,16,6400]{2,1,0:T(8,128)(2,1)S(1)} %get-tuple-element.23), channel_id=1, source_target_pairs={{0,8},{8,0},{16,24},{24,16},{32,40},{40,32},{48,56},{56,48},{64,72... | collective-permute-start | bytes 3072008 | tf_op jit(solution)/shard_map/ppermute | solution.py:366
  70.4 2.3 %collective-permute-done.9.other = bf16[5,16,6400]{2,1,0:T(8,128)(2,1)S(1)} collective-permute-done((bf16[5,16,6400]{2,1,0:T(8,128)(2,1)S(1)}, bf16[5,16,6400]{2,1,0:T(8,128)(2,1)S(1)}, u32[]{:S(2)}, u32[]{:S(2)}) %collective-permute-start.9) | collective-permute-done | bytes 1024032 | tf_op jit(solution)/shard_map/ppermute | solution.py:366
  73.4 2.0 %collective-permute-start.11 = (bf16[16,6400]{1,0:T(8,128)(2,1)S(1)}, bf16[16,6400]{1,0:T(8,128)(2,1)S(1)}, u32[]{:S(2)}, u32[]{:S(2)}) collective-permute-start(bf16[16,6400]{1,0:T(8,128)(2,1)S(1)} %get-tuple-element.26), channel_id=1, source_target_pairs={{0,32},{8,72},{16,48},{24,88},{32,0},{40,104},{48,16},{56,120},{64... | collective-permute-start | bytes 614408 | tf_op jit(solution)/shard_map/ppermute | solution.py:299
  75.4 4.1 %collective-permute-start.13 = (bf16[2,16,6400]{2,1,0:T(8,128)(2,1)S(1)}, bf16[2,16,6400]{2,1,0:T(8,128)(2,1)S(1)}, u32[]{:S(2)}, u32[]{:S(2)}) collective-permute-start(bf16[2,16,6400]{2,1,0:T(8,128)(2,1)S(1)} %get-tuple-element.29), channel_id=1, source_target_pairs={{0,80},{8,120},{16,96},{24,72},{32,112},{40,88},{48,64},{56,104},{... | collective-permute-start | bytes 1228808 | tf_op jit(solution)/shard_map/ppermute | solution.py:299
  80.0 1.2 %collective-permute-start.12 = (bf16[2,16,6400]{2,1,0:T(8,128)(2,1)S(1)}, bf16[2,16,6400]{2,1,0:T(8,128)(2,1)S(1)}, u32[]{:S(2)}, u32[]{:S(2)}) collective-permute-start(bf16[2,16,6400]{2,1,0:T(8,128)(2,1)S(1)} %get-tuple-element.28), channel_id=1, source_target_pairs={{0,64},{8,40},{16,80},{24,56},{32,96},{40,8},{48,112},{56,24},{64,... | collective-permute-start | bytes 1228808 | tf_op jit(solution)/shard_map/ppermute | solution.py:299
  81.1 9.3 %collective-permute-done.13.second = bf16[2,16,6400]{2,1,0:T(8,128)(2,1)S(1)} collective-permute-done((bf16[2,16,6400]{2,1,0:T(8,128)(2,1)S(1)}, bf16[2,16,6400]{2,1,0:T(8,128)(2,1)S(1)}, u32[]{:S(2)}, u32[]{:S(2)}) %collective-permute-start.13) | collective-permute-done | bytes 409632 | tf_op jit(solution)/shard_map/ppermute | solution.py:299
  90.7 5.6 %collective-permute-done.12.first = bf16[2,16,6400]{2,1,0:T(8,128)(2,1)S(1)} collective-permute-done((bf16[2,16,6400]{2,1,0:T(8,128)(2,1)S(1)}, bf16[2,16,6400]{2,1,0:T(8,128)(2,1)S(1)}, u32[]{:S(2)}, u32[]{:S(2)}) %collective-permute-start.12) | collective-permute-done | bytes 409632 | tf_op jit(solution)/shard_map/ppermute | solution.py:299
  96.5 1.4 %collective-permute-done.15.handed = bf16[16,6400]{1,0:T(8,128)(2,1)S(1)} collective-permute-done((bf16[16,6400]{1,0:T(8,128)(2,1)S(1)}, bf16[16,6400]{1,0:T(8,128)(2,1)S(1)}, u32[]{:S(2)}, u32[]{:S(2)}) %collective-permute-start.15) | collective-permute-done | bytes 204832 | tf_op jit(solution)/shard_map/ppermute | solution.py:396
  97.9 0.8 last.1
  (33 shorter events, 4.2 us)
Async XLA Ops:
  0.6 2.8 %collective-permute-start = (bf16[16,6144]{1,0:T(8,128)(2,1)}, bf16[16,6144]{1,0:T(8,128)(2,1)S(1)}, u32[]{:S(2)}, u32[]{:S(2)}) collective-permute-start(bf16[16,6144]{1,0:T(8,128)(2,1)} %rest_0_.1), channel_id=1, source_target_pairs={{0,8},{8,0},{16,24},{24,16},{32,40},{40,32},{48,56},{56,48},{64,72... | collective-permute-start | bytes 589832 | tf_op jit(solution)/shard_map/ppermute | solution.py:284
  2.1 0.9 copy-start
  3.1 24.5 %copy-start.1 = (bf16[16,6144]{1,0:T(8,128)(2,1)S(1)}, bf16[16,6144]{1,0:T(8,128)(2,1)}, u32[]{:S(2)}) copy-start(bf16[16,6144]{1,0:T(8,128)(2,1)} %rest_0_.1) | copy-start | bytes 589828
  3.1 24.5 %copy-start.2 = (bf16[32,6144]{1,0:T(8,128)(2,1)S(1)}, bf16[32,6144]{1,0:T(8,128)(2,1)}, u32[]{:S(2)}) copy-start(bf16[32,6144]{1,0:T(8,128)(2,1)} %cotangent.1) | copy-start | bytes 1179652
  3.1 24.5 %copy-start.4 = (bf16[16,256]{1,0:T(8,128)(2,1)S(1)}, bf16[16,256]{1,0:T(8,128)(2,1)}, u32[]{:S(2)}) copy-start(bf16[16,256]{1,0:T(8,128)(2,1)} %weight.1) | copy-start | bytes 24580
  3.1 24.5 %copy-start.5 = (f32[32]{0:T(128)S(1)}, f32[32]{0:T(128)}, u32[]{:S(2)}) copy-start(f32[32]{0:T(128)} %param.10) | copy-start | bytes 388
  3.7 43.7 %copy-start.3 = (s32[6144]{0:T(1024)S(1)}, s32[6144]{0:T(1024)}, u32[]{:S(2)}) copy-start(s32[6144]{0:T(1024)} %param.14) | copy-start | bytes 73732
  3.7 13.5 %collective-permute-start.1 = (bf16[2,16,6144]{2,1,0:T(8,128)(2,1)S(1)}, bf16[2,16,6144]{2,1,0:T(8,128)(2,1)S(1)}, u32[]{:S(2)}, u32[]{:S(2)}) collective-permute-start(bf16[2,16,6144]{2,1,0:T(8,128)(2,1)S(1)} %place.3.rest_0_), channel_id=1, source_target_pairs={{0,64},{8,40},{16,80},{24,56},{32,96},{40,8},{48,112},{56,24},{64,... | collective-permute-start | bytes 1179656 | tf_op jit(solution)/shard_map/ppermute | solution.py:299
  7.4 14.2 %collective-permute-start.5 = (bf16[2,16,6144]{2,1,0:T(8,128)(2,1)S(1)}, bf16[2,16,6144]{2,1,0:T(8,128)(2,1)S(1)}, u32[]{:S(2)}, u32[]{:S(2)}) collective-permute-start(bf16[2,16,6144]{2,1,0:T(8,128)(2,1)S(1)} %place.3.rest_0_), channel_id=1, source_target_pairs={{0,48},{8,24},{16,0},{24,40},{32,16},{40,56},{48,32},{56,8},{64,11... | collective-permute-start | bytes 1179656 | tf_op jit(solution)/shard_map/ppermute | solution.py:299
  8.2 16.7 %collective-permute-start.3 = (bf16[2,16,6144]{2,1,0:T(8,128)(2,1)S(1)}, bf16[2,16,6144]{2,1,0:T(8,128)(2,1)S(1)}, u32[]{:S(2)}, u32[]{:S(2)}) collective-permute-start(bf16[2,16,6144]{2,1,0:T(8,128)(2,1)S(1)} %place.3.rest_0_), channel_id=1, source_target_pairs={{0,112},{8,88},{16,64},{24,104},{32,80},{40,120},{48,96},{56,72},{... | collective-permute-start | bytes 1179656 | tf_op jit(solution)/shard_map/ppermute | solution.py:299
  17.2 8.2 %collective-permute-start.7 = (bf16[16,6144]{1,0:T(8,128)(2,1)S(1)}, bf16[16,6144]{1,0:T(8,128)(2,1)S(1)}, u32[]{:S(2)}, u32[]{:S(2)}) collective-permute-start(bf16[16,6144]{1,0:T(8,128)(2,1)S(1)} %pick.1), channel_id=1, source_target_pairs={{0,32},{8,72},{16,48},{24,88},{32,0},{40,104},{48,16},{56,120},{64... | collective-permute-start | bytes 589832 | tf_op jit(solution)/shard_map/ppermute | solution.py:299
  21.6 4.6 %collective-permute-start.6 = (bf16[2,16,6144]{2,1,0:T(8,128)(2,1)S(1)}, bf16[2,16,6144]{2,1,0:T(8,128)(2,1)S(1)}, u32[]{:S(2)}, u32[]{:S(2)}) collective-permute-start(bf16[2,16,6144]{2,1,0:T(8,128)(2,1)S(1)} %collective-permute-done.5.rest_6_), channel_id=1, source_target_pairs={{0,8},{8,0},{16,24},{24,16},{32,40},{40,32},{48,56},{56,48},{64,72... | collective-permute-start | bytes 1179656 | tf_op jit(solution)/shard_map/ppermute | solution.py:324
  24.9 1.9 %collective-permute-start.4 = (bf16[2,16,6144]{2,1,0:T(8,128)(2,1)S(1)}, bf16[2,16,6144]{2,1,0:T(8,128)(2,1)S(1)}, u32[]{:S(2)}, u32[]{:S(2)}) collective-permute-start(bf16[2,16,6144]{2,1,0:T(8,128)(2,1)S(1)} %collective-permute-done.3.rest_4_), channel_id=1, source_target_pairs={{0,8},{8,0},{16,24},{24,16},{32,40},{40,32},{48,56},{56,48},{64,72... | collective-permute-start | bytes 1179656 | tf_op jit(solution)/shard_map/ppermute | solution.py:324
  24.9 2.5 %collective-permute-start.2 = (bf16[2,16,6144]{2,1,0:T(8,128)(2,1)S(1)}, bf16[2,16,6144]{2,1,0:T(8,128)(2,1)S(1)}, u32[]{:S(2)}, u32[]{:S(2)}) collective-permute-start(bf16[2,16,6144]{2,1,0:T(8,128)(2,1)S(1)} %collective-permute-done.1.pair.rest_2_), channel_id=1, source_target_pairs={{0,8},{8,0},{16,24},{24,16},{32,40},{40,32},{48,56},{56,48},{64,72... | collective-permute-start | bytes 1179656 | tf_op jit(solution)/shard_map/ppermute | solution.py:324
  25.4 2.2 %collective-permute-start.8 = (bf16[16,6144]{1,0:T(8,128)(2,1)S(1)}, bf16[16,6144]{1,0:T(8,128)(2,1)S(1)}, u32[]{:S(2)}, u32[]{:S(2)}) collective-permute-start(bf16[16,6144]{1,0:T(8,128)(2,1)S(1)} %collective-permute-done.7.rest_8_), channel_id=1, source_target_pairs={{0,8},{8,0},{16,24},{24,16},{32,40},{40,32},{48,56},{56,48},{64,72... | collective-permute-start | bytes 589832 | tf_op jit(solution)/shard_map/ppermute | solution.py:324
  67.3 5.3 %collective-permute-start.9 = (bf16[5,16,6400]{2,1,0:T(8,128)(2,1)S(1)}, bf16[5,16,6400]{2,1,0:T(8,128)(2,1)S(1)}, u32[]{:S(2)}, u32[]{:S(2)}) collective-permute-start(bf16[5,16,6400]{2,1,0:T(8,128)(2,1)S(1)} %get-tuple-element.23), channel_id=1, source_target_pairs={{0,8},{8,0},{16,24},{24,16},{32,40},{40,32},{48,56},{56,48},{64,72... | collective-permute-start | bytes 3072008 | tf_op jit(solution)/shard_map/ppermute | solution.py:366
  72.9 6.9 %collective-permute-start.10 = (bf16[3,16,6400]{2,1,0:T(8,128)(2,1)S(1)}, bf16[3,16,6400]{2,1,0:T(8,128)(2,1)S(1)}, u32[]{:S(2)}, u32[]{:S(2)}) collective-permute-start(bf16[3,16,6400]{2,1,0:T(8,128)(2,1)S(1)} %get-tuple-element.25), channel_id=1, source_target_pairs={{0,8},{8,0},{16,24},{24,16},{32,40},{40,32},{48,56},{56,48},{64,72... | collective-permute-start | bytes 1843208 | tf_op jit(solution)/shard_map/ppermute | solution.py:378
  73.4 6.4 %collective-permute-start.11 = (bf16[16,6400]{1,0:T(8,128)(2,1)S(1)}, bf16[16,6400]{1,0:T(8,128)(2,1)S(1)}, u32[]{:S(2)}, u32[]{:S(2)}) collective-permute-start(bf16[16,6400]{1,0:T(8,128)(2,1)S(1)} %get-tuple-element.26), channel_id=1, source_target_pairs={{0,32},{8,72},{16,48},{24,88},{32,0},{40,104},{48,16},{56,120},{64... | collective-permute-start | bytes 614408 | tf_op jit(solution)/shard_map/ppermute | solution.py:299
  75.4 15.1 %collective-permute-start.13 = (bf16[2,16,6400]{2,1,0:T(8,128)(2,1)S(1)}, bf16[2,16,6400]{2,1,0:T(8,128)(2,1)S(1)}, u32[]{:S(2)}, u32[]{:S(2)}) collective-permute-start(bf16[2,16,6400]{2,1,0:T(8,128)(2,1)S(1)} %get-tuple-element.29), channel_id=1, source_target_pairs={{0,80},{8,120},{16,96},{24,72},{32,112},{40,88},{48,64},{56,104},{... | collective-permute-start | bytes 1228808 | tf_op jit(solution)/shard_map/ppermute | solution.py:299
  79.4 11.3 %collective-permute-start.14 = (bf16[2,16,6400]{2,1,0:T(8,128)(2,1)S(1)}, bf16[2,16,6400]{2,1,0:T(8,128)(2,1)S(1)}, u32[]{:S(2)}, u32[]{:S(2)}) collective-permute-start(bf16[2,16,6400]{2,1,0:T(8,128)(2,1)S(1)} %get-tuple-element.30), channel_id=1, source_target_pairs={{0,16},{8,56},{16,32},{24,8},{32,48},{40,24},{48,0},{56,40},{64,80... | collective-permute-start | bytes 1228808 | tf_op jit(solution)/shard_map/ppermute | solution.py:299
  80.0 16.3 %collective-permute-start.12 = (bf16[2,16,6400]{2,1,0:T(8,128)(2,1)S(1)}, bf16[2,16,6400]{2,1,0:T(8,128)(2,1)S(1)}, u32[]{:S(2)}, u32[]{:S(2)}) collective-permute-start(bf16[2,16,6400]{2,1,0:T(8,128)(2,1)S(1)} %get-tuple-element.28), channel_id=1, source_target_pairs={{0,64},{8,40},{16,80},{24,56},{32,96},{40,8},{48,112},{56,24},{64,... | collective-permute-start | bytes 1228808 | tf_op jit(solution)/shard_map/ppermute | solution.py:299
  96.4 1.5 %collective-permute-start.15 = (bf16[16,6400]{1,0:T(8,128)(2,1)S(1)}, bf16[16,6400]{1,0:T(8,128)(2,1)S(1)}, u32[]{:S(2)}, u32[]{:S(2)}) collective-permute-start(bf16[16,6400]{1,0:T(8,128)(2,1)S(1)} %hand.1), channel_id=1, source_target_pairs={{0,8},{8,0},{16,24},{24,16},{32,40},{40,32},{48,56},{56,48},{64,72... | collective-permute-start | bytes 614408 | tf_op jit(solution)/shard_map/ppermute | solution.py:396

commit v14 on v13

--- a/solution.py
+++ b/solution.py
@@ -130,7 +130,7 @@
         parts, jnp.where(place, 1.0, 0.0).astype(BF), preferred_element_type=F32
     ).astype(BF)
 
-    first, second, third, farthest = (pieces[at : at + 2] for at in (2, 4, 6, 8))
+    first, second, third, farthest = (pieces[at : at + 2] for at in (8, 4, 2, 6))
     for server in range(2):
         held[node_near(0, 0, server)] = pieces[server][...]
         held[node_near(*FARTHEST, server)] = farthest[server][...]
@@ -320,7 +320,7 @@
         name="pick",
     )(first, loaded)
     forwarded = send(picked, FORWARD)
-    for piece in (first, second, third, forwarded):
+    for piece in (third, second, forwarded, first):
         pieces += [piece, lax.ppermute(piece, "node", swap)]
 
     index_scratch = [

time: 99 us -> 99.6 us (level)
  waiting for transfers between devices: 25.3 us -> 18.5 us
  starting transfers between devices: 23.8 us -> 30.2 us
    ppermute x8, waiting for transfers between devices: 19.6 us -> 14 us  [send(): return lax.ppermute(piece, 'node', shared_pairs(steps))]
    ppermute x4, starting transfers between devices: 4.05 us -> 7.18 us  [local(): pieces += [piece, lax.ppermute(piece, 'node', swap)]]
    ppermute x8, starting transfers between devices: 14.6 us -> 17 us  [send(): return lax.ppermute(piece, 'node', shared_pairs(steps))]
  transfers between devices with their start and end apart: 16 -> 16, of which waited for: 12 -> 10; matrix products, arithmetic and copies ran while one was open for 0% -> 0% of each run, Pallas kernels for 7% -> 7%
where the time goes in v14:
time: 99.6 us; the launch traced here: 99.3 us
  starting transfers between devices  30.2 us (30%)
  blocking collectives  29.3 us (29%)
  Pallas kernels  19.6 us (20%)
  waiting for transfers between devices  18.5 us (19%)
    all_to_all x1, blocking collectives, local(): both = lax.all_to_all(mixed, 'feat', 0, 0, tiled=True)  17 us
    ppermute x8, starting transfers between devices, send(): return lax.ppermute(piece, 'node', shared_pairs(steps))  17 us
    ppermute x8, waiting for transfers between devices, send(): return lax.ppermute(piece, 'node', shared_pairs(steps))  14 us
    all_to_all x1, blocking collectives, local(): grads = lax.all_to_all(dense, 'feat', 0, 0, tiled=True)  12.3 us
    ppermute x4, starting transfers between devices, local(): pieces += [piece, lax.ppermute(piece, 'node', swap)]  7.18 us
    pallas_call x1, Pallas kernels, local(): pl.pallas_call(spread_kernel, in_specs=[HBM, HBM] + [VMEM] * 2, out_specs...  6.87 us
    pallas_call x1, Pallas kernels, local(): pl.pallas_call(load_kernel, in_specs=[pl.BlockSpec(memory_space=pltpu.HBM...  6.52 us
    pallas_call x1, Pallas kernels, local(): pl.pallas_call(mix_kernel, in_specs=[HBM, HBM] + [VMEM] * 14, out_specs=V...  3.71 us
  transfers between devices with their start and end apart: 16, of which 10 were waited for; matrix products, arithmetic and copies ran while one was open for 0% of the time, Pallas kernels for 7%

profile of v14, /device:TPU:1, one launch (start us, length us, event | category | flops | bytes accessed | tf_op | source)
XLA Modules:
  0.0 99.3 jit_solution(4200579271300546273)
XLA Ops:
  0.6 1.5 %collective-permute-start = (bf16[16,6144]{1,0:T(8,128)(2,1)}, bf16[16,6144]{1,0:T(8,128)(2,1)S(1)}, u32[]{:S(2)}, u32[]{:S(2)}) collective-permute-start(bf16[16,6144]{1,0:T(8,128)(2,1)} %rest_0_.1), channel_id=1, source_target_pairs={{0,8},{8,0},{16,24},{24,16},{32,40},{40,32},{48,56},{56,48},{64,72... | collective-permute-start | bytes 589832 | tf_op jit(solution)/shard_map/ppermute | solution.py:284
  2.1 0.9 copy-done
  3.7 3.8 %collective-permute-start.5 = (bf16[2,16,6144]{2,1,0:T(8,128)(2,1)S(1)}, bf16[2,16,6144]{2,1,0:T(8,128)(2,1)S(1)}, u32[]{:S(2)}, u32[]{:S(2)}) collective-permute-start(bf16[2,16,6144]{2,1,0:T(8,128)(2,1)S(1)} %place.3.rest_0_), channel_id=1, source_target_pairs={{0,64},{8,40},{16,80},{24,56},{32,96},{40,8},{48,112},{56,24},{64,... | collective-permute-start | bytes 1179656 | tf_op jit(solution)/shard_map/ppermute | solution.py:299
  7.4 3.2 %collective-permute-start.3 = (bf16[2,16,6144]{2,1,0:T(8,128)(2,1)S(1)}, bf16[2,16,6144]{2,1,0:T(8,128)(2,1)S(1)}, u32[]{:S(2)}, u32[]{:S(2)}) collective-permute-start(bf16[2,16,6144]{2,1,0:T(8,128)(2,1)S(1)} %place.3.rest_0_), channel_id=1, source_target_pairs={{0,112},{8,88},{16,64},{24,104},{32,80},{40,120},{48,96},{56,72},{... | collective-permute-start | bytes 1179656 | tf_op jit(solution)/shard_map/ppermute | solution.py:299
  10.6 6.5 %load.1 = (bf16[48,12,128,128]{3,2,1,0:T(8,128)(2,1)S(1)}, f32[8,128]{1,0:T(8,128)S(1)}) custom-call(bf16[48,12,128,128]{3,2,1,0:T(8,128)(2,1)} %values.1, bf16[2,16,6144]{2,1,0:T(8,128)(2,1)S(1)} %place.3.rest_0_), custom_call_target="tpu_custom_call" | custom-call | bytes 37748736 | tf_op jit(solution)/shard_map/load/pallas_call | solution.py:302
  17.6 3.7 %collective-permute-start.8 = (bf16[2,16,6144]{2,1,0:T(8,128)(2,1)S(1)}, bf16[2,16,6144]{2,1,0:T(8,128)(2,1)S(1)}, u32[]{:S(2)}, u32[]{:S(2)}) collective-permute-start(bf16[2,16,6144]{2,1,0:T(8,128)(2,1)S(1)} %collective-permute-done.5.pair.rest_8_), channel_id=1, source_target_pairs={{0,8},{8,0},{16,24},{24,16},{32,40},{40,32},{48,56},{56,48},{64,72... | collective-permute-start | bytes 1179656 | tf_op jit(solution)/shard_map/ppermute | solution.py:324
  21.9 2.4 %collective-permute-start.4 = (bf16[2,16,6144]{2,1,0:T(8,128)(2,1)S(1)}, bf16[2,16,6144]{2,1,0:T(8,128)(2,1)S(1)}, u32[]{:S(2)}, u32[]{:S(2)}) collective-permute-start(bf16[2,16,6144]{2,1,0:T(8,128)(2,1)S(1)} %collective-permute-done.3.rest_4_), channel_id=1, source_target_pairs={{0,8},{8,0},{16,24},{24,16},{32,40},{40,32},{48,56},{56,48},{64,72... | collective-permute-start | bytes 1179656 | tf_op jit(solution)/shard_map/ppermute | solution.py:324
  24.3 1.1 %collective-permute-start.7 = (bf16[16,6144]{1,0:T(8,128)(2,1)S(1)}, bf16[16,6144]{1,0:T(8,128)(2,1)S(1)}, u32[]{:S(2)}, u32[]{:S(2)}) collective-permute-start(bf16[16,6144]{1,0:T(8,128)(2,1)S(1)} %collective-permute-done.6.rest_6_), channel_id=1, source_target_pairs={{0,8},{8,0},{16,24},{24,16},{32,40},{40,32},{48,56},{56,48},{64,72... | collective-permute-start | bytes 589832 | tf_op jit(solution)/shard_map/ppermute | solution.py:324
  26.5 3.7 %mix.1 = bf16[8,16,2816]{2,1,0:T(8,128)(2,1)S(1)} custom-call(s32[12,48]{1,0:T(8,128)} %bitcast.5, s32[48]{0:T(128)} %counts_in.3, bf16[48,12,128,128]{3,2,1,0:T(8,128)(2,1)S(1)} %get-tuple-element.18.values, bf16[32,6144]{1,0:T(8,128)(2,1)S(1)} %copy-done.2, bf16[16,256]{1,0:T(8,128)(2,1)S(1)} %copy-done.4, f32[1,32]{1,0:T(1,128)S(1)} %bitcast.4, ...), custom_call_target="tpu_custom_call" | custom-call | tf_op jit(solution)/shard_map/mix/pallas_call | solution.py:331
  30.2 17.0 %all_to_all.10.both = bf16[8,16,2816]{2,1,0:T(8,128)(2,1)S(1)} all-to-all(bf16[8,16,2816]{2,1,0:T(8,128)(2,1)S(1)} %mix.1), channel_id=1, replica_groups=mesh['node'=16,'feat'=8] {'feat'}, dimensions={0} | all-to-all | bytes 1441792 | tf_op jit(solution)/shard_map/all_to_all | solution.py:341
  47.2 0.7 dense.1
  47.9 12.3 %all_to_all.11.grads = bf16[8,16,2560]{2,1,0:T(8,128)(2,1)S(1)} all-to-all(bf16[8,16,2560]{2,1,0:T(8,128)(2,1)S(1)} %dense.1), channel_id=1, replica_groups=mesh['node'=16,'feat'=8] {'feat'}, dimensions={0} | all-to-all | bytes 1310720 | tf_op jit(solution)/shard_map/all_to_all | solution.py:352
  60.3 6.9 %spread.1 = (bf16[32,6144]{1,0:T(8,128)(2,1)}, bf16[5,16,6400]{2,1,0:T(8,128)(2,1)S(1)}, bf16[5,16,6400]{2,1,0:T(8,128)(2,1)S(1)}, bf16[3,16,6400]{2,1,0:T(8,128)(2,1)S(1)}, bf16[3,16,6400]{2,1,0:T(8,128)(2,1)S(1)}) custom-call(s32[12,48]{1,0:T(8,128)} %bitcast.6, s32[48]{0:T(128)} %counts_in.3, bf16[48,12,128,128]{3,2,1,0:T(8,128)(2,1)S(1)} %get-tuple-element.18.values, ...), custom_call_target="tpu_custom_call" | custom-call | tf_op jit(solution)/shard_map/spread/pallas_call | solution.py:355
  67.1 3.1 %collective-permute-start.9 = (bf16[5,16,6400]{2,1,0:T(8,128)(2,1)S(1)}, bf16[5,16,6400]{2,1,0:T(8,128)(2,1)S(1)}, u32[]{:S(2)}, u32[]{:S(2)}) collective-permute-start(bf16[5,16,6400]{2,1,0:T(8,128)(2,1)S(1)} %get-tuple-element.23), channel_id=1, source_target_pairs={{0,8},{8,0},{16,24},{24,16},{32,40},{40,32},{48,56},{56,48},{64,72... | collective-permute-start | bytes 3072008 | tf_op jit(solution)/shard_map/ppermute | solution.py:366
  70.2 2.3 %collective-permute-done.9.other = bf16[5,16,6400]{2,1,0:T(8,128)(2,1)S(1)} collective-permute-done((bf16[5,16,6400]{2,1,0:T(8,128)(2,1)S(1)}, bf16[5,16,6400]{2,1,0:T(8,128)(2,1)S(1)}, u32[]{:S(2)}, u32[]{:S(2)}) %collective-permute-start.9) | collective-permute-done | bytes 1024032 | tf_op jit(solution)/shard_map/ppermute | solution.py:366
  73.2 2.7 %collective-permute-start.11 = (bf16[16,6400]{1,0:T(8,128)(2,1)S(1)}, bf16[16,6400]{1,0:T(8,128)(2,1)S(1)}, u32[]{:S(2)}, u32[]{:S(2)}) collective-permute-start(bf16[16,6400]{1,0:T(8,128)(2,1)S(1)} %get-tuple-element.26), channel_id=1, source_target_pairs={{0,32},{8,72},{16,48},{24,88},{32,0},{40,104},{48,16},{56,120},{64... | collective-permute-start | bytes 614408 | tf_op jit(solution)/shard_map/ppermute | solution.py:299
  75.9 2.1 %collective-permute-start.13 = (bf16[2,16,6400]{2,1,0:T(8,128)(2,1)S(1)}, bf16[2,16,6400]{2,1,0:T(8,128)(2,1)S(1)}, u32[]{:S(2)}, u32[]{:S(2)}) collective-permute-start(bf16[2,16,6400]{2,1,0:T(8,128)(2,1)S(1)} %get-tuple-element.29), channel_id=1, source_target_pairs={{0,80},{8,120},{16,96},{24,72},{32,112},{40,88},{48,64},{56,104},{... | collective-permute-start | bytes 1228808 | tf_op jit(solution)/shard_map/ppermute | solution.py:299
  78.0 1.4 %collective-permute-start.14 = (bf16[2,16,6400]{2,1,0:T(8,128)(2,1)S(1)}, bf16[2,16,6400]{2,1,0:T(8,128)(2,1)S(1)}, u32[]{:S(2)}, u32[]{:S(2)}) collective-permute-start(bf16[2,16,6400]{2,1,0:T(8,128)(2,1)S(1)} %get-tuple-element.30), channel_id=1, source_target_pairs={{0,16},{8,56},{16,32},{24,8},{32,48},{40,24},{48,0},{56,40},{64,80... | collective-permute-start | bytes 1228808 | tf_op jit(solution)/shard_map/ppermute | solution.py:299
  79.8 3.4 %collective-permute-start.12 = (bf16[2,16,6400]{2,1,0:T(8,128)(2,1)S(1)}, bf16[2,16,6400]{2,1,0:T(8,128)(2,1)S(1)}, u32[]{:S(2)}, u32[]{:S(2)}) collective-permute-start(bf16[2,16,6400]{2,1,0:T(8,128)(2,1)S(1)} %get-tuple-element.28), channel_id=1, source_target_pairs={{0,64},{8,40},{16,80},{24,56},{32,96},{40,8},{48,112},{56,24},{64,... | collective-permute-start | bytes 1228808 | tf_op jit(solution)/shard_map/ppermute | solution.py:299
  83.1 7.2 %collective-permute-done.13.second = bf16[2,16,6400]{2,1,0:T(8,128)(2,1)S(1)} collective-permute-done((bf16[2,16,6400]{2,1,0:T(8,128)(2,1)S(1)}, bf16[2,16,6400]{2,1,0:T(8,128)(2,1)S(1)}, u32[]{:S(2)}, u32[]{:S(2)}) %collective-permute-start.13) | collective-permute-done | bytes 409632 | tf_op jit(solution)/shard_map/ppermute | solution.py:299
  90.3 6.0 %collective-permute-done.12.first = bf16[2,16,6400]{2,1,0:T(8,128)(2,1)S(1)} collective-permute-done((bf16[2,16,6400]{2,1,0:T(8,128)(2,1)S(1)}, bf16[2,16,6400]{2,1,0:T(8,128)(2,1)S(1)}, u32[]{:S(2)}, u32[]{:S(2)}) %collective-permute-start.12) | collective-permute-done | bytes 409632 | tf_op jit(solution)/shard_map/ppermute | solution.py:299
  96.4 1.0 %collective-permute-start.15 = (bf16[16,6400]{1,0:T(8,128)(2,1)S(1)}, bf16[16,6400]{1,0:T(8,128)(2,1)S(1)}, u32[]{:S(2)}, u32[]{:S(2)}) collective-permute-start(bf16[16,6400]{1,0:T(8,128)(2,1)S(1)} %hand.1), channel_id=1, source_target_pairs={{0,8},{8,0},{16,24},{24,16},{32,40},{40,32},{48,56},{56,48},{64,72... | collective-permute-start | bytes 614408 | tf_op jit(solution)/shard_map/ppermute | solution.py:396
  97.4 1.1 %collective-permute-done.15.handed = bf16[16,6400]{1,0:T(8,128)(2,1)S(1)} collective-permute-done((bf16[16,6400]{1,0:T(8,128)(2,1)S(1)}, bf16[16,6400]{1,0:T(8,128)(2,1)S(1)}, u32[]{:S(2)}, u32[]{:S(2)}) %collective-permute-start.15) | collective-permute-done | bytes 204832 | tf_op jit(solution)/shard_map/ppermute | solution.py:396
  98.5 0.8 last.1
  (33 shorter events, 3.8 us)
Async XLA Ops:
  0.6 2.8 %collective-permute-start = (bf16[16,6144]{1,0:T(8,128)(2,1)}, bf16[16,6144]{1,0:T(8,128)(2,1)S(1)}, u32[]{:S(2)}, u32[]{:S(2)}) collective-permute-start(bf16[16,6144]{1,0:T(8,128)(2,1)} %rest_0_.1), channel_id=1, source_target_pairs={{0,8},{8,0},{16,24},{24,16},{32,40},{40,32},{48,56},{56,48},{64,72... | collective-permute-start | bytes 589832 | tf_op jit(solution)/shard_map/ppermute | solution.py:284
  2.1 0.9 copy-start
  3.1 23.4 %copy-start.1 = (bf16[16,6144]{1,0:T(8,128)(2,1)S(1)}, bf16[16,6144]{1,0:T(8,128)(2,1)}, u32[]{:S(2)}) copy-start(bf16[16,6144]{1,0:T(8,128)(2,1)} %rest_0_.1) | copy-start | bytes 589828
  3.1 23.4 %copy-start.2 = (bf16[32,6144]{1,0:T(8,128)(2,1)S(1)}, bf16[32,6144]{1,0:T(8,128)(2,1)}, u32[]{:S(2)}) copy-start(bf16[32,6144]{1,0:T(8,128)(2,1)} %cotangent.1) | copy-start | bytes 1179652
  3.1 23.4 %copy-start.4 = (bf16[16,256]{1,0:T(8,128)(2,1)S(1)}, bf16[16,256]{1,0:T(8,128)(2,1)}, u32[]{:S(2)}) copy-start(bf16[16,256]{1,0:T(8,128)(2,1)} %weight.1) | copy-start | bytes 24580
  3.1 23.4 %copy-start.5 = (f32[32]{0:T(128)S(1)}, f32[32]{0:T(128)}, u32[]{:S(2)}) copy-start(f32[32]{0:T(128)} %param.10) | copy-start | bytes 388
  3.7 43.5 %copy-start.3 = (s32[6144]{0:T(1024)S(1)}, s32[6144]{0:T(1024)}, u32[]{:S(2)}) copy-start(s32[6144]{0:T(1024)} %param.14) | copy-start | bytes 73732
  3.7 13.5 %collective-permute-start.5 = (bf16[2,16,6144]{2,1,0:T(8,128)(2,1)S(1)}, bf16[2,16,6144]{2,1,0:T(8,128)(2,1)S(1)}, u32[]{:S(2)}, u32[]{:S(2)}) collective-permute-start(bf16[2,16,6144]{2,1,0:T(8,128)(2,1)S(1)} %place.3.rest_0_), channel_id=1, source_target_pairs={{0,64},{8,40},{16,80},{24,56},{32,96},{40,8},{48,112},{56,24},{64,... | collective-permute-start | bytes 1179656 | tf_op jit(solution)/shard_map/ppermute | solution.py:299
  7.4 14.5 %collective-permute-start.3 = (bf16[2,16,6144]{2,1,0:T(8,128)(2,1)S(1)}, bf16[2,16,6144]{2,1,0:T(8,128)(2,1)S(1)}, u32[]{:S(2)}, u32[]{:S(2)}) collective-permute-start(bf16[2,16,6144]{2,1,0:T(8,128)(2,1)S(1)} %place.3.rest_0_), channel_id=1, source_target_pairs={{0,112},{8,88},{16,64},{24,104},{32,80},{40,120},{48,96},{56,72},{... | collective-permute-start | bytes 1179656 | tf_op jit(solution)/shard_map/ppermute | solution.py:299
  10.6 13.7 %collective-permute-start.1 = (bf16[2,16,6144]{2,1,0:T(8,128)(2,1)S(1)}, bf16[2,16,6144]{2,1,0:T(8,128)(2,1)S(1)}, u32[]{:S(2)}, u32[]{:S(2)}) collective-permute-start(bf16[2,16,6144]{2,1,0:T(8,128)(2,1)S(1)} %place.3.rest_0_), channel_id=1, source_target_pairs={{0,48},{8,24},{16,0},{24,40},{32,16},{40,56},{48,32},{56,8},{64,11... | collective-permute-start | bytes 1179656 | tf_op jit(solution)/shard_map/ppermute | solution.py:299
  17.2 7.1 %collective-permute-start.6 = (bf16[16,6144]{1,0:T(8,128)(2,1)S(1)}, bf16[16,6144]{1,0:T(8,128)(2,1)S(1)}, u32[]{:S(2)}, u32[]{:S(2)}) collective-permute-start(bf16[16,6144]{1,0:T(8,128)(2,1)S(1)} %pick.1), channel_id=1, source_target_pairs={{0,32},{8,72},{16,48},{24,88},{32,0},{40,104},{48,16},{56,120},{64... | collective-permute-start | bytes 589832 | tf_op jit(solution)/shard_map/ppermute | solution.py:299
  17.6 7.9 %collective-permute-start.8 = (bf16[2,16,6144]{2,1,0:T(8,128)(2,1)S(1)}, bf16[2,16,6144]{2,1,0:T(8,128)(2,1)S(1)}, u32[]{:S(2)}, u32[]{:S(2)}) collective-permute-start(bf16[2,16,6144]{2,1,0:T(8,128)(2,1)S(1)} %collective-permute-done.5.pair.rest_8_), channel_id=1, source_target_pairs={{0,8},{8,0},{16,24},{24,16},{32,40},{40,32},{48,56},{56,48},{64,72... | collective-permute-start | bytes 1179656 | tf_op jit(solution)/shard_map/ppermute | solution.py:324
  21.9 3.7 %collective-permute-start.4 = (bf16[2,16,6144]{2,1,0:T(8,128)(2,1)S(1)}, bf16[2,16,6144]{2,1,0:T(8,128)(2,1)S(1)}, u32[]{:S(2)}, u32[]{:S(2)}) collective-permute-start(bf16[2,16,6144]{2,1,0:T(8,128)(2,1)S(1)} %collective-permute-done.3.rest_4_), channel_id=1, source_target_pairs={{0,8},{8,0},{16,24},{24,16},{32,40},{40,32},{48,56},{56,48},{64,72... | collective-permute-start | bytes 1179656 | tf_op jit(solution)/shard_map/ppermute | solution.py:324
  24.3 1.9 %collective-permute-start.2 = (bf16[2,16,6144]{2,1,0:T(8,128)(2,1)S(1)}, bf16[2,16,6144]{2,1,0:T(8,128)(2,1)S(1)}, u32[]{:S(2)}, u32[]{:S(2)}) collective-permute-start(bf16[2,16,6144]{2,1,0:T(8,128)(2,1)S(1)} %collective-permute-done.1.rest_2_), channel_id=1, source_target_pairs={{0,8},{8,0},{16,24},{24,16},{32,40},{40,32},{48,56},{56,48},{64,72... | collective-permute-start | bytes 1179656 | tf_op jit(solution)/shard_map/ppermute | solution.py:324
  24.3 2.2 %collective-permute-start.7 = (bf16[16,6144]{1,0:T(8,128)(2,1)S(1)}, bf16[16,6144]{1,0:T(8,128)(2,1)S(1)}, u32[]{:S(2)}, u32[]{:S(2)}) collective-permute-start(bf16[16,6144]{1,0:T(8,128)(2,1)S(1)} %collective-permute-done.6.rest_6_), channel_id=1, source_target_pairs={{0,8},{8,0},{16,24},{24,16},{32,40},{40,32},{48,56},{56,48},{64,72... | collective-permute-start | bytes 589832 | tf_op jit(solution)/shard_map/ppermute | solution.py:324
  67.1 5.4 %collective-permute-start.9 = (bf16[5,16,6400]{2,1,0:T(8,128)(2,1)S(1)}, bf16[5,16,6400]{2,1,0:T(8,128)(2,1)S(1)}, u32[]{:S(2)}, u32[]{:S(2)}) collective-permute-start(bf16[5,16,6400]{2,1,0:T(8,128)(2,1)S(1)} %get-tuple-element.23), channel_id=1, source_target_pairs={{0,8},{8,0},{16,24},{24,16},{32,40},{40,32},{48,56},{56,48},{64,72... | collective-permute-start | bytes 3072008 | tf_op jit(solution)/shard_map/ppermute | solution.py:366
  72.7 6.9 %collective-permute-start.10 = (bf16[3,16,6400]{2,1,0:T(8,128)(2,1)S(1)}, bf16[3,16,6400]{2,1,0:T(8,128)(2,1)S(1)}, u32[]{:S(2)}, u32[]{:S(2)}) collective-permute-start(bf16[3,16,6400]{2,1,0:T(8,128)(2,1)S(1)} %get-tuple-element.25), channel_id=1, source_target_pairs={{0,8},{8,0},{16,24},{24,16},{32,40},{40,32},{48,56},{56,48},{64,72... | collective-permute-start | bytes 1843208 | tf_op jit(solution)/shard_map/ppermute | solution.py:378
  73.2 6.4 %collective-permute-start.11 = (bf16[16,6400]{1,0:T(8,128)(2,1)S(1)}, bf16[16,6400]{1,0:T(8,128)(2,1)S(1)}, u32[]{:S(2)}, u32[]{:S(2)}) collective-permute-start(bf16[16,6400]{1,0:T(8,128)(2,1)S(1)} %get-tuple-element.26), channel_id=1, source_target_pairs={{0,32},{8,72},{16,48},{24,88},{32,0},{40,104},{48,16},{56,120},{64... | collective-permute-start | bytes 614408 | tf_op jit(solution)/shard_map/ppermute | solution.py:299
  75.9 14.4 %collective-permute-start.13 = (bf16[2,16,6400]{2,1,0:T(8,128)(2,1)S(1)}, bf16[2,16,6400]{2,1,0:T(8,128)(2,1)S(1)}, u32[]{:S(2)}, u32[]{:S(2)}) collective-permute-start(bf16[2,16,6400]{2,1,0:T(8,128)(2,1)S(1)} %get-tuple-element.29), channel_id=1, source_target_pairs={{0,80},{8,120},{16,96},{24,72},{32,112},{40,88},{48,64},{56,104},{... | collective-permute-start | bytes 1228808 | tf_op jit(solution)/shard_map/ppermute | solution.py:299
  78.0 12.3 %collective-permute-start.14 = (bf16[2,16,6400]{2,1,0:T(8,128)(2,1)S(1)}, bf16[2,16,6400]{2,1,0:T(8,128)(2,1)S(1)}, u32[]{:S(2)}, u32[]{:S(2)}) collective-permute-start(bf16[2,16,6400]{2,1,0:T(8,128)(2,1)S(1)} %get-tuple-element.30), channel_id=1, source_target_pairs={{0,16},{8,56},{16,32},{24,8},{32,48},{40,24},{48,0},{56,40},{64,80... | collective-permute-start | bytes 1228808 | tf_op jit(solution)/shard_map/ppermute | solution.py:299
  79.8 16.6 %collective-permute-start.12 = (bf16[2,16,6400]{2,1,0:T(8,128)(2,1)S(1)}, bf16[2,16,6400]{2,1,0:T(8,128)(2,1)S(1)}, u32[]{:S(2)}, u32[]{:S(2)}) collective-permute-start(bf16[2,16,6400]{2,1,0:T(8,128)(2,1)S(1)} %get-tuple-element.28), channel_id=1, source_target_pairs={{0,64},{8,40},{16,80},{24,56},{32,96},{40,8},{48,112},{56,24},{64,... | collective-permute-start | bytes 1228808 | tf_op jit(solution)/shard_map/ppermute | solution.py:299
  96.4 2.1 %collective-permute-start.15 = (bf16[16,6400]{1,0:T(8,128)(2,1)S(1)}, bf16[16,6400]{1,0:T(8,128)(2,1)S(1)}, u32[]{:S(2)}, u32[]{:S(2)}) collective-permute-start(bf16[16,6400]{1,0:T(8,128)(2,1)S(1)} %hand.1), channel_id=1, source_target_pairs={{0,8},{8,0},{16,24},{24,16},{32,40},{40,32},{48,56},{56,48},{64,72... | collective-permute-start | bytes 614408 | tf_op jit(solution)/shard_map/ppermute | solution.py:396

commit v15 on v14

--- a/solution.py
+++ b/solution.py
@@ -130,7 +130,7 @@
         parts, jnp.where(place, 1.0, 0.0).astype(BF), preferred_element_type=F32
     ).astype(BF)
 
-    first, second, third, farthest = (pieces[at : at + 2] for at in (8, 4, 2, 6))
+    first, second, third, farthest = (pieces[at : at + 2] for at in (8, 2, 4, 6))
     for server in range(2):
         held[node_near(0, 0, server)] = pieces[server][...]
         held[node_near(*FARTHEST, server)] = farthest[server][...]
@@ -320,7 +320,7 @@
         name="pick",
     )(first, loaded)
     forwarded = send(picked, FORWARD)
-    for piece in (third, second, forwarded, first):
+    for piece in (second, third, forwarded, first):
         pieces += [piece, lax.ppermute(piece, "node", swap)]
 
     index_scratch = [

time: 99.6 us -> 98.7 us (level)
  starting transfers between devices: 30.2 us -> 25.5 us
  waiting for transfers between devices: 18.5 us -> 23.2 us
    ppermute x8, waiting for transfers between devices: 14 us -> 18.1 us  [send(): return lax.ppermute(piece, 'node', shared_pairs(steps))]
    ppermute x8, starting transfers between devices: 17 us -> 15 us  [send(): return lax.ppermute(piece, 'node', shared_pairs(steps))]
    ppermute x4, starting transfers between devices: 7.18 us -> 5.36 us  [local(): pieces += [piece, lax.ppermute(piece, 'node', swap)]]
where the time goes in v15:
time: 98.7 us; the launch traced here: 98.4 us
  blocking collectives  28.4 us (29%)
  starting transfers between devices  25.5 us (26%)
  waiting for transfers between devices  23.2 us (24%)
  Pallas kernels  19.6 us (20%)
    ppermute x8, waiting for transfers between devices, send(): return lax.ppermute(piece, 'node', shared_pairs(steps))  18.1 us
    all_to_all x1, blocking collectives, local(): both = lax.all_to_all(mixed, 'feat', 0, 0, tiled=True)  16.1 us
    ppermute x8, starting transfers between devices, send(): return lax.ppermute(piece, 'node', shared_pairs(steps))  15 us
    all_to_all x1, blocking collectives, local(): grads = lax.all_to_all(dense, 'feat', 0, 0, tiled=True)  12.3 us
    pallas_call x1, Pallas kernels, local(): pl.pallas_call(spread_kernel, in_specs=[HBM, HBM] + [VMEM] * 2, out_specs...  6.88 us
    pallas_call x1, Pallas kernels, local(): pl.pallas_call(load_kernel, in_specs=[pl.BlockSpec(memory_space=pltpu.HBM...  6.52 us
    ppermute x4, starting transfers between devices, local(): pieces += [piece, lax.ppermute(piece, 'node', swap)]  5.36 us
    pallas_call x1, Pallas kernels, local(): pl.pallas_call(mix_kernel, in_specs=[HBM, HBM] + [VMEM] * 14, out_specs=V...  3.7 us
  transfers between devices with their start and end apart: 16, of which 10 were waited for; matrix products, arithmetic and copies ran while one was open for 0% of the time, Pallas kernels for 7%

profile of v15, /device:TPU:1, one launch (start us, length us, event | category | flops | bytes accessed | tf_op | source)
XLA Modules:
  0.0 98.4 jit_solution(3945419658989115246)
XLA Ops:
  0.6 1.5 %collective-permute-start = (bf16[16,6144]{1,0:T(8,128)(2,1)}, bf16[16,6144]{1,0:T(8,128)(2,1)S(1)}, u32[]{:S(2)}, u32[]{:S(2)}) collective-permute-start(bf16[16,6144]{1,0:T(8,128)(2,1)} %rest_0_.1), channel_id=1, source_target_pairs={{0,8},{8,0},{16,24},{24,16},{32,40},{40,32},{48,56},{56,48},{64,72... | collective-permute-start | bytes 589832 | tf_op jit(solution)/shard_map/ppermute | solution.py:284
  2.1 0.9 copy-done
  3.7 3.8 %collective-permute-start.5 = (bf16[2,16,6144]{2,1,0:T(8,128)(2,1)S(1)}, bf16[2,16,6144]{2,1,0:T(8,128)(2,1)S(1)}, u32[]{:S(2)}, u32[]{:S(2)}) collective-permute-start(bf16[2,16,6144]{2,1,0:T(8,128)(2,1)S(1)} %place.3.rest_0_), channel_id=1, source_target_pairs={{0,64},{8,40},{16,80},{24,56},{32,96},{40,8},{48,112},{56,24},{64,... | collective-permute-start | bytes 1179656 | tf_op jit(solution)/shard_map/ppermute | solution.py:299
  7.4 0.7 collective-permute-start.3
  8.2 2.5 %collective-permute-start.1 = (bf16[2,16,6144]{2,1,0:T(8,128)(2,1)S(1)}, bf16[2,16,6144]{2,1,0:T(8,128)(2,1)S(1)}, u32[]{:S(2)}, u32[]{:S(2)}) collective-permute-start(bf16[2,16,6144]{2,1,0:T(8,128)(2,1)S(1)} %place.3.rest_0_), channel_id=1, source_target_pairs={{0,112},{8,88},{16,64},{24,104},{32,80},{40,120},{48,96},{56,72},{... | collective-permute-start | bytes 1179656 | tf_op jit(solution)/shard_map/ppermute | solution.py:299
  10.6 6.5 %load.1 = (bf16[48,12,128,128]{3,2,1,0:T(8,128)(2,1)S(1)}, f32[8,128]{1,0:T(8,128)S(1)}) custom-call(bf16[48,12,128,128]{3,2,1,0:T(8,128)(2,1)} %values.1, bf16[2,16,6144]{2,1,0:T(8,128)(2,1)S(1)} %place.3.rest_0_), custom_call_target="tpu_custom_call" | custom-call | bytes 37748736 | tf_op jit(solution)/shard_map/load/pallas_call | solution.py:302
  17.6 1.3 %collective-permute-start.8 = (bf16[2,16,6144]{2,1,0:T(8,128)(2,1)S(1)}, bf16[2,16,6144]{2,1,0:T(8,128)(2,1)S(1)}, u32[]{:S(2)}, u32[]{:S(2)}) collective-permute-start(bf16[2,16,6144]{2,1,0:T(8,128)(2,1)S(1)} %collective-permute-done.5.pair.rest_8_), channel_id=1, source_target_pairs={{0,8},{8,0},{16,24},{24,16},{32,40},{40,32},{48,56},{56,48},{64,72... | collective-permute-start | bytes 1179656 | tf_op jit(solution)/shard_map/ppermute | solution.py:324
  18.9 2.8 %collective-permute-done.3.rest_4_ = bf16[2,16,6144]{2,1,0:T(8,128)(2,1)S(1)} collective-permute-done((bf16[2,16,6144]{2,1,0:T(8,128)(2,1)S(1)}, bf16[2,16,6144]{2,1,0:T(8,128)(2,1)S(1)}, u32[]{:S(2)}, u32[]{:S(2)}) %collective-permute-start.3) | collective-permute-done | bytes 393248 | tf_op jit(solution)/shard_map/ppermute | solution.py:299
  21.6 3.2 %collective-permute-start.4 = (bf16[2,16,6144]{2,1,0:T(8,128)(2,1)S(1)}, bf16[2,16,6144]{2,1,0:T(8,128)(2,1)S(1)}, u32[]{:S(2)}, u32[]{:S(2)}) collective-permute-start(bf16[2,16,6144]{2,1,0:T(8,128)(2,1)S(1)} %collective-permute-done.3.rest_4_), channel_id=1, source_target_pairs={{0,8},{8,0},{16,24},{24,16},{32,40},{40,32},{48,56},{56,48},{64,72... | collective-permute-start | bytes 1179656 | tf_op jit(solution)/shard_map/ppermute | solution.py:324
  24.9 0.8 collective-permute-start.7
  27.1 3.7 %mix.1 = bf16[8,16,2816]{2,1,0:T(8,128)(2,1)S(1)} custom-call(s32[12,48]{1,0:T(8,128)} %bitcast.5, s32[48]{0:T(128)} %counts_in.3, bf16[48,12,128,128]{3,2,1,0:T(8,128)(2,1)S(1)} %get-tuple-element.18.values, bf16[32,6144]{1,0:T(8,128)(2,1)S(1)} %copy-done.2, bf16[16,256]{1,0:T(8,128)(2,1)S(1)} %copy-done.4, f32[1,32]{1,0:T(1,128)S(1)} %bitcast.4, ...), custom_call_target="tpu_custom_call" | custom-call | tf_op jit(solution)/shard_map/mix/pallas_call | solution.py:331
  30.8 16.1 %all_to_all.10.both = bf16[8,16,2816]{2,1,0:T(8,128)(2,1)S(1)} all-to-all(bf16[8,16,2816]{2,1,0:T(8,128)(2,1)S(1)} %mix.1), channel_id=1, replica_groups=mesh['node'=16,'feat'=8] {'feat'}, dimensions={0} | all-to-all | bytes 1441792 | tf_op jit(solution)/shard_map/all_to_all | solution.py:341
  46.8 0.7 dense.1
  47.6 12.3 %all_to_all.11.grads = bf16[8,16,2560]{2,1,0:T(8,128)(2,1)S(1)} all-to-all(bf16[8,16,2560]{2,1,0:T(8,128)(2,1)S(1)} %dense.1), channel_id=1, replica_groups=mesh['node'=16,'feat'=8] {'feat'}, dimensions={0} | all-to-all | bytes 1310720 | tf_op jit(solution)/shard_map/all_to_all | solution.py:352
  59.9 6.9 %spread.1 = (bf16[32,6144]{1,0:T(8,128)(2,1)}, bf16[5,16,6400]{2,1,0:T(8,128)(2,1)S(1)}, bf16[5,16,6400]{2,1,0:T(8,128)(2,1)S(1)}, bf16[3,16,6400]{2,1,0:T(8,128)(2,1)S(1)}, bf16[3,16,6400]{2,1,0:T(8,128)(2,1)S(1)}) custom-call(s32[12,48]{1,0:T(8,128)} %bitcast.6, s32[48]{0:T(128)} %counts_in.3, bf16[48,12,128,128]{3,2,1,0:T(8,128)(2,1)S(1)} %get-tuple-element.18.values, ...), custom_call_target="tpu_custom_call" | custom-call | tf_op jit(solution)/shard_map/spread/pallas_call | solution.py:355
  66.8 3.1 %collective-permute-start.9 = (bf16[5,16,6400]{2,1,0:T(8,128)(2,1)S(1)}, bf16[5,16,6400]{2,1,0:T(8,128)(2,1)S(1)}, u32[]{:S(2)}, u32[]{:S(2)}) collective-permute-start(bf16[5,16,6400]{2,1,0:T(8,128)(2,1)S(1)} %get-tuple-element.23), channel_id=1, source_target_pairs={{0,8},{8,0},{16,24},{24,16},{32,40},{40,32},{48,56},{56,48},{64,72... | collective-permute-start | bytes 3072008 | tf_op jit(solution)/shard_map/ppermute | solution.py:366
  69.9 2.3 %collective-permute-done.9.other = bf16[5,16,6400]{2,1,0:T(8,128)(2,1)S(1)} collective-permute-done((bf16[5,16,6400]{2,1,0:T(8,128)(2,1)S(1)}, bf16[5,16,6400]{2,1,0:T(8,128)(2,1)S(1)}, u32[]{:S(2)}, u32[]{:S(2)}) %collective-permute-start.9) | collective-permute-done | bytes 1024032 | tf_op jit(solution)/shard_map/ppermute | solution.py:366
  72.8 2.2 %collective-permute-start.11 = (bf16[16,6400]{1,0:T(8,128)(2,1)S(1)}, bf16[16,6400]{1,0:T(8,128)(2,1)S(1)}, u32[]{:S(2)}, u32[]{:S(2)}) collective-permute-start(bf16[16,6400]{1,0:T(8,128)(2,1)S(1)} %get-tuple-element.26), channel_id=1, source_target_pairs={{0,32},{8,72},{16,48},{24,88},{32,0},{40,104},{48,16},{56,120},{64... | collective-permute-start | bytes 614408 | tf_op jit(solution)/shard_map/ppermute | solution.py:299
  75.0 3.9 %collective-permute-start.13 = (bf16[2,16,6400]{2,1,0:T(8,128)(2,1)S(1)}, bf16[2,16,6400]{2,1,0:T(8,128)(2,1)S(1)}, u32[]{:S(2)}, u32[]{:S(2)}) collective-permute-start(bf16[2,16,6400]{2,1,0:T(8,128)(2,1)S(1)} %get-tuple-element.29), channel_id=1, source_target_pairs={{0,80},{8,120},{16,96},{24,72},{32,112},{40,88},{48,64},{56,104},{... | collective-permute-start | bytes 1228808 | tf_op jit(solution)/shard_map/ppermute | solution.py:299
  79.4 1.6 %collective-permute-start.12 = (bf16[2,16,6400]{2,1,0:T(8,128)(2,1)S(1)}, bf16[2,16,6400]{2,1,0:T(8,128)(2,1)S(1)}, u32[]{:S(2)}, u32[]{:S(2)}) collective-permute-start(bf16[2,16,6400]{2,1,0:T(8,128)(2,1)S(1)} %get-tuple-element.28), channel_id=1, source_target_pairs={{0,64},{8,40},{16,80},{24,56},{32,96},{40,8},{48,112},{56,24},{64,... | collective-permute-start | bytes 1228808 | tf_op jit(solution)/shard_map/ppermute | solution.py:299
  81.0 10.8 %collective-permute-done.13.second = bf16[2,16,6400]{2,1,0:T(8,128)(2,1)S(1)} collective-permute-done((bf16[2,16,6400]{2,1,0:T(8,128)(2,1)S(1)}, bf16[2,16,6400]{2,1,0:T(8,128)(2,1)S(1)}, u32[]{:S(2)}, u32[]{:S(2)}) %collective-permute-start.13) | collective-permute-done | bytes 409632 | tf_op jit(solution)/shard_map/ppermute | solution.py:299
  91.9 4.2 %collective-permute-done.12.first = bf16[2,16,6400]{2,1,0:T(8,128)(2,1)S(1)} collective-permute-done((bf16[2,16,6400]{2,1,0:T(8,128)(2,1)S(1)}, bf16[2,16,6400]{2,1,0:T(8,128)(2,1)S(1)}, u32[]{:S(2)}, u32[]{:S(2)}) %collective-permute-start.12) | collective-permute-done | bytes 409632 | tf_op jit(solution)/shard_map/ppermute | solution.py:299
  96.2 1.4 %collective-permute-done.15.handed = bf16[16,6400]{1,0:T(8,128)(2,1)S(1)} collective-permute-done((bf16[16,6400]{1,0:T(8,128)(2,1)S(1)}, bf16[16,6400]{1,0:T(8,128)(2,1)S(1)}, u32[]{:S(2)}, u32[]{:S(2)}) %collective-permute-start.15) | collective-permute-done | bytes 204832 | tf_op jit(solution)/shard_map/ppermute | solution.py:396
  97.6 0.8 last.1
  (33 shorter events, 3.7 us)
Async XLA Ops:
  0.6 2.8 %collective-permute-start = (bf16[16,6144]{1,0:T(8,128)(2,1)}, bf16[16,6144]{1,0:T(8,128)(2,1)S(1)}, u32[]{:S(2)}, u32[]{:S(2)}) collective-permute-start(bf16[16,6144]{1,0:T(8,128)(2,1)} %rest_0_.1), channel_id=1, source_target_pairs={{0,8},{8,0},{16,24},{24,16},{32,40},{40,32},{48,56},{56,48},{64,72... | collective-permute-start | bytes 589832 | tf_op jit(solution)/shard_map/ppermute | solution.py:284
  2.1 0.9 copy-start
  3.1 24.0 %copy-start.1 = (bf16[16,6144]{1,0:T(8,128)(2,1)S(1)}, bf16[16,6144]{1,0:T(8,128)(2,1)}, u32[]{:S(2)}) copy-start(bf16[16,6144]{1,0:T(8,128)(2,1)} %rest_0_.1) | copy-start | bytes 589828
  3.1 24.0 %copy-start.2 = (bf16[32,6144]{1,0:T(8,128)(2,1)S(1)}, bf16[32,6144]{1,0:T(8,128)(2,1)}, u32[]{:S(2)}) copy-start(bf16[32,6144]{1,0:T(8,128)(2,1)} %cotangent.1) | copy-start | bytes 1179652
  3.1 24.0 %copy-start.4 = (bf16[16,256]{1,0:T(8,128)(2,1)S(1)}, bf16[16,256]{1,0:T(8,128)(2,1)}, u32[]{:S(2)}) copy-start(bf16[16,256]{1,0:T(8,128)(2,1)} %weight.1) | copy-start | bytes 24580
  3.1 24.0 %copy-start.5 = (f32[32]{0:T(128)S(1)}, f32[32]{0:T(128)}, u32[]{:S(2)}) copy-start(f32[32]{0:T(128)} %param.10) | copy-start | bytes 388
  3.7 43.2 %copy-start.3 = (s32[6144]{0:T(1024)S(1)}, s32[6144]{0:T(1024)}, u32[]{:S(2)}) copy-start(s32[6144]{0:T(1024)} %param.14) | copy-start | bytes 73732
  3.7 13.5 %collective-permute-start.5 = (bf16[2,16,6144]{2,1,0:T(8,128)(2,1)S(1)}, bf16[2,16,6144]{2,1,0:T(8,128)(2,1)S(1)}, u32[]{:S(2)}, u32[]{:S(2)}) collective-permute-start(bf16[2,16,6144]{2,1,0:T(8,128)(2,1)S(1)} %place.3.rest_0_), channel_id=1, source_target_pairs={{0,64},{8,40},{16,80},{24,56},{32,96},{40,8},{48,112},{56,24},{64,... | collective-permute-start | bytes 1179656 | tf_op jit(solution)/shard_map/ppermute | solution.py:299
  7.4 14.2 %collective-permute-start.3 = (bf16[2,16,6144]{2,1,0:T(8,128)(2,1)S(1)}, bf16[2,16,6144]{2,1,0:T(8,128)(2,1)S(1)}, u32[]{:S(2)}, u32[]{:S(2)}) collective-permute-start(bf16[2,16,6144]{2,1,0:T(8,128)(2,1)S(1)} %place.3.rest_0_), channel_id=1, source_target_pairs={{0,48},{8,24},{16,0},{24,40},{32,16},{40,56},{48,32},{56,8},{64,11... | collective-permute-start | bytes 1179656 | tf_op jit(solution)/shard_map/ppermute | solution.py:299
  8.2 16.7 %collective-permute-start.1 = (bf16[2,16,6144]{2,1,0:T(8,128)(2,1)S(1)}, bf16[2,16,6144]{2,1,0:T(8,128)(2,1)S(1)}, u32[]{:S(2)}, u32[]{:S(2)}) collective-permute-start(bf16[2,16,6144]{2,1,0:T(8,128)(2,1)S(1)} %place.3.rest_0_), channel_id=1, source_target_pairs={{0,112},{8,88},{16,64},{24,104},{32,80},{40,120},{48,96},{56,72},{... | collective-permute-start | bytes 1179656 | tf_op jit(solution)/shard_map/ppermute | solution.py:299
  17.2 7.7 %collective-permute-start.6 = (bf16[16,6144]{1,0:T(8,128)(2,1)S(1)}, bf16[16,6144]{1,0:T(8,128)(2,1)S(1)}, u32[]{:S(2)}, u32[]{:S(2)}) collective-permute-start(bf16[16,6144]{1,0:T(8,128)(2,1)S(1)} %pick.1), channel_id=1, source_target_pairs={{0,32},{8,72},{16,48},{24,88},{32,0},{40,104},{48,16},{56,120},{64... | collective-permute-start | bytes 589832 | tf_op jit(solution)/shard_map/ppermute | solution.py:299
  17.6 8.1 %collective-permute-start.8 = (bf16[2,16,6144]{2,1,0:T(8,128)(2,1)S(1)}, bf16[2,16,6144]{2,1,0:T(8,128)(2,1)S(1)}, u32[]{:S(2)}, u32[]{:S(2)}) collective-permute-start(bf16[2,16,6144]{2,1,0:T(8,128)(2,1)S(1)} %collective-permute-done.5.pair.rest_8_), channel_id=1, source_target_pairs={{0,8},{8,0},{16,24},{24,16},{32,40},{40,32},{48,56},{56,48},{64,72... | collective-permute-start | bytes 1179656 | tf_op jit(solution)/shard_map/ppermute | solution.py:324
  21.6 4.6 %collective-permute-start.4 = (bf16[2,16,6144]{2,1,0:T(8,128)(2,1)S(1)}, bf16[2,16,6144]{2,1,0:T(8,128)(2,1)S(1)}, u32[]{:S(2)}, u32[]{:S(2)}) collective-permute-start(bf16[2,16,6144]{2,1,0:T(8,128)(2,1)S(1)} %collective-permute-done.3.rest_4_), channel_id=1, source_target_pairs={{0,8},{8,0},{16,24},{24,16},{32,40},{40,32},{48,56},{56,48},{64,72... | collective-permute-start | bytes 1179656 | tf_op jit(solution)/shard_map/ppermute | solution.py:324
  24.9 1.9 %collective-permute-start.2 = (bf16[2,16,6144]{2,1,0:T(8,128)(2,1)S(1)}, bf16[2,16,6144]{2,1,0:T(8,128)(2,1)S(1)}, u32[]{:S(2)}, u32[]{:S(2)}) collective-permute-start(bf16[2,16,6144]{2,1,0:T(8,128)(2,1)S(1)} %collective-permute-done.1.rest_2_), channel_id=1, source_target_pairs={{0,8},{8,0},{16,24},{24,16},{32,40},{40,32},{48,56},{56,48},{64,72... | collective-permute-start | bytes 1179656 | tf_op jit(solution)/shard_map/ppermute | solution.py:324
  24.9 2.2 %collective-permute-start.7 = (bf16[16,6144]{1,0:T(8,128)(2,1)S(1)}, bf16[16,6144]{1,0:T(8,128)(2,1)S(1)}, u32[]{:S(2)}, u32[]{:S(2)}) collective-permute-start(bf16[16,6144]{1,0:T(8,128)(2,1)S(1)} %collective-permute-done.6.rest_6_), channel_id=1, source_target_pairs={{0,8},{8,0},{16,24},{24,16},{32,40},{40,32},{48,56},{56,48},{64,72... | collective-permute-start | bytes 589832 | tf_op jit(solution)/shard_map/ppermute | solution.py:324
  66.8 5.4 %collective-permute-start.9 = (bf16[5,16,6400]{2,1,0:T(8,128)(2,1)S(1)}, bf16[5,16,6400]{2,1,0:T(8,128)(2,1)S(1)}, u32[]{:S(2)}, u32[]{:S(2)}) collective-permute-start(bf16[5,16,6400]{2,1,0:T(8,128)(2,1)S(1)} %get-tuple-element.23), channel_id=1, source_target_pairs={{0,8},{8,0},{16,24},{24,16},{32,40},{40,32},{48,56},{56,48},{64,72... | collective-permute-start | bytes 3072008 | tf_op jit(solution)/shard_map/ppermute | solution.py:366
  72.4 6.9 %collective-permute-start.10 = (bf16[3,16,6400]{2,1,0:T(8,128)(2,1)S(1)}, bf16[3,16,6400]{2,1,0:T(8,128)(2,1)S(1)}, u32[]{:S(2)}, u32[]{:S(2)}) collective-permute-start(bf16[3,16,6400]{2,1,0:T(8,128)(2,1)S(1)} %get-tuple-element.25), channel_id=1, source_target_pairs={{0,8},{8,0},{16,24},{24,16},{32,40},{40,32},{48,56},{56,48},{64,72... | collective-permute-start | bytes 1843208 | tf_op jit(solution)/shard_map/ppermute | solution.py:378
  72.8 6.4 %collective-permute-start.11 = (bf16[16,6400]{1,0:T(8,128)(2,1)S(1)}, bf16[16,6400]{1,0:T(8,128)(2,1)S(1)}, u32[]{:S(2)}, u32[]{:S(2)}) collective-permute-start(bf16[16,6400]{1,0:T(8,128)(2,1)S(1)} %get-tuple-element.26), channel_id=1, source_target_pairs={{0,32},{8,72},{16,48},{24,88},{32,0},{40,104},{48,16},{56,120},{64... | collective-permute-start | bytes 614408 | tf_op jit(solution)/shard_map/ppermute | solution.py:299
  75.0 16.9 %collective-permute-start.13 = (bf16[2,16,6400]{2,1,0:T(8,128)(2,1)S(1)}, bf16[2,16,6400]{2,1,0:T(8,128)(2,1)S(1)}, u32[]{:S(2)}, u32[]{:S(2)}) collective-permute-start(bf16[2,16,6400]{2,1,0:T(8,128)(2,1)S(1)} %get-tuple-element.29), channel_id=1, source_target_pairs={{0,80},{8,120},{16,96},{24,72},{32,112},{40,88},{48,64},{56,104},{... | collective-permute-start | bytes 1228808 | tf_op jit(solution)/shard_map/ppermute | solution.py:299
  78.9 13.0 %collective-permute-start.14 = (bf16[2,16,6400]{2,1,0:T(8,128)(2,1)S(1)}, bf16[2,16,6400]{2,1,0:T(8,128)(2,1)S(1)}, u32[]{:S(2)}, u32[]{:S(2)}) collective-permute-start(bf16[2,16,6400]{2,1,0:T(8,128)(2,1)S(1)} %get-tuple-element.30), channel_id=1, source_target_pairs={{0,16},{8,56},{16,32},{24,8},{32,48},{40,24},{48,0},{56,40},{64,80... | collective-permute-start | bytes 1228808 | tf_op jit(solution)/shard_map/ppermute | solution.py:299
  79.4 16.6 %collective-permute-start.12 = (bf16[2,16,6400]{2,1,0:T(8,128)(2,1)S(1)}, bf16[2,16,6400]{2,1,0:T(8,128)(2,1)S(1)}, u32[]{:S(2)}, u32[]{:S(2)}) collective-permute-start(bf16[2,16,6400]{2,1,0:T(8,128)(2,1)S(1)} %get-tuple-element.28), channel_id=1, source_target_pairs={{0,64},{8,40},{16,80},{24,56},{32,96},{40,8},{48,112},{56,24},{64,... | collective-permute-start | bytes 1228808 | tf_op jit(solution)/shard_map/ppermute | solution.py:299
  96.1 1.5 %collective-permute-start.15 = (bf16[16,6400]{1,0:T(8,128)(2,1)S(1)}, bf16[16,6400]{1,0:T(8,128)(2,1)S(1)}, u32[]{:S(2)}, u32[]{:S(2)}) collective-permute-start(bf16[16,6400]{1,0:T(8,128)(2,1)S(1)} %hand.1), channel_id=1, source_target_pairs={{0,8},{8,0},{16,24},{24,16},{32,40},{40,32},{48,56},{56,48},{64,72... | collective-permute-start | bytes 614408 | tf_op jit(solution)/shard_map/ppermute | solution.py:396

commit v16 on v13

--- a/solution.py
+++ b/solution.py
@@ -257,7 +257,7 @@
     stay[...] = both(own, other, 2).astype(BF)
 
 
-def hand_kernel(first, second, third, out):
+def hand_kernel(first, third, second, out):
     out[...] = (first[1].astype(F32) + second[1].astype(F32) + third[1].astype(F32)).astype(BF)
 
 
@@ -392,7 +392,7 @@
         out_shape=shape((16, wide)),
         compiler_params=params(16),
         name="hand",
-    )(first, second, third)
+    )(first, third, second)
     handed = lax.ppermute(handed, "node", swap)
     grad_features, grad_weight = pl.pallas_call(
         last_kernel,

time: 99 us -> 98 us (0.990)
  waiting for transfers between devices: 25.3 us -> 23.9 us
  blocking collectives: 28.4 us -> 29.4 us
    all_to_all x1, blocking collectives: 12.3 us -> 13.4 us  [local(): grads = lax.all_to_all(dense, 'feat', 0, 0, tiled=True)]
    ppermute x8, waiting for transfers between devices: 19.6 us -> 18.6 us  [send(): return lax.ppermute(piece, 'node', shared_pairs(steps))]
    ppermute x8, starting transfers between devices: 14.6 us -> 13.6 us  [send(): return lax.ppermute(piece, 'node', shared_pairs(steps))]
  transfers between devices with their start and end apart: 16 -> 16, of which waited for: 12 -> 11; matrix products, arithmetic and copies ran while one was open for 0% -> 0% of each run, Pallas kernels for 7% -> 7%
where the time goes in v16:
time: 98 us; the launch traced here: 97.7 us
  blocking collectives  29.4 us (30%)
  waiting for transfers between devices  23.9 us (24%)
  starting transfers between devices  23.1 us (24%)
  Pallas kernels  19.6 us (20%)
    ppermute x8, waiting for transfers between devices, send(): return lax.ppermute(piece, 'node', shared_pairs(steps))  18.6 us
    all_to_all x1, blocking collectives, local(): both = lax.all_to_all(mixed, 'feat', 0, 0, tiled=True)  16.1 us
    ppermute x8, starting transfers between devices, send(): return lax.ppermute(piece, 'node', shared_pairs(steps))  13.6 us
    all_to_all x1, blocking collectives, local(): grads = lax.all_to_all(dense, 'feat', 0, 0, tiled=True)  13.4 us
    pallas_call x1, Pallas kernels, local(): pl.pallas_call(spread_kernel, in_specs=[HBM, HBM] + [VMEM] * 2, out_specs...  6.88 us
    pallas_call x1, Pallas kernels, local(): pl.pallas_call(load_kernel, in_specs=[pl.BlockSpec(memory_space=pltpu.HBM...  6.52 us
    ppermute x4, starting transfers between devices, local(): pieces += [piece, lax.ppermute(piece, 'node', swap)]  4.05 us
    pallas_call x1, Pallas kernels, local(): pl.pallas_call(mix_kernel, in_specs=[HBM, HBM] + [VMEM] * 14, out_specs=V...  3.71 us
  transfers between devices with their start and end apart: 16, of which 11 were waited for; matrix products, arithmetic and copies ran while one was open for 0% of the time, Pallas kernels for 7%

profile of v16, /device:TPU:1, one launch (start us, length us, event | category | flops | bytes accessed | tf_op | source)
XLA Modules:
  0.0 97.7 jit_solution(11467813816915141248)
XLA Ops:
  0.6 1.5 %collective-permute-start = (bf16[16,6144]{1,0:T(8,128)(2,1)}, bf16[16,6144]{1,0:T(8,128)(2,1)S(1)}, u32[]{:S(2)}, u32[]{:S(2)}) collective-permute-start(bf16[16,6144]{1,0:T(8,128)(2,1)} %rest_0_.1), channel_id=1, source_target_pairs={{0,8},{8,0},{16,24},{24,16},{32,40},{40,32},{48,56},{56,48},{64,72... | collective-permute-start | bytes 589832 | tf_op jit(solution)/shard_map/ppermute | solution.py:284
  2.1 0.9 copy-done
  3.7 3.8 %collective-permute-start.1 = (bf16[2,16,6144]{2,1,0:T(8,128)(2,1)S(1)}, bf16[2,16,6144]{2,1,0:T(8,128)(2,1)S(1)}, u32[]{:S(2)}, u32[]{:S(2)}) collective-permute-start(bf16[2,16,6144]{2,1,0:T(8,128)(2,1)S(1)} %place.3.rest_0_), channel_id=1, source_target_pairs={{0,64},{8,40},{16,80},{24,56},{32,96},{40,8},{48,112},{56,24},{64,... | collective-permute-start | bytes 1179656 | tf_op jit(solution)/shard_map/ppermute | solution.py:299
  7.4 0.7 collective-permute-start.5
  8.2 2.5 %collective-permute-start.3 = (bf16[2,16,6144]{2,1,0:T(8,128)(2,1)S(1)}, bf16[2,16,6144]{2,1,0:T(8,128)(2,1)S(1)}, u32[]{:S(2)}, u32[]{:S(2)}) collective-permute-start(bf16[2,16,6144]{2,1,0:T(8,128)(2,1)S(1)} %place.3.rest_0_), channel_id=1, source_target_pairs={{0,112},{8,88},{16,64},{24,104},{32,80},{40,120},{48,96},{56,72},{... | collective-permute-start | bytes 1179656 | tf_op jit(solution)/shard_map/ppermute | solution.py:299
  10.6 6.5 %load.1 = (bf16[48,12,128,128]{3,2,1,0:T(8,128)(2,1)S(1)}, f32[8,128]{1,0:T(8,128)S(1)}) custom-call(bf16[48,12,128,128]{3,2,1,0:T(8,128)(2,1)} %values.1, bf16[2,16,6144]{2,1,0:T(8,128)(2,1)S(1)} %place.3.rest_0_), custom_call_target="tpu_custom_call" | custom-call | bytes 37748736 | tf_op jit(solution)/shard_map/load/pallas_call | solution.py:302
  17.6 4.1 %collective-permute-done.5.rest_6_ = bf16[2,16,6144]{2,1,0:T(8,128)(2,1)S(1)} collective-permute-done((bf16[2,16,6144]{2,1,0:T(8,128)(2,1)S(1)}, bf16[2,16,6144]{2,1,0:T(8,128)(2,1)S(1)}, u32[]{:S(2)}, u32[]{:S(2)}) %collective-permute-start.5) | collective-permute-done | bytes 393248 | tf_op jit(solution)/shard_map/ppermute | solution.py:299
  21.6 3.2 %collective-permute-start.6 = (bf16[2,16,6144]{2,1,0:T(8,128)(2,1)S(1)}, bf16[2,16,6144]{2,1,0:T(8,128)(2,1)S(1)}, u32[]{:S(2)}, u32[]{:S(2)}) collective-permute-start(bf16[2,16,6144]{2,1,0:T(8,128)(2,1)S(1)} %collective-permute-done.5.rest_6_), channel_id=1, source_target_pairs={{0,8},{8,0},{16,24},{24,16},{32,40},{40,32},{48,56},{56,48},{64,72... | collective-permute-start | bytes 1179656 | tf_op jit(solution)/shard_map/ppermute | solution.py:324
  27.6 3.7 %mix.1 = bf16[8,16,2816]{2,1,0:T(8,128)(2,1)S(1)} custom-call(s32[12,48]{1,0:T(8,128)} %bitcast.5, s32[48]{0:T(128)} %counts_in.3, bf16[48,12,128,128]{3,2,1,0:T(8,128)(2,1)S(1)} %get-tuple-element.18.values, bf16[32,6144]{1,0:T(8,128)(2,1)S(1)} %copy-done.2, bf16[16,256]{1,0:T(8,128)(2,1)S(1)} %copy-done.4, f32[1,32]{1,0:T(1,128)S(1)} %bitcast.4, ...), custom_call_target="tpu_custom_call" | custom-call | tf_op jit(solution)/shard_map/mix/pallas_call | solution.py:331
  31.3 16.1 %all_to_all.10.both = bf16[8,16,2816]{2,1,0:T(8,128)(2,1)S(1)} all-to-all(bf16[8,16,2816]{2,1,0:T(8,128)(2,1)S(1)} %mix.1), channel_id=1, replica_groups=mesh['node'=16,'feat'=8] {'feat'}, dimensions={0} | all-to-all | bytes 1441792 | tf_op jit(solution)/shard_map/all_to_all | solution.py:341
  47.4 0.7 dense.1
  48.1 13.4 %all_to_all.11.grads = bf16[8,16,2560]{2,1,0:T(8,128)(2,1)S(1)} all-to-all(bf16[8,16,2560]{2,1,0:T(8,128)(2,1)S(1)} %dense.1), channel_id=1, replica_groups=mesh['node'=16,'feat'=8] {'feat'}, dimensions={0} | all-to-all | bytes 1310720 | tf_op jit(solution)/shard_map/all_to_all | solution.py:352
  61.5 6.9 %spread.1 = (bf16[32,6144]{1,0:T(8,128)(2,1)}, bf16[5,16,6400]{2,1,0:T(8,128)(2,1)S(1)}, bf16[5,16,6400]{2,1,0:T(8,128)(2,1)S(1)}, bf16[3,16,6400]{2,1,0:T(8,128)(2,1)S(1)}, bf16[3,16,6400]{2,1,0:T(8,128)(2,1)S(1)}) custom-call(s32[12,48]{1,0:T(8,128)} %bitcast.6, s32[48]{0:T(128)} %counts_in.3, bf16[48,12,128,128]{3,2,1,0:T(8,128)(2,1)S(1)} %get-tuple-element.18.values, ...), custom_call_target="tpu_custom_call" | custom-call | tf_op jit(solution)/shard_map/spread/pallas_call | solution.py:355
  68.4 2.6 %collective-permute-start.9 = (bf16[5,16,6400]{2,1,0:T(8,128)(2,1)S(1)}, bf16[5,16,6400]{2,1,0:T(8,128)(2,1)S(1)}, u32[]{:S(2)}, u32[]{:S(2)}) collective-permute-start(bf16[5,16,6400]{2,1,0:T(8,128)(2,1)S(1)} %get-tuple-element.23), channel_id=1, source_target_pairs={{0,8},{8,0},{16,24},{24,16},{32,40},{40,32},{48,56},{56,48},{64,72... | collective-permute-start | bytes 3072008 | tf_op jit(solution)/shard_map/ppermute | solution.py:366
  70.9 2.3 %collective-permute-done.9.other = bf16[5,16,6400]{2,1,0:T(8,128)(2,1)S(1)} collective-permute-done((bf16[5,16,6400]{2,1,0:T(8,128)(2,1)S(1)}, bf16[5,16,6400]{2,1,0:T(8,128)(2,1)S(1)}, u32[]{:S(2)}, u32[]{:S(2)}) %collective-permute-start.9) | collective-permute-done | bytes 1024032 | tf_op jit(solution)/shard_map/ppermute | solution.py:366
  73.9 1.5 %collective-permute-start.11 = (bf16[16,6400]{1,0:T(8,128)(2,1)S(1)}, bf16[16,6400]{1,0:T(8,128)(2,1)S(1)}, u32[]{:S(2)}, u32[]{:S(2)}) collective-permute-start(bf16[16,6400]{1,0:T(8,128)(2,1)S(1)} %get-tuple-element.26), channel_id=1, source_target_pairs={{0,32},{8,72},{16,48},{24,88},{32,0},{40,104},{48,16},{56,120},{64... | collective-permute-start | bytes 614408 | tf_op jit(solution)/shard_map/ppermute | solution.py:299
  75.4 2.8 %collective-permute-start.13 = (bf16[2,16,6400]{2,1,0:T(8,128)(2,1)S(1)}, bf16[2,16,6400]{2,1,0:T(8,128)(2,1)S(1)}, u32[]{:S(2)}, u32[]{:S(2)}) collective-permute-start(bf16[2,16,6400]{2,1,0:T(8,128)(2,1)S(1)} %get-tuple-element.29), channel_id=1, source_target_pairs={{0,16},{8,56},{16,32},{24,8},{32,48},{40,24},{48,0},{56,40},{64,80... | collective-permute-start | bytes 1228808 | tf_op jit(solution)/shard_map/ppermute | solution.py:299
  78.1 1.3 %collective-permute-start.14 = (bf16[2,16,6400]{2,1,0:T(8,128)(2,1)S(1)}, bf16[2,16,6400]{2,1,0:T(8,128)(2,1)S(1)}, u32[]{:S(2)}, u32[]{:S(2)}) collective-permute-start(bf16[2,16,6400]{2,1,0:T(8,128)(2,1)S(1)} %get-tuple-element.30), channel_id=1, source_target_pairs={{0,80},{8,120},{16,96},{24,72},{32,112},{40,88},{48,64},{56,104},{... | collective-permute-start | bytes 1228808 | tf_op jit(solution)/shard_map/ppermute | solution.py:299
  79.4 0.8 collective-permute-done.11.forwarded
  81.1 12.6 %collective-permute-done.13.third = bf16[2,16,6400]{2,1,0:T(8,128)(2,1)S(1)} collective-permute-done((bf16[2,16,6400]{2,1,0:T(8,128)(2,1)S(1)}, bf16[2,16,6400]{2,1,0:T(8,128)(2,1)S(1)}, u32[]{:S(2)}, u32[]{:S(2)}) %collective-permute-start.13) | collective-permute-done | bytes 409632 | tf_op jit(solution)/shard_map/ppermute | solution.py:299
  93.7 1.0 %collective-permute-done.12.first = bf16[2,16,6400]{2,1,0:T(8,128)(2,1)S(1)} collective-permute-done((bf16[2,16,6400]{2,1,0:T(8,128)(2,1)S(1)}, bf16[2,16,6400]{2,1,0:T(8,128)(2,1)S(1)}, u32[]{:S(2)}, u32[]{:S(2)}) %collective-permute-start.12) | collective-permute-done | bytes 409632 | tf_op jit(solution)/shard_map/ppermute | solution.py:299
  94.9 0.9 collective-permute-start.15
  95.8 1.1 %collective-permute-done.15.handed = bf16[16,6400]{1,0:T(8,128)(2,1)S(1)} collective-permute-done((bf16[16,6400]{1,0:T(8,128)(2,1)S(1)}, bf16[16,6400]{1,0:T(8,128)(2,1)S(1)}, u32[]{:S(2)}, u32[]{:S(2)}) %collective-permute-start.15) | collective-permute-done | bytes 204832 | tf_op jit(solution)/shard_map/ppermute | solution.py:396
  96.9 0.8 last.1
  (33 shorter events, 5.3 us)
Async XLA Ops:
  0.6 2.8 %collective-permute-start = (bf16[16,6144]{1,0:T(8,128)(2,1)}, bf16[16,6144]{1,0:T(8,128)(2,1)S(1)}, u32[]{:S(2)}, u32[]{:S(2)}) collective-permute-start(bf16[16,6144]{1,0:T(8,128)(2,1)} %rest_0_.1), channel_id=1, source_target_pairs={{0,8},{8,0},{16,24},{24,16},{32,40},{40,32},{48,56},{56,48},{64,72... | collective-permute-start | bytes 589832 | tf_op jit(solution)/shard_map/ppermute | solution.py:284
  2.1 0.9 copy-start
  3.1 24.5 %copy-start.1 = (bf16[16,6144]{1,0:T(8,128)(2,1)S(1)}, bf16[16,6144]{1,0:T(8,128)(2,1)}, u32[]{:S(2)}) copy-start(bf16[16,6144]{1,0:T(8,128)(2,1)} %rest_0_.1) | copy-start | bytes 589828
  3.1 24.5 %copy-start.2 = (bf16[32,6144]{1,0:T(8,128)(2,1)S(1)}, bf16[32,6144]{1,0:T(8,128)(2,1)}, u32[]{:S(2)}) copy-start(bf16[32,6144]{1,0:T(8,128)(2,1)} %cotangent.1) | copy-start | bytes 1179652
  3.1 24.5 %copy-start.4 = (bf16[16,256]{1,0:T(8,128)(2,1)S(1)}, bf16[16,256]{1,0:T(8,128)(2,1)}, u32[]{:S(2)}) copy-start(bf16[16,256]{1,0:T(8,128)(2,1)} %weight.1) | copy-start | bytes 24580
  3.1 24.5 %copy-start.5 = (f32[32]{0:T(128)S(1)}, f32[32]{0:T(128)}, u32[]{:S(2)}) copy-start(f32[32]{0:T(128)} %param.10) | copy-start | bytes 388
  3.7 43.7 %copy-start.3 = (s32[6144]{0:T(1024)S(1)}, s32[6144]{0:T(1024)}, u32[]{:S(2)}) copy-start(s32[6144]{0:T(1024)} %param.14) | copy-start | bytes 73732
  3.7 13.5 %collective-permute-start.1 = (bf16[2,16,6144]{2,1,0:T(8,128)(2,1)S(1)}, bf16[2,16,6144]{2,1,0:T(8,128)(2,1)S(1)}, u32[]{:S(2)}, u32[]{:S(2)}) collective-permute-start(bf16[2,16,6144]{2,1,0:T(8,128)(2,1)S(1)} %place.3.rest_0_), channel_id=1, source_target_pairs={{0,64},{8,40},{16,80},{24,56},{32,96},{40,8},{48,112},{56,24},{64,... | collective-permute-start | bytes 1179656 | tf_op jit(solution)/shard_map/ppermute | solution.py:299
  7.4 14.2 %collective-permute-start.5 = (bf16[2,16,6144]{2,1,0:T(8,128)(2,1)S(1)}, bf16[2,16,6144]{2,1,0:T(8,128)(2,1)S(1)}, u32[]{:S(2)}, u32[]{:S(2)}) collective-permute-start(bf16[2,16,6144]{2,1,0:T(8,128)(2,1)S(1)} %place.3.rest_0_), channel_id=1, source_target_pairs={{0,48},{8,24},{16,0},{24,40},{32,16},{40,56},{48,32},{56,8},{64,11... | collective-permute-start | bytes 1179656 | tf_op jit(solution)/shard_map/ppermute | solution.py:299
  8.2 16.7 %collective-permute-start.3 = (bf16[2,16,6144]{2,1,0:T(8,128)(2,1)S(1)}, bf16[2,16,6144]{2,1,0:T(8,128)(2,1)S(1)}, u32[]{:S(2)}, u32[]{:S(2)}) collective-permute-start(bf16[2,16,6144]{2,1,0:T(8,128)(2,1)S(1)} %place.3.rest_0_), channel_id=1, source_target_pairs={{0,112},{8,88},{16,64},{24,104},{32,80},{40,120},{48,96},{56,72},{... | collective-permute-start | bytes 1179656 | tf_op jit(solution)/shard_map/ppermute | solution.py:299
  17.2 8.2 %collective-permute-start.7 = (bf16[16,6144]{1,0:T(8,128)(2,1)S(1)}, bf16[16,6144]{1,0:T(8,128)(2,1)S(1)}, u32[]{:S(2)}, u32[]{:S(2)}) collective-permute-start(bf16[16,6144]{1,0:T(8,128)(2,1)S(1)} %pick.1), channel_id=1, source_target_pairs={{0,32},{8,72},{16,48},{24,88},{32,0},{40,104},{48,16},{56,120},{64... | collective-permute-start | bytes 589832 | tf_op jit(solution)/shard_map/ppermute | solution.py:299
  21.6 4.6 %collective-permute-start.6 = (bf16[2,16,6144]{2,1,0:T(8,128)(2,1)S(1)}, bf16[2,16,6144]{2,1,0:T(8,128)(2,1)S(1)}, u32[]{:S(2)}, u32[]{:S(2)}) collective-permute-start(bf16[2,16,6144]{2,1,0:T(8,128)(2,1)S(1)} %collective-permute-done.5.rest_6_), channel_id=1, source_target_pairs={{0,8},{8,0},{16,24},{24,16},{32,40},{40,32},{48,56},{56,48},{64,72... | collective-permute-start | bytes 1179656 | tf_op jit(solution)/shard_map/ppermute | solution.py:324
  24.9 1.9 %collective-permute-start.4 = (bf16[2,16,6144]{2,1,0:T(8,128)(2,1)S(1)}, bf16[2,16,6144]{2,1,0:T(8,128)(2,1)S(1)}, u32[]{:S(2)}, u32[]{:S(2)}) collective-permute-start(bf16[2,16,6144]{2,1,0:T(8,128)(2,1)S(1)} %collective-permute-done.3.rest_4_), channel_id=1, source_target_pairs={{0,8},{8,0},{16,24},{24,16},{32,40},{40,32},{48,56},{56,48},{64,72... | collective-permute-start | bytes 1179656 | tf_op jit(solution)/shard_map/ppermute | solution.py:324
  24.9 2.5 %collective-permute-start.2 = (bf16[2,16,6144]{2,1,0:T(8,128)(2,1)S(1)}, bf16[2,16,6144]{2,1,0:T(8,128)(2,1)S(1)}, u32[]{:S(2)}, u32[]{:S(2)}) collective-permute-start(bf16[2,16,6144]{2,1,0:T(8,128)(2,1)S(1)} %collective-permute-done.1.pair.rest_2_), channel_id=1, source_target_pairs={{0,8},{8,0},{16,24},{24,16},{32,40},{40,32},{48,56},{56,48},{64,72... | collective-permute-start | bytes 1179656 | tf_op jit(solution)/shard_map/ppermute | solution.py:324
  25.4 2.2 %collective-permute-start.8 = (bf16[16,6144]{1,0:T(8,128)(2,1)S(1)}, bf16[16,6144]{1,0:T(8,128)(2,1)S(1)}, u32[]{:S(2)}, u32[]{:S(2)}) collective-permute-start(bf16[16,6144]{1,0:T(8,128)(2,1)S(1)} %collective-permute-done.7.rest_8_), channel_id=1, source_target_pairs={{0,8},{8,0},{16,24},{24,16},{32,40},{40,32},{48,56},{56,48},{64,72... | collective-permute-start | bytes 589832 | tf_op jit(solution)/shard_map/ppermute | solution.py:324
  68.4 4.8 %collective-permute-start.9 = (bf16[5,16,6400]{2,1,0:T(8,128)(2,1)S(1)}, bf16[5,16,6400]{2,1,0:T(8,128)(2,1)S(1)}, u32[]{:S(2)}, u32[]{:S(2)}) collective-permute-start(bf16[5,16,6400]{2,1,0:T(8,128)(2,1)S(1)} %get-tuple-element.23), channel_id=1, source_target_pairs={{0,8},{8,0},{16,24},{24,16},{32,40},{40,32},{48,56},{56,48},{64,72... | collective-permute-start | bytes 3072008 | tf_op jit(solution)/shard_map/ppermute | solution.py:366
  73.4 6.9 %collective-permute-start.10 = (bf16[3,16,6400]{2,1,0:T(8,128)(2,1)S(1)}, bf16[3,16,6400]{2,1,0:T(8,128)(2,1)S(1)}, u32[]{:S(2)}, u32[]{:S(2)}) collective-permute-start(bf16[3,16,6400]{2,1,0:T(8,128)(2,1)S(1)} %get-tuple-element.25), channel_id=1, source_target_pairs={{0,8},{8,0},{16,24},{24,16},{32,40},{40,32},{48,56},{56,48},{64,72... | collective-permute-start | bytes 1843208 | tf_op jit(solution)/shard_map/ppermute | solution.py:378
  73.9 6.4 %collective-permute-start.11 = (bf16[16,6400]{1,0:T(8,128)(2,1)S(1)}, bf16[16,6400]{1,0:T(8,128)(2,1)S(1)}, u32[]{:S(2)}, u32[]{:S(2)}) collective-permute-start(bf16[16,6400]{1,0:T(8,128)(2,1)S(1)} %get-tuple-element.26), channel_id=1, source_target_pairs={{0,32},{8,72},{16,48},{24,88},{32,0},{40,104},{48,16},{56,120},{64... | collective-permute-start | bytes 614408 | tf_op jit(solution)/shard_map/ppermute | solution.py:299
  75.4 18.4 %collective-permute-start.13 = (bf16[2,16,6400]{2,1,0:T(8,128)(2,1)S(1)}, bf16[2,16,6400]{2,1,0:T(8,128)(2,1)S(1)}, u32[]{:S(2)}, u32[]{:S(2)}) collective-permute-start(bf16[2,16,6400]{2,1,0:T(8,128)(2,1)S(1)} %get-tuple-element.29), channel_id=1, source_target_pairs={{0,16},{8,56},{16,32},{24,8},{32,48},{40,24},{48,0},{56,40},{64,80... | collective-permute-start | bytes 1228808 | tf_op jit(solution)/shard_map/ppermute | solution.py:299
  78.1 15.6 %collective-permute-start.14 = (bf16[2,16,6400]{2,1,0:T(8,128)(2,1)S(1)}, bf16[2,16,6400]{2,1,0:T(8,128)(2,1)S(1)}, u32[]{:S(2)}, u32[]{:S(2)}) collective-permute-start(bf16[2,16,6400]{2,1,0:T(8,128)(2,1)S(1)} %get-tuple-element.30), channel_id=1, source_target_pairs={{0,80},{8,120},{16,96},{24,72},{32,112},{40,88},{48,64},{56,104},{... | collective-permute-start | bytes 1228808 | tf_op jit(solution)/shard_map/ppermute | solution.py:299
  80.4 14.3 %collective-permute-start.12 = (bf16[2,16,6400]{2,1,0:T(8,128)(2,1)S(1)}, bf16[2,16,6400]{2,1,0:T(8,128)(2,1)S(1)}, u32[]{:S(2)}, u32[]{:S(2)}) collective-permute-start(bf16[2,16,6400]{2,1,0:T(8,128)(2,1)S(1)} %get-tuple-element.28), channel_id=1, source_target_pairs={{0,64},{8,40},{16,80},{24,56},{32,96},{40,8},{48,112},{56,24},{64,... | collective-permute-start | bytes 1228808 | tf_op jit(solution)/shard_map/ppermute | solution.py:299
  94.9 2.0 %collective-permute-start.15 = (bf16[16,6400]{1,0:T(8,128)(2,1)S(1)}, bf16[16,6400]{1,0:T(8,128)(2,1)S(1)}, u32[]{:S(2)}, u32[]{:S(2)}) collective-permute-start(bf16[16,6400]{1,0:T(8,128)(2,1)S(1)} %hand.1), channel_id=1, source_target_pairs={{0,8},{8,0},{16,24},{24,16},{32,40},{40,32},{48,56},{56,48},{64,72... | collective-permute-start | bytes 614408 | tf_op jit(solution)/shard_map/ppermute | solution.py:396
